TPU v7x, 256 devices: a whole 4x4x8 slice. The times are simulated.
256 devices in a mesh: group: 4 (over x), dev: 64 (over y, z, core).
Axes of the slice: x: 4, y: 4, z: 8, core: 2. Of those that a mesh axis runs over, the one named last changes fastest.
Arguments:
- node_aggregate: bfloat16 [16384, 512], P(('group', 'dev')), may hold values from -6 to 6
- weight: bfloat16 [512, 512], replicated, may hold values from -0.25 to 0.25
- tiles: bfloat16 [8192, 128, 128], P(('group', 'dev'))
- tile_src: int32 [8192], P(('group', 'dev')), may hold values from 0 to 31
- tile_dst: int32 [8192], P(('group', 'dev')), may hold values from 0 to 1
- tile_count: int32 [256], P(('group', 'dev')), may hold values from 8 to 32
- pair_owner: int32 [2097152, 2], P(('group', 'dev')), may hold values from 0 to 63, all different within a row; in each aligned block of 8192 rows (0 to 8191, 8192 to 16383, ...) at most 512 rows name the same one
- pair_row: int32 [2097152, 2], P(('group', 'dev')), may hold values from 0 to 63
Outputs:
- feature_grad: bfloat16 [16384, 512], P(('group', 'dev'))
- weight_grad: float32 [512, 512], replicated
Inputs may be any that keep to these rules, and one draw needn't show every extreme that they name: `pair_owner`: among the 16384 pair ends held by one device, at most 512 name one owner, and the two ends of a pair name different owners.
All inputs are finite; a program needn't handle non-finite values.
Results may differ from a plain program's by a relative error of at most 0.0032.
The roundings to bfloat16 on the way count: a program that leaves them out, or rounds other values in their place, can miss the bound.
Values may be sent and summed in bfloat16 or wider, within the bound.
No kernel may reach another device: no remote copies, remote signals or barrier semaphores. Data moves between devices by JAX's collectives and lax.ppermute only.
A program may use at most 128 MiB of HBM per device.

v0:
```python
import functools
import math

import jax
import jax.numpy as jnp
from jax import lax
from jax.experimental import pallas as pl
from jax.experimental.pallas import tpu as pltpu
from jax.sharding import Mesh, PartitionSpec as P

NX, NY, NZ, NC = 4, 4, 8, 2
NDEV = NY * NZ * NC
ROWS = 64
F = 512
CAP = 512
BF = jnp.bfloat16
F32 = jnp.float32
I32 = jnp.int32
POS = 4096.0
SUB = 256
SUBS = 8
NT = (((1,), (1,)), ((), ()))
TN = (((0,), (0,)), ((), ()))
VMEM = pl.BlockSpec(memory_space=pltpu.VMEM)
SMEM = pl.BlockSpec(memory_space=pltpu.SMEM)
ANY = pl.BlockSpec(memory_space=pl.ANY)


TOKEN = jax.ShapeDtypeStruct((8, 128), F32)


def params(mib=16):
    return pltpu.CompilerParams(vmem_limit_bytes=mib << 20)


def activation(values):
    return jax.nn.gelu(values)


def bucket_kernel(owner_ref, row_ref, out_ref, token_ref, acc):
    token_ref[...] = jnp.zeros_like(token_ref)
    total = owner_ref.shape[1]
    positives = total // 5
    step = SUB * SUBS
    tri = (
        lax.broadcasted_iota(I32, (SUB, SUB), 0) < lax.broadcasted_iota(I32, (SUB, SUB), 1)
    ).astype(BF)
    acc[...] = jnp.zeros_like(acc)
    base = jnp.zeros((NDEV, 1), F32)
    for end in range(2):

        def body(j, base, end=end):
            ranks, parts = [], [[], [], [], []]
            for s in range(SUBS):
                start = pl.multiple_of(j * step + s * SUB, SUB)
                here = pl.ds(start, SUB)
                own = owner_ref[end : end + 1, here]
                same = lax.broadcasted_iota(I32, (NDEV, SUB), 0) == own
                hot = same.astype(F32)
                prefix = jnp.dot(hot.astype(BF), tri, preferred_element_type=F32)
                ranks.append(jnp.sum(hot * (prefix + base), axis=0, keepdims=True))
                base = base + jnp.sum(hot, axis=1, keepdims=True)
                place = start + lax.broadcasted_iota(I32, (1, SUB), 1)
                weight = jnp.where(place < positives, POS, 1.0)
                values = [
                    weight,
                    row_ref[end : end + 1, here].astype(F32),
                    owner_ref[1 - end : 2 - end, here].astype(F32),
                    row_ref[1 - end : 2 - end, here].astype(F32),
                ]
                for v in range(4):
                    parts[v].append((hot * values[v]).astype(BF))
            left = jnp.concatenate([jnp.concatenate(p, axis=1) for p in parts], axis=0)
            rank = jnp.concatenate(ranks, axis=1).astype(I32)
            right = (lax.broadcasted_iota(I32, (CAP, step), 0) == rank).astype(F32).astype(BF)
            acc[...] += lax.dot_general(left, right, NT, preferred_element_type=F32)
            return base

        base = lax.fori_loop(0, total // step, body, base)
    for v in range(4):
        out_ref[:, v * CAP : (v + 1) * CAP] = acc[v * NDEV : (v + 1) * NDEV, :].astype(BF)


def count_kernel(first, coord_ref, _, recv_ref, *refs):
    out_ref, token_ref, left_at, right_at, weight_at = refs[-5:]
    token_ref[...] = jnp.zeros_like(token_ref)
    y, c = coord_ref[0], coord_ref[1]
    weight_at[...] = recv_ref[:, 0:CAP].astype(F32)
    own_row = recv_ref[:, CAP : 2 * CAP].astype(F32).astype(I32)
    owner = recv_ref[:, 2 * CAP : 3 * CAP].astype(F32).astype(I32)
    row = recv_ref[:, 3 * CAP : 4 * CAP].astype(F32).astype(I32)
    piece = ((owner & 1) ^ c) * NY + (((owner >> 4) - y) & (NY - 1))
    left_at[...] = piece * ROWS + own_row
    right_at[...] = ((owner >> 1) & (NZ - 1)) * ROWS + row
    if first:
        out_ref[...] = jnp.zeros_like(out_ref)
    else:
        out_ref[...] = refs[0][...]
    group = 4

    def body(g, carry):
        total = None
        for s in range(group):
            here = pl.ds(g * group + s, 1)
            spots = lax.broadcasted_iota(I32, (CAP, CAP), 0)
            left = jnp.where(spots == left_at[here, :], weight_at[here, :], 0.0).astype(BF)
            right = jnp.where(spots == right_at[here, :], 1.0, 0.0).astype(BF)
            term = lax.dot_general(left, right, NT, preferred_element_type=F32)
            total = term if total is None else total + term
        ones = jnp.floor(total * (1.0 / POS))
        out_ref[0] += total - (POS - 1.0) * ones
        out_ref[1] += ones
        return carry

    half = NDEV // group // 2
    lax.fori_loop(0 if first else half, half if first else 2 * half, body, 0)


def grad_kernel(scale, _, own_ref, count_ref, *refs):
    pieces, out_ref = refs[:-1], refs[-1]
    own = own_ref[...]
    total = jnp.zeros((ROWS, F), F32)
    for k in range(NY * NC):
        nodes = pieces[k][...]
        score = lax.dot_general(own, nodes, NT, preferred_element_type=F32) / math.sqrt(F)
        here = slice(k * ROWS, (k + 1) * ROWS)
        grad = (count_ref[0, here, :] * jax.nn.sigmoid(score) - count_ref[1, here, :]) * scale
        high = grad.astype(BF)
        low = (grad - high.astype(F32)).astype(BF)
        total += jnp.dot(high, nodes, preferred_element_type=F32)
        total += jnp.dot(low, nodes, preferred_element_type=F32)
    out_ref[...] = total


def tiles_kernel(meta_ref, own_ref, other_ref, high_ref, low_ref, token_ref, acc):
    token_ref[...] = jnp.zeros_like(token_ref)
    slots = own_ref.shape[0]
    acc[...] = jnp.zeros_like(acc)
    for part, tiles_ref in enumerate((own_ref, other_ref)):

        def body(s, carry, part=part, tiles_ref=tiles_ref):
            rows = pl.ds(pl.multiple_of(meta_ref[part, s] * ROWS, ROWS), ROWS)
            dst = meta_ref[part, slots + s]
            columns = pl.ds(pl.multiple_of(part * 256 + dst * 128, 128), 128)
            acc[rows, columns] += tiles_ref[s].astype(F32)
            return carry

        lax.fori_loop(0, meta_ref[part, 2 * slots], body, 0)

    def split(k, carry):
        rows = pl.ds(pl.multiple_of(k * 128, 128), 128)
        value = acc[rows, :]
        high = value.astype(BF)
        high_ref[rows, :] = high
        low_ref[rows, :] = (value - high.astype(F32)).astype(BF)
        return carry

    lax.fori_loop(0, acc.shape[0] // 128, split, 0)


def spread_kernel(coord_ref, weight_ref, high_ref, low_ref, pre_ref, *refs):
    out_refs, token_ref, pre = refs[:-2], refs[-2], refs[-1]
    token_ref[...] = jnp.zeros_like(token_ref)
    y, c = coord_ref[0], coord_ref[1]
    for k in range(NX * NC):
        place = pl.multiple_of(((k % NC) ^ c) * NX * ROWS + (k // NC) * ROWS, ROWS)
        pre[pl.ds(place, ROWS), :] = pre_ref[k]
    agg = lax.dot_general(pre[...], weight_ref[...], NT, preferred_element_type=F32).astype(BF)
    size = NZ * ROWS
    for k in range(NY):
        rows = pl.ds(pl.multiple_of(((y + k) & (NY - 1)) * size, size), size)
        part = jnp.dot(high_ref[rows, :], agg, preferred_element_type=F32)
        part += jnp.dot(low_ref[rows, :], agg, preferred_element_type=F32)
        out_refs[k][...] = part.astype(out_refs[k].dtype)


def terms_kernel(_, pre_ref, node_ref, terms_ref):
    total = jnp.zeros(terms_ref.shape, F32)
    for k in range(NX * NC):
        total += lax.dot_general(node_ref[k], pre_ref[k], TN, preferred_element_type=F32)
    terms_ref[...] = total


def swap(values):
    return lax.ppermute(values, "c", [(0, 1), (1, 0)])


def shift(values, axis, size, step):
    return lax.ppermute(values, axis, [(i, (i + step) % size) for i in range(size)])


def exchange(values, axes):
    return lax.all_to_all(values, axes, 0, 0, tiled=True)


def gather(values, axes, size):
    return exchange(jnp.broadcast_to(values[None], (size,) + values.shape), axes)


def pick(values, place):
    return lax.dynamic_index_in_dim(values, place, 0, keepdims=False)


def count(coord, token, received, *counted):
    return pl.pallas_call(
        functools.partial(count_kernel, not counted),
        out_shape=[jax.ShapeDtypeStruct((2, NY * NC * ROWS, NZ * ROWS), F32), TOKEN],
        in_specs=[SMEM, ANY, VMEM] + [VMEM] * len(counted),
        out_specs=[VMEM, VMEM],
        scratch_shapes=[
            pltpu.VMEM((NDEV, CAP), I32),
            pltpu.VMEM((NDEV, CAP), I32),
            pltpu.VMEM((NDEV, CAP), F32),
        ],
        compiler_params=params(),
        cost_estimate=pl.CostEstimate(flops=12_000_000_000, bytes_accessed=2_400_000, transcendentals=0),
        name="count",
    )(coord, token, received, *counted)


def per_device(node_aggregate, weight, tiles, tile_src, tile_dst, tile_count, pair_owner, pair_row):
    pair_total = pair_owner.shape[0]
    slots = tiles.shape[0]
    c = lax.axis_index("c")
    coord = jnp.stack([lax.axis_index("y"), c]).astype(I32)

    with jax.named_scope("hidden"):
        pre_act = jnp.dot(node_aggregate, weight, preferred_element_type=F32)
        hidden, act_back = jax.vjp(activation, pre_act)
        hidden_b = hidden.astype(BF)

    with jax.named_scope("pair_exchange"):
        ring = gather(hidden_b, "z", NZ).reshape(NZ * ROWS, F)
        ends, token = pl.pallas_call(
            bucket_kernel,
            out_shape=[jax.ShapeDtypeStruct((NDEV, 4 * CAP), BF), TOKEN],
            in_specs=[VMEM, VMEM],
            out_specs=[VMEM, VMEM],
            scratch_shapes=[pltpu.VMEM((4 * NDEV, CAP), F32)],
            compiler_params=params(),
            cost_estimate=pl.CostEstimate(flops=9_000_000_000, bytes_accessed=400_000, transcendentals=0),
            name="bucket",
        )(pair_owner.T, pair_row.T)
        ring, ends = lax.optimization_barrier((ring, ends))
        planes = [ring] + [shift(ring, "y", NY, -k) for k in range(1, NY)]
        received = exchange(ends, ("y", "z", "c"))
        counted, token = count(coord, token, received)
        columns = node_aggregate.reshape(ROWS, NX * NC, ROWS).transpose(1, 0, 2)
        planes, columns, token = lax.optimization_barrier((planes, columns, token))
        planes = planes + [swap(plane) for plane in planes]
        counted, _ = count(coord, token, received, counted)

    with jax.named_scope("tile_matrix"):
        halves = tiles.reshape(slots, 2, ROWS, tiles.shape[2]).transpose(1, 0, 2, 3)
        own_half = pick(halves, c)
        other_half = swap(pick(halves, 1 - c))
        meta = jnp.concatenate([tile_src, tile_dst, tile_count]).astype(I32)
        metas = jnp.stack([meta, swap(meta)])
        high, low, token = pl.pallas_call(
            tiles_kernel,
            out_shape=[jax.ShapeDtypeStruct((NY * NZ * ROWS, 512), BF)] * 2 + [TOKEN],
            in_specs=[SMEM, VMEM, VMEM],
            out_specs=[VMEM] * 3,
            scratch_shapes=[pltpu.VMEM((NY * NZ * ROWS, 512), F32)],
            compiler_params=params(),
            cost_estimate=pl.CostEstimate(flops=3_000_000_000, bytes_accessed=5_000_000, transcendentals=0),
            name="tile_sum",
        )(metas, own_half, other_half)
        nodes = exchange(columns, ("x", "c"))

    with jax.named_scope("hidden_grad"):
        own, token, nodes = lax.optimization_barrier((hidden_b, token, nodes))
        hidden_grad = pl.pallas_call(
            functools.partial(grad_kernel, ROWS / (2.0 * pair_total)),
            out_shape=jax.ShapeDtypeStruct((ROWS, F), F32),
            in_specs=[ANY] + [VMEM] * (2 + len(planes)),
            out_specs=VMEM,
            compiler_params=params(),
            cost_estimate=pl.CostEstimate(flops=5_000_000_000, bytes_accessed=6_000_000, transcendentals=262144),
            name="pair_grad",
        )(token, own, counted, *planes)
        pre_grad = act_back(hidden_grad)[0].astype(BF)

    with jax.named_scope("spread"):
        pre_parts = gather(pre_grad, ("x", "c"), NX * NC)
        keep, *send, token = pl.pallas_call(
            spread_kernel,
            out_shape=[
                jax.ShapeDtypeStruct((NZ * ROWS, F), dtype) for dtype in (F32,) + (BF,) * (NY - 1)
            ]
            + [TOKEN],
            in_specs=[SMEM] + [VMEM] * 4,
            out_specs=[VMEM] * (NY + 1),
            scratch_shapes=[pltpu.VMEM((NC * NX * ROWS, F), BF)],
            compiler_params=params(),
            cost_estimate=pl.CostEstimate(flops=5_000_000_000, bytes_accessed=8_000_000, transcendentals=0),
            name="spread",
        )(coord, weight, high, low, pre_parts)
        pre_parts, token = lax.optimization_barrier((pre_parts, token))
        terms = pl.pallas_call(
            terms_kernel,
            out_shape=jax.ShapeDtypeStruct((ROWS, F), F32),
            in_specs=[ANY] + [VMEM] * 2,
            out_specs=VMEM,
            compiler_params=params(),
            cost_estimate=pl.CostEstimate(flops=1_000_000_000, bytes_accessed=700_000, transcendentals=0),
            name="weight_terms",
        )(token, pre_parts, nodes)

    with jax.named_scope("sums"):
        chips = NY * NZ
        part = keep
        for k in (2, 1, 3):
            part = part + shift(send[k - 1], "y", NY, k).astype(F32)
        part = part.astype(BF)
        shares = exchange(terms.reshape(chips, ROWS // chips, F), ("y", "z"))
        share = jnp.sum(shares, axis=0)
        block = gather(share, ("y", "z"), chips).reshape(ROWS, F)
        part, block = lax.optimization_barrier((part, block))
        rings = exchange(part.reshape(NZ, ROWS, F), "z").astype(F32)
        other = swap(block)
        low_first = c == 0
        pair = jnp.stack([jnp.where(low_first, block, other), jnp.where(low_first, other, block)])
        x = lax.axis_index("x")
        blocks = jnp.zeros((NX,) + pair.shape, F32)
        blocks = lax.dynamic_update_index_in_dim(blocks, pair, x, 0)
        for k in range(1, NX):
            blocks = lax.dynamic_update_index_in_dim(
                blocks, shift(pair, "x", NX, -k), (x + k) & (NX - 1), 0
            )
        weight_grad = blocks.reshape(F, F)
        feature_grad = jnp.sum(rings, axis=0).astype(BF)
    return (feature_grad, weight_grad)


def solution(mesh):
    grid = Mesh(mesh.devices.reshape(NX, NY, NZ, NC), ("x", "y", "z", "c"))
    split = P(("x", "y", "z", "c"))
    return jax.shard_map(
        per_device,
        mesh=grid,
        in_specs=(split, P(), split, split, split, split, split, split),
        out_specs=(split, P()),
        check_vma=False,
    )
```

profile of v0, /device:TPU:1, one launch (start us, length us, event | category | flops | bytes accessed | tf_op | source)
XLA Modules:
  0.0 193.4 jit_solution(14665751737363472284)
XLA Ops:
  1.4 0.7 pad_add_fusion.2
  2.1 3.3 %collective-permute-start = (s32[65]{0:T(128)S(1)}, s32[65]{0:T(128)S(1)}, u32[]{:S(2)}, u32[]{:S(2)}) collective-permute-start(s32[65]{0:T(128)S(1)} %pad_add_fusion.2), channel_id=1, source_target_pairs={{0,1},{1,0},{2,3},{3,2},{4,5},{5,4},{6,7},{7,6},{8,9},{9,8},{10,11... | collective-permute-start | bytes 788 | tf_op jit(solution)/shard_map/tile_matrix/ppermute | solution.py:185
  5.4 1.3 multiply_convert_fusion
  6.7 0.8 broadcast_in_dim.34
  7.6 6.4 %all-to-all-start = ((bf16[8,64,512]{2,1,0:T(8,128)(2,1)}), bf16[8,64,512]{2,1,0:T(8,128)(2,1)S(1)}, u32[]{:S(2)}, u32[]{:S(2)}) async-start(bf16[8,64,512]{2,1,0:T(8,128)(2,1)} %broadcast_in_dim.34), calls=%async_computation | async-start | bytes 1048576 | tf_op jit(solution)/shard_map/pair_exchange/all_to_all | solution.py:193
  14.0 0.9 dynamic-slice_bitcast_fusion
  14.9 0.3 collective-permute-start.1
  15.2 7.9 %bucket.1 = (bf16[64,2048]{1,0:T(8,128)(2,1)S(1)}, f32[8,128]{1,0:T(8,128)S(1)}) custom-call(s32[2,8192]{1,0:T(2,128)S(1)} %bitcast.48, s32[2,8192]{1,0:T(2,128)S(1)} %bitcast.49), custom_call_target="tpu_custom_call" | custom-call | flops 8999999488 | bytes 400000 | tf_op jit(solution)/shard_map/pair_exchange/bucket/pallas_call | solution.py:234
  23.1 9.0 %all-to-all-done = bf16[8,64,512]{2,1,0:T(8,128)(2,1)S(1)} async-done(((bf16[8,64,512]{2,1,0:T(8,128)(2,1)}), bf16[8,64,512]{2,1,0:T(8,128)(2,1)S(1)}, u32[]{:S(2)}, u32[]{:S(2)}) %all-to-all-start) | async-done | bytes 524320 | tf_op jit(solution)/shard_map/pair_exchange/all_to_all | solution.py:193
  32.1 0.5 broadcast.28
  32.6 0.8 reduce.1
  33.3 0.9 reshape.41
  34.3 5.5 %all-to-all-start.1 = ((bf16[64,2,1024]{2,1,0:T(2,128)(2,1)}), bf16[64,2,1024]{2,1,0:T(2,128)(2,1)S(1)}, u32[]{:S(2)}, u32[]{:S(2)}) async-start(bf16[64,2,1024]{2,1,0:T(2,128)(2,1)} %reshape.41), calls=%async_computation.1 | async-start | bytes 524288 | tf_op jit(solution)/shard_map/pair_exchange/all_to_all | solution.py:193
  39.8 0.1 fusion.9
  39.8 0.1 pad_add_fusion.1.coord_ref
  39.9 0.1 reshape.36
  40.1 2.0 %tile_sum.1 = (bf16[2048,512]{1,0:T(8,128)(2,1)S(1)}, bf16[2048,512]{1,0:T(8,128)(2,1)S(1)}, f32[8,128]{1,0:T(8,128)S(1)}) custom-call(s32[2,65]{1,0:T(2,128)S(1)} %pad_add_fusion.meta_ref, bf16[32,64,128]{2,1,0:T(8,128)(2,1)S(1)} %get-tuple-element.59.own_ref, bf16[32,64,128]{2,1,0:T(8,128)(2,1)S(1)} %collective-permute-done.1.other_ref), custom_call_target="tpu_custom_call" | custom-call | flops 3000000000 | bytes 5000000 | tf_op jit(solution)/shard_map/tile_matrix/tile_sum/pallas_call | solution.py:259
  42.2 1.4 copy-done.3
  43.5 1.3 copy-done.5
  44.9 2.7 %collective-permute-start.2 = (bf16[512,512]{1,0:T(8,128)(2,1)S(1)}, bf16[512,512]{1,0:T(8,128)(2,1)S(1)}, u32[]{:S(2)}, u32[]{:S(2)}) collective-permute-start(bf16[512,512]{1,0:T(8,128)(2,1)S(1)} %bitcast.40), channel_id=1, source_target_pairs={{0,48},{16,0},{32,16},{48,32},{1,49},{17,1},{33,17},{49,33},{2,50}... | collective-permute-start | bytes 1572872 | tf_op jit(solution)/shard_map/pair_exchange/ppermute | solution.py:189
  47.6 0.5 collective-permute-start.3
  48.1 0.8 collective-permute-start.4
  48.9 2.9 %all-to-all-done.1 = bf16[64,2,1024]{2,1,0:T(2,128)(2,1)S(1)} async-done(((bf16[64,2,1024]{2,1,0:T(2,128)(2,1)}), bf16[64,2,1024]{2,1,0:T(2,128)(2,1)S(1)}, u32[]{:S(2)}, u32[]{:S(2)}) %all-to-all-start.1) | async-done | bytes 262176 | tf_op jit(solution)/shard_map/pair_exchange/all_to_all | solution.py:193
  51.8 0.2 reshape.42
  52.0 0.2 copy.28
  52.1 11.7 %count.2 = (f32[2,512,512]{2,1,0:T(8,128)S(1)}, f32[8,128]{1,0:T(8,128)S(1)}) custom-call(s32[2]{0:T(128)S(1)} %pad_add_fusion.1.coord_ref, f32[8,128]{1,0:T(8,128)S(1)} %get-tuple-element.35._, bf16[64,2048]{1,0:T(8,128)(2,1)S(1)} %bitcast.45), custom_call_target="tpu_custom_call" | custom-call | flops 12000000000 | bytes 2400000 | tf_op jit(solution)/shard_map/pair_exchange/count/pallas_call | solution.py:205
  63.8 1.4 copy-done.9
  65.2 9.0 %collective-permute-done.4.refs_3_ = bf16[512,512]{1,0:T(8,128)(2,1)S(1)} collective-permute-done((bf16[512,512]{1,0:T(8,128)(2,1)S(1)}, bf16[512,512]{1,0:T(8,128)(2,1)S(1)}, u32[]{:S(2)}, u32[]{:S(2)}) %collective-permute-start.4) | collective-permute-done | bytes 524320 | tf_op jit(solution)/shard_map/pair_exchange/ppermute | solution.py:189
  74.2 0.8 reshape.43
  75.0 4.9 %all-to-all-start.2 = ((bf16[8,2,2048]{2,1,0:T(2,128)(2,1)}), bf16[8,2,2048]{2,1,0:T(2,128)(2,1)S(1)}, u32[]{:S(2)}, u32[]{:S(2)}) async-start(bf16[8,2,2048]{2,1,0:T(2,128)(2,1)} %reshape.43), calls=%async_computation.2 | async-start | bytes 131072 | tf_op jit(solution)/shard_map/tile_matrix/all_to_all | solution.py:193
  79.9 0.0 collective-permute-start.5
  79.9 0.5 collective-permute-start.6
  80.4 0.0 collective-permute-start.7
  80.4 0.5 collective-permute-start.8
  80.9 1.6 copy-done.10
  82.5 11.6 %count.3 = (f32[2,512,512]{2,1,0:T(8,128)S(1)}, f32[8,128]{1,0:T(8,128)}) custom-call(s32[2]{0:T(128)S(1)} %pad_add_fusion.1.coord_ref, f32[8,128]{1,0:T(8,128)S(1)} %get-tuple-element.41._, bf16[64,2048]{1,0:T(8,128)(2,1)S(1)} %bitcast.46, f32[2,512,512]{2,1,0:T(8,128)S(1)} %copy-done.10), custom_call_target="tpu_custom_call" | custom-call | flops 12000000000 | bytes 2400000 | tf_op jit(solution)/shard_map/pair_exchange/count/pallas_call | solution.py:205
  94.1 1.4 copy-done.7
  95.5 0.1 reshape.44.node_ref
  95.7 1.6 copy-done.8
  97.3 5.1 %pair_grad.1 = f32[64,512]{1,0:T(8,128)S(1)} custom-call(f32[8,128]{1,0:T(8,128)S(1)} %get-tuple-element.39._, bf16[64,512]{1,0:T(8,128)(2,1)S(1)} %get-tuple-element.40.own_ref, f32[2,512,512]{2,1,0:T(8,128)S(1)} %copy-done.8, bf16[512,512]{1,0:T(8,128)(2,1)S(1)} %bitcast.44, bf16[512,512]{1,0:T(8,128)(2,1)S(1)} %collective-permute-done.2.refs_1_, ...), custom_call_target="tpu_custom_call" | custom-call | flops 5000000000 | bytes 6000000 | tf_op jit(solution)/shard_map/hidden_grad/pair_grad/pallas_call | solution.py:273
  102.4 0.1 fusion.6
  102.6 14.0 %all_to_all.41.pre_ref = bf16[8,64,512]{2,1,0:T(8,128)(2,1)S(1)} all-to-all(bf16[8,64,512]{2,1,0:T(8,128)(2,1)S(1)} %broadcast_in_dim.35), channel_id=1, replica_groups=mesh['x'=4,'y'=4,'z'=8,'c'=2] {'x','c'}, dimensions={0} | all-to-all | bytes 1048576 | tf_op jit(solution)/shard_map/spread/all_to_all | solution.py:193
  116.6 3.2 %spread.1 = (f32[512,512]{1,0:T(8,128)S(1)}, bf16[512,512]{1,0:T(8,128)(2,1)S(1)}, bf16[512,512]{1,0:T(8,128)(2,1)S(1)}, bf16[512,512]{1,0:T(8,128)(2,1)S(1)}, f32[8,128]{1,0:T(8,128)S(1)}) custom-call(s32[2]{0:T(128)S(1)} %pad_add_fusion.1.coord_ref, bf16[512,512]{1,0:T(8,128)(2,1)S(1)} %copy-done, bf16[2048,512]{1,0:T(8,128)(2,1)S(1)} %copy-done.4, ...), custom_call_target="tpu_custom_call" | custom-call | flops 5000000000 | bytes 8000000 | tf_op jit(solution)/shard_map/spread/spread/pallas_call | solution.py:286
  119.8 0.4 collective-permute-start.11
  120.2 1.1 collective-permute-start.10
  121.4 0.6 collective-permute-start.9
  122.0 0.3 weight_terms.1
  122.3 0.1 reshape.37
  122.4 23.0 %all_to_all.42 = f32[32,2,512]{2,1,0:T(2,128)S(1)} all-to-all(f32[32,2,512]{2,1,0:T(2,128)S(1)} %reshape.37), channel_id=1, replica_groups=mesh['x'=4,'y'=4,'z'=8,'c'=2] {'y','z'}, dimensions={0} | all-to-all | bytes 262144 | tf_op jit(solution)/shard_map/sums/all_to_all | solution.py:193
  145.4 0.1 reduce_sum.21
  145.5 17.8 %all_to_all.43 = f32[32,2,512]{2,1,0:T(2,128)S(1)} all-to-all(f32[32,2,512]{2,1,0:T(2,128)S(1)} %broadcast_in_dim.36), channel_id=1, replica_groups=mesh['x'=4,'y'=4,'z'=8,'c'=2] {'y','z'}, dimensions={0} | all-to-all | bytes 262144 | tf_op jit(solution)/shard_map/sums/all_to_all | solution.py:193
  163.2 0.1 reshape.38
  163.4 2.3 %add_convert_fusion = bf16[512,512]{1,0:T(8,128)(2,1)} fusion(bf16[512,512]{1,0:T(8,128)(2,1)S(1)} %collective-permute-done.11, bf16[512,512]{1,0:T(8,128)(2,1)} %collective-permute-done.10, f32[512,512]{1,0:T(8,128)S(1)} %get-tuple-element.48, bf16[512,512]{1,0:T(8,128)(2,1)} %collective-permute-done.9), kind=kLoop, calls=%fused_computation | loop fusion | flops 1835008 | bytes 3145728 | tf_op jit(solution)/shard_map/sums/convert_element_type | solution.py:315
  165.7 3.7 %collective-permute-start.12 = (f32[64,512]{1,0:T(8,128)S(1)}, f32[64,512]{1,0:T(8,128)S(1)}, u32[]{:S(2)}, u32[]{:S(2)}) collective-permute-start(f32[64,512]{1,0:T(8,128)S(1)} %reshape.38), channel_id=1, source_target_pairs={{0,1},{1,0},{2,3},{3,2},{4,5},{5,4},{6,7},{7,6},{8,9},{9,8},{10,11... | collective-permute-start | bytes 393224 | tf_op jit(solution)/shard_map/sums/ppermute | solution.py:185
  169.3 1.0 collective-permute-done.12
  170.4 1.0 collective-permute-start.13
  171.3 3.5 %all-to-all-start.6 = ((bf16[8,64,512]{2,1,0:T(8,128)(2,1)}), bf16[8,64,512]{2,1,0:T(8,128)(2,1)S(1)}, u32[]{:S(2)}, u32[]{:S(2)}) async-start(bf16[8,64,512]{2,1,0:T(8,128)(2,1)} %bitcast.12), calls=%async_computation.6 | async-start | bytes 1048576 | tf_op jit(solution)/shard_map/sums/all_to_all | solution.py:193
  174.9 1.3 collective-permute-start.14
  176.1 0.1 broadcast_in_dim.37
  176.3 1.7 collective-permute-done.13
  178.0 5.7 %collective-permute-done.14 = f32[2,64,512]{2,1,0:T(8,128)S(1)} collective-permute-done((f32[2,64,512]{2,1,0:T(8,128)S(1)}, f32[2,64,512]{2,1,0:T(8,128)S(1)}, u32[]{:S(2)}, u32[]{:S(2)}) %collective-permute-start.14) | collective-permute-done | bytes 262176 | tf_op jit(solution)/shard_map/sums/ppermute | solution.py:189
  183.7 6.6 %collective-permute-done.15 = f32[2,64,512]{2,1,0:T(8,128)S(1)} collective-permute-done((f32[2,64,512]{2,1,0:T(8,128)S(1)}, f32[2,64,512]{2,1,0:T(8,128)S(1)}, u32[]{:S(2)}, u32[]{:S(2)}) %collective-permute-start.15) | collective-permute-done | bytes 262176 | tf_op jit(solution)/shard_map/sums/ppermute | solution.py:189
  190.3 2.4 %all-to-all-done.6 = bf16[8,64,512]{2,1,0:T(8,128)(2,1)S(1)} async-done(((bf16[8,64,512]{2,1,0:T(8,128)(2,1)}), bf16[8,64,512]{2,1,0:T(8,128)(2,1)S(1)}, u32[]{:S(2)}, u32[]{:S(2)}) %all-to-all-start.6) | async-done | bytes 524320 | tf_op jit(solution)/shard_map/sums/all_to_all | solution.py:193
  192.7 0.7 reduce_sum.22
  (49 shorter events, 0.3 us)
Async XLA Ops:
  0.6 13.4 %copy-start.12 = (bf16[32,128,128]{2,1,0:T(8,128)(2,1)S(1)}, bf16[32,128,128]{2,1,0:T(8,128)(2,1)}, u32[]{:S(2)}) copy-start(bf16[32,128,128]{2,1,0:T(8,128)(2,1)} %param.10) | copy-start | bytes 3145732
  2.1 13.1 %copy-start.1 = (s32[8192,2]{0,1:T(2,128)S(1)}, s32[8192,2]{0,1:T(2,128)}, u32[]{:S(2)}) copy-start(s32[8192,2]{0,1:T(2,128)} %param.14) | copy-start | bytes 196612
  2.1 13.1 %copy-start.2 = (s32[8192,2]{0,1:T(2,128)S(1)}, s32[8192,2]{0,1:T(2,128)}, u32[]{:S(2)}) copy-start(s32[8192,2]{0,1:T(2,128)} %param.15) | copy-start | bytes 196612
  2.1 38.0 %collective-permute-start = (s32[65]{0:T(128)S(1)}, s32[65]{0:T(128)S(1)}, u32[]{:S(2)}, u32[]{:S(2)}) collective-permute-start(s32[65]{0:T(128)S(1)} %pad_add_fusion.2), channel_id=1, source_target_pairs={{0,1},{1,0},{2,3},{3,2},{4,5},{5,4},{6,7},{7,6},{8,9},{9,8},{10,11... | collective-permute-start | bytes 788 | tf_op jit(solution)/shard_map/tile_matrix/ppermute | solution.py:185
  7.6 24.5 %all-to-all-start = ((bf16[8,64,512]{2,1,0:T(8,128)(2,1)}), bf16[8,64,512]{2,1,0:T(8,128)(2,1)S(1)}, u32[]{:S(2)}, u32[]{:S(2)}) async-start(bf16[8,64,512]{2,1,0:T(8,128)(2,1)} %broadcast_in_dim.34), calls=%async_computation | async-start | bytes 1048576 | tf_op jit(solution)/shard_map/pair_exchange/all_to_all | solution.py:193
  14.9 25.2 %collective-permute-start.1 = (bf16[32,64,128]{2,1,0:T(8,128)(2,1)}, bf16[32,64,128]{2,1,0:T(8,128)(2,1)S(1)}, u32[]{:S(2)}, u32[]{:S(2)}) collective-permute-start(bf16[32,64,128]{2,1,0:T(8,128)(2,1)} %get-tuple-element.58), channel_id=1, source_target_pairs={{0,1},{1,0},{2,3},{3,2},{4,5},{5,4},{6,7},{7,6},{8,9},{9,8},{10,11... | collective-permute-start | bytes 1572872 | tf_op jit(solution)/shard_map/tile_matrix/ppermute | solution.py:185
  15.2 24.5 %copy-start.14 = (s32[32]{0:T(128)S(1)}, s32[32]{0:T(128)}, u32[]{:S(2)}) copy-start(s32[32]{0:T(128)} %param.12) | copy-start | bytes 388
  15.2 24.5 %copy-start.15 = (s32[32]{0:T(128)S(1)}, s32[32]{0:T(128)}, u32[]{:S(2)}) copy-start(s32[32]{0:T(128)} %param.11) | copy-start | bytes 388
  15.2 24.7 %copy-start.13 = (bf16[64,512]{1,0:T(8,128)(2,1)S(1)}, bf16[64,512]{1,0:T(8,128)(2,1)}, u32[]{:S(2)}) copy-start(bf16[64,512]{1,0:T(8,128)(2,1)} %param.8) | copy-start | bytes 196612
  34.3 17.5 %all-to-all-start.1 = ((bf16[64,2,1024]{2,1,0:T(2,128)(2,1)}), bf16[64,2,1024]{2,1,0:T(2,128)(2,1)S(1)}, u32[]{:S(2)}, u32[]{:S(2)}) async-start(bf16[64,2,1024]{2,1,0:T(2,128)(2,1)} %reshape.41), calls=%async_computation.1 | async-start | bytes 524288 | tf_op jit(solution)/shard_map/pair_exchange/all_to_all | solution.py:193
  42.2 1.4 copy-start.3
  43.5 1.3 copy-start.5
  44.9 20.4 %collective-permute-start.2 = (bf16[512,512]{1,0:T(8,128)(2,1)S(1)}, bf16[512,512]{1,0:T(8,128)(2,1)S(1)}, u32[]{:S(2)}, u32[]{:S(2)}) collective-permute-start(bf16[512,512]{1,0:T(8,128)(2,1)S(1)} %bitcast.40), channel_id=1, source_target_pairs={{0,48},{16,0},{32,16},{48,32},{1,49},{17,1},{33,17},{49,33},{2,50}... | collective-permute-start | bytes 1572872 | tf_op jit(solution)/shard_map/pair_exchange/ppermute | solution.py:189
  47.6 17.7 %collective-permute-start.3 = (bf16[512,512]{1,0:T(8,128)(2,1)S(1)}, bf16[512,512]{1,0:T(8,128)(2,1)S(1)}, u32[]{:S(2)}, u32[]{:S(2)}) collective-permute-start(bf16[512,512]{1,0:T(8,128)(2,1)S(1)} %bitcast.41), channel_id=1, source_target_pairs={{0,32},{16,48},{32,0},{48,16},{1,33},{17,49},{33,1},{49,17},{2,34}... | collective-permute-start | bytes 1572872 | tf_op jit(solution)/shard_map/pair_exchange/ppermute | solution.py:189
  48.1 26.1 %collective-permute-start.4 = (bf16[512,512]{1,0:T(8,128)(2,1)S(1)}, bf16[512,512]{1,0:T(8,128)(2,1)S(1)}, u32[]{:S(2)}, u32[]{:S(2)}) collective-permute-start(bf16[512,512]{1,0:T(8,128)(2,1)S(1)} %bitcast.42), channel_id=1, source_target_pairs={{0,16},{16,32},{32,48},{48,0},{1,17},{17,33},{33,49},{49,1},{2,18}... | collective-permute-start | bytes 1572872 | tf_op jit(solution)/shard_map/pair_exchange/ppermute | solution.py:189
  63.8 1.4 copy-start.9
  75.0 20.6 %all-to-all-start.2 = ((bf16[8,2,2048]{2,1,0:T(2,128)(2,1)}), bf16[8,2,2048]{2,1,0:T(2,128)(2,1)S(1)}, u32[]{:S(2)}, u32[]{:S(2)}) async-start(bf16[8,2,2048]{2,1,0:T(2,128)(2,1)} %reshape.43), calls=%async_computation.2 | async-start | bytes 131072 | tf_op jit(solution)/shard_map/tile_matrix/all_to_all | solution.py:193
  79.9 15.8 %collective-permute-start.5 = (bf16[512,512]{1,0:T(8,128)(2,1)S(1)}, bf16[512,512]{1,0:T(8,128)(2,1)S(1)}, u32[]{:S(2)}, u32[]{:S(2)}) collective-permute-start(bf16[512,512]{1,0:T(8,128)(2,1)S(1)} %bitcast.43), channel_id=1, source_target_pairs={{0,1},{1,0},{2,3},{3,2},{4,5},{5,4},{6,7},{7,6},{8,9},{9,8},{10,11... | collective-permute-start | bytes 1572872 | tf_op jit(solution)/shard_map/pair_exchange/ppermute | solution.py:185
  79.9 15.8 %collective-permute-start.6 = (bf16[512,512]{1,0:T(8,128)(2,1)S(1)}, bf16[512,512]{1,0:T(8,128)(2,1)}, u32[]{:S(2)}, u32[]{:S(2)}) collective-permute-start(bf16[512,512]{1,0:T(8,128)(2,1)S(1)} %collective-permute-done.2.refs_1_), channel_id=1, source_target_pairs={{0,1},{1,0},{2,3},{3,2},{4,5},{5,4},{6,7},{7,6},{8,9},{9,8},{10,11... | collective-permute-start | bytes 1572872 | tf_op jit(solution)/shard_map/pair_exchange/ppermute | solution.py:185
  80.4 15.3 %collective-permute-start.7 = (bf16[512,512]{1,0:T(8,128)(2,1)S(1)}, bf16[512,512]{1,0:T(8,128)(2,1)}, u32[]{:S(2)}, u32[]{:S(2)}) collective-permute-start(bf16[512,512]{1,0:T(8,128)(2,1)S(1)} %collective-permute-done.3.refs_2_), channel_id=1, source_target_pairs={{0,1},{1,0},{2,3},{3,2},{4,5},{5,4},{6,7},{7,6},{8,9},{9,8},{10,11... | collective-permute-start | bytes 1572872 | tf_op jit(solution)/shard_map/pair_exchange/ppermute | solution.py:185
  80.4 15.3 %collective-permute-start.8 = (bf16[512,512]{1,0:T(8,128)(2,1)S(1)}, bf16[512,512]{1,0:T(8,128)(2,1)}, u32[]{:S(2)}, u32[]{:S(2)}) collective-permute-start(bf16[512,512]{1,0:T(8,128)(2,1)S(1)} %collective-permute-done.4.refs_3_), channel_id=1, source_target_pairs={{0,1},{1,0},{2,3},{3,2},{4,5},{5,4},{6,7},{7,6},{8,9},{9,8},{10,11... | collective-permute-start | bytes 1572872 | tf_op jit(solution)/shard_map/pair_exchange/ppermute | solution.py:185
  80.9 1.6 copy-start.10
  94.1 1.4 copy-start.7
  95.7 1.6 copy-start.8
  97.3 19.3 %copy-start = (bf16[512,512]{1,0:T(8,128)(2,1)S(1)}, bf16[512,512]{1,0:T(8,128)(2,1)}, u32[]{:S(2)}) copy-start(bf16[512,512]{1,0:T(8,128)(2,1)} %weight_ref.1) | copy-start | bytes 1572868
  97.3 19.3 %copy-start.4 = (bf16[2048,512]{1,0:T(8,128)(2,1)S(1)}, bf16[2048,512]{1,0:T(8,128)(2,1)}, u32[]{:S(2)}) copy-start(bf16[2048,512]{1,0:T(8,128)(2,1)} %copy-done.3) | copy-start | bytes 6291460
  97.3 19.3 %copy-start.6 = (bf16[2048,512]{1,0:T(8,128)(2,1)S(1)}, bf16[2048,512]{1,0:T(8,128)(2,1)}, u32[]{:S(2)}) copy-start(bf16[2048,512]{1,0:T(8,128)(2,1)} %copy-done.5) | copy-start | bytes 6291460
  119.8 43.5 %collective-permute-start.11 = (bf16[512,512]{1,0:T(8,128)(2,1)S(1)}, bf16[512,512]{1,0:T(8,128)(2,1)S(1)}, u32[]{:S(2)}, u32[]{:S(2)}) collective-permute-start(bf16[512,512]{1,0:T(8,128)(2,1)S(1)} %get-tuple-element.51), channel_id=1, source_target_pairs={{0,48},{16,0},{32,16},{48,32},{1,49},{17,1},{33,17},{49,33},{2,50}... | collective-permute-start | bytes 1572872 | tf_op jit(solution)/shard_map/sums/ppermute | solution.py:189
  120.2 43.1 %collective-permute-start.10 = (bf16[512,512]{1,0:T(8,128)(2,1)S(1)}, bf16[512,512]{1,0:T(8,128)(2,1)}, u32[]{:S(2)}, u32[]{:S(2)}) collective-permute-start(bf16[512,512]{1,0:T(8,128)(2,1)S(1)} %get-tuple-element.50), channel_id=1, source_target_pairs={{0,16},{16,32},{32,48},{48,0},{1,17},{17,33},{33,49},{49,1},{2,18}... | collective-permute-start | bytes 1572872 | tf_op jit(solution)/shard_map/sums/ppermute | solution.py:189
  121.4 42.0 %collective-permute-start.9 = (bf16[512,512]{1,0:T(8,128)(2,1)S(1)}, bf16[512,512]{1,0:T(8,128)(2,1)}, u32[]{:S(2)}, u32[]{:S(2)}) collective-permute-start(bf16[512,512]{1,0:T(8,128)(2,1)S(1)} %get-tuple-element.49), channel_id=1, source_target_pairs={{0,32},{16,48},{32,0},{48,16},{1,33},{17,49},{33,1},{49,17},{2,34}... | collective-permute-start | bytes 1572872 | tf_op jit(solution)/shard_map/sums/ppermute | solution.py:189
  165.7 4.6 %collective-permute-start.12 = (f32[64,512]{1,0:T(8,128)S(1)}, f32[64,512]{1,0:T(8,128)S(1)}, u32[]{:S(2)}, u32[]{:S(2)}) collective-permute-start(f32[64,512]{1,0:T(8,128)S(1)} %reshape.38), channel_id=1, source_target_pairs={{0,1},{1,0},{2,3},{3,2},{4,5},{5,4},{6,7},{7,6},{8,9},{9,8},{10,11... | collective-permute-start | bytes 393224 | tf_op jit(solution)/shard_map/sums/ppermute | solution.py:185
  170.4 7.6 %collective-permute-start.13 = (f32[2,64,512]{2,1,0:T(8,128)S(1)}, f32[2,64,512]{2,1,0:T(8,128)S(1)}, u32[]{:S(2)}, u32[]{:S(2)}) collective-permute-start(f32[2,64,512]{2,1,0:T(8,128)S(1)} %pad_maximum_fusion), channel_id=1, source_target_pairs={{0,192},{64,0},{128,64},{192,128},{1,193},{65,1},{129,65},{193,129... | collective-permute-start | bytes 786440 | tf_op jit(solution)/shard_map/sums/ppermute | solution.py:189
  171.3 21.4 %all-to-all-start.6 = ((bf16[8,64,512]{2,1,0:T(8,128)(2,1)}), bf16[8,64,512]{2,1,0:T(8,128)(2,1)S(1)}, u32[]{:S(2)}, u32[]{:S(2)}) async-start(bf16[8,64,512]{2,1,0:T(8,128)(2,1)} %bitcast.12), calls=%async_computation.6 | async-start | bytes 1048576 | tf_op jit(solution)/shard_map/sums/all_to_all | solution.py:193
  174.9 8.8 %collective-permute-start.14 = (f32[2,64,512]{2,1,0:T(8,128)S(1)}, f32[2,64,512]{2,1,0:T(8,128)S(1)}, u32[]{:S(2)}, u32[]{:S(2)}) collective-permute-start(f32[2,64,512]{2,1,0:T(8,128)S(1)} %pad_maximum_fusion), channel_id=1, source_target_pairs={{0,128},{64,192},{128,0},{192,64},{1,129},{65,193},{129,1},{193,65... | collective-permute-start | bytes 786440 | tf_op jit(solution)/shard_map/sums/ppermute | solution.py:189
  176.1 14.2 %collective-permute-start.15 = (f32[2,64,512]{2,1,0:T(8,128)S(1)}, f32[2,64,512]{2,1,0:T(8,128)S(1)}, u32[]{:S(2)}, u32[]{:S(2)}) collective-permute-start(f32[2,64,512]{2,1,0:T(8,128)S(1)} %pad_maximum_fusion), channel_id=1, source_target_pairs={{0,64},{64,128},{128,192},{192,0},{1,65},{65,129},{129,193},{193,1... | collective-permute-start | bytes 786440 | tf_op jit(solution)/shard_map/sums/ppermute | solution.py:189
  190.3 3.1 %copy-start.11 = (f32[4,2,64,512]{3,2,1,0:T(8,128)}, f32[4,2,64,512]{3,2,1,0:T(8,128)S(1)}, u32[]{:S(2)}) copy-start(f32[4,2,64,512]{3,2,1,0:T(8,128)S(1)} %bitcast_dynamic-update-slice_fusion) | copy-start | bytes 3145732
where the time goes:
time: 194 us; the launch traced here: 193 us
  blocking collectives  54.7 us (28%)
  Pallas kernels  41.9 us (22%)
  waiting for transfers between devices  38.1 us (20%)
  starting transfers between devices  37 us (19%)
  local copies, waits for them, and re-layouts  13.7 us (7%)
  other arithmetic  4.93 us (3%)
    all_to_all x3, blocking collectives, exchange(): return lax.all_to_all(values, axes, 0, 0, tiled=True)  54.7 us
    pallas_call x2, Pallas kernels, count(): pl.pallas_call(functools.partial(count_kernel, not counted), out_shape=[j...  23.3 us
    ppermute x9, waiting for transfers between devices, shift(): lax.ppermute(values, axis, [(i, (i + step) % size) for i in range(size)])  22.9 us
    all_to_all x4, starting transfers between devices, exchange(): return lax.all_to_all(values, axes, 0, 0, tiled=True)  20.3 us
    all_to_all x4, waiting for transfers between devices, exchange(): return lax.all_to_all(values, axes, 0, 0, tiled=True)  14.2 us
    unnamed x36, local copies, waits for them, and re-layouts  10.7 us
    ppermute x9, starting transfers between devices, shift(): lax.ppermute(values, axis, [(i, (i + step) % size) for i in range(size)])  8.42 us
    ppermute x7, starting transfers between devices, swap(): return lax.ppermute(values, 'c', [(0, 1), (1, 0)])  8.27 us
  transfers between devices with their start and end apart: 20, of which 8 were waited for; matrix products, arithmetic and copies ran while one was open for 3% of the time, Pallas kernels for 17%

commit v1 on v0

--- a/solution.py
+++ b/solution.py
@@ -96,24 +96,31 @@
         out_ref[...] = jnp.zeros_like(out_ref)
     else:
         out_ref[...] = refs[0][...]
-    group = 4
-
-    def body(g, carry):
-        total = None
-        for s in range(group):
-            here = pl.ds(g * group + s, 1)
-            spots = lax.broadcasted_iota(I32, (CAP, CAP), 0)
-            left = jnp.where(spots == left_at[here, :], weight_at[here, :], 0.0).astype(BF)
-            right = jnp.where(spots == right_at[here, :], 1.0, 0.0).astype(BF)
-            term = lax.dot_general(left, right, NT, preferred_element_type=F32)
-            total = term if total is None else total + term
+    group = 7
+    groups = NDEV // group
+    half = (groups + 1) // 2
+
+    def add(start, size):
+        spots = lax.broadcasted_iota(I32, (CAP, CAP), 0)
+        left, right = [], []
+        for s in range(size):
+            here = pl.ds(start + s, 1)
+            left.append(jnp.where(spots == left_at[here, :], weight_at[here, :], 0.0).astype(BF))
+            right.append(jnp.where(spots == right_at[here, :], 1.0, 0.0).astype(BF))
+        total = lax.dot_general(
+            jnp.concatenate(left, axis=1), jnp.concatenate(right, axis=1), NT, preferred_element_type=F32
+        )
         ones = jnp.floor(total * (1.0 / POS))
         out_ref[0] += total - (POS - 1.0) * ones
         out_ref[1] += ones
+
+    def body(g, carry):
+        add(g * group, group)
         return carry
 
-    half = NDEV // group // 2
-    lax.fori_loop(0 if first else half, half if first else 2 * half, body, 0)
+    lax.fori_loop(0 if first else half, half if first else groups, body, 0)
+    if not first:
+        add(groups * group, NDEV - groups * group)
 
 
 def grad_kernel(scale, _, own_ref, count_ref, *refs):
@@ -158,13 +165,14 @@
     lax.fori_loop(0, acc.shape[0] // 128, split, 0)
 
 
-def spread_kernel(coord_ref, weight_ref, high_ref, low_ref, pre_ref, *refs):
-    out_refs, token_ref, pre = refs[:-2], refs[-2], refs[-1]
-    token_ref[...] = jnp.zeros_like(token_ref)
-    y, c = coord_ref[0], coord_ref[1]
-    for k in range(NX * NC):
-        place = pl.multiple_of(((k % NC) ^ c) * NX * ROWS + (k // NC) * ROWS, ROWS)
-        pre[pl.ds(place, ROWS), :] = pre_ref[k]
+def spread_kernel(coord_ref, _, weight_ref, high_ref, low_ref, *refs):
+    pre_refs, out_refs, token_ref, pre = refs[:8], refs[8:-2], refs[-2], refs[-1]
+    token_ref[...] = jnp.zeros_like(token_ref)
+    y, x = coord_ref[0], coord_ref[2]
+    for k in range(NC * NX):
+        dc, dx = k // NX, k % NX
+        place = pl.multiple_of((dc * NX + ((x + dx) & (NX - 1))) * ROWS, ROWS)
+        pre[pl.ds(place, ROWS), :] = pre_refs[k][...]
     agg = lax.dot_general(pre[...], weight_ref[...], NT, preferred_element_type=F32).astype(BF)
     size = NZ * ROWS
     for k in range(NY):
@@ -174,11 +182,32 @@
         out_refs[k][...] = part.astype(out_refs[k].dtype)
 
 
-def terms_kernel(_, pre_ref, node_ref, terms_ref):
-    total = jnp.zeros(terms_ref.shape, F32)
-    for k in range(NX * NC):
-        total += lax.dot_general(node_ref[k], pre_ref[k], TN, preferred_element_type=F32)
-    terms_ref[...] = total
+def terms_kernel(coord_ref, node_ref, *refs):
+    pre_refs, out_refs, token_ref, terms = refs[:8], refs[8:12], refs[12], refs[13]
+    token_ref[...] = jnp.zeros_like(token_ref)
+    y, c, x = coord_ref[0], coord_ref[1], coord_ref[2]
+    total = jnp.zeros(terms.shape, F32)
+    for k in range(NC * NX):
+        dc, dx = k // NX, k % NX
+        node = node_ref[((x + dx) & (NX - 1)) * NC + (c ^ dc)]
+        total += lax.dot_general(node, pre_refs[k][...], TN, preferred_element_type=F32)
+    terms[...] = total
+    size = ROWS // NY
+    for k in range(NY):
+        rows = pl.ds(pl.multiple_of(((y + k) & (NY - 1)) * size, size), size)
+        out_refs[k][...] = terms[rows, :]
+
+
+def plane_kernel(coord_ref, _, keep_ref, *refs):
+    in_refs, out_refs, total = refs[:3], refs[3:-1], refs[-1]
+    z = coord_ref[3]
+    value = keep_ref[...]
+    for ref in in_refs:
+        value = value + ref[...].astype(F32)
+    total[...] = value
+    for k in range(NZ):
+        rows = pl.ds(pl.multiple_of(((z + k) & (NZ - 1)) * ROWS, ROWS), ROWS)
+        out_refs[k][...] = total[rows, :].astype(out_refs[k].dtype)
 
 
 def swap(values):
@@ -222,7 +251,9 @@
     pair_total = pair_owner.shape[0]
     slots = tiles.shape[0]
     c = lax.axis_index("c")
-    coord = jnp.stack([lax.axis_index("y"), c]).astype(I32)
+    coord = jnp.stack(
+        [lax.axis_index("y"), c, lax.axis_index("x"), lax.axis_index("z")]
+    ).astype(I32)
 
     with jax.named_scope("hidden"):
         pre_act = jnp.dot(node_aggregate, weight, preferred_element_type=F32)
@@ -241,9 +272,10 @@
             cost_estimate=pl.CostEstimate(flops=9_000_000_000, bytes_accessed=400_000, transcendentals=0),
             name="bucket",
         )(pair_owner.T, pair_row.T)
+        ends = ends.reshape(NDEV, 2, 2 * CAP)
         ring, ends = lax.optimization_barrier((ring, ends))
         planes = [ring] + [shift(ring, "y", NY, -k) for k in range(1, NY)]
-        received = exchange(ends, ("y", "z", "c"))
+        received = exchange(ends, ("y", "z", "c")).reshape(NDEV, 4 * CAP)
         counted, token = count(coord, token, received)
         columns = node_aggregate.reshape(ROWS, NX * NC, ROWS).transpose(1, 0, 2)
         planes, columns, token = lax.optimization_barrier((planes, columns, token))
@@ -282,54 +314,67 @@
         pre_grad = act_back(hidden_grad)[0].astype(BF)
 
     with jax.named_scope("spread"):
-        pre_parts = gather(pre_grad, ("x", "c"), NX * NC)
+        pre_parts = []
+        for dc in range(NC):
+            for dx in range(NX):
+                pairs = [
+                    (((x + dx) % NX) * NC + (b ^ dc), x * NC + b) for x in range(NX) for b in range(NC)
+                ]
+                away = dc + dx > 0
+                pre_parts.append(lax.ppermute(pre_grad, ("x", "c"), pairs) if away else pre_grad)
+        *terms, token = pl.pallas_call(
+            terms_kernel,
+            out_shape=[jax.ShapeDtypeStruct((ROWS // NY, F), F32)] * NY + [TOKEN],
+            in_specs=[SMEM] + [VMEM] * 9,
+            out_specs=[VMEM] * (NY + 1),
+            scratch_shapes=[pltpu.VMEM((ROWS, F), F32)],
+            compiler_params=params(),
+            cost_estimate=pl.CostEstimate(flops=1_000_000_000, bytes_accessed=700_000, transcendentals=0),
+            name="weight_terms",
+        )(coord, nodes, *pre_parts)
         keep, *send, token = pl.pallas_call(
             spread_kernel,
             out_shape=[
                 jax.ShapeDtypeStruct((NZ * ROWS, F), dtype) for dtype in (F32,) + (BF,) * (NY - 1)
             ]
             + [TOKEN],
-            in_specs=[SMEM] + [VMEM] * 4,
+            in_specs=[SMEM, ANY] + [VMEM] * 11,
             out_specs=[VMEM] * (NY + 1),
             scratch_shapes=[pltpu.VMEM((NC * NX * ROWS, F), BF)],
             compiler_params=params(),
             cost_estimate=pl.CostEstimate(flops=5_000_000_000, bytes_accessed=8_000_000, transcendentals=0),
             name="spread",
-        )(coord, weight, high, low, pre_parts)
-        pre_parts, token = lax.optimization_barrier((pre_parts, token))
-        terms = pl.pallas_call(
-            terms_kernel,
-            out_shape=jax.ShapeDtypeStruct((ROWS, F), F32),
-            in_specs=[ANY] + [VMEM] * 2,
-            out_specs=VMEM,
-            compiler_params=params(),
-            cost_estimate=pl.CostEstimate(flops=1_000_000_000, bytes_accessed=700_000, transcendentals=0),
-            name="weight_terms",
-        )(token, pre_parts, nodes)
+        )(coord, token, weight, high, low, *pre_parts)
 
     with jax.named_scope("sums"):
-        chips = NY * NZ
-        part = keep
-        for k in (2, 1, 3):
-            part = part + shift(send[k - 1], "y", NY, k).astype(F32)
-        part = part.astype(BF)
-        shares = exchange(terms.reshape(chips, ROWS // chips, F), ("y", "z"))
-        share = jnp.sum(shares, axis=0)
-        block = gather(share, ("y", "z"), chips).reshape(ROWS, F)
-        part, block = lax.optimization_barrier((part, block))
-        rings = exchange(part.reshape(NZ, ROWS, F), "z").astype(F32)
-        other = swap(block)
-        low_first = c == 0
-        pair = jnp.stack([jnp.where(low_first, block, other), jnp.where(low_first, other, block)])
-        x = lax.axis_index("x")
-        blocks = jnp.zeros((NX,) + pair.shape, F32)
-        blocks = lax.dynamic_update_index_in_dim(blocks, pair, x, 0)
-        for k in range(1, NX):
-            blocks = lax.dynamic_update_index_in_dim(
-                blocks, shift(pair, "x", NX, -k), (x + k) & (NX - 1), 0
-            )
-        weight_grad = blocks.reshape(F, F)
-        feature_grad = jnp.sum(rings, axis=0).astype(BF)
+        planes = [shift(send[k - 1], "y", NY, k) for k in (2, 1, 3)]
+        others = [shift(terms[k], "y", NY, k) for k in range(1, NY)]
+        *others, token = lax.optimization_barrier((*others, token))
+        share = terms[0]
+        for other in others:
+            share = share + other
+        shares = gather(share, "z", NZ)
+        block = shares[0]
+        for k in range(1, NZ):
+            block = block + shares[k]
+        own, *parts = pl.pallas_call(
+            plane_kernel,
+            out_shape=[
+                jax.ShapeDtypeStruct((ROWS, F), dtype) for dtype in (F32,) + (BF,) * (NZ - 1)
+            ],
+            in_specs=[SMEM, ANY] + [VMEM] * 4,
+            out_specs=[VMEM] * NZ,
+            scratch_shapes=[pltpu.VMEM((NZ * ROWS, F), F32)],
+            compiler_params=params(),
+            cost_estimate=pl.CostEstimate(flops=2_000_000_000, bytes_accessed=3_000_000, transcendentals=0),
+            name="plane_sum",
+        )(coord, token, keep, *planes)
+        own, block = lax.optimization_barrier((own, block))
+        feature = own
+        for k in (4, 3, 5, 2, 6, 1, 7):
+            feature = feature + shift(parts[k - 1], "z", NZ, k).astype(F32)
+        feature_grad = feature.astype(BF)
+        weight_grad = gather(block, ("x", "c", "y"), NX * NC * NY).reshape(F, F)
     return (feature_grad, weight_grad)
 
 

time: 194 us -> 185 us (0.954); the launches traced: 193 us -> 181 us
  blocking collectives: 54.7 us -> 0 us
  starting transfers between devices: 37 us -> 64.8 us
  waiting for transfers between devices: 38.1 us -> 51.5 us
  local copies, waits for them, and re-layouts: 13.7 us -> 17.4 us
  other arithmetic: 4.93 us -> 2.61 us
    all_to_all x3 -> x0, blocking collectives: 54.7 us -> none  [exchange(): return lax.all_to_all(values, axes, 0, 0, tiled=True)]
    ppermute x9 -> x16, starting transfers between devices: 8.42 us -> 24 us  [shift(): lax.ppermute(values, axis, [(i, (i + step) % size) for i in range(size)])]
    ppermute x0 -> x7, starting transfers between devices: none -> 8.6 us  [per_device(): lax.ppermute(pre_grad, ('x', 'c'), pairs)]
    all_to_all x4 -> x5, starting transfers between devices: 20.3 us -> 27.6 us  [exchange(): return lax.all_to_all(values, axes, 0, 0, tiled=True)]
    ppermute x9 -> x16, waiting for transfers between devices: 22.9 us -> 29.6 us  [shift(): lax.ppermute(values, axis, [(i, (i + step) % size) for i in range(size)])]
    ppermute x0 -> x7, waiting for transfers between devices: none -> 5.87 us  [per_device(): lax.ppermute(pre_grad, ('x', 'c'), pairs)]
    ppermute x7 -> x6, starting transfers between devices: 8.27 us -> 4.61 us  [swap(): return lax.ppermute(values, 'c', [(0, 1), (1, 0)])]
    unnamed x36 -> x37, local copies, waits for them, and re-layouts: 10.7 us -> 12.6 us
  transfers between devices with their start and end apart: 20 -> 34, of which waited for: 8 -> 11; matrix products, arithmetic and copies ran while one was open for 3% -> 3% of each run, Pallas kernels for 17% -> 19%
where the time goes in v1:
time: 185 us; the launch traced here: 181 us
  starting transfers between devices  64.8 us (35%)
  waiting for transfers between devices  51.5 us (28%)
  Pallas kernels  42.1 us (23%)
  local copies, waits for them, and re-layouts  17.4 us (9%)
  other arithmetic  2.61 us (1%)
    ppermute x16, waiting for transfers between devices, shift(): lax.ppermute(values, axis, [(i, (i + step) % size) for i in range(size)])  29.6 us
    all_to_all x5, starting transfers between devices, exchange(): return lax.all_to_all(values, axes, 0, 0, tiled=True)  27.6 us
    ppermute x16, starting transfers between devices, shift(): lax.ppermute(values, axis, [(i, (i + step) % size) for i in range(size)])  24 us
    pallas_call x2, Pallas kernels, count(): pl.pallas_call(functools.partial(count_kernel, not counted), out_shape=[j...  21.6 us
    all_to_all x5, waiting for transfers between devices, exchange(): return lax.all_to_all(values, axes, 0, 0, tiled=True)  16 us
    unnamed x37, local copies, waits for them, and re-layouts  12.6 us
    ppermute x7, starting transfers between devices, per_device(): lax.ppermute(pre_grad, ('x', 'c'), pairs)  8.6 us
    pallas_call x1, Pallas kernels, per_device(): pl.pallas_call(bucket_kernel, out_shape=[jax.ShapeDtypeStruct((NDEV, 4 *...  7.86 us
  transfers between devices with their start and end apart: 34, of which 11 were waited for; matrix products, arithmetic and copies ran while one was open for 3% of the time, Pallas kernels for 19%

profile of v1, /device:TPU:1, one launch (start us, length us, event | category | flops | bytes accessed | tf_op | source)
XLA Modules:
  0.0 181.5 jit_solution(8118382226394947733)
XLA Ops:
  1.4 0.7 pad_add_fusion.2
  2.1 3.3 %collective-permute-start = (s32[65]{0:T(128)S(1)}, s32[65]{0:T(128)S(1)}, u32[]{:S(2)}, u32[]{:S(2)}) collective-permute-start(s32[65]{0:T(128)S(1)} %pad_add_fusion.2), channel_id=1, source_target_pairs={{0,1},{1,0},{2,3},{3,2},{4,5},{5,4},{6,7},{7,6},{8,9},{9,8},{10,11... | collective-permute-start | bytes 788 | tf_op jit(solution)/shard_map/tile_matrix/ppermute | solution.py:214
  5.4 1.3 multiply_convert_fusion
  6.7 0.9 broadcast_in_dim.6
  7.6 6.4 %all-to-all-start = ((bf16[8,64,512]{2,1,0:T(8,128)(2,1)}), bf16[8,64,512]{2,1,0:T(8,128)(2,1)S(1)}, u32[]{:S(2)}, u32[]{:S(2)}) async-start(bf16[8,64,512]{2,1,0:T(8,128)(2,1)} %broadcast_in_dim.6), calls=%async_computation | async-start | bytes 1048576 | tf_op jit(solution)/shard_map/pair_exchange/all_to_all | solution.py:222
  14.1 0.9 dynamic-slice_bitcast_fusion
  15.3 7.9 %bucket.1 = (bf16[64,2048]{1,0:T(8,128)(2,1)S(1)}, f32[8,128]{1,0:T(8,128)S(1)}) custom-call(s32[2,8192]{1,0:T(2,128)S(1)} %bitcast.36, s32[2,8192]{1,0:T(2,128)S(1)} %bitcast.37), custom_call_target="tpu_custom_call" | custom-call | flops 8999999488 | bytes 400000 | tf_op jit(solution)/shard_map/pair_exchange/bucket/pallas_call | solution.py:265
  23.1 0.9 reshape.35
  24.0 8.1 %all-to-all-done = bf16[8,64,512]{2,1,0:T(8,128)(2,1)S(1)} async-done(((bf16[8,64,512]{2,1,0:T(8,128)(2,1)}), bf16[8,64,512]{2,1,0:T(8,128)(2,1)S(1)}, u32[]{:S(2)}, u32[]{:S(2)}) %all-to-all-start) | async-done | bytes 524320 | tf_op jit(solution)/shard_map/pair_exchange/all_to_all | solution.py:222
  32.1 5.5 %all-to-all-start.1 = ((bf16[64,2,1024]{2,1,0:T(2,128)(2,1)}), bf16[64,2,1024]{2,1,0:T(2,128)(2,1)S(1)}, u32[]{:S(2)}, u32[]{:S(2)}) async-start(bf16[64,2,1024]{2,1,0:T(2,128)(2,1)} %reshape.35), calls=%async_computation.1 | async-start | bytes 524288 | tf_op jit(solution)/shard_map/pair_exchange/all_to_all | solution.py:222
  38.0 2.4 %tile_sum.1 = (bf16[2048,512]{1,0:T(8,128)(2,1)S(1)}, bf16[2048,512]{1,0:T(8,128)(2,1)S(1)}, f32[8,128]{1,0:T(8,128)S(1)}) custom-call(s32[2,65]{1,0:T(2,128)S(1)} %pad_add_fusion.meta_ref, bf16[32,64,128]{2,1,0:T(8,128)(2,1)S(1)} %get-tuple-element.89.own_ref, bf16[32,64,128]{2,1,0:T(8,128)(2,1)S(1)} %collective-permute-done.1.other_ref), custom_call_target="tpu_custom_call" | custom-call | flops 3000000000 | bytes 5000000 | tf_op jit(solution)/shard_map/tile_matrix/tile_sum/pallas_call | solution.py:291
  40.4 1.3 copy-done.5
  41.7 1.4 copy-done.7
  43.1 2.5 %collective-permute-start.2 = (bf16[512,512]{1,0:T(8,128)(2,1)S(1)}, bf16[512,512]{1,0:T(8,128)(2,1)S(1)}, u32[]{:S(2)}, u32[]{:S(2)}) collective-permute-start(bf16[512,512]{1,0:T(8,128)(2,1)S(1)} %bitcast.29), channel_id=1, source_target_pairs={{0,48},{16,0},{32,16},{48,32},{1,49},{17,1},{33,17},{49,33},{2,50}... | collective-permute-start | bytes 1572872 | tf_op jit(solution)/shard_map/pair_exchange/ppermute | solution.py:218
  45.6 0.3 collective-permute-start.3
  45.9 0.9 collective-permute-start.4
  46.8 2.8 %all-to-all-done.1 = bf16[64,2,1024]{2,1,0:T(2,128)(2,1)S(1)} async-done(((bf16[64,2,1024]{2,1,0:T(2,128)(2,1)}), bf16[64,2,1024]{2,1,0:T(2,128)(2,1)S(1)}, u32[]{:S(2)}, u32[]{:S(2)}) %all-to-all-start.1) | async-done | bytes 262176 | tf_op jit(solution)/shard_map/pair_exchange/all_to_all | solution.py:222
  49.6 11.6 %count.2 = (f32[2,512,512]{2,1,0:T(8,128)S(1)}, f32[8,128]{1,0:T(8,128)S(1)}) custom-call(s32[4]{0:T(128)S(1)} %pad_add_fusion.1.coord_ref, f32[8,128]{1,0:T(8,128)S(1)} %get-tuple-element.48._, bf16[64,2048]{1,0:T(8,128)(2,1)S(1)} %bitcast.34), custom_call_target="tpu_custom_call" | custom-call | flops 12000000000 | bytes 2400000 | tf_op jit(solution)/shard_map/pair_exchange/count/pallas_call | solution.py:234
  61.3 1.4 copy-done.11
  62.6 9.5 %collective-permute-done.4.refs_3_ = bf16[512,512]{1,0:T(8,128)(2,1)S(1)} collective-permute-done((bf16[512,512]{1,0:T(8,128)(2,1)S(1)}, bf16[512,512]{1,0:T(8,128)(2,1)S(1)}, u32[]{:S(2)}, u32[]{:S(2)}) %collective-permute-start.4) | collective-permute-done | bytes 524320 | tf_op jit(solution)/shard_map/pair_exchange/ppermute | solution.py:218
  72.2 0.8 reshape.42
  73.0 4.8 %all-to-all-start.2 = ((bf16[8,2,2048]{2,1,0:T(2,128)(2,1)}), bf16[8,2,2048]{2,1,0:T(2,128)(2,1)S(1)}, u32[]{:S(2)}, u32[]{:S(2)}) async-start(bf16[8,2,2048]{2,1,0:T(2,128)(2,1)} %reshape.42), calls=%async_computation.2 | async-start | bytes 131072 | tf_op jit(solution)/shard_map/tile_matrix/all_to_all | solution.py:222
  77.8 0.5 collective-permute-start.6
  78.3 0.5 collective-permute-start.8
  78.8 1.6 copy-done.12
  80.4 10.0 %count.3 = (f32[2,512,512]{2,1,0:T(8,128)S(1)}, f32[8,128]{1,0:T(8,128)}) custom-call(s32[4]{0:T(128)S(1)} %pad_add_fusion.1.coord_ref, f32[8,128]{1,0:T(8,128)S(1)} %get-tuple-element.55._, bf16[64,2048]{1,0:T(8,128)(2,1)S(1)} %bitcast.35, f32[2,512,512]{2,1,0:T(8,128)S(1)} %copy-done.12), custom_call_target="tpu_custom_call" | custom-call | flops 12000000000 | bytes 2400000 | tf_op jit(solution)/shard_map/pair_exchange/count/pallas_call | solution.py:234
  90.4 1.4 copy-done.9
  91.9 1.6 copy-done.10
  93.5 5.1 %pair_grad.1 = f32[64,512]{1,0:T(8,128)S(1)} custom-call(f32[8,128]{1,0:T(8,128)S(1)} %get-tuple-element.53._, bf16[64,512]{1,0:T(8,128)(2,1)S(1)} %get-tuple-element.54.own_ref, f32[2,512,512]{2,1,0:T(8,128)S(1)} %copy-done.10, bf16[512,512]{1,0:T(8,128)(2,1)S(1)} %bitcast.33, bf16[512,512]{1,0:T(8,128)(2,1)S(1)} %collective-permute-done.2.refs_1_, ...), custom_call_target="tpu_custom_call" | custom-call | flops 5000000000 | bytes 6000000 | tf_op jit(solution)/shard_map/hidden_grad/pair_grad/pallas_call | solution.py:305
  98.8 2.7 %collective-permute-start.9 = (bf16[64,512]{1,0:T(8,128)(2,1)S(1)}, bf16[64,512]{1,0:T(8,128)(2,1)S(1)}, u32[]{:S(2)}, u32[]{:S(2)}) collective-permute-start(bf16[64,512]{1,0:T(8,128)(2,1)S(1)} %fusion.6.refs_0_), channel_id=1, source_target_pairs={{64,0},{65,1},{128,64},{129,65},{192,128},{193,129},{0,192},{1,193... | collective-permute-start | bytes 196616 | tf_op jit(solution)/shard_map/spread/ppermute | solution.py:324
  101.4 0.6 collective-permute-start.10
  102.0 0.6 collective-permute-start.11
  102.6 1.2 collective-permute-start.12
  103.8 2.0 %collective-permute-start.13 = (bf16[64,512]{1,0:T(8,128)(2,1)S(1)}, bf16[64,512]{1,0:T(8,128)(2,1)S(1)}, u32[]{:S(2)}, u32[]{:S(2)}) collective-permute-start(bf16[64,512]{1,0:T(8,128)(2,1)S(1)} %fusion.6.refs_0_), channel_id=1, source_target_pairs={{65,0},{64,1},{129,64},{128,65},{193,128},{192,129},{1,192},{0,193... | collective-permute-start | bytes 196616 | tf_op jit(solution)/shard_map/spread/ppermute | solution.py:324
  105.8 1.6 collective-permute-start.14
  107.4 0.6 collective-permute-done.13.refs_5_
  107.9 3.7 %collective-permute-done.14.refs_6_ = bf16[64,512]{1,0:T(8,128)(2,1)S(1)} collective-permute-done((bf16[64,512]{1,0:T(8,128)(2,1)S(1)}, bf16[64,512]{1,0:T(8,128)(2,1)S(1)}, u32[]{:S(2)}, u32[]{:S(2)}) %collective-permute-start.14) | collective-permute-done | bytes 65568 | tf_op jit(solution)/shard_map/spread/ppermute | solution.py:324
  111.7 1.6 collective-permute-done.15.refs_7_
  113.2 0.9 weight_terms.1
  114.2 1.5 collective-permute-start.17
  115.7 1.2 collective-permute-start.18
  116.9 3.3 %spread.1 = (f32[512,512]{1,0:T(8,128)S(1)}, bf16[512,512]{1,0:T(8,128)(2,1)S(1)}, bf16[512,512]{1,0:T(8,128)(2,1)S(1)}, bf16[512,512]{1,0:T(8,128)(2,1)S(1)}, f32[8,128]{1,0:T(8,128)S(1)}) custom-call(s32[4]{0:T(128)S(1)} %pad_add_fusion.1.coord_ref, f32[8,128]{1,0:T(8,128)S(1)} %get-tuple-element.65._, bf16[512,512]{1,0:T(8,128)(2,1)S(1)} %copy-done, ...), custom_call_target="tpu_custom_call" | custom-call | flops 5000000000 | bytes 8000000 | tf_op jit(solution)/shard_map/spread/spread/pallas_call | solution.py:335
  120.2 1.0 copy-done.3
  121.2 0.8 broadcast_in_dim.7
  121.9 6.4 %all-to-all-start.3 = ((f32[8,16,512]{2,1,0:T(8,128)}), f32[8,16,512]{2,1,0:T(8,128)}, u32[]{:S(2)}, u32[]{:S(2)}) async-start(f32[8,16,512]{2,1,0:T(8,128)} %broadcast_in_dim.7), calls=%async_computation.3 | async-start | bytes 524288 | tf_op jit(solution)/shard_map/sums/all_to_all | solution.py:222
  128.3 2.4 %collective-permute-start.19 = (bf16[512,512]{1,0:T(8,128)(2,1)S(1)}, bf16[512,512]{1,0:T(8,128)(2,1)S(1)}, u32[]{:S(2)}, u32[]{:S(2)}) collective-permute-start(bf16[512,512]{1,0:T(8,128)(2,1)S(1)} %get-tuple-element.71), channel_id=1, source_target_pairs={{0,32},{16,48},{32,0},{48,16},{1,33},{17,49},{33,1},{49,17},{2,34}... | collective-permute-start | bytes 1572872 | tf_op jit(solution)/shard_map/sums/ppermute | solution.py:218
  130.6 2.7 %collective-permute-start.21 = (bf16[512,512]{1,0:T(8,128)(2,1)S(1)}, bf16[512,512]{1,0:T(8,128)(2,1)S(1)}, u32[]{:S(2)}, u32[]{:S(2)}) collective-permute-start(bf16[512,512]{1,0:T(8,128)(2,1)S(1)} %get-tuple-element.73), channel_id=1, source_target_pairs={{0,48},{16,0},{32,16},{48,32},{1,49},{17,1},{33,17},{49,33},{2,50}... | collective-permute-start | bytes 1572872 | tf_op jit(solution)/shard_map/sums/ppermute | solution.py:218
  133.3 5.2 %all-to-all-done.3 = f32[8,16,512]{2,1,0:T(8,128)} async-done(((f32[8,16,512]{2,1,0:T(8,128)}), f32[8,16,512]{2,1,0:T(8,128)}, u32[]{:S(2)}, u32[]{:S(2)}) %all-to-all-start.3) | async-done | bytes 262176 | tf_op jit(solution)/shard_map/sums/all_to_all | solution.py:222
  138.5 0.9 fusion.7
  139.4 2.5 %collective-permute-done.19.refs_0_ = bf16[512,512]{1,0:T(8,128)(2,1)S(1)} collective-permute-done((bf16[512,512]{1,0:T(8,128)(2,1)S(1)}, bf16[512,512]{1,0:T(8,128)(2,1)S(1)}, u32[]{:S(2)}, u32[]{:S(2)}) %collective-permute-start.19) | collective-permute-done | bytes 524320 | tf_op jit(solution)/shard_map/sums/ppermute | solution.py:218
  141.9 12.9 %collective-permute-done.20.refs_1_ = bf16[512,512]{1,0:T(8,128)(2,1)S(1)} collective-permute-done((bf16[512,512]{1,0:T(8,128)(2,1)S(1)}, bf16[512,512]{1,0:T(8,128)(2,1)S(1)}, u32[]{:S(2)}, u32[]{:S(2)}) %collective-permute-start.20) | collective-permute-done | bytes 524320 | tf_op jit(solution)/shard_map/sums/ppermute | solution.py:218
  154.9 1.2 copy-done.4
  156.1 1.0 plane_sum.1
  157.1 1.1 broadcast_in_dim.8
  158.2 4.5 %all-to-all-start.4 = ((f32[32,16,512]{2,1,0:T(8,128)}), f32[32,16,512]{2,1,0:T(8,128)S(1)}, u32[]{:S(2)}, u32[]{:S(2)}) async-start(f32[32,16,512]{2,1,0:T(8,128)} %broadcast_in_dim.8), calls=%async_computation.4 | async-start | bytes 2097152 | tf_op jit(solution)/shard_map/sums/all_to_all | solution.py:222
  162.7 2.8 %collective-permute-start.28 = (bf16[64,512]{1,0:T(8,128)(2,1)S(1)}, bf16[64,512]{1,0:T(8,128)(2,1)S(1)}, u32[]{:S(2)}, u32[]{:S(2)}) collective-permute-start(bf16[64,512]{1,0:T(8,128)(2,1)S(1)} %get-tuple-element.86), channel_id=1, source_target_pairs={{0,14},{2,0},{4,2},{6,4},{8,6},{10,8},{12,10},{14,12},{1,15},{3,1}... | collective-permute-start | bytes 196616 | tf_op jit(solution)/shard_map/sums/ppermute | solution.py:218
  165.4 2.4 %collective-permute-start.26 = (bf16[64,512]{1,0:T(8,128)(2,1)S(1)}, bf16[64,512]{1,0:T(8,128)(2,1)S(1)}, u32[]{:S(2)}, u32[]{:S(2)}) collective-permute-start(bf16[64,512]{1,0:T(8,128)(2,1)S(1)} %get-tuple-element.84), channel_id=1, source_target_pairs={{0,12},{2,14},{4,0},{6,2},{8,4},{10,6},{12,8},{14,10},{1,13},{3,15... | collective-permute-start | bytes 196616 | tf_op jit(solution)/shard_map/sums/ppermute | solution.py:218
  167.8 3.3 %collective-permute-start.24 = (bf16[64,512]{1,0:T(8,128)(2,1)S(1)}, bf16[64,512]{1,0:T(8,128)(2,1)S(1)}, u32[]{:S(2)}, u32[]{:S(2)}) collective-permute-start(bf16[64,512]{1,0:T(8,128)(2,1)S(1)} %get-tuple-element.82), channel_id=1, source_target_pairs={{0,10},{2,12},{4,14},{6,0},{8,2},{10,4},{12,6},{14,8},{1,11},{3,13... | collective-permute-start | bytes 196616 | tf_op jit(solution)/shard_map/sums/ppermute | solution.py:218
  171.1 1.2 collective-permute-start.23
  172.3 3.0 %collective-permute-start.22 = (bf16[64,512]{1,0:T(8,128)(2,1)S(1)}, bf16[64,512]{1,0:T(8,128)(2,1)S(1)}, u32[]{:S(2)}, u32[]{:S(2)}) collective-permute-start(bf16[64,512]{1,0:T(8,128)(2,1)S(1)} %get-tuple-element.80), channel_id=1, source_target_pairs={{0,8},{2,10},{4,12},{6,14},{8,0},{10,2},{12,4},{14,6},{1,9},{3,11}... | collective-permute-start | bytes 196616 | tf_op jit(solution)/shard_map/sums/ppermute | solution.py:218
  175.2 2.9 %collective-permute-done.23 = bf16[64,512]{1,0:T(8,128)(2,1)S(1)} collective-permute-done((bf16[64,512]{1,0:T(8,128)(2,1)S(1)}, bf16[64,512]{1,0:T(8,128)(2,1)S(1)}, u32[]{:S(2)}, u32[]{:S(2)}) %collective-permute-start.23) | collective-permute-done | bytes 65568 | tf_op jit(solution)/shard_map/sums/ppermute | solution.py:218
  178.2 1.6 collective-permute-done.22
  179.8 0.7 add_convert_fusion
  180.5 1.0 copy.22
  (66 shorter events, 1.1 us)
Async XLA Ops:
  0.6 13.4 %copy-start.13 = (bf16[32,128,128]{2,1,0:T(8,128)(2,1)S(1)}, bf16[32,128,128]{2,1,0:T(8,128)(2,1)}, u32[]{:S(2)}) copy-start(bf16[32,128,128]{2,1,0:T(8,128)(2,1)} %param.10) | copy-start | bytes 3145732
  2.1 13.1 %copy-start.1 = (s32[8192,2]{0,1:T(2,128)S(1)}, s32[8192,2]{0,1:T(2,128)}, u32[]{:S(2)}) copy-start(s32[8192,2]{0,1:T(2,128)} %param.14) | copy-start | bytes 196612
  2.1 13.1 %copy-start.2 = (s32[8192,2]{0,1:T(2,128)S(1)}, s32[8192,2]{0,1:T(2,128)}, u32[]{:S(2)}) copy-start(s32[8192,2]{0,1:T(2,128)} %param.15) | copy-start | bytes 196612
  2.1 35.8 %collective-permute-start = (s32[65]{0:T(128)S(1)}, s32[65]{0:T(128)S(1)}, u32[]{:S(2)}, u32[]{:S(2)}) collective-permute-start(s32[65]{0:T(128)S(1)} %pad_add_fusion.2), channel_id=1, source_target_pairs={{0,1},{1,0},{2,3},{3,2},{4,5},{5,4},{6,7},{7,6},{8,9},{9,8},{10,11... | collective-permute-start | bytes 788 | tf_op jit(solution)/shard_map/tile_matrix/ppermute | solution.py:214
  7.6 24.5 %all-to-all-start = ((bf16[8,64,512]{2,1,0:T(8,128)(2,1)}), bf16[8,64,512]{2,1,0:T(8,128)(2,1)S(1)}, u32[]{:S(2)}, u32[]{:S(2)}) async-start(bf16[8,64,512]{2,1,0:T(8,128)(2,1)} %broadcast_in_dim.6), calls=%async_computation | async-start | bytes 1048576 | tf_op jit(solution)/shard_map/pair_exchange/all_to_all | solution.py:222
  14.9 23.0 %collective-permute-start.1 = (bf16[32,64,128]{2,1,0:T(8,128)(2,1)}, bf16[32,64,128]{2,1,0:T(8,128)(2,1)S(1)}, u32[]{:S(2)}, u32[]{:S(2)}) collective-permute-start(bf16[32,64,128]{2,1,0:T(8,128)(2,1)} %get-tuple-element.88), channel_id=1, source_target_pairs={{0,1},{1,0},{2,3},{3,2},{4,5},{5,4},{6,7},{7,6},{8,9},{9,8},{10,11... | collective-permute-start | bytes 1572872 | tf_op jit(solution)/shard_map/tile_matrix/ppermute | solution.py:214
  15.2 22.4 %copy-start.15 = (s32[32]{0:T(128)S(1)}, s32[32]{0:T(128)}, u32[]{:S(2)}) copy-start(s32[32]{0:T(128)} %param.12) | copy-start | bytes 388
  15.2 22.4 %copy-start.16 = (s32[32]{0:T(128)S(1)}, s32[32]{0:T(128)}, u32[]{:S(2)}) copy-start(s32[32]{0:T(128)} %param.11) | copy-start | bytes 388
  15.2 22.5 %copy-start.14 = (bf16[64,512]{1,0:T(8,128)(2,1)S(1)}, bf16[64,512]{1,0:T(8,128)(2,1)}, u32[]{:S(2)}) copy-start(bf16[64,512]{1,0:T(8,128)(2,1)} %param.8) | copy-start | bytes 196612
  32.1 17.5 %all-to-all-start.1 = ((bf16[64,2,1024]{2,1,0:T(2,128)(2,1)}), bf16[64,2,1024]{2,1,0:T(2,128)(2,1)S(1)}, u32[]{:S(2)}, u32[]{:S(2)}) async-start(bf16[64,2,1024]{2,1,0:T(2,128)(2,1)} %reshape.35), calls=%async_computation.1 | async-start | bytes 524288 | tf_op jit(solution)/shard_map/pair_exchange/all_to_all | solution.py:222
  40.4 1.3 copy-start.5
  41.7 1.4 copy-start.7
  43.1 19.6 %collective-permute-start.2 = (bf16[512,512]{1,0:T(8,128)(2,1)S(1)}, bf16[512,512]{1,0:T(8,128)(2,1)S(1)}, u32[]{:S(2)}, u32[]{:S(2)}) collective-permute-start(bf16[512,512]{1,0:T(8,128)(2,1)S(1)} %bitcast.29), channel_id=1, source_target_pairs={{0,48},{16,0},{32,16},{48,32},{1,49},{17,1},{33,17},{49,33},{2,50}... | collective-permute-start | bytes 1572872 | tf_op jit(solution)/shard_map/pair_exchange/ppermute | solution.py:218
  45.6 17.0 %collective-permute-start.3 = (bf16[512,512]{1,0:T(8,128)(2,1)S(1)}, bf16[512,512]{1,0:T(8,128)(2,1)S(1)}, u32[]{:S(2)}, u32[]{:S(2)}) collective-permute-start(bf16[512,512]{1,0:T(8,128)(2,1)S(1)} %bitcast.30), channel_id=1, source_target_pairs={{0,32},{16,48},{32,0},{48,16},{1,33},{17,49},{33,1},{49,17},{2,34}... | collective-permute-start | bytes 1572872 | tf_op jit(solution)/shard_map/pair_exchange/ppermute | solution.py:218
  45.9 26.3 %collective-permute-start.4 = (bf16[512,512]{1,0:T(8,128)(2,1)S(1)}, bf16[512,512]{1,0:T(8,128)(2,1)S(1)}, u32[]{:S(2)}, u32[]{:S(2)}) collective-permute-start(bf16[512,512]{1,0:T(8,128)(2,1)S(1)} %bitcast.31), channel_id=1, source_target_pairs={{0,16},{16,32},{32,48},{48,0},{1,17},{17,33},{33,49},{49,1},{2,18}... | collective-permute-start | bytes 1572872 | tf_op jit(solution)/shard_map/pair_exchange/ppermute | solution.py:218
  61.3 1.4 copy-start.11
  73.0 18.7 %all-to-all-start.2 = ((bf16[8,2,2048]{2,1,0:T(2,128)(2,1)}), bf16[8,2,2048]{2,1,0:T(2,128)(2,1)S(1)}, u32[]{:S(2)}, u32[]{:S(2)}) async-start(bf16[8,2,2048]{2,1,0:T(2,128)(2,1)} %reshape.42), calls=%async_computation.2 | async-start | bytes 131072 | tf_op jit(solution)/shard_map/tile_matrix/all_to_all | solution.py:222
  77.8 14.1 %collective-permute-start.5 = (bf16[512,512]{1,0:T(8,128)(2,1)S(1)}, bf16[512,512]{1,0:T(8,128)(2,1)S(1)}, u32[]{:S(2)}, u32[]{:S(2)}) collective-permute-start(bf16[512,512]{1,0:T(8,128)(2,1)S(1)} %bitcast.32), channel_id=1, source_target_pairs={{0,1},{1,0},{2,3},{3,2},{4,5},{5,4},{6,7},{7,6},{8,9},{9,8},{10,11... | collective-permute-start | bytes 1572872 | tf_op jit(solution)/shard_map/pair_exchange/ppermute | solution.py:214
  77.8 14.1 %collective-permute-start.6 = (bf16[512,512]{1,0:T(8,128)(2,1)S(1)}, bf16[512,512]{1,0:T(8,128)(2,1)}, u32[]{:S(2)}, u32[]{:S(2)}) collective-permute-start(bf16[512,512]{1,0:T(8,128)(2,1)S(1)} %collective-permute-done.2.refs_1_), channel_id=1, source_target_pairs={{0,1},{1,0},{2,3},{3,2},{4,5},{5,4},{6,7},{7,6},{8,9},{9,8},{10,11... | collective-permute-start | bytes 1572872 | tf_op jit(solution)/shard_map/pair_exchange/ppermute | solution.py:214
  78.3 13.6 %collective-permute-start.7 = (bf16[512,512]{1,0:T(8,128)(2,1)S(1)}, bf16[512,512]{1,0:T(8,128)(2,1)}, u32[]{:S(2)}, u32[]{:S(2)}) collective-permute-start(bf16[512,512]{1,0:T(8,128)(2,1)S(1)} %collective-permute-done.3.refs_2_), channel_id=1, source_target_pairs={{0,1},{1,0},{2,3},{3,2},{4,5},{5,4},{6,7},{7,6},{8,9},{9,8},{10,11... | collective-permute-start | bytes 1572872 | tf_op jit(solution)/shard_map/pair_exchange/ppermute | solution.py:214
  78.3 13.6 %collective-permute-start.8 = (bf16[512,512]{1,0:T(8,128)(2,1)S(1)}, bf16[512,512]{1,0:T(8,128)(2,1)}, u32[]{:S(2)}, u32[]{:S(2)}) collective-permute-start(bf16[512,512]{1,0:T(8,128)(2,1)S(1)} %collective-permute-done.4.refs_3_), channel_id=1, source_target_pairs={{0,1},{1,0},{2,3},{3,2},{4,5},{5,4},{6,7},{7,6},{8,9},{9,8},{10,11... | collective-permute-start | bytes 1572872 | tf_op jit(solution)/shard_map/pair_exchange/ppermute | solution.py:214
  78.8 1.6 copy-start.12
  90.4 1.4 copy-start.9
  91.9 1.6 copy-start.10
  93.5 23.4 %copy-start.8 = (bf16[2048,512]{1,0:T(8,128)(2,1)S(1)}, bf16[2048,512]{1,0:T(8,128)(2,1)}, u32[]{:S(2)}) copy-start(bf16[2048,512]{1,0:T(8,128)(2,1)} %copy-done.7) | copy-start | bytes 6291460
  98.6 18.3 %copy-start = (bf16[512,512]{1,0:T(8,128)(2,1)S(1)}, bf16[512,512]{1,0:T(8,128)(2,1)}, u32[]{:S(2)}) copy-start(bf16[512,512]{1,0:T(8,128)(2,1)} %weight_ref.1) | copy-start | bytes 1572868
  98.6 18.2 %copy-start.6 = (bf16[2048,512]{1,0:T(8,128)(2,1)S(1)}, bf16[2048,512]{1,0:T(8,128)(2,1)}, u32[]{:S(2)}) copy-start(bf16[2048,512]{1,0:T(8,128)(2,1)} %copy-done.5) | copy-start | bytes 6291460
  98.8 7.0 %collective-permute-start.9 = (bf16[64,512]{1,0:T(8,128)(2,1)S(1)}, bf16[64,512]{1,0:T(8,128)(2,1)S(1)}, u32[]{:S(2)}, u32[]{:S(2)}) collective-permute-start(bf16[64,512]{1,0:T(8,128)(2,1)S(1)} %fusion.6.refs_0_), channel_id=1, source_target_pairs={{64,0},{65,1},{128,64},{129,65},{192,128},{193,129},{0,192},{1,193... | collective-permute-start | bytes 196616 | tf_op jit(solution)/shard_map/spread/ppermute | solution.py:324
  101.4 5.9 %collective-permute-start.10 = (bf16[64,512]{1,0:T(8,128)(2,1)S(1)}, bf16[64,512]{1,0:T(8,128)(2,1)S(1)}, u32[]{:S(2)}, u32[]{:S(2)}) collective-permute-start(bf16[64,512]{1,0:T(8,128)(2,1)S(1)} %fusion.6.refs_0_), channel_id=1, source_target_pairs={{128,0},{129,1},{192,64},{193,65},{0,128},{1,129},{64,192},{65,193... | collective-permute-start | bytes 196616 | tf_op jit(solution)/shard_map/spread/ppermute | solution.py:324
  102.0 5.4 %collective-permute-start.11 = (bf16[64,512]{1,0:T(8,128)(2,1)S(1)}, bf16[64,512]{1,0:T(8,128)(2,1)S(1)}, u32[]{:S(2)}, u32[]{:S(2)}) collective-permute-start(bf16[64,512]{1,0:T(8,128)(2,1)S(1)} %fusion.6.refs_0_), channel_id=1, source_target_pairs={{192,0},{193,1},{0,64},{1,65},{64,128},{65,129},{128,192},{129,193... | collective-permute-start | bytes 196616 | tf_op jit(solution)/shard_map/spread/ppermute | solution.py:324
  102.6 4.8 %collective-permute-start.12 = (bf16[64,512]{1,0:T(8,128)(2,1)S(1)}, bf16[64,512]{1,0:T(8,128)(2,1)S(1)}, u32[]{:S(2)}, u32[]{:S(2)}) collective-permute-start(bf16[64,512]{1,0:T(8,128)(2,1)S(1)} %fusion.6.refs_0_), channel_id=1, source_target_pairs={{1,0},{0,1},{65,64},{64,65},{129,128},{128,129},{193,192},{192,193... | collective-permute-start | bytes 196616 | tf_op jit(solution)/shard_map/spread/ppermute | solution.py:324
  103.8 4.1 %collective-permute-start.13 = (bf16[64,512]{1,0:T(8,128)(2,1)S(1)}, bf16[64,512]{1,0:T(8,128)(2,1)S(1)}, u32[]{:S(2)}, u32[]{:S(2)}) collective-permute-start(bf16[64,512]{1,0:T(8,128)(2,1)S(1)} %fusion.6.refs_0_), channel_id=1, source_target_pairs={{65,0},{64,1},{129,64},{128,65},{193,128},{192,129},{1,192},{0,193... | collective-permute-start | bytes 196616 | tf_op jit(solution)/shard_map/spread/ppermute | solution.py:324
  105.8 5.9 %collective-permute-start.14 = (bf16[64,512]{1,0:T(8,128)(2,1)S(1)}, bf16[64,512]{1,0:T(8,128)(2,1)S(1)}, u32[]{:S(2)}, u32[]{:S(2)}) collective-permute-start(bf16[64,512]{1,0:T(8,128)(2,1)S(1)} %fusion.6.refs_0_), channel_id=1, source_target_pairs={{129,0},{128,1},{193,64},{192,65},{1,128},{0,129},{65,192},{64,193... | collective-permute-start | bytes 196616 | tf_op jit(solution)/shard_map/spread/ppermute | solution.py:324
  107.4 5.9 %collective-permute-start.15 = (bf16[64,512]{1,0:T(8,128)(2,1)S(1)}, bf16[64,512]{1,0:T(8,128)(2,1)S(1)}, u32[]{:S(2)}, u32[]{:S(2)}) collective-permute-start(bf16[64,512]{1,0:T(8,128)(2,1)S(1)} %fusion.6.refs_0_), channel_id=1, source_target_pairs={{193,0},{192,1},{1,64},{0,65},{65,128},{64,129},{129,192},{128,193... | collective-permute-start | bytes 196616 | tf_op jit(solution)/shard_map/spread/ppermute | solution.py:324
  114.1 7.0 %collective-permute-start.16 = (f32[16,512]{1,0:T(8,128)S(1)}, f32[16,512]{1,0:T(8,128)S(1)}, u32[]{:S(2)}, u32[]{:S(2)}) collective-permute-start(f32[16,512]{1,0:T(8,128)S(1)} %get-tuple-element.62), channel_id=1, source_target_pairs={{0,16},{16,32},{32,48},{48,0},{1,17},{17,33},{33,49},{49,1},{2,18}... | collective-permute-start | bytes 98312 | tf_op jit(solution)/shard_map/sums/ppermute | solution.py:218
  114.2 6.9 %collective-permute-start.17 = (f32[16,512]{1,0:T(8,128)S(1)}, f32[16,512]{1,0:T(8,128)S(1)}, u32[]{:S(2)}, u32[]{:S(2)}) collective-permute-start(f32[16,512]{1,0:T(8,128)S(1)} %get-tuple-element.63), channel_id=1, source_target_pairs={{0,32},{16,48},{32,0},{48,16},{1,33},{17,49},{33,1},{49,17},{2,34}... | collective-permute-start | bytes 98312 | tf_op jit(solution)/shard_map/sums/ppermute | solution.py:218
  115.7 5.4 %collective-permute-start.18 = (f32[16,512]{1,0:T(8,128)S(1)}, f32[16,512]{1,0:T(8,128)S(1)}, u32[]{:S(2)}, u32[]{:S(2)}) collective-permute-start(f32[16,512]{1,0:T(8,128)S(1)} %get-tuple-element.64), channel_id=1, source_target_pairs={{0,48},{16,0},{32,16},{48,32},{1,49},{17,1},{33,17},{49,33},{2,50}... | collective-permute-start | bytes 98312 | tf_op jit(solution)/shard_map/sums/ppermute | solution.py:218
  120.2 1.0 copy-start.3
  121.9 16.6 %all-to-all-start.3 = ((f32[8,16,512]{2,1,0:T(8,128)}), f32[8,16,512]{2,1,0:T(8,128)}, u32[]{:S(2)}, u32[]{:S(2)}) async-start(f32[8,16,512]{2,1,0:T(8,128)} %broadcast_in_dim.7), calls=%async_computation.3 | async-start | bytes 524288 | tf_op jit(solution)/shard_map/sums/all_to_all | solution.py:222
  128.3 13.6 %collective-permute-start.19 = (bf16[512,512]{1,0:T(8,128)(2,1)S(1)}, bf16[512,512]{1,0:T(8,128)(2,1)S(1)}, u32[]{:S(2)}, u32[]{:S(2)}) collective-permute-start(bf16[512,512]{1,0:T(8,128)(2,1)S(1)} %get-tuple-element.71), channel_id=1, source_target_pairs={{0,32},{16,48},{32,0},{48,16},{1,33},{17,49},{33,1},{49,17},{2,34}... | collective-permute-start | bytes 1572872 | tf_op jit(solution)/shard_map/sums/ppermute | solution.py:218
  130.6 24.2 %collective-permute-start.20 = (bf16[512,512]{1,0:T(8,128)(2,1)S(1)}, bf16[512,512]{1,0:T(8,128)(2,1)S(1)}, u32[]{:S(2)}, u32[]{:S(2)}) collective-permute-start(bf16[512,512]{1,0:T(8,128)(2,1)S(1)} %get-tuple-element.72), channel_id=1, source_target_pairs={{0,16},{16,32},{32,48},{48,0},{1,17},{17,33},{33,49},{49,1},{2,18}... | collective-permute-start | bytes 1572872 | tf_op jit(solution)/shard_map/sums/ppermute | solution.py:218
  130.6 24.2 %collective-permute-start.21 = (bf16[512,512]{1,0:T(8,128)(2,1)S(1)}, bf16[512,512]{1,0:T(8,128)(2,1)S(1)}, u32[]{:S(2)}, u32[]{:S(2)}) collective-permute-start(bf16[512,512]{1,0:T(8,128)(2,1)S(1)} %get-tuple-element.73), channel_id=1, source_target_pairs={{0,48},{16,0},{32,16},{48,32},{1,49},{17,1},{33,17},{49,33},{2,50}... | collective-permute-start | bytes 1572872 | tf_op jit(solution)/shard_map/sums/ppermute | solution.py:218
  154.9 1.2 copy-start.4
  158.2 22.3 %all-to-all-start.4 = ((f32[32,16,512]{2,1,0:T(8,128)}), f32[32,16,512]{2,1,0:T(8,128)S(1)}, u32[]{:S(2)}, u32[]{:S(2)}) async-start(f32[32,16,512]{2,1,0:T(8,128)} %broadcast_in_dim.8), calls=%async_computation.4 | async-start | bytes 2097152 | tf_op jit(solution)/shard_map/sums/all_to_all | solution.py:222
  162.7 8.4 %collective-permute-start.28 = (bf16[64,512]{1,0:T(8,128)(2,1)S(1)}, bf16[64,512]{1,0:T(8,128)(2,1)S(1)}, u32[]{:S(2)}, u32[]{:S(2)}) collective-permute-start(bf16[64,512]{1,0:T(8,128)(2,1)S(1)} %get-tuple-element.86), channel_id=1, source_target_pairs={{0,14},{2,0},{4,2},{6,4},{8,6},{10,8},{12,10},{14,12},{1,15},{3,1}... | collective-permute-start | bytes 196616 | tf_op jit(solution)/shard_map/sums/ppermute | solution.py:218
  165.4 6.8 %collective-permute-start.27 = (bf16[64,512]{1,0:T(8,128)(2,1)S(1)}, bf16[64,512]{1,0:T(8,128)(2,1)S(1)}, u32[]{:S(2)}, u32[]{:S(2)}) collective-permute-start(bf16[64,512]{1,0:T(8,128)(2,1)S(1)} %get-tuple-element.85), channel_id=1, source_target_pairs={{0,2},{2,4},{4,6},{6,8},{8,10},{10,12},{12,14},{14,0},{1,3},{3,5},... | collective-permute-start | bytes 196616 | tf_op jit(solution)/shard_map/sums/ppermute | solution.py:218
  165.4 9.8 %collective-permute-start.26 = (bf16[64,512]{1,0:T(8,128)(2,1)S(1)}, bf16[64,512]{1,0:T(8,128)(2,1)S(1)}, u32[]{:S(2)}, u32[]{:S(2)}) collective-permute-start(bf16[64,512]{1,0:T(8,128)(2,1)S(1)} %get-tuple-element.84), channel_id=1, source_target_pairs={{0,12},{2,14},{4,0},{6,2},{8,4},{10,6},{12,8},{14,10},{1,13},{3,15... | collective-permute-start | bytes 196616 | tf_op jit(solution)/shard_map/sums/ppermute | solution.py:218
  167.8 7.4 %collective-permute-start.25 = (bf16[64,512]{1,0:T(8,128)(2,1)S(1)}, bf16[64,512]{1,0:T(8,128)(2,1)S(1)}, u32[]{:S(2)}, u32[]{:S(2)}) collective-permute-start(bf16[64,512]{1,0:T(8,128)(2,1)S(1)} %get-tuple-element.83), channel_id=1, source_target_pairs={{0,4},{2,6},{4,8},{6,10},{8,12},{10,14},{12,0},{14,2},{1,5},{3,7},... | collective-permute-start | bytes 196616 | tf_op jit(solution)/shard_map/sums/ppermute | solution.py:218
  167.8 7.4 %collective-permute-start.24 = (bf16[64,512]{1,0:T(8,128)(2,1)S(1)}, bf16[64,512]{1,0:T(8,128)(2,1)S(1)}, u32[]{:S(2)}, u32[]{:S(2)}) collective-permute-start(bf16[64,512]{1,0:T(8,128)(2,1)S(1)} %get-tuple-element.82), channel_id=1, source_target_pairs={{0,10},{2,12},{4,14},{6,0},{8,2},{10,4},{12,6},{14,8},{1,11},{3,13... | collective-permute-start | bytes 196616 | tf_op jit(solution)/shard_map/sums/ppermute | solution.py:218
  171.1 7.1 %collective-permute-start.23 = (bf16[64,512]{1,0:T(8,128)(2,1)S(1)}, bf16[64,512]{1,0:T(8,128)(2,1)S(1)}, u32[]{:S(2)}, u32[]{:S(2)}) collective-permute-start(bf16[64,512]{1,0:T(8,128)(2,1)S(1)} %get-tuple-element.81), channel_id=1, source_target_pairs={{0,6},{2,8},{4,10},{6,12},{8,14},{10,0},{12,2},{14,4},{1,7},{3,9},... | collective-permute-start | bytes 196616 | tf_op jit(solution)/shard_map/sums/ppermute | solution.py:218
  172.3 7.5 %collective-permute-start.22 = (bf16[64,512]{1,0:T(8,128)(2,1)S(1)}, bf16[64,512]{1,0:T(8,128)(2,1)S(1)}, u32[]{:S(2)}, u32[]{:S(2)}) collective-permute-start(bf16[64,512]{1,0:T(8,128)(2,1)S(1)} %get-tuple-element.80), channel_id=1, source_target_pairs={{0,8},{2,10},{4,12},{6,14},{8,0},{10,2},{12,4},{14,6},{1,9},{3,11}... | collective-permute-start | bytes 196616 | tf_op jit(solution)/shard_map/sums/ppermute | solution.py:218

commit v2 on v1

--- a/solution.py
+++ b/solution.py
@@ -81,8 +81,7 @@
         out_ref[:, v * CAP : (v + 1) * CAP] = acc[v * NDEV : (v + 1) * NDEV, :].astype(BF)
 
 
-def count_kernel(first, coord_ref, _, recv_ref, *refs):
-    out_ref, token_ref, left_at, right_at, weight_at = refs[-5:]
+def count_kernel(coord_ref, recv_ref, near_ref, far_ref, token_ref, left_at, right_at, weight_at):
     token_ref[...] = jnp.zeros_like(token_ref)
     y, c = coord_ref[0], coord_ref[1]
     weight_at[...] = recv_ref[:, 0:CAP].astype(F32)
@@ -92,18 +91,16 @@
     piece = ((owner & 1) ^ c) * NY + (((owner >> 4) - y) & (NY - 1))
     left_at[...] = piece * ROWS + own_row
     right_at[...] = ((owner >> 1) & (NZ - 1)) * ROWS + row
-    if first:
-        out_ref[...] = jnp.zeros_like(out_ref)
-    else:
-        out_ref[...] = refs[0][...]
+    near_ref[...] = jnp.zeros_like(near_ref)
+    far_ref[...] = jnp.zeros_like(far_ref)
     group = 7
     groups = NDEV // group
-    half = (groups + 1) // 2
-
-    def add(start, size):
+    size = NY * ROWS
+
+    def add(start, count):
         spots = lax.broadcasted_iota(I32, (CAP, CAP), 0)
         left, right = [], []
-        for s in range(size):
+        for s in range(count):
             here = pl.ds(start + s, 1)
             left.append(jnp.where(spots == left_at[here, :], weight_at[here, :], 0.0).astype(BF))
             right.append(jnp.where(spots == right_at[here, :], 1.0, 0.0).astype(BF))
@@ -111,23 +108,25 @@
             jnp.concatenate(left, axis=1), jnp.concatenate(right, axis=1), NT, preferred_element_type=F32
         )
         ones = jnp.floor(total * (1.0 / POS))
-        out_ref[0] += total - (POS - 1.0) * ones
-        out_ref[1] += ones
+        both = total - (POS - 1.0) * ones
+        near_ref[0] += both[:size]
+        near_ref[1] += ones[:size]
+        far_ref[0] += both[size:]
+        far_ref[1] += ones[size:]
 
     def body(g, carry):
         add(g * group, group)
         return carry
 
-    lax.fori_loop(0 if first else half, half if first else groups, body, 0)
-    if not first:
-        add(groups * group, NDEV - groups * group)
+    lax.fori_loop(0, groups, body, 0)
+    add(groups * group, NDEV - groups * group)
 
 
 def grad_kernel(scale, _, own_ref, count_ref, *refs):
-    pieces, out_ref = refs[:-1], refs[-1]
+    pieces, rest, out_ref = refs[:NY], refs[NY:-1], refs[-1]
     own = own_ref[...]
-    total = jnp.zeros((ROWS, F), F32)
-    for k in range(NY * NC):
+    total = rest[0][...] if rest else jnp.zeros((ROWS, F), F32)
+    for k in range(NY):
         nodes = pieces[k][...]
         score = lax.dot_general(own, nodes, NT, preferred_element_type=F32) / math.sqrt(F)
         here = slice(k * ROWS, (k + 1) * ROWS)
@@ -166,31 +165,32 @@
 
 
 def spread_kernel(coord_ref, _, weight_ref, high_ref, low_ref, *refs):
-    pre_refs, out_refs, token_ref, pre = refs[:8], refs[8:-2], refs[-2], refs[-1]
-    token_ref[...] = jnp.zeros_like(token_ref)
-    y, x = coord_ref[0], coord_ref[2]
+    pre_refs, out_ref, token_ref, pre = refs[:NC], refs[NC], refs[-2], refs[-1]
+    token_ref[...] = jnp.zeros_like(token_ref)
+    x = coord_ref[2]
     for k in range(NC * NX):
         dc, dx = k // NX, k % NX
         place = pl.multiple_of((dc * NX + ((x + dx) & (NX - 1))) * ROWS, ROWS)
-        pre[pl.ds(place, ROWS), :] = pre_refs[k][...]
+        pre[pl.ds(place, ROWS), :] = pre_refs[dc][dx * ROWS : (dx + 1) * ROWS, :]
     agg = lax.dot_general(pre[...], weight_ref[...], NT, preferred_element_type=F32).astype(BF)
     size = NZ * ROWS
     for k in range(NY):
-        rows = pl.ds(pl.multiple_of(((y + k) & (NY - 1)) * size, size), size)
+        rows = slice(k * size, (k + 1) * size)
         part = jnp.dot(high_ref[rows, :], agg, preferred_element_type=F32)
         part += jnp.dot(low_ref[rows, :], agg, preferred_element_type=F32)
-        out_refs[k][...] = part.astype(out_refs[k].dtype)
+        out_ref[k] = part.astype(BF)
 
 
 def terms_kernel(coord_ref, node_ref, *refs):
-    pre_refs, out_refs, token_ref, terms = refs[:8], refs[8:12], refs[12], refs[13]
+    pre_refs, out_refs, token_ref, terms = refs[:NC], refs[NC:-2], refs[-2], refs[-1]
     token_ref[...] = jnp.zeros_like(token_ref)
     y, c, x = coord_ref[0], coord_ref[1], coord_ref[2]
     total = jnp.zeros(terms.shape, F32)
     for k in range(NC * NX):
         dc, dx = k // NX, k % NX
         node = node_ref[((x + dx) & (NX - 1)) * NC + (c ^ dc)]
-        total += lax.dot_general(node, pre_refs[k][...], TN, preferred_element_type=F32)
+        pre = pre_refs[dc][dx * ROWS : (dx + 1) * ROWS, :]
+        total += lax.dot_general(node, pre, TN, preferred_element_type=F32)
     terms[...] = total
     size = ROWS // NY
     for k in range(NY):
@@ -198,18 +198,30 @@
         out_refs[k][...] = terms[rows, :]
 
 
-def plane_kernel(coord_ref, _, keep_ref, *refs):
-    in_refs, out_refs, total = refs[:3], refs[3:-1], refs[-1]
+def plane_kernel(coord_ref, _, in_ref, *refs):
+    out_refs, total = refs[:-1], refs[-1]
     z = coord_ref[3]
-    value = keep_ref[...]
-    for ref in in_refs:
-        value = value + ref[...].astype(F32)
+    value = in_ref[0].astype(F32)
+    for k in range(1, NY):
+        value = value + in_ref[k].astype(F32)
     total[...] = value
     for k in range(NZ):
         rows = pl.ds(pl.multiple_of(((z + k) & (NZ - 1)) * ROWS, ROWS), ROWS)
         out_refs[k][...] = total[rows, :].astype(out_refs[k].dtype)
 
 
+def share_kernel(coord_ref, *refs):
+    in_refs, out_ref, token_ref, parts = refs[:NZ], refs[NZ], refs[NZ + 1], refs[-1]
+    token_ref[...] = jnp.zeros_like(token_ref)
+    z = coord_ref[3]
+    for k in range(NZ):
+        parts[(z + k) & (NZ - 1)] = in_refs[k][...]
+    value = parts[0]
+    for k in range(1, NZ):
+        value = value + parts[k]
+    out_ref[...] = value
+
+
 def swap(values):
     return lax.ppermute(values, "c", [(0, 1), (1, 0)])
 
@@ -230,21 +242,34 @@
     return lax.dynamic_index_in_dim(values, place, 0, keepdims=False)
 
 
-def count(coord, token, received, *counted):
+def count(coord, received):
+    half = jax.ShapeDtypeStruct((2, NY * ROWS, NZ * ROWS), F32)
     return pl.pallas_call(
-        functools.partial(count_kernel, not counted),
-        out_shape=[jax.ShapeDtypeStruct((2, NY * NC * ROWS, NZ * ROWS), F32), TOKEN],
-        in_specs=[SMEM, ANY, VMEM] + [VMEM] * len(counted),
-        out_specs=[VMEM, VMEM],
+        count_kernel,
+        out_shape=[half, half, TOKEN],
+        in_specs=[SMEM, VMEM],
+        out_specs=[VMEM] * 3,
         scratch_shapes=[
             pltpu.VMEM((NDEV, CAP), I32),
             pltpu.VMEM((NDEV, CAP), I32),
             pltpu.VMEM((NDEV, CAP), F32),
         ],
         compiler_params=params(),
-        cost_estimate=pl.CostEstimate(flops=12_000_000_000, bytes_accessed=2_400_000, transcendentals=0),
+        cost_estimate=pl.CostEstimate(flops=24_000_000_000, bytes_accessed=2_400_000, transcendentals=0),
         name="count",
-    )(coord, token, received, *counted)
+    )(coord, received)
+
+
+def pair_grad(scale, token, own, counted, *arrays):
+    return pl.pallas_call(
+        functools.partial(grad_kernel, scale),
+        out_shape=jax.ShapeDtypeStruct((ROWS, F), F32),
+        in_specs=[ANY] + [VMEM] * (2 + len(arrays)),
+        out_specs=VMEM,
+        compiler_params=params(),
+        cost_estimate=pl.CostEstimate(flops=3_000_000_000, bytes_accessed=3_000_000, transcendentals=131072),
+        name="pair_grad",
+    )(token, own, counted, *arrays)
 
 
 def per_device(node_aggregate, weight, tiles, tile_src, tile_dst, tile_count, pair_owner, pair_row):
@@ -276,11 +301,7 @@
         ring, ends = lax.optimization_barrier((ring, ends))
         planes = [ring] + [shift(ring, "y", NY, -k) for k in range(1, NY)]
         received = exchange(ends, ("y", "z", "c")).reshape(NDEV, 4 * CAP)
-        counted, token = count(coord, token, received)
-        columns = node_aggregate.reshape(ROWS, NX * NC, ROWS).transpose(1, 0, 2)
-        planes, columns, token = lax.optimization_barrier((planes, columns, token))
-        planes = planes + [swap(plane) for plane in planes]
-        counted, _ = count(coord, token, received, counted)
+        near, far, token = count(coord, received)
 
     with jax.named_scope("tile_matrix"):
         halves = tiles.reshape(slots, 2, ROWS, tiles.shape[2]).transpose(1, 0, 2, 3)
@@ -288,7 +309,11 @@
         other_half = swap(pick(halves, 1 - c))
         meta = jnp.concatenate([tile_src, tile_dst, tile_count]).astype(I32)
         metas = jnp.stack([meta, swap(meta)])
-        high, low, token = pl.pallas_call(
+        columns = node_aggregate.reshape(ROWS, NX * NC, ROWS).transpose(1, 0, 2)
+        far_ring = swap(ring)
+        *planes, columns, metas, token = lax.optimization_barrier((*planes, columns, metas, token))
+        far_planes = [far_ring] + [swap(plane) for plane in planes[1:]]
+        high, low, tile_token = pl.pallas_call(
             tiles_kernel,
             out_shape=[jax.ShapeDtypeStruct((NY * NZ * ROWS, 512), BF)] * 2 + [TOKEN],
             in_specs=[SMEM, VMEM, VMEM],
@@ -301,45 +326,31 @@
         nodes = exchange(columns, ("x", "c"))
 
     with jax.named_scope("hidden_grad"):
-        own, token, nodes = lax.optimization_barrier((hidden_b, token, nodes))
-        hidden_grad = pl.pallas_call(
-            functools.partial(grad_kernel, ROWS / (2.0 * pair_total)),
-            out_shape=jax.ShapeDtypeStruct((ROWS, F), F32),
-            in_specs=[ANY] + [VMEM] * (2 + len(planes)),
-            out_specs=VMEM,
-            compiler_params=params(),
-            cost_estimate=pl.CostEstimate(flops=5_000_000_000, bytes_accessed=6_000_000, transcendentals=262144),
-            name="pair_grad",
-        )(token, own, counted, *planes)
+        scale = ROWS / (2.0 * pair_total)
+        hidden_grad = pair_grad(scale, token, hidden_b, near, *planes)
+        own, tile_token, nodes = lax.optimization_barrier((hidden_b, tile_token, nodes))
+        hidden_grad = pair_grad(scale, tile_token, own, far, *far_planes, hidden_grad)
         pre_grad = act_back(hidden_grad)[0].astype(BF)
 
     with jax.named_scope("spread"):
-        pre_parts = []
-        for dc in range(NC):
-            for dx in range(NX):
-                pairs = [
-                    (((x + dx) % NX) * NC + (b ^ dc), x * NC + b) for x in range(NX) for b in range(NC)
-                ]
-                away = dc + dx > 0
-                pre_parts.append(lax.ppermute(pre_grad, ("x", "c"), pairs) if away else pre_grad)
+        along_x = [pre_grad] + [shift(pre_grad, "x", NX, -k) for k in range(1, NX)]
+        near_pre = jnp.concatenate(along_x, axis=0)
+        pre_parts = [near_pre, swap(near_pre)]
         *terms, token = pl.pallas_call(
             terms_kernel,
             out_shape=[jax.ShapeDtypeStruct((ROWS // NY, F), F32)] * NY + [TOKEN],
-            in_specs=[SMEM] + [VMEM] * 9,
+            in_specs=[SMEM] + [VMEM] * 3,
             out_specs=[VMEM] * (NY + 1),
             scratch_shapes=[pltpu.VMEM((ROWS, F), F32)],
             compiler_params=params(),
             cost_estimate=pl.CostEstimate(flops=1_000_000_000, bytes_accessed=700_000, transcendentals=0),
             name="weight_terms",
         )(coord, nodes, *pre_parts)
-        keep, *send, token = pl.pallas_call(
+        send, token = pl.pallas_call(
             spread_kernel,
-            out_shape=[
-                jax.ShapeDtypeStruct((NZ * ROWS, F), dtype) for dtype in (F32,) + (BF,) * (NY - 1)
-            ]
-            + [TOKEN],
-            in_specs=[SMEM, ANY] + [VMEM] * 11,
-            out_specs=[VMEM] * (NY + 1),
+            out_shape=[jax.ShapeDtypeStruct((NY, NZ * ROWS, F), BF), TOKEN],
+            in_specs=[SMEM, ANY] + [VMEM] * 5,
+            out_specs=[VMEM] * 2,
             scratch_shapes=[pltpu.VMEM((NC * NX * ROWS, F), BF)],
             compiler_params=params(),
             cost_estimate=pl.CostEstimate(flops=5_000_000_000, bytes_accessed=8_000_000, transcendentals=0),
@@ -347,31 +358,36 @@
         )(coord, token, weight, high, low, *pre_parts)
 
     with jax.named_scope("sums"):
-        planes = [shift(send[k - 1], "y", NY, k) for k in (2, 1, 3)]
-        others = [shift(terms[k], "y", NY, k) for k in range(1, NY)]
-        *others, token = lax.optimization_barrier((*others, token))
+        planes = exchange(send, "y")
+        *terms, token = lax.optimization_barrier((*terms, token))
         share = terms[0]
-        for other in others:
-            share = share + other
-        shares = gather(share, "z", NZ)
-        block = shares[0]
-        for k in range(1, NZ):
-            block = block + shares[k]
+        for k in range(1, NY):
+            share = share + shift(terms[k], "y", NY, k)
+        block, share_token = pl.pallas_call(
+            share_kernel,
+            out_shape=[jax.ShapeDtypeStruct((ROWS // NY, F), F32), TOKEN],
+            in_specs=[SMEM] + [VMEM] * NZ,
+            out_specs=[VMEM] * 2,
+            scratch_shapes=[pltpu.VMEM((NZ, ROWS // NY, F), F32)],
+            compiler_params=params(),
+            cost_estimate=pl.CostEstimate(flops=1_000_000, bytes_accessed=300_000, transcendentals=0),
+            name="share_sum",
+        )(coord, share, *[shift(share, "z", NZ, -k) for k in range(1, NZ)])
+        token, share_token = lax.optimization_barrier((token, share_token))
         own, *parts = pl.pallas_call(
             plane_kernel,
             out_shape=[
                 jax.ShapeDtypeStruct((ROWS, F), dtype) for dtype in (F32,) + (BF,) * (NZ - 1)
             ],
-            in_specs=[SMEM, ANY] + [VMEM] * 4,
+            in_specs=[SMEM, ANY, VMEM],
             out_specs=[VMEM] * NZ,
             scratch_shapes=[pltpu.VMEM((NZ * ROWS, F), F32)],
             compiler_params=params(),
             cost_estimate=pl.CostEstimate(flops=2_000_000_000, bytes_accessed=3_000_000, transcendentals=0),
             name="plane_sum",
-        )(coord, token, keep, *planes)
-        own, block = lax.optimization_barrier((own, block))
+        )(coord, share_token, planes)
         feature = own
-        for k in (4, 3, 5, 2, 6, 1, 7):
+        for k in (1, 7, 4, 2, 6, 3, 5):
             feature = feature + shift(parts[k - 1], "z", NZ, k).astype(F32)
         feature_grad = feature.astype(BF)
         weight_grad = gather(block, ("x", "c", "y"), NX * NC * NY).reshape(F, F)

time: 185 us -> 187 us (1.011)
  starting transfers between devices: 64.8 us -> 76.1 us
  waiting for transfers between devices: 51.5 us -> 43.8 us
    ppermute x16 -> x23, starting transfers between devices: 24 us -> 41.5 us  [shift(): lax.ppermute(values, axis, [(i, (i + step) % size) for i in range(size)])]
    ppermute x7 -> x0, starting transfers between devices: 8.6 us -> none  [per_device(): lax.ppermute(pre_grad, ('x', 'c'), pairs)]
    ppermute x7 -> x0, waiting for transfers between devices: 5.87 us -> none  [per_device(): lax.ppermute(pre_grad, ('x', 'c'), pairs)]
    all_to_all x5, starting transfers between devices: 27.6 us -> 31.4 us  [exchange(): return lax.all_to_all(values, axes, 0, 0, tiled=True)]
    all_to_all x5, waiting for transfers between devices: 16 us -> 13.1 us  [exchange(): return lax.all_to_all(values, axes, 0, 0, tiled=True)]
    pallas_call x4 -> x5, Pallas kernels: 30 us -> 31.6 us  [the longest x1 20.9 us: count(): pl.pallas_call(count_kernel, out_shape=[half, half, TOKEN], in_specs=[SME...]
    ppermute x6 -> x7, starting transfers between devices: 4.61 us -> 3.22 us  [swap(): return lax.ppermute(values, 'c', [(0, 1), (1, 0)])]
    unnamed x37 -> x39, local copies, waits for them, and re-layouts: 12.6 us -> 11.6 us
  transfers between devices with their start and end apart: 34 -> 35, of which waited for: 11 -> 12; matrix products, arithmetic and copies ran while one was open for 3% -> 2% of each run, Pallas kernels for 19% -> 19%
where the time goes in v2:
time: 187 us; the launch traced here: 185 us
  starting transfers between devices  76.1 us (41%)
  waiting for transfers between devices  43.8 us (23%)
  Pallas kernels  43.7 us (23%)
  local copies, waits for them, and re-layouts  16.3 us (9%)
  matrix products  1.98 us (1%)
    ppermute x23, starting transfers between devices, shift(): lax.ppermute(values, axis, [(i, (i + step) % size) for i in range(size)])  41.5 us
    all_to_all x5, starting transfers between devices, exchange(): return lax.all_to_all(values, axes, 0, 0, tiled=True)  31.4 us
    ppermute x23, waiting for transfers between devices, shift(): lax.ppermute(values, axis, [(i, (i + step) % size) for i in range(size)])  29.5 us
    pallas_call x1, Pallas kernels, count(): pl.pallas_call(count_kernel, out_shape=[half, half, TOKEN], in_specs=[SME...  20.9 us
    all_to_all x5, waiting for transfers between devices, exchange(): return lax.all_to_all(values, axes, 0, 0, tiled=True)  13.1 us
    unnamed x39, local copies, waits for them, and re-layouts  11.6 us
    pallas_call x1, Pallas kernels, per_device(): pl.pallas_call(bucket_kernel, out_shape=[jax.ShapeDtypeStruct((NDEV, 4 *...  8.25 us
    pallas_call x2, Pallas kernels, pair_grad(): pl.pallas_call(functools.partial(grad_kernel, scale), out_shape=jax.Shape...  6.3 us
  transfers between devices with their start and end apart: 35, of which 12 were waited for; matrix products, arithmetic and copies ran while one was open for 2% of the time, Pallas kernels for 19%

profile of v2, /device:TPU:1, one launch (start us, length us, event | category | flops | bytes accessed | tf_op | source)
XLA Modules:
  0.0 184.5 jit_solution(10970678707317896301)
XLA Ops:
  0.6 2.0 %multiply_convert_fusion = (bf16[64,512]{1,0:T(8,128)(2,1)S(1)}, f32[64,512]{1,0:T(8,128)}) fusion(bf16[64,512]{1,0:T(8,128)(2,1)} %param.8, bf16[512,512]{1,0:T(8,128)(2,1)} %weight_ref.1), kind=kOutput, calls=%fused_computation.14 | convolution fusion | flops 33849344 | bytes 786432 | tf_op jit(solution)/shard_map/hidden/dot_general | solution.py:284
  2.6 0.8 broadcast_in_dim.4
  3.5 9.0 %all-to-all-start = ((bf16[8,64,512]{2,1,0:T(8,128)(2,1)}), bf16[8,64,512]{2,1,0:T(8,128)(2,1)S(1)}, u32[]{:S(2)}, u32[]{:S(2)}) async-start(bf16[8,64,512]{2,1,0:T(8,128)(2,1)} %broadcast_in_dim.4), calls=%async_computation | async-start | bytes 1048576 | tf_op jit(solution)/shard_map/pair_exchange/all_to_all | solution.py:234
  13.2 8.3 %bucket.1 = (bf16[64,2048]{1,0:T(8,128)(2,1)S(1)}, f32[8,128]{1,0:T(8,128)}) custom-call(s32[2,8192]{1,0:T(2,128)S(1)} %bitcast.33, s32[2,8192]{1,0:T(2,128)S(1)} %bitcast.34), custom_call_target="tpu_custom_call" | custom-call | flops 8999999488 | bytes 400000 | tf_op jit(solution)/shard_map/pair_exchange/bucket/pallas_call | solution.py:290
  21.4 0.9 reshape.29
  22.3 8.1 %all-to-all-done = bf16[8,64,512]{2,1,0:T(8,128)(2,1)S(1)} async-done(((bf16[8,64,512]{2,1,0:T(8,128)(2,1)}), bf16[8,64,512]{2,1,0:T(8,128)(2,1)S(1)}, u32[]{:S(2)}, u32[]{:S(2)}) %all-to-all-start) | async-done | bytes 524320 | tf_op jit(solution)/shard_map/pair_exchange/all_to_all | solution.py:234
  30.4 5.5 %all-to-all-start.1 = ((bf16[64,2,1024]{2,1,0:T(2,128)(2,1)}), bf16[64,2,1024]{2,1,0:T(2,128)(2,1)S(1)}, u32[]{:S(2)}, u32[]{:S(2)}) async-start(bf16[64,2,1024]{2,1,0:T(2,128)(2,1)} %reshape.29), calls=%async_computation.1 | async-start | bytes 524288 | tf_op jit(solution)/shard_map/pair_exchange/all_to_all | solution.py:234
  36.1 0.5 collective-permute-start.3
  36.5 0.9 dynamic-slice_bitcast_fusion
  37.8 0.7 copy.19
  38.5 0.5 collective-permute-start.5
  39.0 1.3 collective-permute-start.2
  40.3 2.6 %collective-permute-start.1 = (bf16[512,512]{1,0:T(8,128)(2,1)S(1)}, bf16[512,512]{1,0:T(8,128)(2,1)S(1)}, u32[]{:S(2)}, u32[]{:S(2)}) collective-permute-start(bf16[512,512]{1,0:T(8,128)(2,1)S(1)} %bitcast.29), channel_id=1, source_target_pairs={{0,32},{16,48},{32,0},{48,16},{1,33},{17,49},{33,1},{49,17},{2,34}... | collective-permute-start | bytes 1572872 | tf_op jit(solution)/shard_map/pair_exchange/ppermute | solution.py:230
  42.9 1.1 collective-permute-start
  44.0 4.0 %all-to-all-done.1 = bf16[64,2,1024]{2,1,0:T(2,128)(2,1)S(1)} async-done(((bf16[64,2,1024]{2,1,0:T(2,128)(2,1)}), bf16[64,2,1024]{2,1,0:T(2,128)(2,1)S(1)}, u32[]{:S(2)}, u32[]{:S(2)}) %all-to-all-start.1) | async-done | bytes 262176 | tf_op jit(solution)/shard_map/pair_exchange/all_to_all | solution.py:234
  48.0 20.9 %count.1 = (f32[2,256,512]{2,1,0:T(8,128)S(1)}, f32[2,256,512]{2,1,0:T(8,128)S(1)}, f32[8,128]{1,0:T(8,128)S(1)}) custom-call(s32[4]{0:T(128)S(1)} %pad_add_fusion.1.coord_ref, bf16[64,2048]{1,0:T(8,128)(2,1)S(1)} %bitcast.32), custom_call_target="tpu_custom_call" | custom-call | flops 24000000000 | bytes 2400000 | tf_op jit(solution)/shard_map/pair_exchange/count/pallas_call | solution.py:247
  69.0 1.0 copy-done.8
  70.0 1.0 copy-done.10
  71.0 0.8 reshape.34
  71.8 4.7 %all-to-all-start.2 = ((bf16[8,2,2048]{2,1,0:T(2,128)(2,1)}), bf16[8,2,2048]{2,1,0:T(2,128)(2,1)S(1)}, u32[]{:S(2)}, u32[]{:S(2)}) async-start(bf16[8,2,2048]{2,1,0:T(2,128)(2,1)} %reshape.34), calls=%async_computation.2 | async-start | bytes 131072 | tf_op jit(solution)/shard_map/tile_matrix/all_to_all | solution.py:234
  76.5 0.5 collective-permute-start.7
  77.1 1.2 copy-done.11
  78.3 2.9 %pair_grad.2.refs_4_ = f32[64,512]{1,0:T(8,128)S(1)} custom-call(f32[8,128]{1,0:T(8,128)S(1)} %get-tuple-element.55._, bf16[64,512]{1,0:T(8,128)(2,1)S(1)} %get-tuple-element.50.own_ref, f32[2,256,512]{2,1,0:T(8,128)S(1)} %copy-done.11, bf16[512,512]{1,0:T(8,128)(2,1)S(1)} %bitcast.31, bf16[512,512]{1,0:T(8,128)(2,1)} %collective-permute-done.refs_1_, ...), custom_call_target="tpu_custom_call" | custom-call | flops 3000000000 | bytes 3000000 | tf_op jit(solution)/shard_map/hidden_grad/pair_grad/pallas_call | solution.py:264
  81.2 2.0 %tile_sum.1 = (bf16[2048,512]{1,0:T(8,128)(2,1)S(1)}, bf16[2048,512]{1,0:T(8,128)(2,1)S(1)}, f32[8,128]{1,0:T(8,128)S(1)}) custom-call(s32[2,65]{1,0:T(2,128)S(1)} %pad_add_fusion.meta_ref, bf16[32,64,128]{2,1,0:T(8,128)(2,1)S(1)} %get-tuple-element.81.own_ref, bf16[32,64,128]{2,1,0:T(8,128)(2,1)S(1)} %collective-permute-done.4.other_ref), custom_call_target="tpu_custom_call" | custom-call | flops 3000000000 | bytes 5000000 | tf_op jit(solution)/shard_map/tile_matrix/tile_sum/pallas_call | solution.py:316
  83.2 1.3 copy-done.4
  84.5 1.4 copy-done.6
  86.1 1.2 copy-done.9
  87.3 3.4 %pair_grad.3 = f32[64,512]{1,0:T(8,128)S(1)} custom-call(f32[8,128]{1,0:T(8,128)S(1)} %get-tuple-element.49._, bf16[64,512]{1,0:T(8,128)(2,1)S(1)} %get-tuple-element.50.own_ref, f32[2,256,512]{2,1,0:T(8,128)S(1)} %copy-done.9, bf16[512,512]{1,0:T(8,128)(2,1)S(1)} %collective-permute-done.5.refs_0_, bf16[512,512]{1,0:T(8,128)(2,1)} %collective-permute-done.6.refs_1_, ...), custom_call_target="tpu_custom_call" | custom-call | flops 3000000000 | bytes 3000000 | tf_op jit(solution)/shard_map/hidden_grad/pair_grad/pallas_call | solution.py:264
  90.9 1.9 %collective-permute-start.11 = (bf16[64,512]{1,0:T(8,128)(2,1)S(1)}, bf16[64,512]{1,0:T(8,128)(2,1)S(1)}, u32[]{:S(2)}, u32[]{:S(2)}) collective-permute-start(bf16[64,512]{1,0:T(8,128)(2,1)S(1)} %fusion.6), channel_id=1, source_target_pairs={{0,64},{64,128},{128,192},{192,0},{1,65},{65,129},{129,193},{193,1... | collective-permute-start | bytes 196616 | tf_op jit(solution)/shard_map/spread/ppermute | solution.py:230
  92.8 2.6 %collective-permute-start.10 = (bf16[64,512]{1,0:T(8,128)(2,1)S(1)}, bf16[64,512]{1,0:T(8,128)(2,1)S(1)}, u32[]{:S(2)}, u32[]{:S(2)}) collective-permute-start(bf16[64,512]{1,0:T(8,128)(2,1)S(1)} %fusion.6), channel_id=1, source_target_pairs={{0,128},{64,192},{128,0},{192,64},{1,129},{65,193},{129,1},{193,65... | collective-permute-start | bytes 196616 | tf_op jit(solution)/shard_map/spread/ppermute | solution.py:230
  95.4 0.9 collective-permute-start.9
  96.5 2.3 %collective-permute-done.10 = bf16[64,512]{1,0:T(8,128)(2,1)S(1)} collective-permute-done((bf16[64,512]{1,0:T(8,128)(2,1)S(1)}, bf16[64,512]{1,0:T(8,128)(2,1)S(1)}, u32[]{:S(2)}, u32[]{:S(2)}) %collective-permute-start.10) | collective-permute-done | bytes 65568 | tf_op jit(solution)/shard_map/spread/ppermute | solution.py:230
  98.9 1.6 collective-permute-start.12
  100.5 1.2 collective-permute-done.12.refs_1_
  101.6 0.9 weight_terms.1
  102.6 3.8 %spread.1 = (bf16[4,512,512]{2,1,0:T(8,128)(2,1)S(1)}, f32[8,128]{1,0:T(8,128)}) custom-call(s32[4]{0:T(128)S(1)} %pad_add_fusion.1.coord_ref, f32[8,128]{1,0:T(8,128)S(1)} %get-tuple-element.67._, bf16[512,512]{1,0:T(8,128)(2,1)S(1)} %copy-done.1, bf16[2048,512]{1,0:T(8,128)(2,1)S(1)} %copy-done.5, bf16[2048,512]{1,0:T(8,128)(2,1)S(1)} %copy-done.7, ...), custom_call_target="tpu_custom_call" | custom-call | flops 5000000000 | bytes 8000000 | tf_op jit(solution)/shard_map/spread/spread/pallas_call | solution.py:349
  106.3 1.3 copy-done
  107.7 3.6 %all-to-all-start.3 = ((bf16[4,512,512]{2,1,0:T(8,128)(2,1)}), bf16[4,512,512]{2,1,0:T(8,128)(2,1)S(1)}, u32[]{:S(2)}, u32[]{:S(2)}) async-start(bf16[4,512,512]{2,1,0:T(8,128)(2,1)} %copy-done), calls=%async_computation.3 | async-start | bytes 4194304 | tf_op jit(solution)/shard_map/sums/all_to_all | solution.py:234
  111.3 1.4 collective-permute-start.13
  112.7 2.4 %collective-permute-start.14 = (f32[16,512]{1,0:T(8,128)S(1)}, f32[16,512]{1,0:T(8,128)S(1)}, u32[]{:S(2)}, u32[]{:S(2)}) collective-permute-start(f32[16,512]{1,0:T(8,128)S(1)} %get-tuple-element.64), channel_id=1, source_target_pairs={{0,32},{16,48},{32,0},{48,16},{1,33},{17,49},{33,1},{49,17},{2,34}... | collective-permute-start | bytes 98312 | tf_op jit(solution)/shard_map/sums/ppermute | solution.py:230
  115.1 1.2 collective-permute-start.15
  116.3 18.3 %collective-permute-done.13 = f32[16,512]{1,0:T(8,128)S(1)} collective-permute-done((f32[16,512]{1,0:T(8,128)S(1)}, f32[16,512]{1,0:T(8,128)S(1)}, u32[]{:S(2)}, u32[]{:S(2)}) %collective-permute-start.13) | collective-permute-done | bytes 32800 | tf_op jit(solution)/shard_map/sums/ppermute | solution.py:230
  134.6 4.1 %collective-permute-done.14 = f32[16,512]{1,0:T(8,128)S(1)} collective-permute-done((f32[16,512]{1,0:T(8,128)S(1)}, f32[16,512]{1,0:T(8,128)S(1)}, u32[]{:S(2)}, u32[]{:S(2)}) %collective-permute-start.14) | collective-permute-done | bytes 32800 | tf_op jit(solution)/shard_map/sums/ppermute | solution.py:230
  138.7 1.3 collective-permute-start.22
  140.0 1.0 collective-permute-start.21
  141.0 1.9 %collective-permute-start.20 = (f32[16,512]{1,0:T(8,128)S(1)}, f32[16,512]{1,0:T(8,128)S(1)}, u32[]{:S(2)}, u32[]{:S(2)}) collective-permute-start(f32[16,512]{1,0:T(8,128)S(1)} %add_add_fusion.refs_0_), channel_id=1, source_target_pairs={{0,6},{2,8},{4,10},{6,12},{8,14},{10,0},{12,2},{14,4},{1,7},{3,9},... | collective-permute-start | bytes 98312 | tf_op jit(solution)/shard_map/sums/ppermute | solution.py:230
  142.9 3.4 %collective-permute-start.19 = (f32[16,512]{1,0:T(8,128)S(1)}, f32[16,512]{1,0:T(8,128)S(1)}, u32[]{:S(2)}, u32[]{:S(2)}) collective-permute-start(f32[16,512]{1,0:T(8,128)S(1)} %add_add_fusion.refs_0_), channel_id=1, source_target_pairs={{0,8},{2,10},{4,12},{6,14},{8,0},{10,2},{12,4},{14,6},{1,9},{3,11}... | collective-permute-start | bytes 98312 | tf_op jit(solution)/shard_map/sums/ppermute | solution.py:230
  146.3 1.3 collective-permute-start.18
  147.5 2.6 %collective-permute-start.17 = (f32[16,512]{1,0:T(8,128)S(1)}, f32[16,512]{1,0:T(8,128)S(1)}, u32[]{:S(2)}, u32[]{:S(2)}) collective-permute-start(f32[16,512]{1,0:T(8,128)S(1)} %add_add_fusion.refs_0_), channel_id=1, source_target_pairs={{0,12},{2,14},{4,0},{6,2},{8,4},{10,6},{12,8},{14,10},{1,13},{3,15... | collective-permute-start | bytes 98312 | tf_op jit(solution)/shard_map/sums/ppermute | solution.py:230
  150.4 0.5 collective-permute-done.18.refs_3_
  150.9 1.6 collective-permute-done.17.refs_2_
  152.9 0.6 share_sum.1
  153.5 1.1 broadcast_in_dim.5
  154.6 8.5 %all-to-all-start.4 = ((f32[32,16,512]{2,1,0:T(8,128)}), f32[32,16,512]{2,1,0:T(8,128)}, u32[]{:S(2)}, u32[]{:S(2)}) async-start(f32[32,16,512]{2,1,0:T(8,128)} %broadcast_in_dim.5), calls=%async_computation.4 | async-start | bytes 2097152 | tf_op jit(solution)/shard_map/sums/all_to_all | solution.py:234
  163.1 1.0 plane_sum.1
  164.2 0.4 collective-permute-start.23
  164.6 2.3 %collective-permute-start.24 = (bf16[64,512]{1,0:T(8,128)(2,1)S(1)}, bf16[64,512]{1,0:T(8,128)(2,1)S(1)}, u32[]{:S(2)}, u32[]{:S(2)}) collective-permute-start(bf16[64,512]{1,0:T(8,128)(2,1)S(1)} %get-tuple-element.73), channel_id=1, source_target_pairs={{0,14},{2,0},{4,2},{6,4},{8,6},{10,8},{12,10},{14,12},{1,15},{3,1}... | collective-permute-start | bytes 196616 | tf_op jit(solution)/shard_map/sums/ppermute | solution.py:230
  166.9 3.5 %collective-permute-start.25 = (bf16[64,512]{1,0:T(8,128)(2,1)S(1)}, bf16[64,512]{1,0:T(8,128)(2,1)S(1)}, u32[]{:S(2)}, u32[]{:S(2)}) collective-permute-start(bf16[64,512]{1,0:T(8,128)(2,1)S(1)} %get-tuple-element.74), channel_id=1, source_target_pairs={{0,8},{2,10},{4,12},{6,14},{8,0},{10,2},{12,4},{14,6},{1,9},{3,11}... | collective-permute-start | bytes 196616 | tf_op jit(solution)/shard_map/sums/ppermute | solution.py:230
  170.4 3.6 %collective-permute-start.27 = (bf16[64,512]{1,0:T(8,128)(2,1)S(1)}, bf16[64,512]{1,0:T(8,128)(2,1)S(1)}, u32[]{:S(2)}, u32[]{:S(2)}) collective-permute-start(bf16[64,512]{1,0:T(8,128)(2,1)S(1)} %get-tuple-element.76), channel_id=1, source_target_pairs={{0,12},{2,14},{4,0},{6,2},{8,4},{10,6},{12,8},{14,10},{1,13},{3,15... | collective-permute-start | bytes 196616 | tf_op jit(solution)/shard_map/sums/ppermute | solution.py:230
  174.0 4.5 %collective-permute-start.29 = (bf16[64,512]{1,0:T(8,128)(2,1)S(1)}, bf16[64,512]{1,0:T(8,128)(2,1)S(1)}, u32[]{:S(2)}, u32[]{:S(2)}) collective-permute-start(bf16[64,512]{1,0:T(8,128)(2,1)S(1)} %get-tuple-element.78), channel_id=1, source_target_pairs={{0,10},{2,12},{4,14},{6,0},{8,2},{10,4},{12,6},{14,8},{1,11},{3,13... | collective-permute-start | bytes 196616 | tf_op jit(solution)/shard_map/sums/ppermute | solution.py:230
  178.5 1.0 all-to-all-done.4
  179.5 2.1 %collective-permute-done.28 = bf16[64,512]{1,0:T(8,128)(2,1)S(1)} collective-permute-done((bf16[64,512]{1,0:T(8,128)(2,1)S(1)}, bf16[64,512]{1,0:T(8,128)(2,1)S(1)}, u32[]{:S(2)}, u32[]{:S(2)}) %collective-permute-start.28) | collective-permute-done | bytes 65568 | tf_op jit(solution)/shard_map/sums/ppermute | solution.py:230
  181.6 0.7 add_convert_fusion
  182.3 2.3 %copy.22 = f32[512,512]{1,0:T(8,128)} copy(f32[512,512]{1,0:T(8,128)} %bitcast.13) | data formatting | bytes 2097152
  (70 shorter events, 1.8 us)
Async XLA Ops:
  0.6 12.5 %copy-start.3 = (s32[8192,2]{0,1:T(2,128)S(1)}, s32[8192,2]{0,1:T(2,128)}, u32[]{:S(2)}) copy-start(s32[8192,2]{0,1:T(2,128)} %param.15) | copy-start | bytes 196612
  0.6 12.5 %copy-start.2 = (s32[8192,2]{0,1:T(2,128)S(1)}, s32[8192,2]{0,1:T(2,128)}, u32[]{:S(2)}) copy-start(s32[8192,2]{0,1:T(2,128)} %param.14) | copy-start | bytes 196612
  3.5 27.0 %all-to-all-start = ((bf16[8,64,512]{2,1,0:T(8,128)(2,1)}), bf16[8,64,512]{2,1,0:T(8,128)(2,1)S(1)}, u32[]{:S(2)}, u32[]{:S(2)}) async-start(bf16[8,64,512]{2,1,0:T(8,128)(2,1)} %broadcast_in_dim.4), calls=%async_computation | async-start | bytes 1048576 | tf_op jit(solution)/shard_map/pair_exchange/all_to_all | solution.py:234
  13.2 22.8 %copy-start.16 = (s32[32]{0:T(128)S(1)}, s32[32]{0:T(128)}, u32[]{:S(2)}) copy-start(s32[32]{0:T(128)} %param.12) | copy-start | bytes 388
  13.2 22.8 %copy-start.17 = (s32[32]{0:T(128)S(1)}, s32[32]{0:T(128)}, u32[]{:S(2)}) copy-start(s32[32]{0:T(128)} %param.11) | copy-start | bytes 388
  13.2 23.4 %copy-start.12 = (bf16[32,128,128]{2,1,0:T(8,128)(2,1)S(1)}, bf16[32,128,128]{2,1,0:T(8,128)(2,1)}, u32[]{:S(2)}) copy-start(bf16[32,128,128]{2,1,0:T(8,128)(2,1)} %param.10) | copy-start | bytes 3145732
  21.4 16.2 %copy-start.15 = (bf16[64,512]{1,0:T(8,128)(2,1)S(1)}, bf16[64,512]{1,0:T(8,128)(2,1)}, u32[]{:S(2)}) copy-start(bf16[64,512]{1,0:T(8,128)(2,1)} %param.8) | copy-start | bytes 196612
  30.4 17.5 %all-to-all-start.1 = ((bf16[64,2,1024]{2,1,0:T(2,128)(2,1)}), bf16[64,2,1024]{2,1,0:T(2,128)(2,1)S(1)}, u32[]{:S(2)}, u32[]{:S(2)}) async-start(bf16[64,2,1024]{2,1,0:T(2,128)(2,1)} %reshape.29), calls=%async_computation.1 | async-start | bytes 524288 | tf_op jit(solution)/shard_map/pair_exchange/all_to_all | solution.py:234
  36.1 2.4 %collective-permute-start.3 = (s32[65]{0:T(128)S(1)}, s32[65]{0:T(128)S(1)}, u32[]{:S(2)}, u32[]{:S(2)}) collective-permute-start(s32[65]{0:T(128)S(1)} %pad_add_fusion.2), channel_id=1, source_target_pairs={{0,1},{1,0},{2,3},{3,2},{4,5},{5,4},{6,7},{7,6},{8,9},{9,8},{10,11... | collective-permute-start | bytes 788 | tf_op jit(solution)/shard_map/tile_matrix/ppermute | solution.py:226
  37.4 43.8 %collective-permute-start.4 = (bf16[32,64,128]{2,1,0:T(8,128)(2,1)}, bf16[32,64,128]{2,1,0:T(8,128)(2,1)S(1)}, u32[]{:S(2)}, u32[]{:S(2)}) collective-permute-start(bf16[32,64,128]{2,1,0:T(8,128)(2,1)} %get-tuple-element.80), channel_id=1, source_target_pairs={{0,1},{1,0},{2,3},{3,2},{4,5},{5,4},{6,7},{7,6},{8,9},{9,8},{10,11... | collective-permute-start | bytes 1572872 | tf_op jit(solution)/shard_map/tile_matrix/ppermute | solution.py:226
  38.5 47.6 %collective-permute-start.5 = (bf16[512,512]{1,0:T(8,128)(2,1)S(1)}, bf16[512,512]{1,0:T(8,128)(2,1)S(1)}, u32[]{:S(2)}, u32[]{:S(2)}) collective-permute-start(bf16[512,512]{1,0:T(8,128)(2,1)S(1)} %bitcast.27), channel_id=1, source_target_pairs={{0,1},{1,0},{2,3},{3,2},{4,5},{5,4},{6,7},{7,6},{8,9},{9,8},{10,11... | collective-permute-start | bytes 1572872 | tf_op jit(solution)/shard_map/tile_matrix/ppermute | solution.py:226
  39.0 32.0 %collective-permute-start.2 = (bf16[512,512]{1,0:T(8,128)(2,1)S(1)}, bf16[512,512]{1,0:T(8,128)(2,1)S(1)}, u32[]{:S(2)}, u32[]{:S(2)}) collective-permute-start(bf16[512,512]{1,0:T(8,128)(2,1)S(1)} %bitcast.28), channel_id=1, source_target_pairs={{0,16},{16,32},{32,48},{48,0},{1,17},{17,33},{33,49},{49,1},{2,18}... | collective-permute-start | bytes 1572872 | tf_op jit(solution)/shard_map/pair_exchange/ppermute | solution.py:230
  40.3 30.7 %collective-permute-start.1 = (bf16[512,512]{1,0:T(8,128)(2,1)S(1)}, bf16[512,512]{1,0:T(8,128)(2,1)S(1)}, u32[]{:S(2)}, u32[]{:S(2)}) collective-permute-start(bf16[512,512]{1,0:T(8,128)(2,1)S(1)} %bitcast.29), channel_id=1, source_target_pairs={{0,32},{16,48},{32,0},{48,16},{1,33},{17,49},{33,1},{49,17},{2,34}... | collective-permute-start | bytes 1572872 | tf_op jit(solution)/shard_map/pair_exchange/ppermute | solution.py:230
  42.9 28.1 %collective-permute-start = (bf16[512,512]{1,0:T(8,128)(2,1)S(1)}, bf16[512,512]{1,0:T(8,128)(2,1)}, u32[]{:S(2)}, u32[]{:S(2)}) collective-permute-start(bf16[512,512]{1,0:T(8,128)(2,1)S(1)} %bitcast.30), channel_id=1, source_target_pairs={{0,48},{16,0},{32,16},{48,32},{1,49},{17,1},{33,17},{49,33},{2,50}... | collective-permute-start | bytes 1572872 | tf_op jit(solution)/shard_map/pair_exchange/ppermute | solution.py:230
  48.0 23.0 %copy-start.13 = (bf16[64,8,64]{2,0,1:T(8,128)(2,1)S(1)}, bf16[64,8,64]{2,0,1:T(8,128)(2,1)}, u32[]{:S(2)}) copy-start(bf16[64,8,64]{2,0,1:T(8,128)(2,1)} %copy.19) | copy-start | bytes 196612
  69.0 1.0 copy-start.8
  70.0 1.0 copy-start.10
  71.8 14.1 %all-to-all-start.2 = ((bf16[8,2,2048]{2,1,0:T(2,128)(2,1)}), bf16[8,2,2048]{2,1,0:T(2,128)(2,1)S(1)}, u32[]{:S(2)}, u32[]{:S(2)}) async-start(bf16[8,2,2048]{2,1,0:T(2,128)(2,1)} %reshape.34), calls=%async_computation.2 | async-start | bytes 131072 | tf_op jit(solution)/shard_map/tile_matrix/all_to_all | solution.py:234
  76.5 9.5 %collective-permute-start.6 = (bf16[512,512]{1,0:T(8,128)(2,1)}, bf16[512,512]{1,0:T(8,128)(2,1)}, u32[]{:S(2)}, u32[]{:S(2)}) collective-permute-start(bf16[512,512]{1,0:T(8,128)(2,1)} %collective-permute-done.refs_1_), channel_id=1, source_target_pairs={{0,1},{1,0},{2,3},{3,2},{4,5},{5,4},{6,7},{7,6},{8,9},{9,8},{10,11... | collective-permute-start | bytes 1572872 | tf_op jit(solution)/shard_map/tile_matrix/ppermute | solution.py:226
  76.5 9.5 %collective-permute-start.7 = (bf16[512,512]{1,0:T(8,128)(2,1)S(1)}, bf16[512,512]{1,0:T(8,128)(2,1)}, u32[]{:S(2)}, u32[]{:S(2)}) collective-permute-start(bf16[512,512]{1,0:T(8,128)(2,1)S(1)} %collective-permute-done.1.refs_2_), channel_id=1, source_target_pairs={{0,1},{1,0},{2,3},{3,2},{4,5},{5,4},{6,7},{7,6},{8,9},{9,8},{10,11... | collective-permute-start | bytes 1572872 | tf_op jit(solution)/shard_map/tile_matrix/ppermute | solution.py:226
  77.1 9.0 %collective-permute-start.8 = (bf16[512,512]{1,0:T(8,128)(2,1)S(1)}, bf16[512,512]{1,0:T(8,128)(2,1)}, u32[]{:S(2)}, u32[]{:S(2)}) collective-permute-start(bf16[512,512]{1,0:T(8,128)(2,1)S(1)} %collective-permute-done.2.refs_3_), channel_id=1, source_target_pairs={{0,1},{1,0},{2,3},{3,2},{4,5},{5,4},{6,7},{7,6},{8,9},{9,8},{10,11... | collective-permute-start | bytes 1572872 | tf_op jit(solution)/shard_map/tile_matrix/ppermute | solution.py:226
  77.1 1.2 copy-start.11
  83.2 1.3 copy-start.4
  84.5 1.4 copy-start.6
  86.1 1.2 copy-start.9
  87.3 3.4 %copy-start.14 = (f32[64,512]{1,0:T(8,128)S(1)}, f32[64,512]{1,0:T(8,128)}, u32[]{:S(2)}) copy-start(f32[64,512]{1,0:T(8,128)} %get-tuple-element.83) | copy-start | bytes 393220
  87.3 15.2 %copy-start.7 = (bf16[2048,512]{1,0:T(8,128)(2,1)S(1)}, bf16[2048,512]{1,0:T(8,128)(2,1)}, u32[]{:S(2)}) copy-start(bf16[2048,512]{1,0:T(8,128)(2,1)} %copy-done.6) | copy-start | bytes 6291460
  90.8 11.7 %copy-start.1 = (bf16[512,512]{1,0:T(8,128)(2,1)S(1)}, bf16[512,512]{1,0:T(8,128)(2,1)}, u32[]{:S(2)}) copy-start(bf16[512,512]{1,0:T(8,128)(2,1)} %weight_ref.1) | copy-start | bytes 1572868
  90.8 11.7 %copy-start.5 = (bf16[2048,512]{1,0:T(8,128)(2,1)S(1)}, bf16[2048,512]{1,0:T(8,128)(2,1)}, u32[]{:S(2)}) copy-start(bf16[2048,512]{1,0:T(8,128)(2,1)} %copy-done.4) | copy-start | bytes 6291460
  90.9 5.7 %collective-permute-start.11 = (bf16[64,512]{1,0:T(8,128)(2,1)S(1)}, bf16[64,512]{1,0:T(8,128)(2,1)S(1)}, u32[]{:S(2)}, u32[]{:S(2)}) collective-permute-start(bf16[64,512]{1,0:T(8,128)(2,1)S(1)} %fusion.6), channel_id=1, source_target_pairs={{0,64},{64,128},{128,192},{192,0},{1,65},{65,129},{129,193},{193,1... | collective-permute-start | bytes 196616 | tf_op jit(solution)/shard_map/spread/ppermute | solution.py:230
  92.8 6.1 %collective-permute-start.10 = (bf16[64,512]{1,0:T(8,128)(2,1)S(1)}, bf16[64,512]{1,0:T(8,128)(2,1)S(1)}, u32[]{:S(2)}, u32[]{:S(2)}) collective-permute-start(bf16[64,512]{1,0:T(8,128)(2,1)S(1)} %fusion.6), channel_id=1, source_target_pairs={{0,128},{64,192},{128,0},{192,64},{1,129},{65,193},{129,1},{193,65... | collective-permute-start | bytes 196616 | tf_op jit(solution)/shard_map/spread/ppermute | solution.py:230
  95.4 3.5 %collective-permute-start.9 = (bf16[64,512]{1,0:T(8,128)(2,1)S(1)}, bf16[64,512]{1,0:T(8,128)(2,1)S(1)}, u32[]{:S(2)}, u32[]{:S(2)}) collective-permute-start(bf16[64,512]{1,0:T(8,128)(2,1)S(1)} %fusion.6), channel_id=1, source_target_pairs={{0,192},{64,0},{128,64},{192,128},{1,193},{65,1},{129,65},{193,129... | collective-permute-start | bytes 196616 | tf_op jit(solution)/shard_map/spread/ppermute | solution.py:230
  98.9 2.8 %collective-permute-start.12 = (bf16[256,512]{1,0:T(8,128)(2,1)S(1)}, bf16[256,512]{1,0:T(8,128)(2,1)S(1)}, u32[]{:S(2)}, u32[]{:S(2)}) collective-permute-start(bf16[256,512]{1,0:T(8,128)(2,1)S(1)} %pad_maximum_fusion.refs_0_), channel_id=1, source_target_pairs={{0,1},{1,0},{2,3},{3,2},{4,5},{5,4},{6,7},{7,6},{8,9},{9,8},{10,11... | collective-permute-start | bytes 786440 | tf_op jit(solution)/shard_map/spread/ppermute | solution.py:226
  106.3 1.3 copy-start
  107.7 45.8 %all-to-all-start.3 = ((bf16[4,512,512]{2,1,0:T(8,128)(2,1)}), bf16[4,512,512]{2,1,0:T(8,128)(2,1)S(1)}, u32[]{:S(2)}, u32[]{:S(2)}) async-start(bf16[4,512,512]{2,1,0:T(8,128)(2,1)} %copy-done), calls=%async_computation.3 | async-start | bytes 4194304 | tf_op jit(solution)/shard_map/sums/all_to_all | solution.py:234
  111.3 23.3 %collective-permute-start.13 = (f32[16,512]{1,0:T(8,128)S(1)}, f32[16,512]{1,0:T(8,128)S(1)}, u32[]{:S(2)}, u32[]{:S(2)}) collective-permute-start(f32[16,512]{1,0:T(8,128)S(1)} %get-tuple-element.63), channel_id=1, source_target_pairs={{0,16},{16,32},{32,48},{48,0},{1,17},{17,33},{33,49},{49,1},{2,18}... | collective-permute-start | bytes 98312 | tf_op jit(solution)/shard_map/sums/ppermute | solution.py:230
  112.7 26.0 %collective-permute-start.14 = (f32[16,512]{1,0:T(8,128)S(1)}, f32[16,512]{1,0:T(8,128)S(1)}, u32[]{:S(2)}, u32[]{:S(2)}) collective-permute-start(f32[16,512]{1,0:T(8,128)S(1)} %get-tuple-element.64), channel_id=1, source_target_pairs={{0,32},{16,48},{32,0},{48,16},{1,33},{17,49},{33,1},{49,17},{2,34}... | collective-permute-start | bytes 98312 | tf_op jit(solution)/shard_map/sums/ppermute | solution.py:230
  115.1 23.6 %collective-permute-start.15 = (f32[16,512]{1,0:T(8,128)S(1)}, f32[16,512]{1,0:T(8,128)S(1)}, u32[]{:S(2)}, u32[]{:S(2)}) collective-permute-start(f32[16,512]{1,0:T(8,128)S(1)} %get-tuple-element.65), channel_id=1, source_target_pairs={{0,48},{16,0},{32,16},{48,32},{1,49},{17,1},{33,17},{49,33},{2,50}... | collective-permute-start | bytes 98312 | tf_op jit(solution)/shard_map/sums/ppermute | solution.py:230
  138.7 8.8 %collective-permute-start.22 = (f32[16,512]{1,0:T(8,128)S(1)}, f32[16,512]{1,0:T(8,128)S(1)}, u32[]{:S(2)}, u32[]{:S(2)}) collective-permute-start(f32[16,512]{1,0:T(8,128)S(1)} %add_add_fusion.refs_0_), channel_id=1, source_target_pairs={{0,2},{2,4},{4,6},{6,8},{8,10},{10,12},{12,14},{14,0},{1,3},{3,5},... | collective-permute-start | bytes 98312 | tf_op jit(solution)/shard_map/sums/ppermute | solution.py:230
  140.0 10.1 %collective-permute-start.21 = (f32[16,512]{1,0:T(8,128)S(1)}, f32[16,512]{1,0:T(8,128)S(1)}, u32[]{:S(2)}, u32[]{:S(2)}) collective-permute-start(f32[16,512]{1,0:T(8,128)S(1)} %add_add_fusion.refs_0_), channel_id=1, source_target_pairs={{0,4},{2,6},{4,8},{6,10},{8,12},{10,14},{12,0},{14,2},{1,5},{3,7},... | collective-permute-start | bytes 98312 | tf_op jit(solution)/shard_map/sums/ppermute | solution.py:230
  141.0 9.5 %collective-permute-start.20 = (f32[16,512]{1,0:T(8,128)S(1)}, f32[16,512]{1,0:T(8,128)S(1)}, u32[]{:S(2)}, u32[]{:S(2)}) collective-permute-start(f32[16,512]{1,0:T(8,128)S(1)} %add_add_fusion.refs_0_), channel_id=1, source_target_pairs={{0,6},{2,8},{4,10},{6,12},{8,14},{10,0},{12,2},{14,4},{1,7},{3,9},... | collective-permute-start | bytes 98312 | tf_op jit(solution)/shard_map/sums/ppermute | solution.py:230
  142.9 7.6 %collective-permute-start.19 = (f32[16,512]{1,0:T(8,128)S(1)}, f32[16,512]{1,0:T(8,128)S(1)}, u32[]{:S(2)}, u32[]{:S(2)}) collective-permute-start(f32[16,512]{1,0:T(8,128)S(1)} %add_add_fusion.refs_0_), channel_id=1, source_target_pairs={{0,8},{2,10},{4,12},{6,14},{8,0},{10,2},{12,4},{14,6},{1,9},{3,11}... | collective-permute-start | bytes 98312 | tf_op jit(solution)/shard_map/sums/ppermute | solution.py:230
  146.3 4.7 %collective-permute-start.18 = (f32[16,512]{1,0:T(8,128)S(1)}, f32[16,512]{1,0:T(8,128)S(1)}, u32[]{:S(2)}, u32[]{:S(2)}) collective-permute-start(f32[16,512]{1,0:T(8,128)S(1)} %add_add_fusion.refs_0_), channel_id=1, source_target_pairs={{0,10},{2,12},{4,14},{6,0},{8,2},{10,4},{12,6},{14,8},{1,11},{3,13... | collective-permute-start | bytes 98312 | tf_op jit(solution)/shard_map/sums/ppermute | solution.py:230
  147.5 5.0 %collective-permute-start.17 = (f32[16,512]{1,0:T(8,128)S(1)}, f32[16,512]{1,0:T(8,128)S(1)}, u32[]{:S(2)}, u32[]{:S(2)}) collective-permute-start(f32[16,512]{1,0:T(8,128)S(1)} %add_add_fusion.refs_0_), channel_id=1, source_target_pairs={{0,12},{2,14},{4,0},{6,2},{8,4},{10,6},{12,8},{14,10},{1,13},{3,15... | collective-permute-start | bytes 98312 | tf_op jit(solution)/shard_map/sums/ppermute | solution.py:230
  150.1 2.8 %collective-permute-start.16 = (f32[16,512]{1,0:T(8,128)S(1)}, f32[16,512]{1,0:T(8,128)S(1)}, u32[]{:S(2)}, u32[]{:S(2)}) collective-permute-start(f32[16,512]{1,0:T(8,128)S(1)} %add_add_fusion.refs_0_), channel_id=1, source_target_pairs={{0,14},{2,0},{4,2},{6,4},{8,6},{10,8},{12,10},{14,12},{1,15},{3,1}... | collective-permute-start | bytes 98312 | tf_op jit(solution)/shard_map/sums/ppermute | solution.py:230
  154.6 24.9 %all-to-all-start.4 = ((f32[32,16,512]{2,1,0:T(8,128)}), f32[32,16,512]{2,1,0:T(8,128)}, u32[]{:S(2)}, u32[]{:S(2)}) async-start(f32[32,16,512]{2,1,0:T(8,128)} %broadcast_in_dim.5), calls=%async_computation.4 | async-start | bytes 2097152 | tf_op jit(solution)/shard_map/sums/all_to_all | solution.py:234
  164.2 9.9 %collective-permute-start.23 = (bf16[64,512]{1,0:T(8,128)(2,1)S(1)}, bf16[64,512]{1,0:T(8,128)(2,1)S(1)}, u32[]{:S(2)}, u32[]{:S(2)}) collective-permute-start(bf16[64,512]{1,0:T(8,128)(2,1)S(1)} %get-tuple-element.72), channel_id=1, source_target_pairs={{0,2},{2,4},{4,6},{6,8},{8,10},{10,12},{12,14},{14,0},{1,3},{3,5},... | collective-permute-start | bytes 196616 | tf_op jit(solution)/shard_map/sums/ppermute | solution.py:230
  164.6 9.4 %collective-permute-start.24 = (bf16[64,512]{1,0:T(8,128)(2,1)S(1)}, bf16[64,512]{1,0:T(8,128)(2,1)S(1)}, u32[]{:S(2)}, u32[]{:S(2)}) collective-permute-start(bf16[64,512]{1,0:T(8,128)(2,1)S(1)} %get-tuple-element.73), channel_id=1, source_target_pairs={{0,14},{2,0},{4,2},{6,4},{8,6},{10,8},{12,10},{14,12},{1,15},{3,1}... | collective-permute-start | bytes 196616 | tf_op jit(solution)/shard_map/sums/ppermute | solution.py:230
  166.9 12.6 %collective-permute-start.25 = (bf16[64,512]{1,0:T(8,128)(2,1)S(1)}, bf16[64,512]{1,0:T(8,128)(2,1)S(1)}, u32[]{:S(2)}, u32[]{:S(2)}) collective-permute-start(bf16[64,512]{1,0:T(8,128)(2,1)S(1)} %get-tuple-element.74), channel_id=1, source_target_pairs={{0,8},{2,10},{4,12},{6,14},{8,0},{10,2},{12,4},{14,6},{1,9},{3,11}... | collective-permute-start | bytes 196616 | tf_op jit(solution)/shard_map/sums/ppermute | solution.py:230
  170.4 9.1 %collective-permute-start.26 = (bf16[64,512]{1,0:T(8,128)(2,1)S(1)}, bf16[64,512]{1,0:T(8,128)(2,1)S(1)}, u32[]{:S(2)}, u32[]{:S(2)}) collective-permute-start(bf16[64,512]{1,0:T(8,128)(2,1)S(1)} %get-tuple-element.75), channel_id=1, source_target_pairs={{0,4},{2,6},{4,8},{6,10},{8,12},{10,14},{12,0},{14,2},{1,5},{3,7},... | collective-permute-start | bytes 196616 | tf_op jit(solution)/shard_map/sums/ppermute | solution.py:230
  170.4 9.1 %collective-permute-start.27 = (bf16[64,512]{1,0:T(8,128)(2,1)S(1)}, bf16[64,512]{1,0:T(8,128)(2,1)S(1)}, u32[]{:S(2)}, u32[]{:S(2)}) collective-permute-start(bf16[64,512]{1,0:T(8,128)(2,1)S(1)} %get-tuple-element.76), channel_id=1, source_target_pairs={{0,12},{2,14},{4,0},{6,2},{8,4},{10,6},{12,8},{14,10},{1,13},{3,15... | collective-permute-start | bytes 196616 | tf_op jit(solution)/shard_map/sums/ppermute | solution.py:230
  174.0 7.6 %collective-permute-start.28 = (bf16[64,512]{1,0:T(8,128)(2,1)S(1)}, bf16[64,512]{1,0:T(8,128)(2,1)S(1)}, u32[]{:S(2)}, u32[]{:S(2)}) collective-permute-start(bf16[64,512]{1,0:T(8,128)(2,1)S(1)} %get-tuple-element.77), channel_id=1, source_target_pairs={{0,6},{2,8},{4,10},{6,12},{8,14},{10,0},{12,2},{14,4},{1,7},{3,9},... | collective-permute-start | bytes 196616 | tf_op jit(solution)/shard_map/sums/ppermute | solution.py:230
  174.0 7.6 %collective-permute-start.29 = (bf16[64,512]{1,0:T(8,128)(2,1)S(1)}, bf16[64,512]{1,0:T(8,128)(2,1)S(1)}, u32[]{:S(2)}, u32[]{:S(2)}) collective-permute-start(bf16[64,512]{1,0:T(8,128)(2,1)S(1)} %get-tuple-element.78), channel_id=1, source_target_pairs={{0,10},{2,12},{4,14},{6,0},{8,2},{10,4},{12,6},{14,8},{1,11},{3,13... | collective-permute-start | bytes 196616 | tf_op jit(solution)/shard_map/sums/ppermute | solution.py:230

commit v3 on v2

--- a/solution.py
+++ b/solution.py
@@ -138,8 +138,7 @@
     out_ref[...] = total
 
 
-def tiles_kernel(meta_ref, own_ref, other_ref, high_ref, low_ref, token_ref, acc):
-    token_ref[...] = jnp.zeros_like(token_ref)
+def tiles_kernel(meta_ref, own_ref, other_ref, high_ref, low_ref, acc):
     slots = own_ref.shape[0]
     acc[...] = jnp.zeros_like(acc)
     for part, tiles_ref in enumerate((own_ref, other_ref)):
@@ -184,13 +183,10 @@
 def terms_kernel(coord_ref, node_ref, *refs):
     pre_refs, out_refs, token_ref, terms = refs[:NC], refs[NC:-2], refs[-2], refs[-1]
     token_ref[...] = jnp.zeros_like(token_ref)
-    y, c, x = coord_ref[0], coord_ref[1], coord_ref[2]
-    total = jnp.zeros(terms.shape, F32)
-    for k in range(NC * NX):
-        dc, dx = k // NX, k % NX
-        node = node_ref[((x + dx) & (NX - 1)) * NC + (c ^ dc)]
-        pre = pre_refs[dc][dx * ROWS : (dx + 1) * ROWS, :]
-        total += lax.dot_general(node, pre, TN, preferred_element_type=F32)
+    y = coord_ref[0]
+    half = NX * ROWS
+    total = lax.dot_general(node_ref[:half, :], pre_refs[0][...], TN, preferred_element_type=F32)
+    total += lax.dot_general(node_ref[half:, :], pre_refs[1][...], TN, preferred_element_type=F32)
     terms[...] = total
     size = ROWS // NY
     for k in range(NY):
@@ -298,7 +294,13 @@
             name="bucket",
         )(pair_owner.T, pair_row.T)
         ends = ends.reshape(NDEV, 2, 2 * CAP)
-        ring, ends = lax.optimization_barrier((ring, ends))
+        near_nodes = jnp.concatenate(
+            [node_aggregate] + [shift(node_aggregate, "x", NX, -k) for k in range(1, NX)], axis=0
+        )
+        nodes = jnp.concatenate([near_nodes, swap(near_nodes)], axis=0)
+        column = (lax.axis_index("x") * NC + c) * ROWS
+        nodes = lax.dynamic_slice_in_dim(nodes, column, ROWS, axis=1)
+        ring, ends, nodes = lax.optimization_barrier((ring, ends, nodes))
         planes = [ring] + [shift(ring, "y", NY, -k) for k in range(1, NY)]
         received = exchange(ends, ("y", "z", "c")).reshape(NDEV, 4 * CAP)
         near, far, token = count(coord, received)
@@ -309,30 +311,27 @@
         other_half = swap(pick(halves, 1 - c))
         meta = jnp.concatenate([tile_src, tile_dst, tile_count]).astype(I32)
         metas = jnp.stack([meta, swap(meta)])
-        columns = node_aggregate.reshape(ROWS, NX * NC, ROWS).transpose(1, 0, 2)
         far_ring = swap(ring)
-        *planes, columns, metas, token = lax.optimization_barrier((*planes, columns, metas, token))
+        *planes, token = lax.optimization_barrier((*planes, token))
         far_planes = [far_ring] + [swap(plane) for plane in planes[1:]]
-        high, low, tile_token = pl.pallas_call(
+    with jax.named_scope("hidden_grad"):
+        scale = ROWS / (2.0 * pair_total)
+        hidden_grad = pair_grad(scale, token, hidden_b, near, *planes)
+        hidden_grad = pair_grad(scale, token, hidden_b, far, *far_planes, hidden_grad)
+        pre_grad = act_back(hidden_grad)[0].astype(BF)
+        pre_grad, metas = lax.optimization_barrier((pre_grad, metas))
+
+    with jax.named_scope("spread"):
+        high, low = pl.pallas_call(
             tiles_kernel,
-            out_shape=[jax.ShapeDtypeStruct((NY * NZ * ROWS, 512), BF)] * 2 + [TOKEN],
+            out_shape=[jax.ShapeDtypeStruct((NY * NZ * ROWS, 512), BF)] * 2,
             in_specs=[SMEM, VMEM, VMEM],
-            out_specs=[VMEM] * 3,
+            out_specs=[VMEM] * 2,
             scratch_shapes=[pltpu.VMEM((NY * NZ * ROWS, 512), F32)],
             compiler_params=params(),
             cost_estimate=pl.CostEstimate(flops=3_000_000_000, bytes_accessed=5_000_000, transcendentals=0),
             name="tile_sum",
         )(metas, own_half, other_half)
-        nodes = exchange(columns, ("x", "c"))
-
-    with jax.named_scope("hidden_grad"):
-        scale = ROWS / (2.0 * pair_total)
-        hidden_grad = pair_grad(scale, token, hidden_b, near, *planes)
-        own, tile_token, nodes = lax.optimization_barrier((hidden_b, tile_token, nodes))
-        hidden_grad = pair_grad(scale, tile_token, own, far, *far_planes, hidden_grad)
-        pre_grad = act_back(hidden_grad)[0].astype(BF)
-
-    with jax.named_scope("spread"):
         along_x = [pre_grad] + [shift(pre_grad, "x", NX, -k) for k in range(1, NX)]
         near_pre = jnp.concatenate(along_x, axis=0)
         pre_parts = [near_pre, swap(near_pre)]
@@ -346,6 +345,7 @@
             cost_estimate=pl.CostEstimate(flops=1_000_000_000, bytes_accessed=700_000, transcendentals=0),
             name="weight_terms",
         )(coord, nodes, *pre_parts)
+        others = [shift(terms[k], "y", NY, k) for k in range(1, NY)]
         send, token = pl.pallas_call(
             spread_kernel,
             out_shape=[jax.ShapeDtypeStruct((NY, NZ * ROWS, F), BF), TOKEN],
@@ -358,11 +358,11 @@
         )(coord, token, weight, high, low, *pre_parts)
 
     with jax.named_scope("sums"):
+        *others, send, token = lax.optimization_barrier((*others, send, token))
         planes = exchange(send, "y")
-        *terms, token = lax.optimization_barrier((*terms, token))
         share = terms[0]
-        for k in range(1, NY):
-            share = share + shift(terms[k], "y", NY, k)
+        for other in others:
+            share = share + other
         block, share_token = pl.pallas_call(
             share_kernel,
             out_shape=[jax.ShapeDtypeStruct((ROWS // NY, F), F32), TOKEN],

time: 187 us -> 160 us (0.86); the launches traced: 185 us -> 160 us
  waiting for transfers between devices: 43.8 us -> 33.8 us
  local copies, waits for them, and re-layouts: 16.3 us -> 6.75 us
  starting transfers between devices: 76.1 us -> 72.5 us
    ppermute x23 -> x26, waiting for transfers between devices: 29.5 us -> 9.47 us  [shift(): lax.ppermute(values, axis, [(i, (i + step) % size) for i in range(size)])]
    all_to_all x5 -> x4, waiting for transfers between devices: 13.1 us -> 23.2 us  [exchange(): return lax.all_to_all(values, axes, 0, 0, tiled=True)]
    unnamed x39 -> x25, local copies, waits for them, and re-layouts: 11.6 us -> 3.73 us
    all_to_all x5 -> x4, starting transfers between devices: 31.4 us -> 25.6 us  [exchange(): return lax.all_to_all(values, axes, 0, 0, tiled=True)]
    ppermute x7 -> x8, starting transfers between devices: 3.22 us -> 5.44 us  [swap(): return lax.ppermute(values, 'c', [(0, 1), (1, 0)])]
    ppermute x23 -> x26, starting transfers between devices: 41.5 us -> 41.5 us  [shift(): lax.ppermute(values, axis, [(i, (i + step) % size) for i in range(size)])]
  transfers between devices with their start and end apart: 35 -> 38, of which waited for: 12 -> 10; matrix products, arithmetic and copies ran while one was open for 2% -> 2% of each run, Pallas kernels for 19% -> 26%
where the time goes in v3:
time: 160 us
  starting transfers between devices  72.5 us (45%)
  Pallas kernels  42.5 us (27%)
  waiting for transfers between devices  33.8 us (21%)
  local copies, waits for them, and re-layouts  6.75 us (4%)
  between operations  1.65 us (1%)
    ppermute x26, starting transfers between devices, shift(): lax.ppermute(values, axis, [(i, (i + step) % size) for i in range(size)])  41.5 us
    all_to_all x4, starting transfers between devices, exchange(): return lax.all_to_all(values, axes, 0, 0, tiled=True)  25.6 us
    all_to_all x4, waiting for transfers between devices, exchange(): return lax.all_to_all(values, axes, 0, 0, tiled=True)  23.2 us
    pallas_call x1, Pallas kernels, count(): pl.pallas_call(count_kernel, out_shape=[half, half, TOKEN], in_specs=[SME...  21 us
    ppermute x26, waiting for transfers between devices, shift(): lax.ppermute(values, axis, [(i, (i + step) % size) for i in range(size)])  9.47 us
    pallas_call x1, Pallas kernels, per_device(): pl.pallas_call(bucket_kernel, out_shape=[jax.ShapeDtypeStruct((NDEV, 4 *...  8.25 us
    ppermute x8, starting transfers between devices, swap(): return lax.ppermute(values, 'c', [(0, 1), (1, 0)])  5.44 us
    pallas_call x2, Pallas kernels, pair_grad(): pl.pallas_call(functools.partial(grad_kernel, scale), out_shape=jax.Shape...  4.8 us
  transfers between devices with their start and end apart: 38, of which 10 were waited for; matrix products, arithmetic and copies ran while one was open for 2% of the time, Pallas kernels for 26%

profile of v3, /device:TPU:1, one launch (start us, length us, event | category | flops | bytes accessed | tf_op | source)
XLA Modules:
  0.0 159.6 jit_solution(2128092598407436113)
XLA Ops:
  0.6 2.1 %collective-permute-start.2 = (bf16[64,512]{1,0:T(8,128)(2,1)}, bf16[64,512]{1,0:T(8,128)(2,1)S(1)}, u32[]{:S(2)}, u32[]{:S(2)}) collective-permute-start(bf16[64,512]{1,0:T(8,128)(2,1)} %param.8), channel_id=1, source_target_pairs={{0,64},{64,128},{128,192},{192,0},{1,65},{65,129},{129,193},{193,1... | collective-permute-start | bytes 196616 | tf_op jit(solution)/shard_map/pair_exchange/ppermute | solution.py:226
  2.8 2.5 %collective-permute-start.1 = (bf16[64,512]{1,0:T(8,128)(2,1)}, bf16[64,512]{1,0:T(8,128)(2,1)S(1)}, u32[]{:S(2)}, u32[]{:S(2)}) collective-permute-start(bf16[64,512]{1,0:T(8,128)(2,1)} %param.8), channel_id=1, source_target_pairs={{0,128},{64,192},{128,0},{192,64},{1,129},{65,193},{129,1},{193,65... | collective-permute-start | bytes 196616 | tf_op jit(solution)/shard_map/pair_exchange/ppermute | solution.py:226
  5.2 1.2 collective-permute-start
  6.4 1.3 multiply_convert_fusion
  7.7 0.8 broadcast_in_dim.4
  8.5 8.2 %all-to-all-start = ((bf16[8,64,512]{2,1,0:T(8,128)(2,1)}), bf16[8,64,512]{2,1,0:T(8,128)(2,1)S(1)}, u32[]{:S(2)}, u32[]{:S(2)}) async-start(bf16[8,64,512]{2,1,0:T(8,128)(2,1)} %broadcast_in_dim.4), calls=%async_computation | async-start | bytes 1048576 | tf_op jit(solution)/shard_map/pair_exchange/all_to_all | solution.py:230
  16.7 8.2 %bucket.1 = (bf16[64,2048]{1,0:T(8,128)(2,1)S(1)}, f32[8,128]{1,0:T(8,128)}) custom-call(s32[2,8192]{1,0:T(2,128)S(1)} %bitcast.30, s32[2,8192]{1,0:T(2,128)S(1)} %bitcast.31), custom_call_target="tpu_custom_call" | custom-call | flops 8999999488 | bytes 400000 | tf_op jit(solution)/shard_map/pair_exchange/bucket/pallas_call | solution.py:286
  25.0 0.9 reshape.26
  26.0 1.9 %collective-permute-start.3 = (bf16[256,512]{1,0:T(8,128)(2,1)S(1)}, bf16[256,512]{1,0:T(8,128)(2,1)S(1)}, u32[]{:S(2)}, u32[]{:S(2)}) collective-permute-start(bf16[256,512]{1,0:T(8,128)(2,1)S(1)} %pad_maximum_fusion), channel_id=1, source_target_pairs={{0,1},{1,0},{2,3},{3,2},{4,5},{5,4},{6,7},{7,6},{8,9},{9,8},{10,11... | collective-permute-start | bytes 786440 | tf_op jit(solution)/shard_map/pair_exchange/ppermute | solution.py:222
  27.9 1.1 collective-permute-done.3
  29.0 0.1 constant_dynamic-slice_fusion.node_ref
  29.1 3.5 %all-to-all-done = bf16[8,64,512]{2,1,0:T(8,128)(2,1)S(1)} async-done(((bf16[8,64,512]{2,1,0:T(8,128)(2,1)}), bf16[8,64,512]{2,1,0:T(8,128)(2,1)S(1)}, u32[]{:S(2)}, u32[]{:S(2)}) %all-to-all-start) | async-done | bytes 524320 | tf_op jit(solution)/shard_map/pair_exchange/all_to_all | solution.py:230
  32.7 7.5 %all-to-all-start.1 = ((bf16[64,2,1024]{2,1,0:T(2,128)(2,1)}), bf16[64,2,1024]{2,1,0:T(2,128)(2,1)S(1)}, u32[]{:S(2)}, u32[]{:S(2)}) async-start(bf16[64,2,1024]{2,1,0:T(2,128)(2,1)} %reshape.26), calls=%async_computation.1 | async-start | bytes 524288 | tf_op jit(solution)/shard_map/pair_exchange/all_to_all | solution.py:230
  40.9 0.5 collective-permute-start.11
  41.6 1.4 collective-permute-start.6
  43.0 2.6 %collective-permute-start.5 = (bf16[512,512]{1,0:T(8,128)(2,1)S(1)}, bf16[512,512]{1,0:T(8,128)(2,1)S(1)}, u32[]{:S(2)}, u32[]{:S(2)}) collective-permute-start(bf16[512,512]{1,0:T(8,128)(2,1)S(1)} %bitcast.26), channel_id=1, source_target_pairs={{0,32},{16,48},{32,0},{48,16},{1,33},{17,49},{33,1},{49,17},{2,34}... | collective-permute-start | bytes 1572872 | tf_op jit(solution)/shard_map/pair_exchange/ppermute | solution.py:226
  45.6 1.1 collective-permute-start.4
  46.6 5.6 %all-to-all-done.1 = bf16[64,2,1024]{2,1,0:T(2,128)(2,1)S(1)} async-done(((bf16[64,2,1024]{2,1,0:T(2,128)(2,1)}), bf16[64,2,1024]{2,1,0:T(2,128)(2,1)S(1)}, u32[]{:S(2)}, u32[]{:S(2)}) %all-to-all-start.1) | async-done | bytes 262176 | tf_op jit(solution)/shard_map/pair_exchange/all_to_all | solution.py:230
  52.3 21.0 %count.1 = (f32[2,256,512]{2,1,0:T(8,128)S(1)}, f32[2,256,512]{2,1,0:T(8,128)S(1)}, f32[8,128]{1,0:T(8,128)S(1)}) custom-call(s32[4]{0:T(128)S(1)} %pad_add_fusion.1.coord_ref, bf16[64,2048]{1,0:T(8,128)(2,1)S(1)} %bitcast.29), custom_call_target="tpu_custom_call" | custom-call | flops 24000000000 | bytes 2400000 | tf_op jit(solution)/shard_map/pair_exchange/count/pallas_call | solution.py:243
  73.3 0.7 collective-permute-start.8
  74.0 0.1 collective-permute-start.9
  74.1 0.4 collective-permute-start.10
  74.7 0.1 collective-permute-start.19
  74.8 2.9 %pair_grad.2.refs_4_ = f32[64,512]{1,0:T(8,128)S(1)} custom-call(f32[8,128]{1,0:T(8,128)S(1)} %get-tuple-element.43._, bf16[64,512]{1,0:T(8,128)(2,1)S(1)} %get-tuple-element.76.own_ref, f32[2,256,512]{2,1,0:T(8,128)S(1)} %get-tuple-element.48.count_ref, bf16[512,512]{1,0:T(8,128)(2,1)S(1)} %bitcast.28, bf16[512,512]{1,0:T(8,128)(2,1)} %collective-permute-done.4.refs_1_, ...), custom_call_target="tpu_custom_call" | custom-call | flops 3000000000 | bytes 3000000 | tf_op jit(solution)/shard_map/hidden_grad/pair_grad/pallas_call | solution.py:260
  77.8 1.9 %pair_grad.3 = f32[64,512]{1,0:T(8,128)S(1)} custom-call(f32[8,128]{1,0:T(8,128)S(1)} %get-tuple-element.43._, bf16[64,512]{1,0:T(8,128)(2,1)S(1)} %get-tuple-element.76.own_ref, f32[2,256,512]{2,1,0:T(8,128)S(1)} %get-tuple-element.44.count_ref, bf16[512,512]{1,0:T(8,128)(2,1)S(1)} %collective-permute-done.7.refs_0_, ...), custom_call_target="tpu_custom_call" | custom-call | flops 3000000000 | bytes 3000000 | tf_op jit(solution)/shard_map/hidden_grad/pair_grad/pallas_call | solution.py:260
  79.8 0.4 collective-permute-start.14
  80.2 0.9 collective-permute-start.13
  81.0 1.6 %collective-permute-start.12 = (bf16[64,512]{1,0:T(8,128)(2,1)S(1)}, bf16[64,512]{1,0:T(8,128)(2,1)S(1)}, u32[]{:S(2)}, u32[]{:S(2)}) collective-permute-start(bf16[64,512]{1,0:T(8,128)(2,1)S(1)} %fusion.6), channel_id=1, source_target_pairs={{0,192},{64,0},{128,64},{192,128},{1,193},{65,1},{129,65},{193,129... | collective-permute-start | bytes 196616 | tf_op jit(solution)/shard_map/spread/ppermute | solution.py:226
  82.7 3.3 %collective-permute-done.12 = bf16[64,512]{1,0:T(8,128)(2,1)S(1)} collective-permute-done((bf16[64,512]{1,0:T(8,128)(2,1)S(1)}, bf16[64,512]{1,0:T(8,128)(2,1)S(1)}, u32[]{:S(2)}, u32[]{:S(2)}) %collective-permute-start.12) | collective-permute-done | bytes 65568 | tf_op jit(solution)/shard_map/spread/ppermute | solution.py:226
  86.0 1.6 %collective-permute-start.15 = (bf16[256,512]{1,0:T(8,128)(2,1)S(1)}, bf16[256,512]{1,0:T(8,128)(2,1)S(1)}, u32[]{:S(2)}, u32[]{:S(2)}) collective-permute-start(bf16[256,512]{1,0:T(8,128)(2,1)S(1)} %constant_dynamic-update-slice_fusion.5.refs_0_), channel_id=1, source_target_pairs={{0,1},{1,0},{2,3},{3,2},{4,5},{5,4},{6,7},{7,6},{8,9},{9,8},{10,11... | collective-permute-start | bytes 786440 | tf_op jit(solution)/shard_map/spread/ppermute | solution.py:222
  87.7 2.3 %tile_sum.1 = (bf16[2048,512]{1,0:T(8,128)(2,1)S(1)}, bf16[2048,512]{1,0:T(8,128)(2,1)S(1)}) custom-call(s32[2,65]{1,0:T(2,128)S(1)} %pad_add_fusion.meta_ref, bf16[32,64,128]{2,1,0:T(8,128)(2,1)S(1)} %get-tuple-element.75.own_ref, bf16[32,64,128]{2,1,0:T(8,128)(2,1)S(1)} %collective-permute-done.19.other_ref), custom_call_target="tpu_custom_call" | custom-call | flops 3000000000 | bytes 5000000 | tf_op jit(solution)/shard_map/spread/tile_sum/pallas_call | solution.py:325
  90.0 0.8 weight_terms.1
  90.8 0.7 collective-permute-start.16
  91.5 2.9 %collective-permute-start.17 = (f32[16,512]{1,0:T(8,128)S(1)}, f32[16,512]{1,0:T(8,128)S(1)}, u32[]{:S(2)}, u32[]{:S(2)}) collective-permute-start(f32[16,512]{1,0:T(8,128)S(1)} %get-tuple-element.53), channel_id=1, source_target_pairs={{0,32},{16,48},{32,0},{48,16},{1,33},{17,49},{33,1},{49,17},{2,34}... | collective-permute-start | bytes 98312 | tf_op jit(solution)/shard_map/spread/ppermute | solution.py:226
  94.4 0.8 collective-permute-start.18
  95.2 3.8 %spread.1 = (bf16[4,512,512]{2,1,0:T(8,128)(2,1)S(1)}, f32[8,128]{1,0:T(8,128)}) custom-call(s32[4]{0:T(128)S(1)} %pad_add_fusion.1.coord_ref, f32[8,128]{1,0:T(8,128)S(1)} %get-tuple-element.55._, bf16[512,512]{1,0:T(8,128)(2,1)S(1)} %copy-done.1, bf16[2048,512]{1,0:T(8,128)(2,1)S(1)} %get-tuple-element.57.high_ref, ...), custom_call_target="tpu_custom_call" | custom-call | flops 5000000000 | bytes 8000000 | tf_op jit(solution)/shard_map/spread/spread/pallas_call | solution.py:349
  99.0 1.3 copy-done
  100.4 3.6 %all-to-all-start.2 = ((bf16[4,512,512]{2,1,0:T(8,128)(2,1)}), bf16[4,512,512]{2,1,0:T(8,128)(2,1)S(1)}, u32[]{:S(2)}, u32[]{:S(2)}) async-start(bf16[4,512,512]{2,1,0:T(8,128)(2,1)} %copy-done), calls=%async_computation.2 | async-start | bytes 4194304 | tf_op jit(solution)/shard_map/sums/all_to_all | solution.py:230
  104.0 0.9 collective-permute-start.26
  104.9 0.9 collective-permute-start.25
  105.9 1.4 collective-permute-start.24
  107.2 3.7 %collective-permute-start.23 = (f32[16,512]{1,0:T(8,128)S(1)}, f32[16,512]{1,0:T(8,128)S(1)}, u32[]{:S(2)}, u32[]{:S(2)}) collective-permute-start(f32[16,512]{1,0:T(8,128)S(1)} %add_add_fusion.refs_0_), channel_id=1, source_target_pairs={{0,8},{2,10},{4,12},{6,14},{8,0},{10,2},{12,4},{14,6},{1,9},{3,11}... | collective-permute-start | bytes 98312 | tf_op jit(solution)/shard_map/sums/ppermute | solution.py:226
  110.9 1.3 collective-permute-start.22
  112.2 2.2 %collective-permute-start.21 = (f32[16,512]{1,0:T(8,128)S(1)}, f32[16,512]{1,0:T(8,128)S(1)}, u32[]{:S(2)}, u32[]{:S(2)}) collective-permute-start(f32[16,512]{1,0:T(8,128)S(1)} %add_add_fusion.refs_0_), channel_id=1, source_target_pairs={{0,12},{2,14},{4,0},{6,2},{8,4},{10,6},{12,8},{14,10},{1,13},{3,15... | collective-permute-start | bytes 98312 | tf_op jit(solution)/shard_map/sums/ppermute | solution.py:226
  114.4 0.7 collective-permute-start.20
  115.1 0.7 collective-permute-done.22.refs_3_
  115.8 1.9 %collective-permute-done.21.refs_2_ = f32[16,512]{1,0:T(8,128)S(1)} collective-permute-done((f32[16,512]{1,0:T(8,128)S(1)}, f32[16,512]{1,0:T(8,128)S(1)}, u32[]{:S(2)}, u32[]{:S(2)}) %collective-permute-start.21) | collective-permute-done | bytes 32800 | tf_op jit(solution)/shard_map/sums/ppermute | solution.py:226
  117.7 0.2 collective-permute-done.20.refs_1_
  117.9 0.6 share_sum.1
  118.5 11.1 %all-to-all-done.2.in_ref = bf16[4,512,512]{2,1,0:T(8,128)(2,1)S(1)} async-done(((bf16[4,512,512]{2,1,0:T(8,128)(2,1)}), bf16[4,512,512]{2,1,0:T(8,128)(2,1)S(1)}, u32[]{:S(2)}, u32[]{:S(2)}) %all-to-all-start.2) | async-done | bytes 2097184 | tf_op jit(solution)/shard_map/sums/all_to_all | solution.py:230
  129.5 1.1 broadcast_in_dim.5
  130.6 6.3 %all-to-all-start.3 = ((f32[32,16,512]{2,1,0:T(8,128)}), f32[32,16,512]{2,1,0:T(8,128)}, u32[]{:S(2)}, u32[]{:S(2)}) async-start(f32[32,16,512]{2,1,0:T(8,128)} %broadcast_in_dim.5), calls=%async_computation.3 | async-start | bytes 2097152 | tf_op jit(solution)/shard_map/sums/all_to_all | solution.py:230
  136.9 1.0 plane_sum.1
  138.0 0.9 collective-permute-start.27
  138.9 1.8 %collective-permute-start.28 = (bf16[64,512]{1,0:T(8,128)(2,1)S(1)}, bf16[64,512]{1,0:T(8,128)(2,1)S(1)}, u32[]{:S(2)}, u32[]{:S(2)}) collective-permute-start(bf16[64,512]{1,0:T(8,128)(2,1)S(1)} %get-tuple-element.67), channel_id=1, source_target_pairs={{0,14},{2,0},{4,2},{6,4},{8,6},{10,8},{12,10},{14,12},{1,15},{3,1}... | collective-permute-start | bytes 196616 | tf_op jit(solution)/shard_map/sums/ppermute | solution.py:226
  140.7 1.5 collective-permute-start.29
  142.2 0.8 collective-permute-start.30
  143.0 2.8 %collective-permute-start.31 = (bf16[64,512]{1,0:T(8,128)(2,1)S(1)}, bf16[64,512]{1,0:T(8,128)(2,1)S(1)}, u32[]{:S(2)}, u32[]{:S(2)}) collective-permute-start(bf16[64,512]{1,0:T(8,128)(2,1)S(1)} %get-tuple-element.70), channel_id=1, source_target_pairs={{0,12},{2,14},{4,0},{6,2},{8,4},{10,6},{12,8},{14,10},{1,13},{3,15... | collective-permute-start | bytes 196616 | tf_op jit(solution)/shard_map/sums/ppermute | solution.py:226
  145.8 0.3 collective-permute-start.32
  146.1 4.2 %collective-permute-start.33 = (bf16[64,512]{1,0:T(8,128)(2,1)S(1)}, bf16[64,512]{1,0:T(8,128)(2,1)S(1)}, u32[]{:S(2)}, u32[]{:S(2)}) collective-permute-start(bf16[64,512]{1,0:T(8,128)(2,1)S(1)} %get-tuple-element.72), channel_id=1, source_target_pairs={{0,10},{2,12},{4,14},{6,0},{8,2},{10,4},{12,6},{14,8},{1,11},{3,13... | collective-permute-start | bytes 196616 | tf_op jit(solution)/shard_map/sums/ppermute | solution.py:226
  150.3 3.0 %all-to-all-done.3 = f32[32,16,512]{2,1,0:T(8,128)} async-done(((f32[32,16,512]{2,1,0:T(8,128)}), f32[32,16,512]{2,1,0:T(8,128)}, u32[]{:S(2)}, u32[]{:S(2)}) %all-to-all-start.3) | async-done | bytes 1048608 | tf_op jit(solution)/shard_map/sums/all_to_all | solution.py:230
  153.3 3.4 %collective-permute-done.32 = bf16[64,512]{1,0:T(8,128)(2,1)S(1)} collective-permute-done((bf16[64,512]{1,0:T(8,128)(2,1)S(1)}, bf16[64,512]{1,0:T(8,128)(2,1)S(1)}, u32[]{:S(2)}, u32[]{:S(2)}) %collective-permute-start.32) | collective-permute-done | bytes 65568 | tf_op jit(solution)/shard_map/sums/ppermute | solution.py:226
  156.6 0.7 add_convert_fusion
  157.3 2.3 %copy.24 = f32[512,512]{1,0:T(8,128)} copy(f32[512,512]{1,0:T(8,128)} %bitcast.12) | data formatting | bytes 2097152
  (62 shorter events, 0.7 us)
Async XLA Ops:
  0.6 16.1 %copy-start.3 = (s32[8192,2]{0,1:T(2,128)S(1)}, s32[8192,2]{0,1:T(2,128)}, u32[]{:S(2)}) copy-start(s32[8192,2]{0,1:T(2,128)} %param.15) | copy-start | bytes 196612
  0.6 16.1 %copy-start.2 = (s32[8192,2]{0,1:T(2,128)S(1)}, s32[8192,2]{0,1:T(2,128)}, u32[]{:S(2)}) copy-start(s32[8192,2]{0,1:T(2,128)} %param.14) | copy-start | bytes 196612
  0.6 25.3 %collective-permute-start.2 = (bf16[64,512]{1,0:T(8,128)(2,1)}, bf16[64,512]{1,0:T(8,128)(2,1)S(1)}, u32[]{:S(2)}, u32[]{:S(2)}) collective-permute-start(bf16[64,512]{1,0:T(8,128)(2,1)} %param.8), channel_id=1, source_target_pairs={{0,64},{64,128},{128,192},{192,0},{1,65},{65,129},{129,193},{193,1... | collective-permute-start | bytes 196616 | tf_op jit(solution)/shard_map/pair_exchange/ppermute | solution.py:226
  2.8 23.1 %collective-permute-start.1 = (bf16[64,512]{1,0:T(8,128)(2,1)}, bf16[64,512]{1,0:T(8,128)(2,1)S(1)}, u32[]{:S(2)}, u32[]{:S(2)}) collective-permute-start(bf16[64,512]{1,0:T(8,128)(2,1)} %param.8), channel_id=1, source_target_pairs={{0,128},{64,192},{128,0},{192,64},{1,129},{65,193},{129,1},{193,65... | collective-permute-start | bytes 196616 | tf_op jit(solution)/shard_map/pair_exchange/ppermute | solution.py:226
  5.2 20.7 %collective-permute-start = (bf16[64,512]{1,0:T(8,128)(2,1)}, bf16[64,512]{1,0:T(8,128)(2,1)S(1)}, u32[]{:S(2)}, u32[]{:S(2)}) collective-permute-start(bf16[64,512]{1,0:T(8,128)(2,1)} %param.8), channel_id=1, source_target_pairs={{0,192},{64,0},{128,64},{192,128},{1,193},{65,1},{129,65},{193,129... | collective-permute-start | bytes 196616 | tf_op jit(solution)/shard_map/pair_exchange/ppermute | solution.py:226
  8.5 24.1 %all-to-all-start = ((bf16[8,64,512]{2,1,0:T(8,128)(2,1)}), bf16[8,64,512]{2,1,0:T(8,128)(2,1)S(1)}, u32[]{:S(2)}, u32[]{:S(2)}) async-start(bf16[8,64,512]{2,1,0:T(8,128)(2,1)} %broadcast_in_dim.4), calls=%async_computation | async-start | bytes 1048576 | tf_op jit(solution)/shard_map/pair_exchange/all_to_all | solution.py:230
  16.7 9.2 %copy-start.5 = (bf16[64,512]{1,0:T(8,128)(2,1)S(1)}, bf16[64,512]{1,0:T(8,128)(2,1)}, u32[]{:S(2)}) copy-start(bf16[64,512]{1,0:T(8,128)(2,1)} %param.8) | copy-start | bytes 196612
  25.0 15.9 %copy-start.6 = (s32[32]{0:T(128)S(1)}, s32[32]{0:T(128)}, u32[]{:S(2)}) copy-start(s32[32]{0:T(128)} %param.12) | copy-start | bytes 388
  25.0 15.9 %copy-start.7 = (s32[32]{0:T(128)S(1)}, s32[32]{0:T(128)}, u32[]{:S(2)}) copy-start(s32[32]{0:T(128)} %param.11) | copy-start | bytes 388
  26.0 3.0 %collective-permute-start.3 = (bf16[256,512]{1,0:T(8,128)(2,1)S(1)}, bf16[256,512]{1,0:T(8,128)(2,1)S(1)}, u32[]{:S(2)}, u32[]{:S(2)}) collective-permute-start(bf16[256,512]{1,0:T(8,128)(2,1)S(1)} %pad_maximum_fusion), channel_id=1, source_target_pairs={{0,1},{1,0},{2,3},{3,2},{4,5},{5,4},{6,7},{7,6},{8,9},{9,8},{10,11... | collective-permute-start | bytes 786440 | tf_op jit(solution)/shard_map/pair_exchange/ppermute | solution.py:222
  32.7 19.5 %all-to-all-start.1 = ((bf16[64,2,1024]{2,1,0:T(2,128)(2,1)}), bf16[64,2,1024]{2,1,0:T(2,128)(2,1)S(1)}, u32[]{:S(2)}, u32[]{:S(2)}) async-start(bf16[64,2,1024]{2,1,0:T(2,128)(2,1)} %reshape.26), calls=%async_computation.1 | async-start | bytes 524288 | tf_op jit(solution)/shard_map/pair_exchange/all_to_all | solution.py:230
  40.9 33.7 %collective-permute-start.11 = (s32[65]{0:T(128)S(1)}, s32[65]{0:T(128)S(1)}, u32[]{:S(2)}, u32[]{:S(2)}) collective-permute-start(s32[65]{0:T(128)S(1)} %pad_add_fusion.2), channel_id=1, source_target_pairs={{0,1},{1,0},{2,3},{3,2},{4,5},{5,4},{6,7},{7,6},{8,9},{9,8},{10,11... | collective-permute-start | bytes 788 | tf_op jit(solution)/shard_map/tile_matrix/ppermute | solution.py:222
  41.5 36.2 %collective-permute-start.7 = (bf16[512,512]{1,0:T(8,128)(2,1)S(1)}, bf16[512,512]{1,0:T(8,128)(2,1)S(1)}, u32[]{:S(2)}, u32[]{:S(2)}) collective-permute-start(bf16[512,512]{1,0:T(8,128)(2,1)S(1)} %bitcast.24), channel_id=1, source_target_pairs={{0,1},{1,0},{2,3},{3,2},{4,5},{5,4},{6,7},{7,6},{8,9},{9,8},{10,11... | collective-permute-start | bytes 1572872 | tf_op jit(solution)/shard_map/tile_matrix/ppermute | solution.py:222
  41.6 31.7 %collective-permute-start.6 = (bf16[512,512]{1,0:T(8,128)(2,1)S(1)}, bf16[512,512]{1,0:T(8,128)(2,1)S(1)}, u32[]{:S(2)}, u32[]{:S(2)}) collective-permute-start(bf16[512,512]{1,0:T(8,128)(2,1)S(1)} %bitcast.25), channel_id=1, source_target_pairs={{0,16},{16,32},{32,48},{48,0},{1,17},{17,33},{33,49},{49,1},{2,18}... | collective-permute-start | bytes 1572872 | tf_op jit(solution)/shard_map/pair_exchange/ppermute | solution.py:226
  43.0 30.3 %collective-permute-start.5 = (bf16[512,512]{1,0:T(8,128)(2,1)S(1)}, bf16[512,512]{1,0:T(8,128)(2,1)S(1)}, u32[]{:S(2)}, u32[]{:S(2)}) collective-permute-start(bf16[512,512]{1,0:T(8,128)(2,1)S(1)} %bitcast.26), channel_id=1, source_target_pairs={{0,32},{16,48},{32,0},{48,16},{1,33},{17,49},{33,1},{49,17},{2,34}... | collective-permute-start | bytes 1572872 | tf_op jit(solution)/shard_map/pair_exchange/ppermute | solution.py:226
  45.6 27.7 %collective-permute-start.4 = (bf16[512,512]{1,0:T(8,128)(2,1)S(1)}, bf16[512,512]{1,0:T(8,128)(2,1)}, u32[]{:S(2)}, u32[]{:S(2)}) collective-permute-start(bf16[512,512]{1,0:T(8,128)(2,1)S(1)} %bitcast.27), channel_id=1, source_target_pairs={{0,48},{16,0},{32,16},{48,32},{1,49},{17,1},{33,17},{49,33},{2,50}... | collective-permute-start | bytes 1572872 | tf_op jit(solution)/shard_map/pair_exchange/ppermute | solution.py:226
  52.3 22.2 %copy-start.4 = (bf16[32,128,128]{2,1,0:T(8,128)(2,1)S(1)}, bf16[32,128,128]{2,1,0:T(8,128)(2,1)}, u32[]{:S(2)}) copy-start(bf16[32,128,128]{2,1,0:T(8,128)(2,1)} %param.10) | copy-start | bytes 3145732
  73.3 4.5 %collective-permute-start.8 = (bf16[512,512]{1,0:T(8,128)(2,1)}, bf16[512,512]{1,0:T(8,128)(2,1)S(1)}, u32[]{:S(2)}, u32[]{:S(2)}) collective-permute-start(bf16[512,512]{1,0:T(8,128)(2,1)} %collective-permute-done.4.refs_1_), channel_id=1, source_target_pairs={{0,1},{1,0},{2,3},{3,2},{4,5},{5,4},{6,7},{7,6},{8,9},{9,8},{10,11... | collective-permute-start | bytes 1572872 | tf_op jit(solution)/shard_map/tile_matrix/ppermute | solution.py:222
  74.0 3.8 %collective-permute-start.9 = (bf16[512,512]{1,0:T(8,128)(2,1)S(1)}, bf16[512,512]{1,0:T(8,128)(2,1)S(1)}, u32[]{:S(2)}, u32[]{:S(2)}) collective-permute-start(bf16[512,512]{1,0:T(8,128)(2,1)S(1)} %collective-permute-done.5.refs_2_), channel_id=1, source_target_pairs={{0,1},{1,0},{2,3},{3,2},{4,5},{5,4},{6,7},{7,6},{8,9},{9,8},{10,11... | collective-permute-start | bytes 1572872 | tf_op jit(solution)/shard_map/tile_matrix/ppermute | solution.py:222
  74.1 3.7 %collective-permute-start.10 = (bf16[512,512]{1,0:T(8,128)(2,1)S(1)}, bf16[512,512]{1,0:T(8,128)(2,1)S(1)}, u32[]{:S(2)}, u32[]{:S(2)}) collective-permute-start(bf16[512,512]{1,0:T(8,128)(2,1)S(1)} %collective-permute-done.6.refs_3_), channel_id=1, source_target_pairs={{0,1},{1,0},{2,3},{3,2},{4,5},{5,4},{6,7},{7,6},{8,9},{9,8},{10,11... | collective-permute-start | bytes 1572872 | tf_op jit(solution)/shard_map/tile_matrix/ppermute | solution.py:222
  74.7 13.0 %collective-permute-start.19 = (bf16[32,64,128]{2,1,0:T(8,128)(2,1)S(1)}, bf16[32,64,128]{2,1,0:T(8,128)(2,1)S(1)}, u32[]{:S(2)}, u32[]{:S(2)}) collective-permute-start(bf16[32,64,128]{2,1,0:T(8,128)(2,1)S(1)} %get-tuple-element.74), channel_id=1, source_target_pairs={{0,1},{1,0},{2,3},{3,2},{4,5},{5,4},{6,7},{7,6},{8,9},{9,8},{10,11... | collective-permute-start | bytes 1572872 | tf_op jit(solution)/shard_map/tile_matrix/ppermute | solution.py:222
  79.8 6.3 %collective-permute-start.14 = (bf16[64,512]{1,0:T(8,128)(2,1)S(1)}, bf16[64,512]{1,0:T(8,128)(2,1)S(1)}, u32[]{:S(2)}, u32[]{:S(2)}) collective-permute-start(bf16[64,512]{1,0:T(8,128)(2,1)S(1)} %fusion.6), channel_id=1, source_target_pairs={{0,64},{64,128},{128,192},{192,0},{1,65},{65,129},{129,193},{193,1... | collective-permute-start | bytes 196616 | tf_op jit(solution)/shard_map/spread/ppermute | solution.py:226
  80.2 5.8 %collective-permute-start.13 = (bf16[64,512]{1,0:T(8,128)(2,1)S(1)}, bf16[64,512]{1,0:T(8,128)(2,1)S(1)}, u32[]{:S(2)}, u32[]{:S(2)}) collective-permute-start(bf16[64,512]{1,0:T(8,128)(2,1)S(1)} %fusion.6), channel_id=1, source_target_pairs={{0,128},{64,192},{128,0},{192,64},{1,129},{65,193},{129,1},{193,65... | collective-permute-start | bytes 196616 | tf_op jit(solution)/shard_map/spread/ppermute | solution.py:226
  81.0 5.0 %collective-permute-start.12 = (bf16[64,512]{1,0:T(8,128)(2,1)S(1)}, bf16[64,512]{1,0:T(8,128)(2,1)S(1)}, u32[]{:S(2)}, u32[]{:S(2)}) collective-permute-start(bf16[64,512]{1,0:T(8,128)(2,1)S(1)} %fusion.6), channel_id=1, source_target_pairs={{0,192},{64,0},{128,64},{192,128},{1,193},{65,1},{129,65},{193,129... | collective-permute-start | bytes 196616 | tf_op jit(solution)/shard_map/spread/ppermute | solution.py:226
  86.0 4.0 %collective-permute-start.15 = (bf16[256,512]{1,0:T(8,128)(2,1)S(1)}, bf16[256,512]{1,0:T(8,128)(2,1)S(1)}, u32[]{:S(2)}, u32[]{:S(2)}) collective-permute-start(bf16[256,512]{1,0:T(8,128)(2,1)S(1)} %constant_dynamic-update-slice_fusion.5.refs_0_), channel_id=1, source_target_pairs={{0,1},{1,0},{2,3},{3,2},{4,5},{5,4},{6,7},{7,6},{8,9},{9,8},{10,11... | collective-permute-start | bytes 786440 | tf_op jit(solution)/shard_map/spread/ppermute | solution.py:222
  90.0 5.2 %copy-start.1 = (bf16[512,512]{1,0:T(8,128)(2,1)S(1)}, bf16[512,512]{1,0:T(8,128)(2,1)}, u32[]{:S(2)}) copy-start(bf16[512,512]{1,0:T(8,128)(2,1)} %weight_ref.1) | copy-start | bytes 1572868
  90.8 9.6 %collective-permute-start.16 = (f32[16,512]{1,0:T(8,128)S(1)}, f32[16,512]{1,0:T(8,128)S(1)}, u32[]{:S(2)}, u32[]{:S(2)}) collective-permute-start(f32[16,512]{1,0:T(8,128)S(1)} %get-tuple-element.52), channel_id=1, source_target_pairs={{0,16},{16,32},{32,48},{48,0},{1,17},{17,33},{33,49},{49,1},{2,18}... | collective-permute-start | bytes 98312 | tf_op jit(solution)/shard_map/spread/ppermute | solution.py:226
  91.5 8.9 %collective-permute-start.17 = (f32[16,512]{1,0:T(8,128)S(1)}, f32[16,512]{1,0:T(8,128)S(1)}, u32[]{:S(2)}, u32[]{:S(2)}) collective-permute-start(f32[16,512]{1,0:T(8,128)S(1)} %get-tuple-element.53), channel_id=1, source_target_pairs={{0,32},{16,48},{32,0},{48,16},{1,33},{17,49},{33,1},{49,17},{2,34}... | collective-permute-start | bytes 98312 | tf_op jit(solution)/shard_map/spread/ppermute | solution.py:226
  94.4 5.9 %collective-permute-start.18 = (f32[16,512]{1,0:T(8,128)S(1)}, f32[16,512]{1,0:T(8,128)S(1)}, u32[]{:S(2)}, u32[]{:S(2)}) collective-permute-start(f32[16,512]{1,0:T(8,128)S(1)} %get-tuple-element.54), channel_id=1, source_target_pairs={{0,48},{16,0},{32,16},{48,32},{1,49},{17,1},{33,17},{49,33},{2,50}... | collective-permute-start | bytes 98312 | tf_op jit(solution)/shard_map/spread/ppermute | solution.py:226
  99.0 1.3 copy-start
  100.4 29.2 %all-to-all-start.2 = ((bf16[4,512,512]{2,1,0:T(8,128)(2,1)}), bf16[4,512,512]{2,1,0:T(8,128)(2,1)S(1)}, u32[]{:S(2)}, u32[]{:S(2)}) async-start(bf16[4,512,512]{2,1,0:T(8,128)(2,1)} %copy-done), calls=%async_computation.2 | async-start | bytes 4194304 | tf_op jit(solution)/shard_map/sums/all_to_all | solution.py:230
  104.0 8.2 %collective-permute-start.26 = (f32[16,512]{1,0:T(8,128)S(1)}, f32[16,512]{1,0:T(8,128)S(1)}, u32[]{:S(2)}, u32[]{:S(2)}) collective-permute-start(f32[16,512]{1,0:T(8,128)S(1)} %add_add_fusion.refs_0_), channel_id=1, source_target_pairs={{0,2},{2,4},{4,6},{6,8},{8,10},{10,12},{12,14},{14,0},{1,3},{3,5},... | collective-permute-start | bytes 98312 | tf_op jit(solution)/shard_map/sums/ppermute | solution.py:226
  104.9 9.5 %collective-permute-start.25 = (f32[16,512]{1,0:T(8,128)S(1)}, f32[16,512]{1,0:T(8,128)S(1)}, u32[]{:S(2)}, u32[]{:S(2)}) collective-permute-start(f32[16,512]{1,0:T(8,128)S(1)} %add_add_fusion.refs_0_), channel_id=1, source_target_pairs={{0,4},{2,6},{4,8},{6,10},{8,12},{10,14},{12,0},{14,2},{1,5},{3,7},... | collective-permute-start | bytes 98312 | tf_op jit(solution)/shard_map/sums/ppermute | solution.py:226
  105.9 9.3 %collective-permute-start.24 = (f32[16,512]{1,0:T(8,128)S(1)}, f32[16,512]{1,0:T(8,128)S(1)}, u32[]{:S(2)}, u32[]{:S(2)}) collective-permute-start(f32[16,512]{1,0:T(8,128)S(1)} %add_add_fusion.refs_0_), channel_id=1, source_target_pairs={{0,6},{2,8},{4,10},{6,12},{8,14},{10,0},{12,2},{14,4},{1,7},{3,9},... | collective-permute-start | bytes 98312 | tf_op jit(solution)/shard_map/sums/ppermute | solution.py:226
  107.2 7.9 %collective-permute-start.23 = (f32[16,512]{1,0:T(8,128)S(1)}, f32[16,512]{1,0:T(8,128)S(1)}, u32[]{:S(2)}, u32[]{:S(2)}) collective-permute-start(f32[16,512]{1,0:T(8,128)S(1)} %add_add_fusion.refs_0_), channel_id=1, source_target_pairs={{0,8},{2,10},{4,12},{6,14},{8,0},{10,2},{12,4},{14,6},{1,9},{3,11}... | collective-permute-start | bytes 98312 | tf_op jit(solution)/shard_map/sums/ppermute | solution.py:226
  110.9 4.9 %collective-permute-start.22 = (f32[16,512]{1,0:T(8,128)S(1)}, f32[16,512]{1,0:T(8,128)S(1)}, u32[]{:S(2)}, u32[]{:S(2)}) collective-permute-start(f32[16,512]{1,0:T(8,128)S(1)} %add_add_fusion.refs_0_), channel_id=1, source_target_pairs={{0,10},{2,12},{4,14},{6,0},{8,2},{10,4},{12,6},{14,8},{1,11},{3,13... | collective-permute-start | bytes 98312 | tf_op jit(solution)/shard_map/sums/ppermute | solution.py:226
  112.2 5.5 %collective-permute-start.21 = (f32[16,512]{1,0:T(8,128)S(1)}, f32[16,512]{1,0:T(8,128)S(1)}, u32[]{:S(2)}, u32[]{:S(2)}) collective-permute-start(f32[16,512]{1,0:T(8,128)S(1)} %add_add_fusion.refs_0_), channel_id=1, source_target_pairs={{0,12},{2,14},{4,0},{6,2},{8,4},{10,6},{12,8},{14,10},{1,13},{3,15... | collective-permute-start | bytes 98312 | tf_op jit(solution)/shard_map/sums/ppermute | solution.py:226
  114.4 3.5 %collective-permute-start.20 = (f32[16,512]{1,0:T(8,128)S(1)}, f32[16,512]{1,0:T(8,128)S(1)}, u32[]{:S(2)}, u32[]{:S(2)}) collective-permute-start(f32[16,512]{1,0:T(8,128)S(1)} %add_add_fusion.refs_0_), channel_id=1, source_target_pairs={{0,14},{2,0},{4,2},{6,4},{8,6},{10,8},{12,10},{14,12},{1,15},{3,1}... | collective-permute-start | bytes 98312 | tf_op jit(solution)/shard_map/sums/ppermute | solution.py:226
  130.6 22.6 %all-to-all-start.3 = ((f32[32,16,512]{2,1,0:T(8,128)}), f32[32,16,512]{2,1,0:T(8,128)}, u32[]{:S(2)}, u32[]{:S(2)}) async-start(f32[32,16,512]{2,1,0:T(8,128)} %broadcast_in_dim.5), calls=%async_computation.3 | async-start | bytes 2097152 | tf_op jit(solution)/shard_map/sums/all_to_all | solution.py:230
  138.0 7.8 %collective-permute-start.27 = (bf16[64,512]{1,0:T(8,128)(2,1)S(1)}, bf16[64,512]{1,0:T(8,128)(2,1)S(1)}, u32[]{:S(2)}, u32[]{:S(2)}) collective-permute-start(bf16[64,512]{1,0:T(8,128)(2,1)S(1)} %get-tuple-element.66), channel_id=1, source_target_pairs={{0,2},{2,4},{4,6},{6,8},{8,10},{10,12},{12,14},{14,0},{1,3},{3,5},... | collective-permute-start | bytes 196616 | tf_op jit(solution)/shard_map/sums/ppermute | solution.py:226
  138.9 7.2 %collective-permute-start.28 = (bf16[64,512]{1,0:T(8,128)(2,1)S(1)}, bf16[64,512]{1,0:T(8,128)(2,1)S(1)}, u32[]{:S(2)}, u32[]{:S(2)}) collective-permute-start(bf16[64,512]{1,0:T(8,128)(2,1)S(1)} %get-tuple-element.67), channel_id=1, source_target_pairs={{0,14},{2,0},{4,2},{6,4},{8,6},{10,8},{12,10},{14,12},{1,15},{3,1}... | collective-permute-start | bytes 196616 | tf_op jit(solution)/shard_map/sums/ppermute | solution.py:226
  140.7 12.6 %collective-permute-start.29 = (bf16[64,512]{1,0:T(8,128)(2,1)S(1)}, bf16[64,512]{1,0:T(8,128)(2,1)S(1)}, u32[]{:S(2)}, u32[]{:S(2)}) collective-permute-start(bf16[64,512]{1,0:T(8,128)(2,1)S(1)} %get-tuple-element.68), channel_id=1, source_target_pairs={{0,8},{2,10},{4,12},{6,14},{8,0},{10,2},{12,4},{14,6},{1,9},{3,11}... | collective-permute-start | bytes 196616 | tf_op jit(solution)/shard_map/sums/ppermute | solution.py:226
  142.2 11.1 %collective-permute-start.30 = (bf16[64,512]{1,0:T(8,128)(2,1)S(1)}, bf16[64,512]{1,0:T(8,128)(2,1)S(1)}, u32[]{:S(2)}, u32[]{:S(2)}) collective-permute-start(bf16[64,512]{1,0:T(8,128)(2,1)S(1)} %get-tuple-element.69), channel_id=1, source_target_pairs={{0,4},{2,6},{4,8},{6,10},{8,12},{10,14},{12,0},{14,2},{1,5},{3,7},... | collective-permute-start | bytes 196616 | tf_op jit(solution)/shard_map/sums/ppermute | solution.py:226
  143.0 10.3 %collective-permute-start.31 = (bf16[64,512]{1,0:T(8,128)(2,1)S(1)}, bf16[64,512]{1,0:T(8,128)(2,1)S(1)}, u32[]{:S(2)}, u32[]{:S(2)}) collective-permute-start(bf16[64,512]{1,0:T(8,128)(2,1)S(1)} %get-tuple-element.70), channel_id=1, source_target_pairs={{0,12},{2,14},{4,0},{6,2},{8,4},{10,6},{12,8},{14,10},{1,13},{3,15... | collective-permute-start | bytes 196616 | tf_op jit(solution)/shard_map/sums/ppermute | solution.py:226
  145.8 10.9 %collective-permute-start.32 = (bf16[64,512]{1,0:T(8,128)(2,1)S(1)}, bf16[64,512]{1,0:T(8,128)(2,1)S(1)}, u32[]{:S(2)}, u32[]{:S(2)}) collective-permute-start(bf16[64,512]{1,0:T(8,128)(2,1)S(1)} %get-tuple-element.71), channel_id=1, source_target_pairs={{0,6},{2,8},{4,10},{6,12},{8,14},{10,0},{12,2},{14,4},{1,7},{3,9},... | collective-permute-start | bytes 196616 | tf_op jit(solution)/shard_map/sums/ppermute | solution.py:226
  146.1 10.6 %collective-permute-start.33 = (bf16[64,512]{1,0:T(8,128)(2,1)S(1)}, bf16[64,512]{1,0:T(8,128)(2,1)S(1)}, u32[]{:S(2)}, u32[]{:S(2)}) collective-permute-start(bf16[64,512]{1,0:T(8,128)(2,1)S(1)} %get-tuple-element.72), channel_id=1, source_target_pairs={{0,10},{2,12},{4,14},{6,0},{8,2},{10,4},{12,6},{14,8},{1,11},{3,13... | collective-permute-start | bytes 196616 | tf_op jit(solution)/shard_map/sums/ppermute | solution.py:226

commit v4 on v3

--- a/solution.py
+++ b/solution.py
@@ -164,8 +164,7 @@
 
 
 def spread_kernel(coord_ref, _, weight_ref, high_ref, low_ref, *refs):
-    pre_refs, out_ref, token_ref, pre = refs[:NC], refs[NC], refs[-2], refs[-1]
-    token_ref[...] = jnp.zeros_like(token_ref)
+    pre_refs, out_ref, pre = refs[:NC], refs[NC], refs[-1]
     x = coord_ref[2]
     for k in range(NC * NX):
         dc, dx = k // NX, k % NX
@@ -194,21 +193,27 @@
         out_refs[k][...] = terms[rows, :]
 
 
-def plane_kernel(coord_ref, _, in_ref, *refs):
-    out_refs, total = refs[:-1], refs[-1]
-    z = coord_ref[3]
+def plane_kernel(in_ref, out_ref):
     value = in_ref[0].astype(F32)
     for k in range(1, NY):
         value = value + in_ref[k].astype(F32)
-    total[...] = value
     for k in range(NZ):
-        rows = pl.ds(pl.multiple_of(((z + k) & (NZ - 1)) * ROWS, ROWS), ROWS)
-        out_refs[k][...] = total[rows, :].astype(out_refs[k].dtype)
+        out_ref[k] = value[k * ROWS : (k + 1) * ROWS, :].astype(BF)
+
+
+def place_kernel(coord_ref, near_ref, far_ref, out_ref):
+    y, c, x = coord_ref[0], coord_ref[1], coord_ref[2]
+    size = ROWS // NY
+    for dc, ref in enumerate((near_ref, far_ref)):
+        for dx in range(NX):
+            for dy in range(NY):
+                start = (((x + dx) & (NX - 1)) * NC + (c ^ dc)) * ROWS + ((y + dy) & (NY - 1)) * size
+                here = (dx * NY + dy) * size
+                out_ref[pl.ds(pl.multiple_of(start, size), size), :] = ref[here : here + size, :]
 
 
 def share_kernel(coord_ref, *refs):
-    in_refs, out_ref, token_ref, parts = refs[:NZ], refs[NZ], refs[NZ + 1], refs[-1]
-    token_ref[...] = jnp.zeros_like(token_ref)
+    in_refs, out_ref, parts = refs[:NZ], refs[NZ], refs[-1]
     z = coord_ref[3]
     for k in range(NZ):
         parts[(z + k) & (NZ - 1)] = in_refs[k][...]
@@ -294,8 +299,9 @@
             name="bucket",
         )(pair_owner.T, pair_row.T)
         ends = ends.reshape(NDEV, 2, 2 * CAP)
+        ends, late_nodes = lax.optimization_barrier((ends, node_aggregate))
         near_nodes = jnp.concatenate(
-            [node_aggregate] + [shift(node_aggregate, "x", NX, -k) for k in range(1, NX)], axis=0
+            [late_nodes] + [shift(late_nodes, "x", NX, -k) for k in range(1, NX)], axis=0
         )
         nodes = jnp.concatenate([near_nodes, swap(near_nodes)], axis=0)
         column = (lax.axis_index("x") * NC + c) * ROWS
@@ -346,11 +352,11 @@
             name="weight_terms",
         )(coord, nodes, *pre_parts)
         others = [shift(terms[k], "y", NY, k) for k in range(1, NY)]
-        send, token = pl.pallas_call(
+        send = pl.pallas_call(
             spread_kernel,
-            out_shape=[jax.ShapeDtypeStruct((NY, NZ * ROWS, F), BF), TOKEN],
+            out_shape=jax.ShapeDtypeStruct((NY, NZ * ROWS, F), BF),
             in_specs=[SMEM, ANY] + [VMEM] * 5,
-            out_specs=[VMEM] * 2,
+            out_specs=VMEM,
             scratch_shapes=[pltpu.VMEM((NC * NX * ROWS, F), BF)],
             compiler_params=params(),
             cost_estimate=pl.CostEstimate(flops=5_000_000_000, bytes_accessed=8_000_000, transcendentals=0),
@@ -358,39 +364,46 @@
         )(coord, token, weight, high, low, *pre_parts)
 
     with jax.named_scope("sums"):
-        *others, send, token = lax.optimization_barrier((*others, send, token))
+        *others, send = lax.optimization_barrier((*others, send))
         planes = exchange(send, "y")
         share = terms[0]
         for other in others:
             share = share + other
-        block, share_token = pl.pallas_call(
+        block = pl.pallas_call(
             share_kernel,
-            out_shape=[jax.ShapeDtypeStruct((ROWS // NY, F), F32), TOKEN],
+            out_shape=jax.ShapeDtypeStruct((ROWS // NY, F), F32),
             in_specs=[SMEM] + [VMEM] * NZ,
-            out_specs=[VMEM] * 2,
+            out_specs=VMEM,
             scratch_shapes=[pltpu.VMEM((NZ, ROWS // NY, F), F32)],
             compiler_params=params(),
             cost_estimate=pl.CostEstimate(flops=1_000_000, bytes_accessed=300_000, transcendentals=0),
             name="share_sum",
         )(coord, share, *[shift(share, "z", NZ, -k) for k in range(1, NZ)])
-        token, share_token = lax.optimization_barrier((token, share_token))
-        own, *parts = pl.pallas_call(
+        part = pl.pallas_call(
             plane_kernel,
-            out_shape=[
-                jax.ShapeDtypeStruct((ROWS, F), dtype) for dtype in (F32,) + (BF,) * (NZ - 1)
-            ],
-            in_specs=[SMEM, ANY, VMEM],
-            out_specs=[VMEM] * NZ,
-            scratch_shapes=[pltpu.VMEM((NZ * ROWS, F), F32)],
+            out_shape=jax.ShapeDtypeStruct((NZ, ROWS, F), BF),
+            in_specs=[VMEM],
+            out_specs=VMEM,
             compiler_params=params(),
             cost_estimate=pl.CostEstimate(flops=2_000_000_000, bytes_accessed=3_000_000, transcendentals=0),
             name="plane_sum",
-        )(coord, share_token, planes)
-        feature = own
-        for k in (1, 7, 4, 2, 6, 3, 5):
-            feature = feature + shift(parts[k - 1], "z", NZ, k).astype(F32)
-        feature_grad = feature.astype(BF)
-        weight_grad = gather(block, ("x", "c", "y"), NX * NC * NY).reshape(F, F)
+        )(planes)
+        rings = exchange(part, "z").astype(F32)
+        block = jnp.concatenate([block] + [shift(block, "y", NY, -k) for k in range(1, NY)], axis=0)
+        block, part = lax.optimization_barrier((block, part))
+        near_block = jnp.concatenate(
+            [block] + [shift(block, "x", NX, -k) for k in range(1, NX)], axis=0
+        )
+        weight_grad = pl.pallas_call(
+            place_kernel,
+            out_shape=jax.ShapeDtypeStruct((F, F), F32),
+            in_specs=[SMEM, VMEM, VMEM],
+            out_specs=VMEM,
+            compiler_params=params(),
+            cost_estimate=pl.CostEstimate(flops=1_000_000, bytes_accessed=2_000_000, transcendentals=0),
+            name="place",
+        )(coord, near_block, swap(near_block))
+        feature_grad = jnp.sum(rings, axis=0).astype(BF)
     return (feature_grad, weight_grad)
 
 

time: 160 us -> 159 us (level)
  local copies, waits for them, and re-layouts: 6.75 us -> 2.11 us
  Pallas kernels: 42.5 us -> 44.6 us
    all_to_all x4, waiting for transfers between devices: 23.2 us -> 9.45 us  [exchange(): return lax.all_to_all(values, axes, 0, 0, tiled=True)]
    ppermute x26 -> x25, waiting for transfers between devices: 9.47 us -> 22.5 us  [shift(): lax.ppermute(values, axis, [(i, (i + step) % size) for i in range(size)])]
    ppermute x26 -> x25, starting transfers between devices: 41.5 us -> 37.6 us  [shift(): lax.ppermute(values, axis, [(i, (i + step) % size) for i in range(size)])]
    unnamed x25, local copies, waits for them, and re-layouts: 3.73 us -> 0.16 us
    ppermute x8 -> x9, starting transfers between devices: 5.44 us -> 8.54 us  [swap(): return lax.ppermute(values, 'c', [(0, 1), (1, 0)])]
    pallas_call x3 -> x4, Pallas kernels: 5.4 us -> 7.82 us  [the longest x1 4.58 us: per_device(): pl.pallas_call(spread_kernel, out_shape=jax.ShapeDtypeStruct((NY, NZ * RO...]
  transfers between devices with their start and end apart: 38 -> 38, of which waited for: 10 -> 11; matrix products, arithmetic and copies ran while one was open for 2% -> 1% of each run, Pallas kernels for 26% -> 27%
where the time goes in v4:
time: 159 us
  starting transfers between devices  73 us (46%)
  Pallas kernels  44.6 us (28%)
  waiting for transfers between devices  34.6 us (22%)
  local copies, waits for them, and re-layouts  2.11 us (1%)
  between operations  1.69 us (1%)
    ppermute x25, starting transfers between devices, shift(): lax.ppermute(values, axis, [(i, (i + step) % size) for i in range(size)])  37.6 us
    all_to_all x4, starting transfers between devices, exchange(): return lax.all_to_all(values, axes, 0, 0, tiled=True)  26.9 us
    ppermute x25, waiting for transfers between devices, shift(): lax.ppermute(values, axis, [(i, (i + step) % size) for i in range(size)])  22.5 us
    pallas_call x1, Pallas kernels, count(): pl.pallas_call(count_kernel, out_shape=[half, half, TOKEN], in_specs=[SME...  21 us
    all_to_all x4, waiting for transfers between devices, exchange(): return lax.all_to_all(values, axes, 0, 0, tiled=True)  9.45 us
    ppermute x9, starting transfers between devices, swap(): return lax.ppermute(values, 'c', [(0, 1), (1, 0)])  8.54 us
    pallas_call x1, Pallas kernels, per_device(): pl.pallas_call(bucket_kernel, out_shape=[jax.ShapeDtypeStruct((NDEV, 4 *...  8.24 us
    pallas_call x2, Pallas kernels, pair_grad(): pl.pallas_call(functools.partial(grad_kernel, scale), out_shape=jax.Shape...  4.78 us
  transfers between devices with their start and end apart: 38, of which 11 were waited for; matrix products, arithmetic and copies ran while one was open for 1% of the time, Pallas kernels for 27%

profile of v4, /device:TPU:1, one launch (start us, length us, event | category | flops | bytes accessed | tf_op | source)
XLA Modules:
  0.0 158.5 jit_solution(6019203461179263304)
XLA Ops:
  0.6 1.4 multiply_convert_fusion
  2.0 0.8 broadcast_in_dim.2
  2.8 9.0 %all-to-all-start = ((bf16[8,64,512]{2,1,0:T(8,128)(2,1)}), bf16[8,64,512]{2,1,0:T(8,128)(2,1)S(1)}, u32[]{:S(2)}, u32[]{:S(2)}) async-start(bf16[8,64,512]{2,1,0:T(8,128)(2,1)} %broadcast_in_dim.2), calls=%async_computation | async-start | bytes 1048576 | tf_op jit(solution)/shard_map/pair_exchange/all_to_all | solution.py:235
  11.9 8.2 %bucket.1 = (bf16[64,2048]{1,0:T(8,128)(2,1)S(1)}, f32[8,128]{1,0:T(8,128)}) custom-call(s32[2,8192]{1,0:T(2,128)S(1)} %bitcast.29, s32[2,8192]{1,0:T(2,128)S(1)} %bitcast.30), custom_call_target="tpu_custom_call" | custom-call | flops 8999999488 | bytes 400000 | tf_op jit(solution)/shard_map/pair_exchange/bucket/pallas_call | solution.py:291
  20.1 0.9 reshape.22
  21.0 1.2 collective-permute-start.2
  22.3 2.4 %collective-permute-start.1 = (bf16[64,512]{1,0:T(8,128)(2,1)S(1)}, bf16[64,512]{1,0:T(8,128)(2,1)S(1)}, u32[]{:S(2)}, u32[]{:S(2)}) collective-permute-start(bf16[64,512]{1,0:T(8,128)(2,1)S(1)} %copy-done.4), channel_id=1, source_target_pairs={{0,128},{64,192},{128,0},{192,64},{1,129},{65,193},{129,1},{193,65... | collective-permute-start | bytes 196616 | tf_op jit(solution)/shard_map/pair_exchange/ppermute | solution.py:231
  24.7 1.2 collective-permute-start
  25.9 1.3 collective-permute-done.1
  27.2 1.5 collective-permute-done
  28.7 1.9 %collective-permute-start.3 = (bf16[256,512]{1,0:T(8,128)(2,1)S(1)}, bf16[256,512]{1,0:T(8,128)(2,1)S(1)}, u32[]{:S(2)}, u32[]{:S(2)}) collective-permute-start(bf16[256,512]{1,0:T(8,128)(2,1)S(1)} %pad_maximum_fusion), channel_id=1, source_target_pairs={{0,1},{1,0},{2,3},{3,2},{4,5},{5,4},{6,7},{7,6},{8,9},{9,8},{10,11... | collective-permute-start | bytes 786440 | tf_op jit(solution)/shard_map/pair_exchange/ppermute | solution.py:227
  30.6 1.1 collective-permute-done.3
  31.8 0.1 constant_dynamic-slice_fusion.node_ref
  31.9 10.8 %all-to-all-start.1 = ((bf16[64,2,1024]{2,1,0:T(2,128)(2,1)}), bf16[64,2,1024]{2,1,0:T(2,128)(2,1)S(1)}, u32[]{:S(2)}, u32[]{:S(2)}) async-start(bf16[64,2,1024]{2,1,0:T(2,128)(2,1)} %reshape.22), calls=%async_computation.1 | async-start | bytes 524288 | tf_op jit(solution)/shard_map/pair_exchange/all_to_all | solution.py:235
  43.4 0.5 collective-permute-start.11
  44.1 1.4 collective-permute-start.6
  45.5 2.6 %collective-permute-start.5 = (bf16[512,512]{1,0:T(8,128)(2,1)S(1)}, bf16[512,512]{1,0:T(8,128)(2,1)S(1)}, u32[]{:S(2)}, u32[]{:S(2)}) collective-permute-start(bf16[512,512]{1,0:T(8,128)(2,1)S(1)} %bitcast.25), channel_id=1, source_target_pairs={{0,32},{16,48},{32,0},{48,16},{1,33},{17,49},{33,1},{49,17},{2,34}... | collective-permute-start | bytes 1572872 | tf_op jit(solution)/shard_map/pair_exchange/ppermute | solution.py:231
  48.1 1.1 collective-permute-start.4
  49.1 5.6 %all-to-all-done.1 = bf16[64,2,1024]{2,1,0:T(2,128)(2,1)S(1)} async-done(((bf16[64,2,1024]{2,1,0:T(2,128)(2,1)}), bf16[64,2,1024]{2,1,0:T(2,128)(2,1)S(1)}, u32[]{:S(2)}, u32[]{:S(2)}) %all-to-all-start.1) | async-done | bytes 262176 | tf_op jit(solution)/shard_map/pair_exchange/all_to_all | solution.py:235
  54.8 21.0 %count.1 = (f32[2,256,512]{2,1,0:T(8,128)S(1)}, f32[2,256,512]{2,1,0:T(8,128)S(1)}, f32[8,128]{1,0:T(8,128)S(1)}) custom-call(s32[4]{0:T(128)S(1)} %pad_add_fusion.1.coord_ref, bf16[64,2048]{1,0:T(8,128)(2,1)S(1)} %bitcast.28), custom_call_target="tpu_custom_call" | custom-call | flops 24000000000 | bytes 2400000 | tf_op jit(solution)/shard_map/pair_exchange/count/pallas_call | solution.py:248
  75.8 0.7 collective-permute-start.8
  76.5 0.1 collective-permute-start.9
  76.6 0.4 collective-permute-start.10
  77.1 0.1 fusion.9
  77.1 0.1 collective-permute-start.19
  77.3 2.9 %pair_grad.2.refs_4_ = f32[64,512]{1,0:T(8,128)S(1)} custom-call(f32[8,128]{1,0:T(8,128)S(1)} %get-tuple-element.37._, bf16[64,512]{1,0:T(8,128)(2,1)S(1)} %get-tuple-element.60.own_ref, f32[2,256,512]{2,1,0:T(8,128)S(1)} %get-tuple-element.42.count_ref, bf16[512,512]{1,0:T(8,128)(2,1)S(1)} %bitcast.27, bf16[512,512]{1,0:T(8,128)(2,1)} %collective-permute-done.4.refs_1_, ...), custom_call_target="tpu_custom_call" | custom-call | flops 3000000000 | bytes 3000000 | tf_op jit(solution)/shard_map/hidden_grad/pair_grad/pallas_call | solution.py:265
  80.3 1.9 %pair_grad.3 = f32[64,512]{1,0:T(8,128)S(1)} custom-call(f32[8,128]{1,0:T(8,128)S(1)} %get-tuple-element.37._, bf16[64,512]{1,0:T(8,128)(2,1)S(1)} %get-tuple-element.60.own_ref, f32[2,256,512]{2,1,0:T(8,128)S(1)} %get-tuple-element.38.count_ref, bf16[512,512]{1,0:T(8,128)(2,1)S(1)} %collective-permute-done.7.refs_0_, ...), custom_call_target="tpu_custom_call" | custom-call | flops 3000000000 | bytes 3000000 | tf_op jit(solution)/shard_map/hidden_grad/pair_grad/pallas_call | solution.py:265
  82.1 0.1 fusion.6
  82.2 0.4 collective-permute-start.14
  82.6 3.3 %collective-permute-start.13 = (bf16[64,512]{1,0:T(8,128)(2,1)S(1)}, bf16[64,512]{1,0:T(8,128)(2,1)S(1)}, u32[]{:S(2)}, u32[]{:S(2)}) collective-permute-start(bf16[64,512]{1,0:T(8,128)(2,1)S(1)} %fusion.6), channel_id=1, source_target_pairs={{0,128},{64,192},{128,0},{192,64},{1,129},{65,193},{129,1},{193,65... | collective-permute-start | bytes 196616 | tf_op jit(solution)/shard_map/spread/ppermute | solution.py:231
  85.9 3.5 %collective-permute-done.12 = bf16[64,512]{1,0:T(8,128)(2,1)S(1)} collective-permute-done((bf16[64,512]{1,0:T(8,128)(2,1)S(1)}, bf16[64,512]{1,0:T(8,128)(2,1)S(1)}, u32[]{:S(2)}, u32[]{:S(2)}) %collective-permute-start.12) | collective-permute-done | bytes 65568 | tf_op jit(solution)/shard_map/spread/ppermute | solution.py:231
  89.4 1.8 %collective-permute-start.15 = (bf16[256,512]{1,0:T(8,128)(2,1)S(1)}, bf16[256,512]{1,0:T(8,128)(2,1)S(1)}, u32[]{:S(2)}, u32[]{:S(2)}) collective-permute-start(bf16[256,512]{1,0:T(8,128)(2,1)S(1)} %constant_dynamic-update-slice_fusion.5.refs_0_), channel_id=1, source_target_pairs={{0,1},{1,0},{2,3},{3,2},{4,5},{5,4},{6,7},{7,6},{8,9},{9,8},{10,11... | collective-permute-start | bytes 786440 | tf_op jit(solution)/shard_map/spread/ppermute | solution.py:227
  91.2 2.0 %tile_sum.1 = (bf16[2048,512]{1,0:T(8,128)(2,1)S(1)}, bf16[2048,512]{1,0:T(8,128)(2,1)S(1)}) custom-call(s32[2,65]{1,0:T(2,128)S(1)} %pad_add_fusion.meta_ref, bf16[32,64,128]{2,1,0:T(8,128)(2,1)S(1)} %get-tuple-element.59.own_ref, bf16[32,64,128]{2,1,0:T(8,128)(2,1)S(1)} %collective-permute-done.19.other_ref), custom_call_target="tpu_custom_call" | custom-call | flops 3000000000 | bytes 5000000 | tf_op jit(solution)/shard_map/spread/tile_sum/pallas_call | solution.py:331
  93.3 0.8 weight_terms.1
  94.1 1.0 collective-permute-start.16
  95.1 2.7 %collective-permute-start.17 = (f32[16,512]{1,0:T(8,128)S(1)}, f32[16,512]{1,0:T(8,128)S(1)}, u32[]{:S(2)}, u32[]{:S(2)}) collective-permute-start(f32[16,512]{1,0:T(8,128)S(1)} %get-tuple-element.46), channel_id=1, source_target_pairs={{0,32},{16,48},{32,0},{48,16},{1,33},{17,49},{33,1},{49,17},{2,34}... | collective-permute-start | bytes 98312 | tf_op jit(solution)/shard_map/spread/ppermute | solution.py:231
  97.8 0.7 collective-permute-start.18
  98.5 4.6 %spread.1 = bf16[4,512,512]{2,1,0:T(8,128)(2,1)} custom-call(s32[4]{0:T(128)S(1)} %pad_add_fusion.1.coord_ref, f32[8,128]{1,0:T(8,128)S(1)} %get-tuple-element.48._, bf16[512,512]{1,0:T(8,128)(2,1)S(1)} %copy-done, bf16[2048,512]{1,0:T(8,128)(2,1)S(1)} %get-tuple-element.50.high_ref, bf16[2048,512]{1,0:T(8,128)(2,1)S(1)} %get-tuple-element.51.low_ref, ...), custom_call_target="tpu_custom_call" | custom-call | flops 5000000000 | bytes 8000000 | tf_op jit(solution)/shard_map/spread/spread/pallas_call | solution.py:355
  103.1 3.6 %all-to-all-start.2 = ((bf16[4,512,512]{2,1,0:T(8,128)(2,1)}), bf16[4,512,512]{2,1,0:T(8,128)(2,1)S(1)}, u32[]{:S(2)}, u32[]{:S(2)}) async-start(bf16[4,512,512]{2,1,0:T(8,128)(2,1)} %spread.1), calls=%async_computation.2 | async-start | bytes 4194304 | tf_op jit(solution)/shard_map/sums/all_to_all | solution.py:235
  106.8 0.8 collective-permute-start.26
  107.6 1.0 collective-permute-start.25
  108.7 2.0 %collective-permute-start.24 = (f32[16,512]{1,0:T(8,128)S(1)}, f32[16,512]{1,0:T(8,128)S(1)}, u32[]{:S(2)}, u32[]{:S(2)}) collective-permute-start(f32[16,512]{1,0:T(8,128)S(1)} %add_add_fusion.refs_0_), channel_id=1, source_target_pairs={{0,6},{2,8},{4,10},{6,12},{8,14},{10,0},{12,2},{14,4},{1,7},{3,9},... | collective-permute-start | bytes 98312 | tf_op jit(solution)/shard_map/sums/ppermute | solution.py:231
  110.7 3.0 %collective-permute-start.23 = (f32[16,512]{1,0:T(8,128)S(1)}, f32[16,512]{1,0:T(8,128)S(1)}, u32[]{:S(2)}, u32[]{:S(2)}) collective-permute-start(f32[16,512]{1,0:T(8,128)S(1)} %add_add_fusion.refs_0_), channel_id=1, source_target_pairs={{0,8},{2,10},{4,12},{6,14},{8,0},{10,2},{12,4},{14,6},{1,9},{3,11}... | collective-permute-start | bytes 98312 | tf_op jit(solution)/shard_map/sums/ppermute | solution.py:231
  113.7 1.6 %collective-permute-start.22 = (f32[16,512]{1,0:T(8,128)S(1)}, f32[16,512]{1,0:T(8,128)S(1)}, u32[]{:S(2)}, u32[]{:S(2)}) collective-permute-start(f32[16,512]{1,0:T(8,128)S(1)} %add_add_fusion.refs_0_), channel_id=1, source_target_pairs={{0,10},{2,12},{4,14},{6,0},{8,2},{10,4},{12,6},{14,8},{1,11},{3,13... | collective-permute-start | bytes 98312 | tf_op jit(solution)/shard_map/sums/ppermute | solution.py:231
  115.3 2.2 %collective-permute-start.21 = (f32[16,512]{1,0:T(8,128)S(1)}, f32[16,512]{1,0:T(8,128)S(1)}, u32[]{:S(2)}, u32[]{:S(2)}) collective-permute-start(f32[16,512]{1,0:T(8,128)S(1)} %add_add_fusion.refs_0_), channel_id=1, source_target_pairs={{0,12},{2,14},{4,0},{6,2},{8,4},{10,6},{12,8},{14,10},{1,13},{3,15... | collective-permute-start | bytes 98312 | tf_op jit(solution)/shard_map/sums/ppermute | solution.py:231
  117.5 0.8 collective-permute-start.20
  118.3 1.4 collective-permute-done.21.refs_2_
  119.7 1.0 collective-permute-done.20.refs_1_
  120.7 0.6 share_sum.1
  121.3 1.7 %collective-permute-start.29 = (f32[16,512]{1,0:T(8,128)S(1)}, f32[16,512]{1,0:T(8,128)S(1)}, u32[]{:S(2)}, u32[]{:S(2)}) collective-permute-start(f32[16,512]{1,0:T(8,128)S(1)} %share_sum.1), channel_id=1, source_target_pairs={{0,16},{16,32},{32,48},{48,0},{1,17},{17,33},{33,49},{49,1},{2,18}... | collective-permute-start | bytes 98312 | tf_op jit(solution)/shard_map/sums/ppermute | solution.py:231
  122.9 2.4 %collective-permute-start.28 = (f32[16,512]{1,0:T(8,128)S(1)}, f32[16,512]{1,0:T(8,128)S(1)}, u32[]{:S(2)}, u32[]{:S(2)}) collective-permute-start(f32[16,512]{1,0:T(8,128)S(1)} %share_sum.1), channel_id=1, source_target_pairs={{0,32},{16,48},{32,0},{48,16},{1,33},{17,49},{33,1},{49,17},{2,34}... | collective-permute-start | bytes 98312 | tf_op jit(solution)/shard_map/sums/ppermute | solution.py:231
  125.3 1.2 collective-permute-start.27
  126.5 8.1 %collective-permute-done.29 = f32[16,512]{1,0:T(8,128)S(1)} collective-permute-done((f32[16,512]{1,0:T(8,128)S(1)}, f32[16,512]{1,0:T(8,128)S(1)}, u32[]{:S(2)}, u32[]{:S(2)}) %collective-permute-start.29) | collective-permute-done | bytes 32800 | tf_op jit(solution)/shard_map/sums/ppermute | solution.py:231
  134.6 1.1 plane_sum.1
  135.6 1.5 collective-permute-start.30
  137.2 3.5 %all-to-all-start.3 = ((bf16[8,64,512]{2,1,0:T(8,128)(2,1)}), bf16[8,64,512]{2,1,0:T(8,128)(2,1)S(1)}, u32[]{:S(2)}, u32[]{:S(2)}) async-start(bf16[8,64,512]{2,1,0:T(8,128)(2,1)} %plane_sum.1), calls=%async_computation.3 | async-start | bytes 1048576 | tf_op jit(solution)/shard_map/sums/all_to_all | solution.py:235
  140.7 0.1 collective-permute-start.32
  140.8 1.3 collective-permute-start.31
  142.1 5.7 %collective-permute-done.31 = f32[64,512]{1,0:T(8,128)S(1)} collective-permute-done((f32[64,512]{1,0:T(8,128)S(1)}, f32[64,512]{1,0:T(8,128)S(1)}, u32[]{:S(2)}, u32[]{:S(2)}) %collective-permute-start.31) | collective-permute-done | bytes 131104 | tf_op jit(solution)/shard_map/sums/ppermute | solution.py:231
  147.9 2.9 %collective-permute-start.33 = (f32[256,512]{1,0:T(8,128)S(1)}, f32[256,512]{1,0:T(8,128)S(1)}, u32[]{:S(2)}, u32[]{:S(2)}) collective-permute-start(f32[256,512]{1,0:T(8,128)S(1)} %constant_dynamic-update-slice_fusion.9.near_ref), channel_id=1, source_target_pairs={{0,1},{1,0},{2,3},{3,2},{4,5},{5,4},{6,7},{7,6},{8,9},{9,8},{10,11... | collective-permute-start | bytes 1572872 | tf_op jit(solution)/shard_map/sums/ppermute | solution.py:227
  150.8 1.5 collective-permute-done.33.far_ref
  152.3 1.6 %place.1 = f32[512,512]{1,0:T(8,128)} custom-call(s32[4]{0:T(128)S(1)} %pad_add_fusion.1.coord_ref, f32[256,512]{1,0:T(8,128)S(1)} %constant_dynamic-update-slice_fusion.9.near_ref, f32[256,512]{1,0:T(8,128)S(1)} %collective-permute-done.33.far_ref), custom_call_target="tpu_custom_call" | custom-call | flops 1000000 | bytes 2000000 | tf_op jit(solution)/shard_map/sums/place/pallas_call | solution.py:397
  153.9 3.9 %all-to-all-done.3 = bf16[8,64,512]{2,1,0:T(8,128)(2,1)S(1)} async-done(((bf16[8,64,512]{2,1,0:T(8,128)(2,1)}), bf16[8,64,512]{2,1,0:T(8,128)(2,1)S(1)}, u32[]{:S(2)}, u32[]{:S(2)}) %all-to-all-start.3) | async-done | bytes 524320 | tf_op jit(solution)/shard_map/sums/all_to_all | solution.py:235
  157.8 0.7 reduce_sum.12
  (64 shorter events, 0.6 us)
Async XLA Ops:
  0.6 11.2 %copy-start.2 = (s32[8192,2]{0,1:T(2,128)S(1)}, s32[8192,2]{0,1:T(2,128)}, u32[]{:S(2)}) copy-start(s32[8192,2]{0,1:T(2,128)} %param.15) | copy-start | bytes 196612
  0.6 11.2 %copy-start.1 = (s32[8192,2]{0,1:T(2,128)S(1)}, s32[8192,2]{0,1:T(2,128)}, u32[]{:S(2)}) copy-start(s32[8192,2]{0,1:T(2,128)} %param.14) | copy-start | bytes 196612
  2.8 29.0 %all-to-all-start = ((bf16[8,64,512]{2,1,0:T(8,128)(2,1)}), bf16[8,64,512]{2,1,0:T(8,128)(2,1)S(1)}, u32[]{:S(2)}, u32[]{:S(2)}) async-start(bf16[8,64,512]{2,1,0:T(8,128)(2,1)} %broadcast_in_dim.2), calls=%async_computation | async-start | bytes 1048576 | tf_op jit(solution)/shard_map/pair_exchange/all_to_all | solution.py:235
  11.9 9.2 %copy-start.4 = (bf16[64,512]{1,0:T(8,128)(2,1)S(1)}, bf16[64,512]{1,0:T(8,128)(2,1)}, u32[]{:S(2)}) copy-start(bf16[64,512]{1,0:T(8,128)(2,1)} %param.8) | copy-start | bytes 196612
  20.1 23.2 %copy-start.5 = (s32[32]{0:T(128)S(1)}, s32[32]{0:T(128)}, u32[]{:S(2)}) copy-start(s32[32]{0:T(128)} %param.12) | copy-start | bytes 388
  20.1 23.2 %copy-start.6 = (s32[32]{0:T(128)S(1)}, s32[32]{0:T(128)}, u32[]{:S(2)}) copy-start(s32[32]{0:T(128)} %param.11) | copy-start | bytes 388
  21.0 4.8 %collective-permute-start.2 = (bf16[64,512]{1,0:T(8,128)(2,1)S(1)}, bf16[64,512]{1,0:T(8,128)(2,1)S(1)}, u32[]{:S(2)}, u32[]{:S(2)}) collective-permute-start(bf16[64,512]{1,0:T(8,128)(2,1)S(1)} %copy-done.4), channel_id=1, source_target_pairs={{0,64},{64,128},{128,192},{192,0},{1,65},{65,129},{129,193},{193,1... | collective-permute-start | bytes 196616 | tf_op jit(solution)/shard_map/pair_exchange/ppermute | solution.py:231
  22.3 4.9 %collective-permute-start.1 = (bf16[64,512]{1,0:T(8,128)(2,1)S(1)}, bf16[64,512]{1,0:T(8,128)(2,1)S(1)}, u32[]{:S(2)}, u32[]{:S(2)}) collective-permute-start(bf16[64,512]{1,0:T(8,128)(2,1)S(1)} %copy-done.4), channel_id=1, source_target_pairs={{0,128},{64,192},{128,0},{192,64},{1,129},{65,193},{129,1},{193,65... | collective-permute-start | bytes 196616 | tf_op jit(solution)/shard_map/pair_exchange/ppermute | solution.py:231
  24.7 3.9 %collective-permute-start = (bf16[64,512]{1,0:T(8,128)(2,1)S(1)}, bf16[64,512]{1,0:T(8,128)(2,1)S(1)}, u32[]{:S(2)}, u32[]{:S(2)}) collective-permute-start(bf16[64,512]{1,0:T(8,128)(2,1)S(1)} %copy-done.4), channel_id=1, source_target_pairs={{0,192},{64,0},{128,64},{192,128},{1,193},{65,1},{129,65},{193,129... | collective-permute-start | bytes 196616 | tf_op jit(solution)/shard_map/pair_exchange/ppermute | solution.py:231
  28.7 3.1 %collective-permute-start.3 = (bf16[256,512]{1,0:T(8,128)(2,1)S(1)}, bf16[256,512]{1,0:T(8,128)(2,1)S(1)}, u32[]{:S(2)}, u32[]{:S(2)}) collective-permute-start(bf16[256,512]{1,0:T(8,128)(2,1)S(1)} %pad_maximum_fusion), channel_id=1, source_target_pairs={{0,1},{1,0},{2,3},{3,2},{4,5},{5,4},{6,7},{7,6},{8,9},{9,8},{10,11... | collective-permute-start | bytes 786440 | tf_op jit(solution)/shard_map/pair_exchange/ppermute | solution.py:227
  31.9 22.8 %all-to-all-start.1 = ((bf16[64,2,1024]{2,1,0:T(2,128)(2,1)}), bf16[64,2,1024]{2,1,0:T(2,128)(2,1)S(1)}, u32[]{:S(2)}, u32[]{:S(2)}) async-start(bf16[64,2,1024]{2,1,0:T(2,128)(2,1)} %reshape.22), calls=%async_computation.1 | async-start | bytes 524288 | tf_op jit(solution)/shard_map/pair_exchange/all_to_all | solution.py:235
  43.4 33.7 %collective-permute-start.11 = (s32[65]{0:T(128)S(1)}, s32[65]{0:T(128)S(1)}, u32[]{:S(2)}, u32[]{:S(2)}) collective-permute-start(s32[65]{0:T(128)S(1)} %pad_add_fusion.2), channel_id=1, source_target_pairs={{0,1},{1,0},{2,3},{3,2},{4,5},{5,4},{6,7},{7,6},{8,9},{9,8},{10,11... | collective-permute-start | bytes 788 | tf_op jit(solution)/shard_map/tile_matrix/ppermute | solution.py:227
  44.0 36.2 %collective-permute-start.7 = (bf16[512,512]{1,0:T(8,128)(2,1)S(1)}, bf16[512,512]{1,0:T(8,128)(2,1)S(1)}, u32[]{:S(2)}, u32[]{:S(2)}) collective-permute-start(bf16[512,512]{1,0:T(8,128)(2,1)S(1)} %bitcast.23), channel_id=1, source_target_pairs={{0,1},{1,0},{2,3},{3,2},{4,5},{5,4},{6,7},{7,6},{8,9},{9,8},{10,11... | collective-permute-start | bytes 1572872 | tf_op jit(solution)/shard_map/tile_matrix/ppermute | solution.py:227
  44.1 31.7 %collective-permute-start.6 = (bf16[512,512]{1,0:T(8,128)(2,1)S(1)}, bf16[512,512]{1,0:T(8,128)(2,1)S(1)}, u32[]{:S(2)}, u32[]{:S(2)}) collective-permute-start(bf16[512,512]{1,0:T(8,128)(2,1)S(1)} %bitcast.24), channel_id=1, source_target_pairs={{0,16},{16,32},{32,48},{48,0},{1,17},{17,33},{33,49},{49,1},{2,18}... | collective-permute-start | bytes 1572872 | tf_op jit(solution)/shard_map/pair_exchange/ppermute | solution.py:231
  45.5 30.3 %collective-permute-start.5 = (bf16[512,512]{1,0:T(8,128)(2,1)S(1)}, bf16[512,512]{1,0:T(8,128)(2,1)S(1)}, u32[]{:S(2)}, u32[]{:S(2)}) collective-permute-start(bf16[512,512]{1,0:T(8,128)(2,1)S(1)} %bitcast.25), channel_id=1, source_target_pairs={{0,32},{16,48},{32,0},{48,16},{1,33},{17,49},{33,1},{49,17},{2,34}... | collective-permute-start | bytes 1572872 | tf_op jit(solution)/shard_map/pair_exchange/ppermute | solution.py:231
  48.1 27.7 %collective-permute-start.4 = (bf16[512,512]{1,0:T(8,128)(2,1)S(1)}, bf16[512,512]{1,0:T(8,128)(2,1)}, u32[]{:S(2)}, u32[]{:S(2)}) collective-permute-start(bf16[512,512]{1,0:T(8,128)(2,1)S(1)} %bitcast.26), channel_id=1, source_target_pairs={{0,48},{16,0},{32,16},{48,32},{1,49},{17,1},{33,17},{49,33},{2,50}... | collective-permute-start | bytes 1572872 | tf_op jit(solution)/shard_map/pair_exchange/ppermute | solution.py:231
  54.7 22.2 %copy-start.3 = (bf16[32,128,128]{2,1,0:T(8,128)(2,1)S(1)}, bf16[32,128,128]{2,1,0:T(8,128)(2,1)}, u32[]{:S(2)}) copy-start(bf16[32,128,128]{2,1,0:T(8,128)(2,1)} %param.10) | copy-start | bytes 3145732
  75.8 4.5 %collective-permute-start.8 = (bf16[512,512]{1,0:T(8,128)(2,1)}, bf16[512,512]{1,0:T(8,128)(2,1)S(1)}, u32[]{:S(2)}, u32[]{:S(2)}) collective-permute-start(bf16[512,512]{1,0:T(8,128)(2,1)} %collective-permute-done.4.refs_1_), channel_id=1, source_target_pairs={{0,1},{1,0},{2,3},{3,2},{4,5},{5,4},{6,7},{7,6},{8,9},{9,8},{10,11... | collective-permute-start | bytes 1572872 | tf_op jit(solution)/shard_map/tile_matrix/ppermute | solution.py:227
  76.5 3.8 %collective-permute-start.9 = (bf16[512,512]{1,0:T(8,128)(2,1)S(1)}, bf16[512,512]{1,0:T(8,128)(2,1)S(1)}, u32[]{:S(2)}, u32[]{:S(2)}) collective-permute-start(bf16[512,512]{1,0:T(8,128)(2,1)S(1)} %collective-permute-done.5.refs_2_), channel_id=1, source_target_pairs={{0,1},{1,0},{2,3},{3,2},{4,5},{5,4},{6,7},{7,6},{8,9},{9,8},{10,11... | collective-permute-start | bytes 1572872 | tf_op jit(solution)/shard_map/tile_matrix/ppermute | solution.py:227
  76.6 3.7 %collective-permute-start.10 = (bf16[512,512]{1,0:T(8,128)(2,1)S(1)}, bf16[512,512]{1,0:T(8,128)(2,1)S(1)}, u32[]{:S(2)}, u32[]{:S(2)}) collective-permute-start(bf16[512,512]{1,0:T(8,128)(2,1)S(1)} %collective-permute-done.6.refs_3_), channel_id=1, source_target_pairs={{0,1},{1,0},{2,3},{3,2},{4,5},{5,4},{6,7},{7,6},{8,9},{9,8},{10,11... | collective-permute-start | bytes 1572872 | tf_op jit(solution)/shard_map/tile_matrix/ppermute | solution.py:227
  77.1 14.1 %collective-permute-start.19 = (bf16[32,64,128]{2,1,0:T(8,128)(2,1)S(1)}, bf16[32,64,128]{2,1,0:T(8,128)(2,1)S(1)}, u32[]{:S(2)}, u32[]{:S(2)}) collective-permute-start(bf16[32,64,128]{2,1,0:T(8,128)(2,1)S(1)} %get-tuple-element.58), channel_id=1, source_target_pairs={{0,1},{1,0},{2,3},{3,2},{4,5},{5,4},{6,7},{7,6},{8,9},{9,8},{10,11... | collective-permute-start | bytes 1572872 | tf_op jit(solution)/shard_map/tile_matrix/ppermute | solution.py:227
  82.2 7.2 %collective-permute-start.14 = (bf16[64,512]{1,0:T(8,128)(2,1)S(1)}, bf16[64,512]{1,0:T(8,128)(2,1)S(1)}, u32[]{:S(2)}, u32[]{:S(2)}) collective-permute-start(bf16[64,512]{1,0:T(8,128)(2,1)S(1)} %fusion.6), channel_id=1, source_target_pairs={{0,64},{64,128},{128,192},{192,0},{1,65},{65,129},{129,193},{193,1... | collective-permute-start | bytes 196616 | tf_op jit(solution)/shard_map/spread/ppermute | solution.py:231
  82.6 6.8 %collective-permute-start.13 = (bf16[64,512]{1,0:T(8,128)(2,1)S(1)}, bf16[64,512]{1,0:T(8,128)(2,1)S(1)}, u32[]{:S(2)}, u32[]{:S(2)}) collective-permute-start(bf16[64,512]{1,0:T(8,128)(2,1)S(1)} %fusion.6), channel_id=1, source_target_pairs={{0,128},{64,192},{128,0},{192,64},{1,129},{65,193},{129,1},{193,65... | collective-permute-start | bytes 196616 | tf_op jit(solution)/shard_map/spread/ppermute | solution.py:231
  85.9 3.5 %collective-permute-start.12 = (bf16[64,512]{1,0:T(8,128)(2,1)S(1)}, bf16[64,512]{1,0:T(8,128)(2,1)S(1)}, u32[]{:S(2)}, u32[]{:S(2)}) collective-permute-start(bf16[64,512]{1,0:T(8,128)(2,1)S(1)} %fusion.6), channel_id=1, source_target_pairs={{0,192},{64,0},{128,64},{192,128},{1,193},{65,1},{129,65},{193,129... | collective-permute-start | bytes 196616 | tf_op jit(solution)/shard_map/spread/ppermute | solution.py:231
  89.4 3.9 %collective-permute-start.15 = (bf16[256,512]{1,0:T(8,128)(2,1)S(1)}, bf16[256,512]{1,0:T(8,128)(2,1)S(1)}, u32[]{:S(2)}, u32[]{:S(2)}) collective-permute-start(bf16[256,512]{1,0:T(8,128)(2,1)S(1)} %constant_dynamic-update-slice_fusion.5.refs_0_), channel_id=1, source_target_pairs={{0,1},{1,0},{2,3},{3,2},{4,5},{5,4},{6,7},{7,6},{8,9},{9,8},{10,11... | collective-permute-start | bytes 786440 | tf_op jit(solution)/shard_map/spread/ppermute | solution.py:227
  93.3 5.2 %copy-start = (bf16[512,512]{1,0:T(8,128)(2,1)S(1)}, bf16[512,512]{1,0:T(8,128)(2,1)}, u32[]{:S(2)}) copy-start(bf16[512,512]{1,0:T(8,128)(2,1)} %weight_ref.1) | copy-start | bytes 1572868
  94.1 9.0 %collective-permute-start.16 = (f32[16,512]{1,0:T(8,128)S(1)}, f32[16,512]{1,0:T(8,128)S(1)}, u32[]{:S(2)}, u32[]{:S(2)}) collective-permute-start(f32[16,512]{1,0:T(8,128)S(1)} %get-tuple-element.45), channel_id=1, source_target_pairs={{0,16},{16,32},{32,48},{48,0},{1,17},{17,33},{33,49},{49,1},{2,18}... | collective-permute-start | bytes 98312 | tf_op jit(solution)/shard_map/spread/ppermute | solution.py:231
  95.1 8.0 %collective-permute-start.17 = (f32[16,512]{1,0:T(8,128)S(1)}, f32[16,512]{1,0:T(8,128)S(1)}, u32[]{:S(2)}, u32[]{:S(2)}) collective-permute-start(f32[16,512]{1,0:T(8,128)S(1)} %get-tuple-element.46), channel_id=1, source_target_pairs={{0,32},{16,48},{32,0},{48,16},{1,33},{17,49},{33,1},{49,17},{2,34}... | collective-permute-start | bytes 98312 | tf_op jit(solution)/shard_map/spread/ppermute | solution.py:231
  97.8 5.3 %collective-permute-start.18 = (f32[16,512]{1,0:T(8,128)S(1)}, f32[16,512]{1,0:T(8,128)S(1)}, u32[]{:S(2)}, u32[]{:S(2)}) collective-permute-start(f32[16,512]{1,0:T(8,128)S(1)} %get-tuple-element.47), channel_id=1, source_target_pairs={{0,48},{16,0},{32,16},{48,32},{1,49},{17,1},{33,17},{49,33},{2,50}... | collective-permute-start | bytes 98312 | tf_op jit(solution)/shard_map/spread/ppermute | solution.py:231
  103.1 31.5 %all-to-all-start.2 = ((bf16[4,512,512]{2,1,0:T(8,128)(2,1)}), bf16[4,512,512]{2,1,0:T(8,128)(2,1)S(1)}, u32[]{:S(2)}, u32[]{:S(2)}) async-start(bf16[4,512,512]{2,1,0:T(8,128)(2,1)} %spread.1), calls=%async_computation.2 | async-start | bytes 4194304 | tf_op jit(solution)/shard_map/sums/all_to_all | solution.py:235
  106.8 8.5 %collective-permute-start.26 = (f32[16,512]{1,0:T(8,128)S(1)}, f32[16,512]{1,0:T(8,128)S(1)}, u32[]{:S(2)}, u32[]{:S(2)}) collective-permute-start(f32[16,512]{1,0:T(8,128)S(1)} %add_add_fusion.refs_0_), channel_id=1, source_target_pairs={{0,2},{2,4},{4,6},{6,8},{8,10},{10,12},{12,14},{14,0},{1,3},{3,5},... | collective-permute-start | bytes 98312 | tf_op jit(solution)/shard_map/sums/ppermute | solution.py:231
  107.6 9.9 %collective-permute-start.25 = (f32[16,512]{1,0:T(8,128)S(1)}, f32[16,512]{1,0:T(8,128)S(1)}, u32[]{:S(2)}, u32[]{:S(2)}) collective-permute-start(f32[16,512]{1,0:T(8,128)S(1)} %add_add_fusion.refs_0_), channel_id=1, source_target_pairs={{0,4},{2,6},{4,8},{6,10},{8,12},{10,14},{12,0},{14,2},{1,5},{3,7},... | collective-permute-start | bytes 98312 | tf_op jit(solution)/shard_map/sums/ppermute | solution.py:231
  108.7 9.6 %collective-permute-start.24 = (f32[16,512]{1,0:T(8,128)S(1)}, f32[16,512]{1,0:T(8,128)S(1)}, u32[]{:S(2)}, u32[]{:S(2)}) collective-permute-start(f32[16,512]{1,0:T(8,128)S(1)} %add_add_fusion.refs_0_), channel_id=1, source_target_pairs={{0,6},{2,8},{4,10},{6,12},{8,14},{10,0},{12,2},{14,4},{1,7},{3,9},... | collective-permute-start | bytes 98312 | tf_op jit(solution)/shard_map/sums/ppermute | solution.py:231
  110.7 7.6 %collective-permute-start.23 = (f32[16,512]{1,0:T(8,128)S(1)}, f32[16,512]{1,0:T(8,128)S(1)}, u32[]{:S(2)}, u32[]{:S(2)}) collective-permute-start(f32[16,512]{1,0:T(8,128)S(1)} %add_add_fusion.refs_0_), channel_id=1, source_target_pairs={{0,8},{2,10},{4,12},{6,14},{8,0},{10,2},{12,4},{14,6},{1,9},{3,11}... | collective-permute-start | bytes 98312 | tf_op jit(solution)/shard_map/sums/ppermute | solution.py:231
  113.7 4.6 %collective-permute-start.22 = (f32[16,512]{1,0:T(8,128)S(1)}, f32[16,512]{1,0:T(8,128)S(1)}, u32[]{:S(2)}, u32[]{:S(2)}) collective-permute-start(f32[16,512]{1,0:T(8,128)S(1)} %add_add_fusion.refs_0_), channel_id=1, source_target_pairs={{0,10},{2,12},{4,14},{6,0},{8,2},{10,4},{12,6},{14,8},{1,11},{3,13... | collective-permute-start | bytes 98312 | tf_op jit(solution)/shard_map/sums/ppermute | solution.py:231
  115.3 4.4 %collective-permute-start.21 = (f32[16,512]{1,0:T(8,128)S(1)}, f32[16,512]{1,0:T(8,128)S(1)}, u32[]{:S(2)}, u32[]{:S(2)}) collective-permute-start(f32[16,512]{1,0:T(8,128)S(1)} %add_add_fusion.refs_0_), channel_id=1, source_target_pairs={{0,12},{2,14},{4,0},{6,2},{8,4},{10,6},{12,8},{14,10},{1,13},{3,15... | collective-permute-start | bytes 98312 | tf_op jit(solution)/shard_map/sums/ppermute | solution.py:231
  117.5 3.1 %collective-permute-start.20 = (f32[16,512]{1,0:T(8,128)S(1)}, f32[16,512]{1,0:T(8,128)S(1)}, u32[]{:S(2)}, u32[]{:S(2)}) collective-permute-start(f32[16,512]{1,0:T(8,128)S(1)} %add_add_fusion.refs_0_), channel_id=1, source_target_pairs={{0,14},{2,0},{4,2},{6,4},{8,6},{10,8},{12,10},{14,12},{1,15},{3,1}... | collective-permute-start | bytes 98312 | tf_op jit(solution)/shard_map/sums/ppermute | solution.py:231
  121.3 13.3 %collective-permute-start.29 = (f32[16,512]{1,0:T(8,128)S(1)}, f32[16,512]{1,0:T(8,128)S(1)}, u32[]{:S(2)}, u32[]{:S(2)}) collective-permute-start(f32[16,512]{1,0:T(8,128)S(1)} %share_sum.1), channel_id=1, source_target_pairs={{0,16},{16,32},{32,48},{48,0},{1,17},{17,33},{33,49},{49,1},{2,18}... | collective-permute-start | bytes 98312 | tf_op jit(solution)/shard_map/sums/ppermute | solution.py:231
  122.9 11.6 %collective-permute-start.28 = (f32[16,512]{1,0:T(8,128)S(1)}, f32[16,512]{1,0:T(8,128)S(1)}, u32[]{:S(2)}, u32[]{:S(2)}) collective-permute-start(f32[16,512]{1,0:T(8,128)S(1)} %share_sum.1), channel_id=1, source_target_pairs={{0,32},{16,48},{32,0},{48,16},{1,33},{17,49},{33,1},{49,17},{2,34}... | collective-permute-start | bytes 98312 | tf_op jit(solution)/shard_map/sums/ppermute | solution.py:231
  125.3 9.2 %collective-permute-start.27 = (f32[16,512]{1,0:T(8,128)S(1)}, f32[16,512]{1,0:T(8,128)S(1)}, u32[]{:S(2)}, u32[]{:S(2)}) collective-permute-start(f32[16,512]{1,0:T(8,128)S(1)} %share_sum.1), channel_id=1, source_target_pairs={{0,48},{16,0},{32,16},{48,32},{1,49},{17,1},{33,17},{49,33},{2,50}... | collective-permute-start | bytes 98312 | tf_op jit(solution)/shard_map/sums/ppermute | solution.py:231
  135.6 6.4 %collective-permute-start.30 = (f32[64,512]{1,0:T(8,128)S(1)}, f32[64,512]{1,0:T(8,128)S(1)}, u32[]{:S(2)}, u32[]{:S(2)}) collective-permute-start(f32[64,512]{1,0:T(8,128)S(1)} %pad_maximum_fusion.1), channel_id=1, source_target_pairs={{0,192},{64,0},{128,64},{192,128},{1,193},{65,1},{129,65},{193,129... | collective-permute-start | bytes 393224 | tf_op jit(solution)/shard_map/sums/ppermute | solution.py:231
  137.2 20.6 %all-to-all-start.3 = ((bf16[8,64,512]{2,1,0:T(8,128)(2,1)}), bf16[8,64,512]{2,1,0:T(8,128)(2,1)S(1)}, u32[]{:S(2)}, u32[]{:S(2)}) async-start(bf16[8,64,512]{2,1,0:T(8,128)(2,1)} %plane_sum.1), calls=%async_computation.3 | async-start | bytes 1048576 | tf_op jit(solution)/shard_map/sums/all_to_all | solution.py:235
  140.7 7.2 %collective-permute-start.32 = (f32[64,512]{1,0:T(8,128)S(1)}, f32[64,512]{1,0:T(8,128)S(1)}, u32[]{:S(2)}, u32[]{:S(2)}) collective-permute-start(f32[64,512]{1,0:T(8,128)S(1)} %pad_maximum_fusion.1), channel_id=1, source_target_pairs={{0,64},{64,128},{128,192},{192,0},{1,65},{65,129},{129,193},{193,1... | collective-permute-start | bytes 393224 | tf_op jit(solution)/shard_map/sums/ppermute | solution.py:231
  140.8 7.1 %collective-permute-start.31 = (f32[64,512]{1,0:T(8,128)S(1)}, f32[64,512]{1,0:T(8,128)S(1)}, u32[]{:S(2)}, u32[]{:S(2)}) collective-permute-start(f32[64,512]{1,0:T(8,128)S(1)} %pad_maximum_fusion.1), channel_id=1, source_target_pairs={{0,128},{64,192},{128,0},{192,64},{1,129},{65,193},{129,1},{193,65... | collective-permute-start | bytes 393224 | tf_op jit(solution)/shard_map/sums/ppermute | solution.py:231
  147.9 4.4 %collective-permute-start.33 = (f32[256,512]{1,0:T(8,128)S(1)}, f32[256,512]{1,0:T(8,128)S(1)}, u32[]{:S(2)}, u32[]{:S(2)}) collective-permute-start(f32[256,512]{1,0:T(8,128)S(1)} %constant_dynamic-update-slice_fusion.9.near_ref), channel_id=1, source_target_pairs={{0,1},{1,0},{2,3},{3,2},{4,5},{5,4},{6,7},{7,6},{8,9},{9,8},{10,11... | collective-permute-start | bytes 1572872 | tf_op jit(solution)/shard_map/sums/ppermute | solution.py:227

commit v5 on v4

--- a/solution.py
+++ b/solution.py
@@ -138,7 +138,8 @@
     out_ref[...] = total
 
 
-def tiles_kernel(meta_ref, own_ref, other_ref, high_ref, low_ref, acc):
+def tiles_kernel(meta_ref, own_ref, other_ref, high_ref, low_ref, token_ref, acc):
+    token_ref[...] = jnp.zeros_like(token_ref)
     slots = own_ref.shape[0]
     acc[...] = jnp.zeros_like(acc)
     for part, tiles_ref in enumerate((own_ref, other_ref)):
@@ -164,12 +165,12 @@
 
 
 def spread_kernel(coord_ref, _, weight_ref, high_ref, low_ref, *refs):
-    pre_refs, out_ref, pre = refs[:NC], refs[NC], refs[-1]
+    pre_refs, out_ref, pre = refs[: NC * NX], refs[-2], refs[-1]
     x = coord_ref[2]
     for k in range(NC * NX):
         dc, dx = k // NX, k % NX
         place = pl.multiple_of((dc * NX + ((x + dx) & (NX - 1))) * ROWS, ROWS)
-        pre[pl.ds(place, ROWS), :] = pre_refs[dc][dx * ROWS : (dx + 1) * ROWS, :]
+        pre[pl.ds(place, ROWS), :] = pre_refs[k][...]
     agg = lax.dot_general(pre[...], weight_ref[...], NT, preferred_element_type=F32).astype(BF)
     size = NZ * ROWS
     for k in range(NY):
@@ -179,18 +180,20 @@
         out_ref[k] = part.astype(BF)
 
 
-def terms_kernel(coord_ref, node_ref, *refs):
-    pre_refs, out_refs, token_ref, terms = refs[:NC], refs[NC:-2], refs[-2], refs[-1]
+def terms_kernel(coord_ref, _, *refs):
+    pieces = NC * NX
+    node_refs, pre_refs = refs[:pieces], refs[pieces : 2 * pieces]
+    out_refs, token_ref, terms = refs[2 * pieces : -2], refs[-2], refs[-1]
     token_ref[...] = jnp.zeros_like(token_ref)
-    y = coord_ref[0]
-    half = NX * ROWS
-    total = lax.dot_general(node_ref[:half, :], pre_refs[0][...], TN, preferred_element_type=F32)
-    total += lax.dot_general(node_ref[half:, :], pre_refs[1][...], TN, preferred_element_type=F32)
-    terms[...] = total
+    y, c, x = coord_ref[0], coord_ref[1], coord_ref[2]
+    columns = pl.ds(pl.multiple_of(x * NC * ROWS, NC * ROWS), NC * ROWS)
+    node = jnp.concatenate([ref[:, columns] for ref in node_refs], axis=0)
+    pre = jnp.concatenate([ref[...] for ref in pre_refs], axis=0)
+    terms[...] = lax.dot_general(node, pre, TN, preferred_element_type=F32)
     size = ROWS // NY
     for k in range(NY):
-        rows = pl.ds(pl.multiple_of(((y + k) & (NY - 1)) * size, size), size)
-        out_refs[k][...] = terms[rows, :]
+        start = c * ROWS + ((y + k) & (NY - 1)) * size
+        out_refs[k][...] = terms[pl.ds(pl.multiple_of(start, size), size), :]
 
 
 def plane_kernel(in_ref, out_ref):
@@ -287,7 +290,6 @@
         hidden_b = hidden.astype(BF)
 
     with jax.named_scope("pair_exchange"):
-        ring = gather(hidden_b, "z", NZ).reshape(NZ * ROWS, F)
         ends, token = pl.pallas_call(
             bucket_kernel,
             out_shape=[jax.ShapeDtypeStruct((NDEV, 4 * CAP), BF), TOKEN],
@@ -299,14 +301,11 @@
             name="bucket",
         )(pair_owner.T, pair_row.T)
         ends = ends.reshape(NDEV, 2, 2 * CAP)
-        ends, late_nodes = lax.optimization_barrier((ends, node_aggregate))
-        near_nodes = jnp.concatenate(
-            [late_nodes] + [shift(late_nodes, "x", NX, -k) for k in range(1, NX)], axis=0
-        )
-        nodes = jnp.concatenate([near_nodes, swap(near_nodes)], axis=0)
-        column = (lax.axis_index("x") * NC + c) * ROWS
-        nodes = lax.dynamic_slice_in_dim(nodes, column, ROWS, axis=1)
-        ring, ends, nodes = lax.optimization_barrier((ring, ends, nodes))
+        hidden_b, late_nodes = lax.optimization_barrier((hidden_b, node_aggregate))
+        ring = gather(hidden_b, "z", NZ).reshape(NZ * ROWS, F)
+        nodes = [late_nodes] + [shift(late_nodes, "x", NX, -k) for k in range(1, NX)]
+        nodes = nodes + [swap(node) for node in nodes]
+        ring, ends, *nodes = lax.optimization_barrier((ring, ends, *nodes))
         planes = [ring] + [shift(ring, "y", NY, -k) for k in range(1, NY)]
         received = exchange(ends, ("y", "z", "c")).reshape(NDEV, 4 * CAP)
         near, far, token = count(coord, received)
@@ -328,34 +327,35 @@
         pre_grad, metas = lax.optimization_barrier((pre_grad, metas))
 
     with jax.named_scope("spread"):
-        high, low = pl.pallas_call(
+        high, low, tile_token = pl.pallas_call(
             tiles_kernel,
-            out_shape=[jax.ShapeDtypeStruct((NY * NZ * ROWS, 512), BF)] * 2,
+            out_shape=[jax.ShapeDtypeStruct((NY * NZ * ROWS, 512), BF)] * 2 + [TOKEN],
             in_specs=[SMEM, VMEM, VMEM],
-            out_specs=[VMEM] * 2,
+            out_specs=[VMEM] * 3,
             scratch_shapes=[pltpu.VMEM((NY * NZ * ROWS, 512), F32)],
             compiler_params=params(),
             cost_estimate=pl.CostEstimate(flops=3_000_000_000, bytes_accessed=5_000_000, transcendentals=0),
             name="tile_sum",
         )(metas, own_half, other_half)
-        along_x = [pre_grad] + [shift(pre_grad, "x", NX, -k) for k in range(1, NX)]
-        near_pre = jnp.concatenate(along_x, axis=0)
-        pre_parts = [near_pre, swap(near_pre)]
+        along_x = [shift(pre_grad, "x", NX, -k) for k in range(1, NX)]
+        *along_x, tile_token = lax.optimization_barrier((*along_x, tile_token))
+        pre_parts = [pre_grad] + along_x
+        pre_parts = pre_parts + [swap(part) for part in pre_parts]
         *terms, token = pl.pallas_call(
             terms_kernel,
             out_shape=[jax.ShapeDtypeStruct((ROWS // NY, F), F32)] * NY + [TOKEN],
-            in_specs=[SMEM] + [VMEM] * 3,
+            in_specs=[SMEM, ANY] + [VMEM] * (2 * NC * NX),
             out_specs=[VMEM] * (NY + 1),
-            scratch_shapes=[pltpu.VMEM((ROWS, F), F32)],
+            scratch_shapes=[pltpu.VMEM((NC * ROWS, F), F32)],
             compiler_params=params(),
             cost_estimate=pl.CostEstimate(flops=1_000_000_000, bytes_accessed=700_000, transcendentals=0),
             name="weight_terms",
-        )(coord, nodes, *pre_parts)
+        )(coord, tile_token, *nodes, *pre_parts)
         others = [shift(terms[k], "y", NY, k) for k in range(1, NY)]
         send = pl.pallas_call(
             spread_kernel,
             out_shape=jax.ShapeDtypeStruct((NY, NZ * ROWS, F), BF),
-            in_specs=[SMEM, ANY] + [VMEM] * 5,
+            in_specs=[SMEM, ANY] + [VMEM] * (3 + NC * NX),
             out_specs=VMEM,
             scratch_shapes=[pltpu.VMEM((NC * NX * ROWS, F), BF)],
             compiler_params=params(),

time: 159 us -> 169 us (1.063); the launches traced: 159 us -> 166 us
  starting transfers between devices: 73 us -> 84.6 us
  waiting for transfers between devices: 34.6 us -> 31.1 us
    ppermute x25, starting transfers between devices: 37.6 us -> 47.7 us  [shift(): lax.ppermute(values, axis, [(i, (i + step) % size) for i in range(size)])]
    ppermute x25, waiting for transfers between devices: 22.5 us -> 19.2 us  [shift(): lax.ppermute(values, axis, [(i, (i + step) % size) for i in range(size)])]
    ppermute x9 -> x15, starting transfers between devices: 8.54 us -> 10.3 us  [swap(): return lax.ppermute(values, 'c', [(0, 1), (1, 0)])]
  transfers between devices with their start and end apart: 38 -> 44, of which waited for: 11 -> 14; matrix products, arithmetic and copies ran while one was open for 1% -> 1% of each run, Pallas kernels for 27% -> 25%
where the time goes in v5:
time: 169 us; the launch traced here: 166 us
  starting transfers between devices  84.6 us (50%)
  Pallas kernels  43.7 us (26%)
  waiting for transfers between devices  31.1 us (18%)
  matrix products  1.97 us (1%)
  local copies, waits for them, and re-layouts  1.92 us (1%)
  between operations  1.81 us (1%)
    ppermute x25, starting transfers between devices, shift(): lax.ppermute(values, axis, [(i, (i + step) % size) for i in range(size)])  47.7 us
    all_to_all x4, starting transfers between devices, exchange(): return lax.all_to_all(values, axes, 0, 0, tiled=True)  26.6 us
    pallas_call x1, Pallas kernels, count(): pl.pallas_call(count_kernel, out_shape=[half, half, TOKEN], in_specs=[SME...  21 us
    ppermute x25, waiting for transfers between devices, shift(): lax.ppermute(values, axis, [(i, (i + step) % size) for i in range(size)])  19.2 us
    ppermute x15, starting transfers between devices, swap(): return lax.ppermute(values, 'c', [(0, 1), (1, 0)])  10.3 us
    all_to_all x4, waiting for transfers between devices, exchange(): return lax.all_to_all(values, axes, 0, 0, tiled=True)  9.22 us
    pallas_call x1, Pallas kernels, per_device(): pl.pallas_call(bucket_kernel, out_shape=[jax.ShapeDtypeStruct((NDEV, 4 *...  8.24 us
    pallas_call x1, Pallas kernels, per_device(): pl.pallas_call(spread_kernel, out_shape=jax.ShapeDtypeStruct((NY, NZ * RO...  4.62 us
  transfers between devices with their start and end apart: 44, of which 14 were waited for; matrix products, arithmetic and copies ran while one was open for 1% of the time, Pallas kernels for 25%

profile of v5, /device:TPU:1, one launch (start us, length us, event | category | flops | bytes accessed | tf_op | source)
XLA Modules:
  0.0 166.1 jit_solution(11113524561860553170)
XLA Ops:
  0.7 2.0 %multiply_convert_fusion = (bf16[64,512]{1,0:T(8,128)(2,1)S(1)}, f32[64,512]{1,0:T(8,128)}) fusion(bf16[64,512]{1,0:T(8,128)(2,1)} %refs_0_, bf16[512,512]{1,0:T(8,128)(2,1)} %weight_ref.1), kind=kOutput, calls=%fused_computation.12 | convolution fusion | flops 33849344 | bytes 786432 | tf_op jit(solution)/shard_map/hidden/dot_general | solution.py:288
  2.6 0.8 broadcast_in_dim.2
  3.5 9.0 %all-to-all-start = ((bf16[8,64,512]{2,1,0:T(8,128)(2,1)}), bf16[8,64,512]{2,1,0:T(8,128)(2,1)S(1)}, u32[]{:S(2)}, u32[]{:S(2)}) async-start(bf16[8,64,512]{2,1,0:T(8,128)(2,1)} %broadcast_in_dim.2), calls=%async_computation | async-start | bytes 1048576 | tf_op jit(solution)/shard_map/pair_exchange/all_to_all | solution.py:238
  12.5 1.3 collective-permute-start.2
  13.8 2.4 %collective-permute-start.1 = (bf16[64,512]{1,0:T(8,128)(2,1)S(1)}, bf16[64,512]{1,0:T(8,128)(2,1)S(1)}, u32[]{:S(2)}, u32[]{:S(2)}) collective-permute-start(bf16[64,512]{1,0:T(8,128)(2,1)S(1)} %copy-done.1), channel_id=1, source_target_pairs={{0,128},{64,192},{128,0},{192,64},{1,129},{65,193},{129,1},{193,65... | collective-permute-start | bytes 196616 | tf_op jit(solution)/shard_map/pair_exchange/ppermute | solution.py:234
  16.2 1.2 collective-permute-start
  17.4 1.8 %collective-permute-start.3 = (bf16[64,512]{1,0:T(8,128)(2,1)S(1)}, bf16[64,512]{1,0:T(8,128)(2,1)S(1)}, u32[]{:S(2)}, u32[]{:S(2)}) collective-permute-start(bf16[64,512]{1,0:T(8,128)(2,1)S(1)} %copy-done.1), channel_id=1, source_target_pairs={{0,1},{1,0},{2,3},{3,2},{4,5},{5,4},{6,7},{7,6},{8,9},{9,8},{10,11... | collective-permute-start | bytes 196616 | tf_op jit(solution)/shard_map/pair_exchange/ppermute | solution.py:230
  19.2 0.5 collective-permute-start.6
  19.7 1.1 collective-permute-start.5
  20.8 1.2 collective-permute-start.4
  22.0 8.2 %bucket.1 = (bf16[64,2048]{1,0:T(8,128)(2,1)S(1)}, f32[8,128]{1,0:T(8,128)}) custom-call(s32[2,8192]{1,0:T(2,128)S(1)} %bitcast.29, s32[2,8192]{1,0:T(2,128)S(1)} %bitcast.30), custom_call_target="tpu_custom_call" | custom-call | flops 8999999488 | bytes 400000 | tf_op jit(solution)/shard_map/pair_exchange/bucket/pallas_call | solution.py:293
  30.3 0.9 reshape.22
  31.2 10.4 %all-to-all-start.1 = ((bf16[64,2,1024]{2,1,0:T(2,128)(2,1)}), bf16[64,2,1024]{2,1,0:T(2,128)(2,1)S(1)}, u32[]{:S(2)}, u32[]{:S(2)}) async-start(bf16[64,2,1024]{2,1,0:T(2,128)(2,1)} %reshape.22), calls=%async_computation.1 | async-start | bytes 524288 | tf_op jit(solution)/shard_map/pair_exchange/all_to_all | solution.py:238
  42.4 0.5 collective-permute-start.14
  43.0 1.4 collective-permute-start.9
  44.4 2.6 %collective-permute-start.8 = (bf16[512,512]{1,0:T(8,128)(2,1)S(1)}, bf16[512,512]{1,0:T(8,128)(2,1)S(1)}, u32[]{:S(2)}, u32[]{:S(2)}) collective-permute-start(bf16[512,512]{1,0:T(8,128)(2,1)S(1)} %bitcast.25), channel_id=1, source_target_pairs={{0,32},{16,48},{32,0},{48,16},{1,33},{17,49},{33,1},{49,17},{2,34}... | collective-permute-start | bytes 1572872 | tf_op jit(solution)/shard_map/pair_exchange/ppermute | solution.py:234
  47.0 1.3 collective-permute-start.7
  48.3 5.3 %all-to-all-done.1 = bf16[64,2,1024]{2,1,0:T(2,128)(2,1)S(1)} async-done(((bf16[64,2,1024]{2,1,0:T(2,128)(2,1)}), bf16[64,2,1024]{2,1,0:T(2,128)(2,1)S(1)}, u32[]{:S(2)}, u32[]{:S(2)}) %all-to-all-start.1) | async-done | bytes 262176 | tf_op jit(solution)/shard_map/pair_exchange/all_to_all | solution.py:238
  53.7 21.0 %count.1 = (f32[2,256,512]{2,1,0:T(8,128)S(1)}, f32[2,256,512]{2,1,0:T(8,128)S(1)}, f32[8,128]{1,0:T(8,128)S(1)}) custom-call(s32[4]{0:T(128)S(1)} %pad_add_fusion.1.coord_ref, bf16[64,2048]{1,0:T(8,128)(2,1)S(1)} %bitcast.28), custom_call_target="tpu_custom_call" | custom-call | flops 24000000000 | bytes 2400000 | tf_op jit(solution)/shard_map/pair_exchange/count/pallas_call | solution.py:251
  74.7 0.5 collective-permute-start.11
  75.3 0.4 collective-permute-start.13
  76.1 1.9 %pair_grad.2.refs_4_ = f32[64,512]{1,0:T(8,128)S(1)} custom-call(f32[8,128]{1,0:T(8,128)S(1)} %get-tuple-element.48._, bf16[64,512]{1,0:T(8,128)(2,1)S(1)} %get-tuple-element.42.own_ref, f32[2,256,512]{2,1,0:T(8,128)S(1)} %get-tuple-element.53.count_ref, bf16[512,512]{1,0:T(8,128)(2,1)S(1)} %bitcast.27, bf16[512,512]{1,0:T(8,128)(2,1)S(1)} %collective-permute-done.7.refs_1_, ...), custom_call_target="tpu_custom_call" | custom-call | flops 3000000000 | bytes 3000000 | tf_op jit(solution)/shard_map/hidden_grad/pair_grad/pallas_call | solution.py:268
  78.3 1.9 %pair_grad.3 = f32[64,512]{1,0:T(8,128)S(1)} custom-call(f32[8,128]{1,0:T(8,128)S(1)} %get-tuple-element.48._, bf16[64,512]{1,0:T(8,128)(2,1)S(1)} %get-tuple-element.42.own_ref, f32[2,256,512]{2,1,0:T(8,128)S(1)} %get-tuple-element.49.count_ref, bf16[512,512]{1,0:T(8,128)(2,1)S(1)} %collective-permute-done.10.refs_0_, ...), custom_call_target="tpu_custom_call" | custom-call | flops 3000000000 | bytes 3000000 | tf_op jit(solution)/shard_map/hidden_grad/pair_grad/pallas_call | solution.py:268
  80.3 0.5 collective-permute-start.19
  80.7 0.5 collective-permute-start.17
  81.2 3.1 %collective-permute-start.16 = (bf16[64,512]{1,0:T(8,128)(2,1)S(1)}, bf16[64,512]{1,0:T(8,128)(2,1)S(1)}, u32[]{:S(2)}, u32[]{:S(2)}) collective-permute-start(bf16[64,512]{1,0:T(8,128)(2,1)S(1)} %fusion.6.refs_8_.refs_0_), channel_id=1, source_target_pairs={{0,128},{64,192},{128,0},{192,64},{1,129},{65,193},{129,1},{193,65... | collective-permute-start | bytes 196616 | tf_op jit(solution)/shard_map/spread/ppermute | solution.py:234
  84.4 2.1 %tile_sum.1 = (bf16[2048,512]{1,0:T(8,128)(2,1)S(1)}, bf16[2048,512]{1,0:T(8,128)(2,1)S(1)}, f32[8,128]{1,0:T(8,128)S(1)}) custom-call(s32[2,65]{1,0:T(2,128)S(1)} %pad_add_fusion.meta_ref, bf16[32,64,128]{2,1,0:T(8,128)(2,1)S(1)} %get-tuple-element.83.own_ref, bf16[32,64,128]{2,1,0:T(8,128)(2,1)S(1)} %collective-permute-done.18.other_ref), custom_call_target="tpu_custom_call" | custom-call | flops 3000000000 | bytes 5000000 | tf_op jit(solution)/shard_map/spread/tile_sum/pallas_call | solution.py:330
  86.5 1.3 collective-permute-done.16.refs_10_.refs_2_
  87.8 1.5 collective-permute-start.20
  89.3 0.5 collective-permute-start.22
  89.8 0.4 collective-permute-done.20.refs_13_.refs_5_
  90.2 0.4 collective-permute-done.21.refs_14_.refs_6_
  90.7 0.8 weight_terms.1
  91.5 10.6 %collective-permute-start.23 = (f32[16,512]{1,0:T(8,128)S(1)}, f32[16,512]{1,0:T(8,128)S(1)}, u32[]{:S(2)}, u32[]{:S(2)}) collective-permute-start(f32[16,512]{1,0:T(8,128)S(1)} %get-tuple-element.70), channel_id=1, source_target_pairs={{0,16},{16,32},{32,48},{48,0},{1,17},{17,33},{33,49},{49,1},{2,18}... | collective-permute-start | bytes 98312 | tf_op jit(solution)/shard_map/spread/ppermute | solution.py:234
  102.1 2.6 %collective-permute-start.24 = (f32[16,512]{1,0:T(8,128)S(1)}, f32[16,512]{1,0:T(8,128)S(1)}, u32[]{:S(2)}, u32[]{:S(2)}) collective-permute-start(f32[16,512]{1,0:T(8,128)S(1)} %get-tuple-element.71), channel_id=1, source_target_pairs={{0,32},{16,48},{32,0},{48,16},{1,33},{17,49},{33,1},{49,17},{2,34}... | collective-permute-start | bytes 98312 | tf_op jit(solution)/shard_map/spread/ppermute | solution.py:234
  104.7 1.1 collective-permute-start.25
  105.8 4.6 %spread.1 = bf16[4,512,512]{2,1,0:T(8,128)(2,1)} custom-call(s32[4]{0:T(128)S(1)} %pad_add_fusion.1.coord_ref, f32[8,128]{1,0:T(8,128)S(1)} %get-tuple-element.73._, bf16[512,512]{1,0:T(8,128)(2,1)S(1)} %copy-done, bf16[2048,512]{1,0:T(8,128)(2,1)S(1)} %get-tuple-element.74.high_ref, bf16[2048,512]{1,0:T(8,128)(2,1)S(1)} %get-tuple-element.75.low_ref, ...), custom_call_target="tpu_custom_call" | custom-call | flops 5000000000 | bytes 8000000 | tf_op jit(solution)/shard_map/spread/spread/pallas_call | solution.py:355
  110.5 3.6 %all-to-all-start.2 = ((bf16[4,512,512]{2,1,0:T(8,128)(2,1)}), bf16[4,512,512]{2,1,0:T(8,128)(2,1)S(1)}, u32[]{:S(2)}, u32[]{:S(2)}) async-start(bf16[4,512,512]{2,1,0:T(8,128)(2,1)} %spread.1), calls=%async_computation.2 | async-start | bytes 4194304 | tf_op jit(solution)/shard_map/sums/all_to_all | solution.py:238
  114.1 0.8 collective-permute-start.32
  114.9 0.9 collective-permute-start.31
  115.8 1.9 %collective-permute-start.30 = (f32[16,512]{1,0:T(8,128)S(1)}, f32[16,512]{1,0:T(8,128)S(1)}, u32[]{:S(2)}, u32[]{:S(2)}) collective-permute-start(f32[16,512]{1,0:T(8,128)S(1)} %add_add_fusion.refs_0_), channel_id=1, source_target_pairs={{0,6},{2,8},{4,10},{6,12},{8,14},{10,0},{12,2},{14,4},{1,7},{3,9},... | collective-permute-start | bytes 98312 | tf_op jit(solution)/shard_map/sums/ppermute | solution.py:234
  117.7 3.4 %collective-permute-start.29 = (f32[16,512]{1,0:T(8,128)S(1)}, f32[16,512]{1,0:T(8,128)S(1)}, u32[]{:S(2)}, u32[]{:S(2)}) collective-permute-start(f32[16,512]{1,0:T(8,128)S(1)} %add_add_fusion.refs_0_), channel_id=1, source_target_pairs={{0,8},{2,10},{4,12},{6,14},{8,0},{10,2},{12,4},{14,6},{1,9},{3,11}... | collective-permute-start | bytes 98312 | tf_op jit(solution)/shard_map/sums/ppermute | solution.py:234
  121.1 1.3 collective-permute-start.28
  122.3 2.1 %collective-permute-start.27 = (f32[16,512]{1,0:T(8,128)S(1)}, f32[16,512]{1,0:T(8,128)S(1)}, u32[]{:S(2)}, u32[]{:S(2)}) collective-permute-start(f32[16,512]{1,0:T(8,128)S(1)} %add_add_fusion.refs_0_), channel_id=1, source_target_pairs={{0,12},{2,14},{4,0},{6,2},{8,4},{10,6},{12,8},{14,10},{1,13},{3,15... | collective-permute-start | bytes 98312 | tf_op jit(solution)/shard_map/sums/ppermute | solution.py:234
  124.5 0.9 collective-permute-start.26
  125.4 0.3 collective-permute-done.28.refs_3_
  125.7 1.4 collective-permute-done.27.refs_2_
  127.1 0.9 collective-permute-done.26.refs_1_
  128.0 0.6 share_sum.1
  128.6 1.7 %collective-permute-start.35 = (f32[16,512]{1,0:T(8,128)S(1)}, f32[16,512]{1,0:T(8,128)S(1)}, u32[]{:S(2)}, u32[]{:S(2)}) collective-permute-start(f32[16,512]{1,0:T(8,128)S(1)} %share_sum.1), channel_id=1, source_target_pairs={{0,16},{16,32},{32,48},{48,0},{1,17},{17,33},{33,49},{49,1},{2,18}... | collective-permute-start | bytes 98312 | tf_op jit(solution)/shard_map/sums/ppermute | solution.py:234
  130.3 2.4 %collective-permute-start.34 = (f32[16,512]{1,0:T(8,128)S(1)}, f32[16,512]{1,0:T(8,128)S(1)}, u32[]{:S(2)}, u32[]{:S(2)}) collective-permute-start(f32[16,512]{1,0:T(8,128)S(1)} %share_sum.1), channel_id=1, source_target_pairs={{0,32},{16,48},{32,0},{48,16},{1,33},{17,49},{33,1},{49,17},{2,34}... | collective-permute-start | bytes 98312 | tf_op jit(solution)/shard_map/sums/ppermute | solution.py:234
  132.7 1.2 collective-permute-start.33
  133.9 8.0 %collective-permute-done.35 = f32[16,512]{1,0:T(8,128)S(1)} collective-permute-done((f32[16,512]{1,0:T(8,128)S(1)}, f32[16,512]{1,0:T(8,128)S(1)}, u32[]{:S(2)}, u32[]{:S(2)}) %collective-permute-start.35) | collective-permute-done | bytes 32800 | tf_op jit(solution)/shard_map/sums/ppermute | solution.py:234
  141.9 1.1 plane_sum.1
  143.0 1.6 collective-permute-start.36
  144.6 3.5 %all-to-all-start.3 = ((bf16[8,64,512]{2,1,0:T(8,128)(2,1)}), bf16[8,64,512]{2,1,0:T(8,128)(2,1)S(1)}, u32[]{:S(2)}, u32[]{:S(2)}) async-start(bf16[8,64,512]{2,1,0:T(8,128)(2,1)} %plane_sum.1), calls=%async_computation.3 | async-start | bytes 1048576 | tf_op jit(solution)/shard_map/sums/all_to_all | solution.py:238
  148.2 1.2 collective-permute-start.37
  149.4 5.8 %collective-permute-done.37 = f32[64,512]{1,0:T(8,128)S(1)} collective-permute-done((f32[64,512]{1,0:T(8,128)S(1)}, f32[64,512]{1,0:T(8,128)S(1)}, u32[]{:S(2)}, u32[]{:S(2)}) %collective-permute-start.37) | collective-permute-done | bytes 131104 | tf_op jit(solution)/shard_map/sums/ppermute | solution.py:234
  155.2 1.5 collective-permute-done.38
  156.7 1.5 collective-permute-start.39
  158.2 1.5 collective-permute-done.39.far_ref
  159.7 1.6 place.1
  161.3 3.9 %all-to-all-done.3 = bf16[8,64,512]{2,1,0:T(8,128)(2,1)S(1)} async-done(((bf16[8,64,512]{2,1,0:T(8,128)(2,1)}), bf16[8,64,512]{2,1,0:T(8,128)(2,1)S(1)}, u32[]{:S(2)}, u32[]{:S(2)}) %all-to-all-start.3) | async-done | bytes 524320 | tf_op jit(solution)/shard_map/sums/all_to_all | solution.py:238
  165.2 0.7 reduce_sum.12
  (67 shorter events, 1.7 us)
Async XLA Ops:
  0.6 11.9 %copy-start.1 = (bf16[64,512]{1,0:T(8,128)(2,1)S(1)}, bf16[64,512]{1,0:T(8,128)(2,1)}, u32[]{:S(2)}) copy-start(bf16[64,512]{1,0:T(8,128)(2,1)} %refs_0_) | copy-start | bytes 196612
  0.6 21.4 %copy-start.3 = (s32[8192,2]{0,1:T(2,128)S(1)}, s32[8192,2]{0,1:T(2,128)}, u32[]{:S(2)}) copy-start(s32[8192,2]{0,1:T(2,128)} %param.15) | copy-start | bytes 196612
  0.6 21.4 %copy-start.2 = (s32[8192,2]{0,1:T(2,128)S(1)}, s32[8192,2]{0,1:T(2,128)}, u32[]{:S(2)}) copy-start(s32[8192,2]{0,1:T(2,128)} %param.14) | copy-start | bytes 196612
  3.5 27.7 %all-to-all-start = ((bf16[8,64,512]{2,1,0:T(8,128)(2,1)}), bf16[8,64,512]{2,1,0:T(8,128)(2,1)S(1)}, u32[]{:S(2)}, u32[]{:S(2)}) async-start(bf16[8,64,512]{2,1,0:T(8,128)(2,1)} %broadcast_in_dim.2), calls=%async_computation | async-start | bytes 1048576 | tf_op jit(solution)/shard_map/pair_exchange/all_to_all | solution.py:238
  12.5 6.7 %collective-permute-start.2 = (bf16[64,512]{1,0:T(8,128)(2,1)S(1)}, bf16[64,512]{1,0:T(8,128)(2,1)S(1)}, u32[]{:S(2)}, u32[]{:S(2)}) collective-permute-start(bf16[64,512]{1,0:T(8,128)(2,1)S(1)} %copy-done.1), channel_id=1, source_target_pairs={{0,64},{64,128},{128,192},{192,0},{1,65},{65,129},{129,193},{193,1... | collective-permute-start | bytes 196616 | tf_op jit(solution)/shard_map/pair_exchange/ppermute | solution.py:234
  13.8 5.9 %collective-permute-start.1 = (bf16[64,512]{1,0:T(8,128)(2,1)S(1)}, bf16[64,512]{1,0:T(8,128)(2,1)S(1)}, u32[]{:S(2)}, u32[]{:S(2)}) collective-permute-start(bf16[64,512]{1,0:T(8,128)(2,1)S(1)} %copy-done.1), channel_id=1, source_target_pairs={{0,128},{64,192},{128,0},{192,64},{1,129},{65,193},{129,1},{193,65... | collective-permute-start | bytes 196616 | tf_op jit(solution)/shard_map/pair_exchange/ppermute | solution.py:234
  16.2 4.6 %collective-permute-start = (bf16[64,512]{1,0:T(8,128)(2,1)S(1)}, bf16[64,512]{1,0:T(8,128)(2,1)S(1)}, u32[]{:S(2)}, u32[]{:S(2)}) collective-permute-start(bf16[64,512]{1,0:T(8,128)(2,1)S(1)} %copy-done.1), channel_id=1, source_target_pairs={{0,192},{64,0},{128,64},{192,128},{1,193},{65,1},{129,65},{193,129... | collective-permute-start | bytes 196616 | tf_op jit(solution)/shard_map/pair_exchange/ppermute | solution.py:234
  17.4 13.8 %collective-permute-start.3 = (bf16[64,512]{1,0:T(8,128)(2,1)S(1)}, bf16[64,512]{1,0:T(8,128)(2,1)S(1)}, u32[]{:S(2)}, u32[]{:S(2)}) collective-permute-start(bf16[64,512]{1,0:T(8,128)(2,1)S(1)} %copy-done.1), channel_id=1, source_target_pairs={{0,1},{1,0},{2,3},{3,2},{4,5},{5,4},{6,7},{7,6},{8,9},{9,8},{10,11... | collective-permute-start | bytes 196616 | tf_op jit(solution)/shard_map/pair_exchange/ppermute | solution.py:230
  19.2 12.0 %collective-permute-start.6 = (bf16[64,512]{1,0:T(8,128)(2,1)S(1)}, bf16[64,512]{1,0:T(8,128)(2,1)S(1)}, u32[]{:S(2)}, u32[]{:S(2)}) collective-permute-start(bf16[64,512]{1,0:T(8,128)(2,1)S(1)} %collective-permute-done.2.refs_3_), channel_id=1, source_target_pairs={{0,1},{1,0},{2,3},{3,2},{4,5},{5,4},{6,7},{7,6},{8,9},{9,8},{10,11... | collective-permute-start | bytes 196616 | tf_op jit(solution)/shard_map/pair_exchange/ppermute | solution.py:230
  19.7 11.5 %collective-permute-start.5 = (bf16[64,512]{1,0:T(8,128)(2,1)S(1)}, bf16[64,512]{1,0:T(8,128)(2,1)S(1)}, u32[]{:S(2)}, u32[]{:S(2)}) collective-permute-start(bf16[64,512]{1,0:T(8,128)(2,1)S(1)} %collective-permute-done.1.refs_2_), channel_id=1, source_target_pairs={{0,1},{1,0},{2,3},{3,2},{4,5},{5,4},{6,7},{7,6},{8,9},{9,8},{10,11... | collective-permute-start | bytes 196616 | tf_op jit(solution)/shard_map/pair_exchange/ppermute | solution.py:230
  20.8 10.4 %collective-permute-start.4 = (bf16[64,512]{1,0:T(8,128)(2,1)S(1)}, bf16[64,512]{1,0:T(8,128)(2,1)S(1)}, u32[]{:S(2)}, u32[]{:S(2)}) collective-permute-start(bf16[64,512]{1,0:T(8,128)(2,1)S(1)} %collective-permute-done.refs_1_), channel_id=1, source_target_pairs={{0,1},{1,0},{2,3},{3,2},{4,5},{5,4},{6,7},{7,6},{8,9},{9,8},{10,11... | collective-permute-start | bytes 196616 | tf_op jit(solution)/shard_map/pair_exchange/ppermute | solution.py:230
  22.0 20.3 %copy-start.6 = (s32[32]{0:T(128)S(1)}, s32[32]{0:T(128)}, u32[]{:S(2)}) copy-start(s32[32]{0:T(128)} %param.12) | copy-start | bytes 388
  22.0 20.3 %copy-start.7 = (s32[32]{0:T(128)S(1)}, s32[32]{0:T(128)}, u32[]{:S(2)}) copy-start(s32[32]{0:T(128)} %param.11) | copy-start | bytes 388
  31.2 22.4 %all-to-all-start.1 = ((bf16[64,2,1024]{2,1,0:T(2,128)(2,1)}), bf16[64,2,1024]{2,1,0:T(2,128)(2,1)S(1)}, u32[]{:S(2)}, u32[]{:S(2)}) async-start(bf16[64,2,1024]{2,1,0:T(2,128)(2,1)} %reshape.22), calls=%async_computation.1 | async-start | bytes 524288 | tf_op jit(solution)/shard_map/pair_exchange/all_to_all | solution.py:238
  42.4 33.5 %collective-permute-start.14 = (s32[65]{0:T(128)S(1)}, s32[65]{0:T(128)S(1)}, u32[]{:S(2)}, u32[]{:S(2)}) collective-permute-start(s32[65]{0:T(128)S(1)} %pad_add_fusion.2), channel_id=1, source_target_pairs={{0,1},{1,0},{2,3},{3,2},{4,5},{5,4},{6,7},{7,6},{8,9},{9,8},{10,11... | collective-permute-start | bytes 788 | tf_op jit(solution)/shard_map/tile_matrix/ppermute | solution.py:230
  42.9 35.0 %collective-permute-start.10 = (bf16[512,512]{1,0:T(8,128)(2,1)S(1)}, bf16[512,512]{1,0:T(8,128)(2,1)S(1)}, u32[]{:S(2)}, u32[]{:S(2)}) collective-permute-start(bf16[512,512]{1,0:T(8,128)(2,1)S(1)} %bitcast.23), channel_id=1, source_target_pairs={{0,1},{1,0},{2,3},{3,2},{4,5},{5,4},{6,7},{7,6},{8,9},{9,8},{10,11... | collective-permute-start | bytes 1572872 | tf_op jit(solution)/shard_map/tile_matrix/ppermute | solution.py:230
  43.0 31.7 %collective-permute-start.9 = (bf16[512,512]{1,0:T(8,128)(2,1)S(1)}, bf16[512,512]{1,0:T(8,128)(2,1)S(1)}, u32[]{:S(2)}, u32[]{:S(2)}) collective-permute-start(bf16[512,512]{1,0:T(8,128)(2,1)S(1)} %bitcast.24), channel_id=1, source_target_pairs={{0,16},{16,32},{32,48},{48,0},{1,17},{17,33},{33,49},{49,1},{2,18}... | collective-permute-start | bytes 1572872 | tf_op jit(solution)/shard_map/pair_exchange/ppermute | solution.py:234
  44.4 30.3 %collective-permute-start.8 = (bf16[512,512]{1,0:T(8,128)(2,1)S(1)}, bf16[512,512]{1,0:T(8,128)(2,1)S(1)}, u32[]{:S(2)}, u32[]{:S(2)}) collective-permute-start(bf16[512,512]{1,0:T(8,128)(2,1)S(1)} %bitcast.25), channel_id=1, source_target_pairs={{0,32},{16,48},{32,0},{48,16},{1,33},{17,49},{33,1},{49,17},{2,34}... | collective-permute-start | bytes 1572872 | tf_op jit(solution)/shard_map/pair_exchange/ppermute | solution.py:234
  47.0 27.7 %collective-permute-start.7 = (bf16[512,512]{1,0:T(8,128)(2,1)S(1)}, bf16[512,512]{1,0:T(8,128)(2,1)S(1)}, u32[]{:S(2)}, u32[]{:S(2)}) collective-permute-start(bf16[512,512]{1,0:T(8,128)(2,1)S(1)} %bitcast.26), channel_id=1, source_target_pairs={{0,48},{16,0},{32,16},{48,32},{1,49},{17,1},{33,17},{49,33},{2,50}... | collective-permute-start | bytes 1572872 | tf_op jit(solution)/shard_map/pair_exchange/ppermute | solution.py:234
  53.7 22.1 %copy-start.4 = (bf16[32,128,128]{2,1,0:T(8,128)(2,1)S(1)}, bf16[32,128,128]{2,1,0:T(8,128)(2,1)}, u32[]{:S(2)}) copy-start(bf16[32,128,128]{2,1,0:T(8,128)(2,1)} %param.10) | copy-start | bytes 3145732
  74.7 3.3 %collective-permute-start.11 = (bf16[512,512]{1,0:T(8,128)(2,1)S(1)}, bf16[512,512]{1,0:T(8,128)(2,1)S(1)}, u32[]{:S(2)}, u32[]{:S(2)}) collective-permute-start(bf16[512,512]{1,0:T(8,128)(2,1)S(1)} %collective-permute-done.7.refs_1_), channel_id=1, source_target_pairs={{0,1},{1,0},{2,3},{3,2},{4,5},{5,4},{6,7},{7,6},{8,9},{9,8},{10,11... | collective-permute-start | bytes 1572872 | tf_op jit(solution)/shard_map/tile_matrix/ppermute | solution.py:230
  75.2 2.7 %collective-permute-start.12 = (bf16[512,512]{1,0:T(8,128)(2,1)S(1)}, bf16[512,512]{1,0:T(8,128)(2,1)S(1)}, u32[]{:S(2)}, u32[]{:S(2)}) collective-permute-start(bf16[512,512]{1,0:T(8,128)(2,1)S(1)} %collective-permute-done.8.refs_2_), channel_id=1, source_target_pairs={{0,1},{1,0},{2,3},{3,2},{4,5},{5,4},{6,7},{7,6},{8,9},{9,8},{10,11... | collective-permute-start | bytes 1572872 | tf_op jit(solution)/shard_map/tile_matrix/ppermute | solution.py:230
  75.3 2.9 %collective-permute-start.13 = (bf16[512,512]{1,0:T(8,128)(2,1)S(1)}, bf16[512,512]{1,0:T(8,128)(2,1)S(1)}, u32[]{:S(2)}, u32[]{:S(2)}) collective-permute-start(bf16[512,512]{1,0:T(8,128)(2,1)S(1)} %collective-permute-done.9.refs_3_), channel_id=1, source_target_pairs={{0,1},{1,0},{2,3},{3,2},{4,5},{5,4},{6,7},{7,6},{8,9},{9,8},{10,11... | collective-permute-start | bytes 1572872 | tf_op jit(solution)/shard_map/tile_matrix/ppermute | solution.py:230
  75.9 8.5 %collective-permute-start.18 = (bf16[32,64,128]{2,1,0:T(8,128)(2,1)S(1)}, bf16[32,64,128]{2,1,0:T(8,128)(2,1)S(1)}, u32[]{:S(2)}, u32[]{:S(2)}) collective-permute-start(bf16[32,64,128]{2,1,0:T(8,128)(2,1)S(1)} %get-tuple-element.82), channel_id=1, source_target_pairs={{0,1},{1,0},{2,3},{3,2},{4,5},{5,4},{6,7},{7,6},{8,9},{9,8},{10,11... | collective-permute-start | bytes 1572872 | tf_op jit(solution)/shard_map/tile_matrix/ppermute | solution.py:230
  78.3 1.9 %copy-start.5 = (f32[64,512]{1,0:T(8,128)S(1)}, f32[64,512]{1,0:T(8,128)}, u32[]{:S(2)}) copy-start(f32[64,512]{1,0:T(8,128)} %get-tuple-element.85) | copy-start | bytes 393220
  80.3 9.5 %collective-permute-start.19 = (bf16[64,512]{1,0:T(8,128)(2,1)S(1)}, bf16[64,512]{1,0:T(8,128)(2,1)S(1)}, u32[]{:S(2)}, u32[]{:S(2)}) collective-permute-start(bf16[64,512]{1,0:T(8,128)(2,1)S(1)} %fusion.6.refs_8_.refs_0_), channel_id=1, source_target_pairs={{0,1},{1,0},{2,3},{3,2},{4,5},{5,4},{6,7},{7,6},{8,9},{9,8},{10,11... | collective-permute-start | bytes 196616 | tf_op jit(solution)/shard_map/spread/ppermute | solution.py:230
  80.7 5.8 %collective-permute-start.17 = (bf16[64,512]{1,0:T(8,128)(2,1)S(1)}, bf16[64,512]{1,0:T(8,128)(2,1)S(1)}, u32[]{:S(2)}, u32[]{:S(2)}) collective-permute-start(bf16[64,512]{1,0:T(8,128)(2,1)S(1)} %fusion.6.refs_8_.refs_0_), channel_id=1, source_target_pairs={{0,64},{64,128},{128,192},{192,0},{1,65},{65,129},{129,193},{193,1... | collective-permute-start | bytes 196616 | tf_op jit(solution)/shard_map/spread/ppermute | solution.py:234
  81.2 6.5 %collective-permute-start.16 = (bf16[64,512]{1,0:T(8,128)(2,1)S(1)}, bf16[64,512]{1,0:T(8,128)(2,1)S(1)}, u32[]{:S(2)}, u32[]{:S(2)}) collective-permute-start(bf16[64,512]{1,0:T(8,128)(2,1)S(1)} %fusion.6.refs_8_.refs_0_), channel_id=1, source_target_pairs={{0,128},{64,192},{128,0},{192,64},{1,129},{65,193},{129,1},{193,65... | collective-permute-start | bytes 196616 | tf_op jit(solution)/shard_map/spread/ppermute | solution.py:234
  84.3 3.5 %collective-permute-start.15 = (bf16[64,512]{1,0:T(8,128)(2,1)S(1)}, bf16[64,512]{1,0:T(8,128)(2,1)S(1)}, u32[]{:S(2)}, u32[]{:S(2)}) collective-permute-start(bf16[64,512]{1,0:T(8,128)(2,1)S(1)} %fusion.6.refs_8_.refs_0_), channel_id=1, source_target_pairs={{0,192},{64,0},{128,64},{192,128},{1,193},{65,1},{129,65},{193,129... | collective-permute-start | bytes 196616 | tf_op jit(solution)/shard_map/spread/ppermute | solution.py:234
  86.5 19.3 %copy-start = (bf16[512,512]{1,0:T(8,128)(2,1)S(1)}, bf16[512,512]{1,0:T(8,128)(2,1)}, u32[]{:S(2)}) copy-start(bf16[512,512]{1,0:T(8,128)(2,1)} %weight_ref.1) | copy-start | bytes 1572868
  87.8 2.4 %collective-permute-start.20 = (bf16[64,512]{1,0:T(8,128)(2,1)S(1)}, bf16[64,512]{1,0:T(8,128)(2,1)S(1)}, u32[]{:S(2)}, u32[]{:S(2)}) collective-permute-start(bf16[64,512]{1,0:T(8,128)(2,1)S(1)} %collective-permute-done.15.refs_9_.refs_1_), channel_id=1, source_target_pairs={{0,1},{1,0},{2,3},{3,2},{4,5},{5,4},{6,7},{7,6},{8,9},{9,8},{10,11... | collective-permute-start | bytes 196616 | tf_op jit(solution)/shard_map/spread/ppermute | solution.py:230
  89.3 1.3 collective-permute-start.21
  89.3 1.4 collective-permute-start.22
  91.5 19.0 %collective-permute-start.23 = (f32[16,512]{1,0:T(8,128)S(1)}, f32[16,512]{1,0:T(8,128)S(1)}, u32[]{:S(2)}, u32[]{:S(2)}) collective-permute-start(f32[16,512]{1,0:T(8,128)S(1)} %get-tuple-element.70), channel_id=1, source_target_pairs={{0,16},{16,32},{32,48},{48,0},{1,17},{17,33},{33,49},{49,1},{2,18}... | collective-permute-start | bytes 98312 | tf_op jit(solution)/shard_map/spread/ppermute | solution.py:234
  102.1 8.3 %collective-permute-start.24 = (f32[16,512]{1,0:T(8,128)S(1)}, f32[16,512]{1,0:T(8,128)S(1)}, u32[]{:S(2)}, u32[]{:S(2)}) collective-permute-start(f32[16,512]{1,0:T(8,128)S(1)} %get-tuple-element.71), channel_id=1, source_target_pairs={{0,32},{16,48},{32,0},{48,16},{1,33},{17,49},{33,1},{49,17},{2,34}... | collective-permute-start | bytes 98312 | tf_op jit(solution)/shard_map/spread/ppermute | solution.py:234
  104.7 5.7 %collective-permute-start.25 = (f32[16,512]{1,0:T(8,128)S(1)}, f32[16,512]{1,0:T(8,128)S(1)}, u32[]{:S(2)}, u32[]{:S(2)}) collective-permute-start(f32[16,512]{1,0:T(8,128)S(1)} %get-tuple-element.72), channel_id=1, source_target_pairs={{0,48},{16,0},{32,16},{48,32},{1,49},{17,1},{33,17},{49,33},{2,50}... | collective-permute-start | bytes 98312 | tf_op jit(solution)/shard_map/spread/ppermute | solution.py:234
  110.5 31.5 %all-to-all-start.2 = ((bf16[4,512,512]{2,1,0:T(8,128)(2,1)}), bf16[4,512,512]{2,1,0:T(8,128)(2,1)S(1)}, u32[]{:S(2)}, u32[]{:S(2)}) async-start(bf16[4,512,512]{2,1,0:T(8,128)(2,1)} %spread.1), calls=%async_computation.2 | async-start | bytes 4194304 | tf_op jit(solution)/shard_map/sums/all_to_all | solution.py:238
  114.1 8.2 %collective-permute-start.32 = (f32[16,512]{1,0:T(8,128)S(1)}, f32[16,512]{1,0:T(8,128)S(1)}, u32[]{:S(2)}, u32[]{:S(2)}) collective-permute-start(f32[16,512]{1,0:T(8,128)S(1)} %add_add_fusion.refs_0_), channel_id=1, source_target_pairs={{0,2},{2,4},{4,6},{6,8},{8,10},{10,12},{12,14},{14,0},{1,3},{3,5},... | collective-permute-start | bytes 98312 | tf_op jit(solution)/shard_map/sums/ppermute | solution.py:234
  114.9 9.6 %collective-permute-start.31 = (f32[16,512]{1,0:T(8,128)S(1)}, f32[16,512]{1,0:T(8,128)S(1)}, u32[]{:S(2)}, u32[]{:S(2)}) collective-permute-start(f32[16,512]{1,0:T(8,128)S(1)} %add_add_fusion.refs_0_), channel_id=1, source_target_pairs={{0,4},{2,6},{4,8},{6,10},{8,12},{10,14},{12,0},{14,2},{1,5},{3,7},... | collective-permute-start | bytes 98312 | tf_op jit(solution)/shard_map/sums/ppermute | solution.py:234
  115.8 9.7 %collective-permute-start.30 = (f32[16,512]{1,0:T(8,128)S(1)}, f32[16,512]{1,0:T(8,128)S(1)}, u32[]{:S(2)}, u32[]{:S(2)}) collective-permute-start(f32[16,512]{1,0:T(8,128)S(1)} %add_add_fusion.refs_0_), channel_id=1, source_target_pairs={{0,6},{2,8},{4,10},{6,12},{8,14},{10,0},{12,2},{14,4},{1,7},{3,9},... | collective-permute-start | bytes 98312 | tf_op jit(solution)/shard_map/sums/ppermute | solution.py:234
  117.7 7.7 %collective-permute-start.29 = (f32[16,512]{1,0:T(8,128)S(1)}, f32[16,512]{1,0:T(8,128)S(1)}, u32[]{:S(2)}, u32[]{:S(2)}) collective-permute-start(f32[16,512]{1,0:T(8,128)S(1)} %add_add_fusion.refs_0_), channel_id=1, source_target_pairs={{0,8},{2,10},{4,12},{6,14},{8,0},{10,2},{12,4},{14,6},{1,9},{3,11}... | collective-permute-start | bytes 98312 | tf_op jit(solution)/shard_map/sums/ppermute | solution.py:234
  121.1 4.7 %collective-permute-start.28 = (f32[16,512]{1,0:T(8,128)S(1)}, f32[16,512]{1,0:T(8,128)S(1)}, u32[]{:S(2)}, u32[]{:S(2)}) collective-permute-start(f32[16,512]{1,0:T(8,128)S(1)} %add_add_fusion.refs_0_), channel_id=1, source_target_pairs={{0,10},{2,12},{4,14},{6,0},{8,2},{10,4},{12,6},{14,8},{1,11},{3,13... | collective-permute-start | bytes 98312 | tf_op jit(solution)/shard_map/sums/ppermute | solution.py:234
  122.3 4.8 %collective-permute-start.27 = (f32[16,512]{1,0:T(8,128)S(1)}, f32[16,512]{1,0:T(8,128)S(1)}, u32[]{:S(2)}, u32[]{:S(2)}) collective-permute-start(f32[16,512]{1,0:T(8,128)S(1)} %add_add_fusion.refs_0_), channel_id=1, source_target_pairs={{0,12},{2,14},{4,0},{6,2},{8,4},{10,6},{12,8},{14,10},{1,13},{3,15... | collective-permute-start | bytes 98312 | tf_op jit(solution)/shard_map/sums/ppermute | solution.py:234
  124.5 3.5 %collective-permute-start.26 = (f32[16,512]{1,0:T(8,128)S(1)}, f32[16,512]{1,0:T(8,128)S(1)}, u32[]{:S(2)}, u32[]{:S(2)}) collective-permute-start(f32[16,512]{1,0:T(8,128)S(1)} %add_add_fusion.refs_0_), channel_id=1, source_target_pairs={{0,14},{2,0},{4,2},{6,4},{8,6},{10,8},{12,10},{14,12},{1,15},{3,1}... | collective-permute-start | bytes 98312 | tf_op jit(solution)/shard_map/sums/ppermute | solution.py:234
  128.6 13.3 %collective-permute-start.35 = (f32[16,512]{1,0:T(8,128)S(1)}, f32[16,512]{1,0:T(8,128)S(1)}, u32[]{:S(2)}, u32[]{:S(2)}) collective-permute-start(f32[16,512]{1,0:T(8,128)S(1)} %share_sum.1), channel_id=1, source_target_pairs={{0,16},{16,32},{32,48},{48,0},{1,17},{17,33},{33,49},{49,1},{2,18}... | collective-permute-start | bytes 98312 | tf_op jit(solution)/shard_map/sums/ppermute | solution.py:234
  130.3 11.6 %collective-permute-start.34 = (f32[16,512]{1,0:T(8,128)S(1)}, f32[16,512]{1,0:T(8,128)S(1)}, u32[]{:S(2)}, u32[]{:S(2)}) collective-permute-start(f32[16,512]{1,0:T(8,128)S(1)} %share_sum.1), channel_id=1, source_target_pairs={{0,32},{16,48},{32,0},{48,16},{1,33},{17,49},{33,1},{49,17},{2,34}... | collective-permute-start | bytes 98312 | tf_op jit(solution)/shard_map/sums/ppermute | solution.py:234
  132.7 9.2 %collective-permute-start.33 = (f32[16,512]{1,0:T(8,128)S(1)}, f32[16,512]{1,0:T(8,128)S(1)}, u32[]{:S(2)}, u32[]{:S(2)}) collective-permute-start(f32[16,512]{1,0:T(8,128)S(1)} %share_sum.1), channel_id=1, source_target_pairs={{0,48},{16,0},{32,16},{48,32},{1,49},{17,1},{33,17},{49,33},{2,50}... | collective-permute-start | bytes 98312 | tf_op jit(solution)/shard_map/sums/ppermute | solution.py:234
  143.0 6.4 %collective-permute-start.36 = (f32[64,512]{1,0:T(8,128)S(1)}, f32[64,512]{1,0:T(8,128)S(1)}, u32[]{:S(2)}, u32[]{:S(2)}) collective-permute-start(f32[64,512]{1,0:T(8,128)S(1)} %pad_maximum_fusion), channel_id=1, source_target_pairs={{0,192},{64,0},{128,64},{192,128},{1,193},{65,1},{129,65},{193,129... | collective-permute-start | bytes 393224 | tf_op jit(solution)/shard_map/sums/ppermute | solution.py:234
  144.6 20.6 %all-to-all-start.3 = ((bf16[8,64,512]{2,1,0:T(8,128)(2,1)}), bf16[8,64,512]{2,1,0:T(8,128)(2,1)S(1)}, u32[]{:S(2)}, u32[]{:S(2)}) async-start(bf16[8,64,512]{2,1,0:T(8,128)(2,1)} %plane_sum.1), calls=%async_computation.3 | async-start | bytes 1048576 | tf_op jit(solution)/shard_map/sums/all_to_all | solution.py:238
  148.1 8.6 %collective-permute-start.38 = (f32[64,512]{1,0:T(8,128)S(1)}, f32[64,512]{1,0:T(8,128)S(1)}, u32[]{:S(2)}, u32[]{:S(2)}) collective-permute-start(f32[64,512]{1,0:T(8,128)S(1)} %pad_maximum_fusion), channel_id=1, source_target_pairs={{0,64},{64,128},{128,192},{192,0},{1,65},{65,129},{129,193},{193,1... | collective-permute-start | bytes 393224 | tf_op jit(solution)/shard_map/sums/ppermute | solution.py:234
  148.2 7.0 %collective-permute-start.37 = (f32[64,512]{1,0:T(8,128)S(1)}, f32[64,512]{1,0:T(8,128)S(1)}, u32[]{:S(2)}, u32[]{:S(2)}) collective-permute-start(f32[64,512]{1,0:T(8,128)S(1)} %pad_maximum_fusion), channel_id=1, source_target_pairs={{0,128},{64,192},{128,0},{192,64},{1,129},{65,193},{129,1},{193,65... | collective-permute-start | bytes 393224 | tf_op jit(solution)/shard_map/sums/ppermute | solution.py:234
  156.7 3.0 %collective-permute-start.39 = (f32[256,512]{1,0:T(8,128)S(1)}, f32[256,512]{1,0:T(8,128)S(1)}, u32[]{:S(2)}, u32[]{:S(2)}) collective-permute-start(f32[256,512]{1,0:T(8,128)S(1)} %constant_dynamic-update-slice_fusion.near_ref), channel_id=1, source_target_pairs={{0,1},{1,0},{2,3},{3,2},{4,5},{5,4},{6,7},{7,6},{8,9},{9,8},{10,11... | collective-permute-start | bytes 1572872 | tf_op jit(solution)/shard_map/sums/ppermute | solution.py:230

commit v6 on v5

--- a/solution.py
+++ b/solution.py
@@ -170,7 +170,7 @@
     for k in range(NC * NX):
         dc, dx = k // NX, k % NX
         place = pl.multiple_of((dc * NX + ((x + dx) & (NX - 1))) * ROWS, ROWS)
-        pre[pl.ds(place, ROWS), :] = pre_refs[k][...]
+        pre[pl.ds(place, ROWS), :] = pre_refs[k][:, :F]
     agg = lax.dot_general(pre[...], weight_ref[...], NT, preferred_element_type=F32).astype(BF)
     size = NZ * ROWS
     for k in range(NY):
@@ -181,14 +181,12 @@
 
 
 def terms_kernel(coord_ref, _, *refs):
-    pieces = NC * NX
-    node_refs, pre_refs = refs[:pieces], refs[pieces : 2 * pieces]
-    out_refs, token_ref, terms = refs[2 * pieces : -2], refs[-2], refs[-1]
+    part_refs, out_refs = refs[: NC * NX], refs[NC * NX : -2]
+    token_ref, terms = refs[-2:]
     token_ref[...] = jnp.zeros_like(token_ref)
-    y, c, x = coord_ref[0], coord_ref[1], coord_ref[2]
-    columns = pl.ds(pl.multiple_of(x * NC * ROWS, NC * ROWS), NC * ROWS)
-    node = jnp.concatenate([ref[:, columns] for ref in node_refs], axis=0)
-    pre = jnp.concatenate([ref[...] for ref in pre_refs], axis=0)
+    y, c = coord_ref[0], coord_ref[1]
+    node = jnp.concatenate([ref[:, F:] for ref in part_refs], axis=0)
+    pre = jnp.concatenate([ref[:, :F] for ref in part_refs], axis=0)
     terms[...] = lax.dot_general(node, pre, TN, preferred_element_type=F32)
     size = ROWS // NY
     for k in range(NY):
@@ -301,11 +299,8 @@
             name="bucket",
         )(pair_owner.T, pair_row.T)
         ends = ends.reshape(NDEV, 2, 2 * CAP)
-        hidden_b, late_nodes = lax.optimization_barrier((hidden_b, node_aggregate))
         ring = gather(hidden_b, "z", NZ).reshape(NZ * ROWS, F)
-        nodes = [late_nodes] + [shift(late_nodes, "x", NX, -k) for k in range(1, NX)]
-        nodes = nodes + [swap(node) for node in nodes]
-        ring, ends, *nodes = lax.optimization_barrier((ring, ends, *nodes))
+        ring, ends = lax.optimization_barrier((ring, ends))
         planes = [ring] + [shift(ring, "y", NY, -k) for k in range(1, NY)]
         received = exchange(ends, ("y", "z", "c")).reshape(NDEV, 4 * CAP)
         near, far, token = count(coord, received)
@@ -337,20 +332,27 @@
             cost_estimate=pl.CostEstimate(flops=3_000_000_000, bytes_accessed=5_000_000, transcendentals=0),
             name="tile_sum",
         )(metas, own_half, other_half)
-        along_x = [shift(pre_grad, "x", NX, -k) for k in range(1, NX)]
+        width = F // NX
+        x = lax.axis_index("x")
+        rows = []
+        for k in range(NX):
+            there = ((x - k) & (NX - 1)) * width
+            node = lax.dynamic_slice_in_dim(node_aggregate, there, width, axis=1)
+            rows.append(jnp.concatenate([pre_grad, node], axis=1))
+        along_x = [shift(rows[k], "x", NX, -k) for k in range(1, NX)]
         *along_x, tile_token = lax.optimization_barrier((*along_x, tile_token))
-        pre_parts = [pre_grad] + along_x
-        pre_parts = pre_parts + [swap(part) for part in pre_parts]
+        parts = [rows[0]] + along_x
+        parts = parts + [swap(part) for part in parts]
         *terms, token = pl.pallas_call(
             terms_kernel,
             out_shape=[jax.ShapeDtypeStruct((ROWS // NY, F), F32)] * NY + [TOKEN],
-            in_specs=[SMEM, ANY] + [VMEM] * (2 * NC * NX),
+            in_specs=[SMEM, ANY] + [VMEM] * (NC * NX),
             out_specs=[VMEM] * (NY + 1),
             scratch_shapes=[pltpu.VMEM((NC * ROWS, F), F32)],
             compiler_params=params(),
             cost_estimate=pl.CostEstimate(flops=1_000_000_000, bytes_accessed=700_000, transcendentals=0),
             name="weight_terms",
-        )(coord, tile_token, *nodes, *pre_parts)
+        )(coord, tile_token, *parts)
         others = [shift(terms[k], "y", NY, k) for k in range(1, NY)]
         send = pl.pallas_call(
             spread_kernel,
@@ -361,7 +363,7 @@
             compiler_params=params(),
             cost_estimate=pl.CostEstimate(flops=5_000_000_000, bytes_accessed=8_000_000, transcendentals=0),
             name="spread",
-        )(coord, token, weight, high, low, *pre_parts)
+        )(coord, token, weight, high, low, *parts)
 
     with jax.named_scope("sums"):
         *others, send = lax.optimization_barrier((*others, send))

time: 169 us -> 152 us (0.90); the launches traced: 166 us -> 152 us
  starting transfers between devices: 84.6 us -> 63.1 us
  waiting for transfers between devices: 31.1 us -> 37.1 us
    ppermute x25 -> x22, starting transfers between devices: 47.7 us -> 36 us  [shift(): lax.ppermute(values, axis, [(i, (i + step) % size) for i in range(size)])]
    all_to_all x4, waiting for transfers between devices: 9.22 us -> 16.7 us  [exchange(): return lax.all_to_all(values, axes, 0, 0, tiled=True)]
    all_to_all x4, starting transfers between devices: 26.6 us -> 21.6 us  [exchange(): return lax.all_to_all(values, axes, 0, 0, tiled=True)]
    ppermute x15 -> x11, starting transfers between devices: 10.3 us -> 5.51 us  [swap(): return lax.ppermute(values, 'c', [(0, 1), (1, 0)])]
    ppermute x25 -> x22, waiting for transfers between devices: 19.2 us -> 17.7 us  [shift(): lax.ppermute(values, axis, [(i, (i + step) % size) for i in range(size)])]
  transfers between devices with their start and end apart: 44 -> 37, of which waited for: 14 -> 12; matrix products, arithmetic and copies ran while one was open for 1% -> 1% of each run, Pallas kernels for 25% -> 28%
where the time goes in v6:
time: 152 us
  starting transfers between devices  63.1 us (42%)
  Pallas kernels  44.7 us (29%)
  waiting for transfers between devices  37.1 us (24%)
  local copies, waits for them, and re-layouts  2.74 us (2%)
  between operations  1.65 us (1%)
    ppermute x22, starting transfers between devices, shift(): lax.ppermute(values, axis, [(i, (i + step) % size) for i in range(size)])  36 us
    all_to_all x4, starting transfers between devices, exchange(): return lax.all_to_all(values, axes, 0, 0, tiled=True)  21.6 us
    pallas_call x1, Pallas kernels, count(): pl.pallas_call(count_kernel, out_shape=[half, half, TOKEN], in_specs=[SME...  20.9 us
    ppermute x22, waiting for transfers between devices, shift(): lax.ppermute(values, axis, [(i, (i + step) % size) for i in range(size)])  17.7 us
    all_to_all x4, waiting for transfers between devices, exchange(): return lax.all_to_all(values, axes, 0, 0, tiled=True)  16.7 us
    pallas_call x1, Pallas kernels, per_device(): pl.pallas_call(bucket_kernel, out_shape=[jax.ShapeDtypeStruct((NDEV, 4 *...  8.24 us
    ppermute x11, starting transfers between devices, swap(): return lax.ppermute(values, 'c', [(0, 1), (1, 0)])  5.51 us
    pallas_call x2, Pallas kernels, pair_grad(): pl.pallas_call(functools.partial(grad_kernel, scale), out_shape=jax.Shape...  4.81 us
  transfers between devices with their start and end apart: 37, of which 12 were waited for; matrix products, arithmetic and copies ran while one was open for 1% of the time, Pallas kernels for 28%

profile of v6, /device:TPU:1, one launch (start us, length us, event | category | flops | bytes accessed | tf_op | source)
XLA Modules:
  0.0 151.8 jit_solution(13980490179595357875)
XLA Ops:
  0.6 1.4 multiply_convert_fusion
  2.0 0.8 broadcast_in_dim.2
  2.8 9.0 %all-to-all-start = ((bf16[8,64,512]{2,1,0:T(8,128)(2,1)}), bf16[8,64,512]{2,1,0:T(8,128)(2,1)S(1)}, u32[]{:S(2)}, u32[]{:S(2)}) async-start(bf16[8,64,512]{2,1,0:T(8,128)(2,1)} %broadcast_in_dim.2), calls=%async_computation | async-start | bytes 1048576 | tf_op jit(solution)/shard_map/pair_exchange/all_to_all | solution.py:236
  11.9 8.2 %bucket.1 = (bf16[64,2048]{1,0:T(8,128)(2,1)S(1)}, f32[8,128]{1,0:T(8,128)}) custom-call(s32[2,8192]{1,0:T(2,128)S(1)} %bitcast.29, s32[2,8192]{1,0:T(2,128)S(1)} %bitcast.30), custom_call_target="tpu_custom_call" | custom-call | flops 8999999488 | bytes 400000 | tf_op jit(solution)/shard_map/pair_exchange/bucket/pallas_call | solution.py:291
  20.2 0.9 reshape.22
  21.0 8.8 %all-to-all-done = bf16[8,64,512]{2,1,0:T(8,128)(2,1)S(1)} async-done(((bf16[8,64,512]{2,1,0:T(8,128)(2,1)}), bf16[8,64,512]{2,1,0:T(8,128)(2,1)S(1)}, u32[]{:S(2)}, u32[]{:S(2)}) %all-to-all-start) | async-done | bytes 524320 | tf_op jit(solution)/shard_map/pair_exchange/all_to_all | solution.py:236
  29.8 5.5 %all-to-all-start.1 = ((bf16[64,2,1024]{2,1,0:T(2,128)(2,1)}), bf16[64,2,1024]{2,1,0:T(2,128)(2,1)S(1)}, u32[]{:S(2)}, u32[]{:S(2)}) async-start(bf16[64,2,1024]{2,1,0:T(2,128)(2,1)} %reshape.22), calls=%async_computation.1 | async-start | bytes 524288 | tf_op jit(solution)/shard_map/pair_exchange/all_to_all | solution.py:236
  36.1 0.5 collective-permute-start.7
  36.7 0.9 dynamic-slice_bitcast_fusion
  37.6 1.4 collective-permute-start.2
  39.0 2.6 %collective-permute-start.1 = (bf16[512,512]{1,0:T(8,128)(2,1)S(1)}, bf16[512,512]{1,0:T(8,128)(2,1)S(1)}, u32[]{:S(2)}, u32[]{:S(2)}) collective-permute-start(bf16[512,512]{1,0:T(8,128)(2,1)S(1)} %bitcast.25), channel_id=1, source_target_pairs={{0,32},{16,48},{32,0},{48,16},{1,33},{17,49},{33,1},{49,17},{2,34}... | collective-permute-start | bytes 1572872 | tf_op jit(solution)/shard_map/pair_exchange/ppermute | solution.py:232
  41.6 1.1 collective-permute-start
  42.6 4.7 %all-to-all-done.1 = bf16[64,2,1024]{2,1,0:T(2,128)(2,1)S(1)} async-done(((bf16[64,2,1024]{2,1,0:T(2,128)(2,1)}), bf16[64,2,1024]{2,1,0:T(2,128)(2,1)S(1)}, u32[]{:S(2)}, u32[]{:S(2)}) %all-to-all-start.1) | async-done | bytes 262176 | tf_op jit(solution)/shard_map/pair_exchange/all_to_all | solution.py:236
  47.4 20.9 %count.1 = (f32[2,256,512]{2,1,0:T(8,128)S(1)}, f32[2,256,512]{2,1,0:T(8,128)S(1)}, f32[8,128]{1,0:T(8,128)S(1)}) custom-call(s32[4]{0:T(128)S(1)} %pad_add_fusion.1.coord_ref, bf16[64,2048]{1,0:T(8,128)(2,1)S(1)} %bitcast.28), custom_call_target="tpu_custom_call" | custom-call | flops 24000000000 | bytes 2400000 | tf_op jit(solution)/shard_map/pair_exchange/count/pallas_call | solution.py:249
  68.4 0.5 collective-permute-start.4
  69.0 0.1 collective-permute-start.5
  69.1 0.4 collective-permute-start.6
  69.6 0.3 collective-permute-start.11
  69.9 2.9 %pair_grad.2.refs_4_ = f32[64,512]{1,0:T(8,128)S(1)} custom-call(f32[8,128]{1,0:T(8,128)S(1)} %get-tuple-element.36._, bf16[64,512]{1,0:T(8,128)(2,1)S(1)} %get-tuple-element.72.own_ref, f32[2,256,512]{2,1,0:T(8,128)S(1)} %get-tuple-element.41.count_ref, bf16[512,512]{1,0:T(8,128)(2,1)S(1)} %bitcast.27, bf16[512,512]{1,0:T(8,128)(2,1)} %collective-permute-done.refs_1_, ...), custom_call_target="tpu_custom_call" | custom-call | flops 3000000000 | bytes 3000000 | tf_op jit(solution)/shard_map/hidden_grad/pair_grad/pallas_call | solution.py:266
  72.9 1.9 %pair_grad.3 = f32[64,512]{1,0:T(8,128)S(1)} custom-call(f32[8,128]{1,0:T(8,128)S(1)} %get-tuple-element.36._, bf16[64,512]{1,0:T(8,128)(2,1)S(1)} %get-tuple-element.72.own_ref, f32[2,256,512]{2,1,0:T(8,128)S(1)} %get-tuple-element.37.count_ref, bf16[512,512]{1,0:T(8,128)(2,1)S(1)} %collective-permute-done.3.refs_0_, ...), custom_call_target="tpu_custom_call" | custom-call | flops 3000000000 | bytes 3000000 | tf_op jit(solution)/shard_map/hidden_grad/pair_grad/pallas_call | solution.py:266
  74.8 0.1 fusion.6
  74.9 2.8 %collective-permute-start.9 = (bf16[64,640]{1,0:T(8,128)(2,1)S(1)}, bf16[64,640]{1,0:T(8,128)(2,1)S(1)}, u32[]{:S(2)}, u32[]{:S(2)}) collective-permute-start(bf16[64,640]{1,0:T(8,128)(2,1)S(1)} %get-tuple-element.65), channel_id=1, source_target_pairs={{0,128},{64,192},{128,0},{192,64},{1,129},{65,193},{129,1},{193,65... | collective-permute-start | bytes 245768 | tf_op jit(solution)/shard_map/spread/ppermute | solution.py:232
  77.8 0.3 collective-permute-start.10
  78.1 2.4 %collective-permute-start.8 = (bf16[64,640]{1,0:T(8,128)(2,1)S(1)}, bf16[64,640]{1,0:T(8,128)(2,1)S(1)}, u32[]{:S(2)}, u32[]{:S(2)}) collective-permute-start(bf16[64,640]{1,0:T(8,128)(2,1)S(1)} %get-tuple-element.67), channel_id=1, source_target_pairs={{0,192},{64,0},{128,64},{192,128},{1,193},{65,1},{129,65},{193,129... | collective-permute-start | bytes 245768 | tf_op jit(solution)/shard_map/spread/ppermute | solution.py:232
  80.4 1.2 collective-permute-start.12
  81.7 2.1 %tile_sum.1 = (bf16[2048,512]{1,0:T(8,128)(2,1)S(1)}, bf16[2048,512]{1,0:T(8,128)(2,1)S(1)}, f32[8,128]{1,0:T(8,128)S(1)}) custom-call(s32[2,65]{1,0:T(2,128)S(1)} %pad_add_fusion.meta_ref, bf16[32,64,128]{2,1,0:T(8,128)(2,1)S(1)} %get-tuple-element.63.own_ref, bf16[32,64,128]{2,1,0:T(8,128)(2,1)S(1)} %collective-permute-done.11.other_ref), custom_call_target="tpu_custom_call" | custom-call | flops 3000000000 | bytes 5000000 | tf_op jit(solution)/shard_map/spread/tile_sum/pallas_call | solution.py:325
  83.8 0.3 collective-permute-start.13
  84.1 0.3 collective-permute-start.14
  84.4 0.2 collective-permute-start.15
  84.6 0.6 collective-permute-done.13.refs_5_
  85.2 0.2 collective-permute-done.14.refs_6_
  85.4 0.3 collective-permute-done.15.refs_7_
  85.7 0.8 weight_terms.1
  86.5 1.0 collective-permute-start.16
  87.6 2.5 %collective-permute-start.17 = (f32[16,512]{1,0:T(8,128)S(1)}, f32[16,512]{1,0:T(8,128)S(1)}, u32[]{:S(2)}, u32[]{:S(2)}) collective-permute-start(f32[16,512]{1,0:T(8,128)S(1)} %get-tuple-element.51), channel_id=1, source_target_pairs={{0,32},{16,48},{32,0},{48,16},{1,33},{17,49},{33,1},{49,17},{2,34}... | collective-permute-start | bytes 98312 | tf_op jit(solution)/shard_map/spread/ppermute | solution.py:232
  90.0 0.9 collective-permute-start.18
  91.0 4.6 %spread.1 = bf16[4,512,512]{2,1,0:T(8,128)(2,1)} custom-call(s32[4]{0:T(128)S(1)} %pad_add_fusion.1.coord_ref, f32[8,128]{1,0:T(8,128)S(1)} %get-tuple-element.53._, bf16[512,512]{1,0:T(8,128)(2,1)S(1)} %copy-done, bf16[2048,512]{1,0:T(8,128)(2,1)S(1)} %get-tuple-element.54.high_ref, bf16[2048,512]{1,0:T(8,128)(2,1)S(1)} %get-tuple-element.55.low_ref, ...), custom_call_target="tpu_custom_call" | custom-call | flops 5000000000 | bytes 8000000 | tf_op jit(solution)/shard_map/spread/spread/pallas_call | solution.py:357
  95.6 3.6 %all-to-all-start.2 = ((bf16[4,512,512]{2,1,0:T(8,128)(2,1)}), bf16[4,512,512]{2,1,0:T(8,128)(2,1)S(1)}, u32[]{:S(2)}, u32[]{:S(2)}) async-start(bf16[4,512,512]{2,1,0:T(8,128)(2,1)} %spread.1), calls=%async_computation.2 | async-start | bytes 4194304 | tf_op jit(solution)/shard_map/sums/all_to_all | solution.py:236
  99.2 0.9 collective-permute-start.25
  100.2 0.9 collective-permute-start.24
  101.1 1.9 %collective-permute-start.23 = (f32[16,512]{1,0:T(8,128)S(1)}, f32[16,512]{1,0:T(8,128)S(1)}, u32[]{:S(2)}, u32[]{:S(2)}) collective-permute-start(f32[16,512]{1,0:T(8,128)S(1)} %add_add_fusion.refs_0_), channel_id=1, source_target_pairs={{0,6},{2,8},{4,10},{6,12},{8,14},{10,0},{12,2},{14,4},{1,7},{3,9},... | collective-permute-start | bytes 98312 | tf_op jit(solution)/shard_map/sums/ppermute | solution.py:232
  103.0 3.5 %collective-permute-start.22 = (f32[16,512]{1,0:T(8,128)S(1)}, f32[16,512]{1,0:T(8,128)S(1)}, u32[]{:S(2)}, u32[]{:S(2)}) collective-permute-start(f32[16,512]{1,0:T(8,128)S(1)} %add_add_fusion.refs_0_), channel_id=1, source_target_pairs={{0,8},{2,10},{4,12},{6,14},{8,0},{10,2},{12,4},{14,6},{1,9},{3,11}... | collective-permute-start | bytes 98312 | tf_op jit(solution)/shard_map/sums/ppermute | solution.py:232
  106.4 1.0 collective-permute-start.21
  107.4 3.1 %collective-permute-start.20 = (f32[16,512]{1,0:T(8,128)S(1)}, f32[16,512]{1,0:T(8,128)S(1)}, u32[]{:S(2)}, u32[]{:S(2)}) collective-permute-start(f32[16,512]{1,0:T(8,128)S(1)} %add_add_fusion.refs_0_), channel_id=1, source_target_pairs={{0,12},{2,14},{4,0},{6,2},{8,4},{10,6},{12,8},{14,10},{1,13},{3,15... | collective-permute-start | bytes 98312 | tf_op jit(solution)/shard_map/sums/ppermute | solution.py:232
  110.5 0.5 collective-permute-start.19
  111.1 2.2 %collective-permute-done.20.refs_2_ = f32[16,512]{1,0:T(8,128)S(1)} collective-permute-done((f32[16,512]{1,0:T(8,128)S(1)}, f32[16,512]{1,0:T(8,128)S(1)}, u32[]{:S(2)}, u32[]{:S(2)}) %collective-permute-start.20) | collective-permute-done | bytes 32800 | tf_op jit(solution)/shard_map/sums/ppermute | solution.py:232
  113.3 0.4 collective-permute-done.19.refs_1_
  113.7 0.6 share_sum.1
  114.3 1.4 collective-permute-start.28
  115.7 2.4 %collective-permute-start.27 = (f32[16,512]{1,0:T(8,128)S(1)}, f32[16,512]{1,0:T(8,128)S(1)}, u32[]{:S(2)}, u32[]{:S(2)}) collective-permute-start(f32[16,512]{1,0:T(8,128)S(1)} %share_sum.1), channel_id=1, source_target_pairs={{0,32},{16,48},{32,0},{48,16},{1,33},{17,49},{33,1},{49,17},{2,34}... | collective-permute-start | bytes 98312 | tf_op jit(solution)/shard_map/sums/ppermute | solution.py:232
  118.1 1.2 collective-permute-start.26
  119.2 7.8 %collective-permute-done.28 = f32[16,512]{1,0:T(8,128)S(1)} collective-permute-done((f32[16,512]{1,0:T(8,128)S(1)}, f32[16,512]{1,0:T(8,128)S(1)}, u32[]{:S(2)}, u32[]{:S(2)}) %collective-permute-start.28) | collective-permute-done | bytes 32800 | tf_op jit(solution)/shard_map/sums/ppermute | solution.py:232
  127.1 1.1 plane_sum.1
  128.1 3.0 %collective-permute-start.29 = (f32[64,512]{1,0:T(8,128)S(1)}, f32[64,512]{1,0:T(8,128)S(1)}, u32[]{:S(2)}, u32[]{:S(2)}) collective-permute-start(f32[64,512]{1,0:T(8,128)S(1)} %pad_maximum_fusion), channel_id=1, source_target_pairs={{0,192},{64,0},{128,64},{192,128},{1,193},{65,1},{129,65},{193,129... | collective-permute-start | bytes 393224 | tf_op jit(solution)/shard_map/sums/ppermute | solution.py:232
  131.1 3.5 %all-to-all-start.3 = ((bf16[8,64,512]{2,1,0:T(8,128)(2,1)}), bf16[8,64,512]{2,1,0:T(8,128)(2,1)S(1)}, u32[]{:S(2)}, u32[]{:S(2)}) async-start(bf16[8,64,512]{2,1,0:T(8,128)(2,1)} %plane_sum.1), calls=%async_computation.3 | async-start | bytes 1048576 | tf_op jit(solution)/shard_map/sums/all_to_all | solution.py:236
  134.6 0.1 collective-permute-start.31
  134.7 1.2 collective-permute-start.30
  135.9 5.8 %collective-permute-done.30 = f32[64,512]{1,0:T(8,128)S(1)} collective-permute-done((f32[64,512]{1,0:T(8,128)S(1)}, f32[64,512]{1,0:T(8,128)S(1)}, u32[]{:S(2)}, u32[]{:S(2)}) %collective-permute-start.30) | collective-permute-done | bytes 131104 | tf_op jit(solution)/shard_map/sums/ppermute | solution.py:232
  141.7 1.4 collective-permute-done.31
  143.1 1.6 %collective-permute-start.32 = (f32[256,512]{1,0:T(8,128)S(1)}, f32[256,512]{1,0:T(8,128)S(1)}, u32[]{:S(2)}, u32[]{:S(2)}) collective-permute-start(f32[256,512]{1,0:T(8,128)S(1)} %constant_dynamic-update-slice_fusion.near_ref), channel_id=1, source_target_pairs={{0,1},{1,0},{2,3},{3,2},{4,5},{5,4},{6,7},{7,6},{8,9},{9,8},{10,11... | collective-permute-start | bytes 1572872 | tf_op jit(solution)/shard_map/sums/ppermute | solution.py:228
  144.7 1.5 %collective-permute-done.32.far_ref = f32[256,512]{1,0:T(8,128)S(1)} collective-permute-done((f32[256,512]{1,0:T(8,128)S(1)}, f32[256,512]{1,0:T(8,128)S(1)}, u32[]{:S(2)}, u32[]{:S(2)}) %collective-permute-start.32) | collective-permute-done | bytes 524320 | tf_op jit(solution)/shard_map/sums/ppermute | solution.py:228
  146.2 1.6 %place.1 = f32[512,512]{1,0:T(8,128)} custom-call(s32[4]{0:T(128)S(1)} %pad_add_fusion.1.coord_ref, f32[256,512]{1,0:T(8,128)S(1)} %constant_dynamic-update-slice_fusion.near_ref, f32[256,512]{1,0:T(8,128)S(1)} %collective-permute-done.32.far_ref), custom_call_target="tpu_custom_call" | custom-call | flops 1000000 | bytes 2000000 | tf_op jit(solution)/shard_map/sums/place/pallas_call | solution.py:399
  147.8 3.2 %all-to-all-done.3 = bf16[8,64,512]{2,1,0:T(8,128)(2,1)S(1)} async-done(((bf16[8,64,512]{2,1,0:T(8,128)(2,1)}), bf16[8,64,512]{2,1,0:T(8,128)(2,1)S(1)}, u32[]{:S(2)}, u32[]{:S(2)}) %all-to-all-start.3) | async-done | bytes 524320 | tf_op jit(solution)/shard_map/sums/all_to_all | solution.py:236
  151.1 0.7 reduce_sum.12
  (55 shorter events, 0.6 us)
Async XLA Ops:
  0.6 11.2 %copy-start.2 = (s32[8192,2]{0,1:T(2,128)S(1)}, s32[8192,2]{0,1:T(2,128)}, u32[]{:S(2)}) copy-start(s32[8192,2]{0,1:T(2,128)} %param.15) | copy-start | bytes 196612
  0.6 11.2 %copy-start.1 = (s32[8192,2]{0,1:T(2,128)S(1)}, s32[8192,2]{0,1:T(2,128)}, u32[]{:S(2)}) copy-start(s32[8192,2]{0,1:T(2,128)} %param.14) | copy-start | bytes 196612
  2.8 27.0 %all-to-all-start = ((bf16[8,64,512]{2,1,0:T(8,128)(2,1)}), bf16[8,64,512]{2,1,0:T(8,128)(2,1)S(1)}, u32[]{:S(2)}, u32[]{:S(2)}) async-start(bf16[8,64,512]{2,1,0:T(8,128)(2,1)} %broadcast_in_dim.2), calls=%async_computation | async-start | bytes 1048576 | tf_op jit(solution)/shard_map/pair_exchange/all_to_all | solution.py:236
  11.9 24.1 %copy-start.6 = (s32[32]{0:T(128)S(1)}, s32[32]{0:T(128)}, u32[]{:S(2)}) copy-start(s32[32]{0:T(128)} %param.12) | copy-start | bytes 388
  11.9 24.1 %copy-start.7 = (s32[32]{0:T(128)S(1)}, s32[32]{0:T(128)}, u32[]{:S(2)}) copy-start(s32[32]{0:T(128)} %param.11) | copy-start | bytes 388
  11.9 24.8 %copy-start.3 = (bf16[32,128,128]{2,1,0:T(8,128)(2,1)S(1)}, bf16[32,128,128]{2,1,0:T(8,128)(2,1)}, u32[]{:S(2)}) copy-start(bf16[32,128,128]{2,1,0:T(8,128)(2,1)} %param.10) | copy-start | bytes 3145732
  29.8 17.5 %all-to-all-start.1 = ((bf16[64,2,1024]{2,1,0:T(2,128)(2,1)}), bf16[64,2,1024]{2,1,0:T(2,128)(2,1)S(1)}, u32[]{:S(2)}, u32[]{:S(2)}) async-start(bf16[64,2,1024]{2,1,0:T(2,128)(2,1)} %reshape.22), calls=%async_computation.1 | async-start | bytes 524288 | tf_op jit(solution)/shard_map/pair_exchange/all_to_all | solution.py:236
  36.1 33.5 %collective-permute-start.7 = (s32[65]{0:T(128)S(1)}, s32[65]{0:T(128)S(1)}, u32[]{:S(2)}, u32[]{:S(2)}) collective-permute-start(s32[65]{0:T(128)S(1)} %pad_add_fusion.2), channel_id=1, source_target_pairs={{0,1},{1,0},{2,3},{3,2},{4,5},{5,4},{6,7},{7,6},{8,9},{9,8},{10,11... | collective-permute-start | bytes 788 | tf_op jit(solution)/shard_map/tile_matrix/ppermute | solution.py:228
  37.5 35.3 %collective-permute-start.3 = (bf16[512,512]{1,0:T(8,128)(2,1)S(1)}, bf16[512,512]{1,0:T(8,128)(2,1)S(1)}, u32[]{:S(2)}, u32[]{:S(2)}) collective-permute-start(bf16[512,512]{1,0:T(8,128)(2,1)S(1)} %bitcast.23), channel_id=1, source_target_pairs={{0,1},{1,0},{2,3},{3,2},{4,5},{5,4},{6,7},{7,6},{8,9},{9,8},{10,11... | collective-permute-start | bytes 1572872 | tf_op jit(solution)/shard_map/tile_matrix/ppermute | solution.py:228
  37.6 30.8 %collective-permute-start.2 = (bf16[512,512]{1,0:T(8,128)(2,1)S(1)}, bf16[512,512]{1,0:T(8,128)(2,1)S(1)}, u32[]{:S(2)}, u32[]{:S(2)}) collective-permute-start(bf16[512,512]{1,0:T(8,128)(2,1)S(1)} %bitcast.24), channel_id=1, source_target_pairs={{0,16},{16,32},{32,48},{48,0},{1,17},{17,33},{33,49},{49,1},{2,18}... | collective-permute-start | bytes 1572872 | tf_op jit(solution)/shard_map/pair_exchange/ppermute | solution.py:232
  39.0 29.4 %collective-permute-start.1 = (bf16[512,512]{1,0:T(8,128)(2,1)S(1)}, bf16[512,512]{1,0:T(8,128)(2,1)S(1)}, u32[]{:S(2)}, u32[]{:S(2)}) collective-permute-start(bf16[512,512]{1,0:T(8,128)(2,1)S(1)} %bitcast.25), channel_id=1, source_target_pairs={{0,32},{16,48},{32,0},{48,16},{1,33},{17,49},{33,1},{49,17},{2,34}... | collective-permute-start | bytes 1572872 | tf_op jit(solution)/shard_map/pair_exchange/ppermute | solution.py:232
  41.6 26.8 %collective-permute-start = (bf16[512,512]{1,0:T(8,128)(2,1)S(1)}, bf16[512,512]{1,0:T(8,128)(2,1)}, u32[]{:S(2)}, u32[]{:S(2)}) collective-permute-start(bf16[512,512]{1,0:T(8,128)(2,1)S(1)} %bitcast.26), channel_id=1, source_target_pairs={{0,48},{16,0},{32,16},{48,32},{1,49},{17,1},{33,17},{49,33},{2,50}... | collective-permute-start | bytes 1572872 | tf_op jit(solution)/shard_map/pair_exchange/ppermute | solution.py:232
  47.4 22.1 %copy-start.5 = (bf16[64,512]{1,0:T(8,128)(2,1)S(1)}, bf16[64,512]{1,0:T(8,128)(2,1)}, u32[]{:S(2)}) copy-start(bf16[64,512]{1,0:T(8,128)(2,1)} %param.8) | copy-start | bytes 196612
  47.4 22.1 %copy-start.4 = (bf16[32,64,128]{2,1,0:T(8,128)(2,1)S(1)}, bf16[32,64,128]{2,1,0:T(8,128)(2,1)}, u32[]{:S(2)}) copy-start(bf16[32,64,128]{2,1,0:T(8,128)(2,1)} %get-tuple-element.62) | copy-start | bytes 1572868
  68.4 4.4 %collective-permute-start.4 = (bf16[512,512]{1,0:T(8,128)(2,1)}, bf16[512,512]{1,0:T(8,128)(2,1)S(1)}, u32[]{:S(2)}, u32[]{:S(2)}) collective-permute-start(bf16[512,512]{1,0:T(8,128)(2,1)} %collective-permute-done.refs_1_), channel_id=1, source_target_pairs={{0,1},{1,0},{2,3},{3,2},{4,5},{5,4},{6,7},{7,6},{8,9},{9,8},{10,11... | collective-permute-start | bytes 1572872 | tf_op jit(solution)/shard_map/tile_matrix/ppermute | solution.py:228
  69.0 3.9 %collective-permute-start.5 = (bf16[512,512]{1,0:T(8,128)(2,1)S(1)}, bf16[512,512]{1,0:T(8,128)(2,1)S(1)}, u32[]{:S(2)}, u32[]{:S(2)}) collective-permute-start(bf16[512,512]{1,0:T(8,128)(2,1)S(1)} %collective-permute-done.1.refs_2_), channel_id=1, source_target_pairs={{0,1},{1,0},{2,3},{3,2},{4,5},{5,4},{6,7},{7,6},{8,9},{9,8},{10,11... | collective-permute-start | bytes 1572872 | tf_op jit(solution)/shard_map/tile_matrix/ppermute | solution.py:228
  69.1 3.8 %collective-permute-start.6 = (bf16[512,512]{1,0:T(8,128)(2,1)S(1)}, bf16[512,512]{1,0:T(8,128)(2,1)S(1)}, u32[]{:S(2)}, u32[]{:S(2)}) collective-permute-start(bf16[512,512]{1,0:T(8,128)(2,1)S(1)} %collective-permute-done.2.refs_3_), channel_id=1, source_target_pairs={{0,1},{1,0},{2,3},{3,2},{4,5},{5,4},{6,7},{7,6},{8,9},{9,8},{10,11... | collective-permute-start | bytes 1572872 | tf_op jit(solution)/shard_map/tile_matrix/ppermute | solution.py:228
  69.6 12.1 %collective-permute-start.11 = (bf16[32,64,128]{2,1,0:T(8,128)(2,1)S(1)}, bf16[32,64,128]{2,1,0:T(8,128)(2,1)S(1)}, u32[]{:S(2)}, u32[]{:S(2)}) collective-permute-start(bf16[32,64,128]{2,1,0:T(8,128)(2,1)S(1)} %copy-done.4), channel_id=1, source_target_pairs={{0,1},{1,0},{2,3},{3,2},{4,5},{5,4},{6,7},{7,6},{8,9},{9,8},{10,11... | collective-permute-start | bytes 1572872 | tf_op jit(solution)/shard_map/tile_matrix/ppermute | solution.py:228
  74.9 8.9 %collective-permute-start.9 = (bf16[64,640]{1,0:T(8,128)(2,1)S(1)}, bf16[64,640]{1,0:T(8,128)(2,1)S(1)}, u32[]{:S(2)}, u32[]{:S(2)}) collective-permute-start(bf16[64,640]{1,0:T(8,128)(2,1)S(1)} %get-tuple-element.65), channel_id=1, source_target_pairs={{0,128},{64,192},{128,0},{192,64},{1,129},{65,193},{129,1},{193,65... | collective-permute-start | bytes 245768 | tf_op jit(solution)/shard_map/spread/ppermute | solution.py:232
  77.8 6.0 %collective-permute-start.10 = (bf16[64,640]{1,0:T(8,128)(2,1)S(1)}, bf16[64,640]{1,0:T(8,128)(2,1)S(1)}, u32[]{:S(2)}, u32[]{:S(2)}) collective-permute-start(bf16[64,640]{1,0:T(8,128)(2,1)S(1)} %get-tuple-element.66), channel_id=1, source_target_pairs={{0,64},{64,128},{128,192},{192,0},{1,65},{65,129},{129,193},{193,1... | collective-permute-start | bytes 245768 | tf_op jit(solution)/shard_map/spread/ppermute | solution.py:232
  78.1 5.7 %collective-permute-start.8 = (bf16[64,640]{1,0:T(8,128)(2,1)S(1)}, bf16[64,640]{1,0:T(8,128)(2,1)S(1)}, u32[]{:S(2)}, u32[]{:S(2)}) collective-permute-start(bf16[64,640]{1,0:T(8,128)(2,1)S(1)} %get-tuple-element.67), channel_id=1, source_target_pairs={{0,192},{64,0},{128,64},{192,128},{1,193},{65,1},{129,65},{193,129... | collective-permute-start | bytes 245768 | tf_op jit(solution)/shard_map/spread/ppermute | solution.py:232
  80.4 4.2 %collective-permute-start.12 = (bf16[64,640]{1,0:T(8,128)(2,1)S(1)}, bf16[64,640]{1,0:T(8,128)(2,1)S(1)}, u32[]{:S(2)}, u32[]{:S(2)}) collective-permute-start(bf16[64,640]{1,0:T(8,128)(2,1)S(1)} %get-tuple-element.64.refs_0_), channel_id=1, source_target_pairs={{0,1},{1,0},{2,3},{3,2},{4,5},{5,4},{6,7},{7,6},{8,9},{9,8},{10,11... | collective-permute-start | bytes 245768 | tf_op jit(solution)/shard_map/spread/ppermute | solution.py:228
  83.8 7.2 %copy-start = (bf16[512,512]{1,0:T(8,128)(2,1)S(1)}, bf16[512,512]{1,0:T(8,128)(2,1)}, u32[]{:S(2)}) copy-start(bf16[512,512]{1,0:T(8,128)(2,1)} %weight_ref.1) | copy-start | bytes 1572868
  83.8 1.4 collective-permute-start.13
  84.1 1.3 collective-permute-start.14
  84.4 1.3 collective-permute-start.15
  86.5 9.0 %collective-permute-start.16 = (f32[16,512]{1,0:T(8,128)S(1)}, f32[16,512]{1,0:T(8,128)S(1)}, u32[]{:S(2)}, u32[]{:S(2)}) collective-permute-start(f32[16,512]{1,0:T(8,128)S(1)} %get-tuple-element.50), channel_id=1, source_target_pairs={{0,16},{16,32},{32,48},{48,0},{1,17},{17,33},{33,49},{49,1},{2,18}... | collective-permute-start | bytes 98312 | tf_op jit(solution)/shard_map/spread/ppermute | solution.py:232
  87.6 8.0 %collective-permute-start.17 = (f32[16,512]{1,0:T(8,128)S(1)}, f32[16,512]{1,0:T(8,128)S(1)}, u32[]{:S(2)}, u32[]{:S(2)}) collective-permute-start(f32[16,512]{1,0:T(8,128)S(1)} %get-tuple-element.51), channel_id=1, source_target_pairs={{0,32},{16,48},{32,0},{48,16},{1,33},{17,49},{33,1},{49,17},{2,34}... | collective-permute-start | bytes 98312 | tf_op jit(solution)/shard_map/spread/ppermute | solution.py:232
  90.0 5.5 %collective-permute-start.18 = (f32[16,512]{1,0:T(8,128)S(1)}, f32[16,512]{1,0:T(8,128)S(1)}, u32[]{:S(2)}, u32[]{:S(2)}) collective-permute-start(f32[16,512]{1,0:T(8,128)S(1)} %get-tuple-element.52), channel_id=1, source_target_pairs={{0,48},{16,0},{32,16},{48,32},{1,49},{17,1},{33,17},{49,33},{2,50}... | collective-permute-start | bytes 98312 | tf_op jit(solution)/shard_map/spread/ppermute | solution.py:232
  95.6 31.5 %all-to-all-start.2 = ((bf16[4,512,512]{2,1,0:T(8,128)(2,1)}), bf16[4,512,512]{2,1,0:T(8,128)(2,1)S(1)}, u32[]{:S(2)}, u32[]{:S(2)}) async-start(bf16[4,512,512]{2,1,0:T(8,128)(2,1)} %spread.1), calls=%async_computation.2 | async-start | bytes 4194304 | tf_op jit(solution)/shard_map/sums/all_to_all | solution.py:236
  99.2 8.2 %collective-permute-start.25 = (f32[16,512]{1,0:T(8,128)S(1)}, f32[16,512]{1,0:T(8,128)S(1)}, u32[]{:S(2)}, u32[]{:S(2)}) collective-permute-start(f32[16,512]{1,0:T(8,128)S(1)} %add_add_fusion.refs_0_), channel_id=1, source_target_pairs={{0,2},{2,4},{4,6},{6,8},{8,10},{10,12},{12,14},{14,0},{1,3},{3,5},... | collective-permute-start | bytes 98312 | tf_op jit(solution)/shard_map/sums/ppermute | solution.py:232
  100.2 10.4 %collective-permute-start.24 = (f32[16,512]{1,0:T(8,128)S(1)}, f32[16,512]{1,0:T(8,128)S(1)}, u32[]{:S(2)}, u32[]{:S(2)}) collective-permute-start(f32[16,512]{1,0:T(8,128)S(1)} %add_add_fusion.refs_0_), channel_id=1, source_target_pairs={{0,4},{2,6},{4,8},{6,10},{8,12},{10,14},{12,0},{14,2},{1,5},{3,7},... | collective-permute-start | bytes 98312 | tf_op jit(solution)/shard_map/sums/ppermute | solution.py:232
  101.1 10.0 %collective-permute-start.23 = (f32[16,512]{1,0:T(8,128)S(1)}, f32[16,512]{1,0:T(8,128)S(1)}, u32[]{:S(2)}, u32[]{:S(2)}) collective-permute-start(f32[16,512]{1,0:T(8,128)S(1)} %add_add_fusion.refs_0_), channel_id=1, source_target_pairs={{0,6},{2,8},{4,10},{6,12},{8,14},{10,0},{12,2},{14,4},{1,7},{3,9},... | collective-permute-start | bytes 98312 | tf_op jit(solution)/shard_map/sums/ppermute | solution.py:232
  103.0 8.1 %collective-permute-start.22 = (f32[16,512]{1,0:T(8,128)S(1)}, f32[16,512]{1,0:T(8,128)S(1)}, u32[]{:S(2)}, u32[]{:S(2)}) collective-permute-start(f32[16,512]{1,0:T(8,128)S(1)} %add_add_fusion.refs_0_), channel_id=1, source_target_pairs={{0,8},{2,10},{4,12},{6,14},{8,0},{10,2},{12,4},{14,6},{1,9},{3,11}... | collective-permute-start | bytes 98312 | tf_op jit(solution)/shard_map/sums/ppermute | solution.py:232
  106.4 4.6 %collective-permute-start.21 = (f32[16,512]{1,0:T(8,128)S(1)}, f32[16,512]{1,0:T(8,128)S(1)}, u32[]{:S(2)}, u32[]{:S(2)}) collective-permute-start(f32[16,512]{1,0:T(8,128)S(1)} %add_add_fusion.refs_0_), channel_id=1, source_target_pairs={{0,10},{2,12},{4,14},{6,0},{8,2},{10,4},{12,6},{14,8},{1,11},{3,13... | collective-permute-start | bytes 98312 | tf_op jit(solution)/shard_map/sums/ppermute | solution.py:232
  107.4 5.9 %collective-permute-start.20 = (f32[16,512]{1,0:T(8,128)S(1)}, f32[16,512]{1,0:T(8,128)S(1)}, u32[]{:S(2)}, u32[]{:S(2)}) collective-permute-start(f32[16,512]{1,0:T(8,128)S(1)} %add_add_fusion.refs_0_), channel_id=1, source_target_pairs={{0,12},{2,14},{4,0},{6,2},{8,4},{10,6},{12,8},{14,10},{1,13},{3,15... | collective-permute-start | bytes 98312 | tf_op jit(solution)/shard_map/sums/ppermute | solution.py:232
  110.5 3.2 %collective-permute-start.19 = (f32[16,512]{1,0:T(8,128)S(1)}, f32[16,512]{1,0:T(8,128)S(1)}, u32[]{:S(2)}, u32[]{:S(2)}) collective-permute-start(f32[16,512]{1,0:T(8,128)S(1)} %add_add_fusion.refs_0_), channel_id=1, source_target_pairs={{0,14},{2,0},{4,2},{6,4},{8,6},{10,8},{12,10},{14,12},{1,15},{3,1}... | collective-permute-start | bytes 98312 | tf_op jit(solution)/shard_map/sums/ppermute | solution.py:232
  114.3 12.7 %collective-permute-start.28 = (f32[16,512]{1,0:T(8,128)S(1)}, f32[16,512]{1,0:T(8,128)S(1)}, u32[]{:S(2)}, u32[]{:S(2)}) collective-permute-start(f32[16,512]{1,0:T(8,128)S(1)} %share_sum.1), channel_id=1, source_target_pairs={{0,16},{16,32},{32,48},{48,0},{1,17},{17,33},{33,49},{49,1},{2,18}... | collective-permute-start | bytes 98312 | tf_op jit(solution)/shard_map/sums/ppermute | solution.py:232
  115.7 11.4 %collective-permute-start.27 = (f32[16,512]{1,0:T(8,128)S(1)}, f32[16,512]{1,0:T(8,128)S(1)}, u32[]{:S(2)}, u32[]{:S(2)}) collective-permute-start(f32[16,512]{1,0:T(8,128)S(1)} %share_sum.1), channel_id=1, source_target_pairs={{0,32},{16,48},{32,0},{48,16},{1,33},{17,49},{33,1},{49,17},{2,34}... | collective-permute-start | bytes 98312 | tf_op jit(solution)/shard_map/sums/ppermute | solution.py:232
  118.1 9.0 %collective-permute-start.26 = (f32[16,512]{1,0:T(8,128)S(1)}, f32[16,512]{1,0:T(8,128)S(1)}, u32[]{:S(2)}, u32[]{:S(2)}) collective-permute-start(f32[16,512]{1,0:T(8,128)S(1)} %share_sum.1), channel_id=1, source_target_pairs={{0,48},{16,0},{32,16},{48,32},{1,49},{17,1},{33,17},{49,33},{2,50}... | collective-permute-start | bytes 98312 | tf_op jit(solution)/shard_map/sums/ppermute | solution.py:232
  128.1 7.7 %collective-permute-start.29 = (f32[64,512]{1,0:T(8,128)S(1)}, f32[64,512]{1,0:T(8,128)S(1)}, u32[]{:S(2)}, u32[]{:S(2)}) collective-permute-start(f32[64,512]{1,0:T(8,128)S(1)} %pad_maximum_fusion), channel_id=1, source_target_pairs={{0,192},{64,0},{128,64},{192,128},{1,193},{65,1},{129,65},{193,129... | collective-permute-start | bytes 393224 | tf_op jit(solution)/shard_map/sums/ppermute | solution.py:232
  131.1 20.0 %all-to-all-start.3 = ((bf16[8,64,512]{2,1,0:T(8,128)(2,1)}), bf16[8,64,512]{2,1,0:T(8,128)(2,1)S(1)}, u32[]{:S(2)}, u32[]{:S(2)}) async-start(bf16[8,64,512]{2,1,0:T(8,128)(2,1)} %plane_sum.1), calls=%async_computation.3 | async-start | bytes 1048576 | tf_op jit(solution)/shard_map/sums/all_to_all | solution.py:236
  134.6 8.5 %collective-permute-start.31 = (f32[64,512]{1,0:T(8,128)S(1)}, f32[64,512]{1,0:T(8,128)S(1)}, u32[]{:S(2)}, u32[]{:S(2)}) collective-permute-start(f32[64,512]{1,0:T(8,128)S(1)} %pad_maximum_fusion), channel_id=1, source_target_pairs={{0,64},{64,128},{128,192},{192,0},{1,65},{65,129},{129,193},{193,1... | collective-permute-start | bytes 393224 | tf_op jit(solution)/shard_map/sums/ppermute | solution.py:232
  134.7 7.0 %collective-permute-start.30 = (f32[64,512]{1,0:T(8,128)S(1)}, f32[64,512]{1,0:T(8,128)S(1)}, u32[]{:S(2)}, u32[]{:S(2)}) collective-permute-start(f32[64,512]{1,0:T(8,128)S(1)} %pad_maximum_fusion), channel_id=1, source_target_pairs={{0,128},{64,192},{128,0},{192,64},{1,129},{65,193},{129,1},{193,65... | collective-permute-start | bytes 393224 | tf_op jit(solution)/shard_map/sums/ppermute | solution.py:232
  143.1 3.1 %collective-permute-start.32 = (f32[256,512]{1,0:T(8,128)S(1)}, f32[256,512]{1,0:T(8,128)S(1)}, u32[]{:S(2)}, u32[]{:S(2)}) collective-permute-start(f32[256,512]{1,0:T(8,128)S(1)} %constant_dynamic-update-slice_fusion.near_ref), channel_id=1, source_target_pairs={{0,1},{1,0},{2,3},{3,2},{4,5},{5,4},{6,7},{7,6},{8,9},{9,8},{10,11... | collective-permute-start | bytes 1572872 | tf_op jit(solution)/shard_map/sums/ppermute | solution.py:228

commit v7 on v6

--- a/solution.py
+++ b/solution.py
@@ -138,7 +138,7 @@
     out_ref[...] = total
 
 
-def tiles_kernel(meta_ref, own_ref, other_ref, high_ref, low_ref, token_ref, acc):
+def tiles_kernel(meta_ref, own_ref, other_ref, sum_ref, token_ref, acc):
     token_ref[...] = jnp.zeros_like(token_ref)
     slots = own_ref.shape[0]
     acc[...] = jnp.zeros_like(acc)
@@ -155,16 +155,13 @@
 
     def split(k, carry):
         rows = pl.ds(pl.multiple_of(k * 128, 128), 128)
-        value = acc[rows, :]
-        high = value.astype(BF)
-        high_ref[rows, :] = high
-        low_ref[rows, :] = (value - high.astype(F32)).astype(BF)
+        sum_ref[rows, :] = acc[rows, :].astype(BF)
         return carry
 
     lax.fori_loop(0, acc.shape[0] // 128, split, 0)
 
 
-def spread_kernel(coord_ref, _, weight_ref, high_ref, low_ref, *refs):
+def spread_kernel(coord_ref, _, weight_ref, tile_ref, *refs):
     pre_refs, out_ref, pre = refs[: NC * NX], refs[-2], refs[-1]
     x = coord_ref[2]
     for k in range(NC * NX):
@@ -175,8 +172,7 @@
     size = NZ * ROWS
     for k in range(NY):
         rows = slice(k * size, (k + 1) * size)
-        part = jnp.dot(high_ref[rows, :], agg, preferred_element_type=F32)
-        part += jnp.dot(low_ref[rows, :], agg, preferred_element_type=F32)
+        part = jnp.dot(tile_ref[rows, :], agg, preferred_element_type=F32)
         out_ref[k] = part.astype(BF)
 
 
@@ -322,11 +318,11 @@
         pre_grad, metas = lax.optimization_barrier((pre_grad, metas))
 
     with jax.named_scope("spread"):
-        high, low, tile_token = pl.pallas_call(
+        tile_matrix, tile_token = pl.pallas_call(
             tiles_kernel,
-            out_shape=[jax.ShapeDtypeStruct((NY * NZ * ROWS, 512), BF)] * 2 + [TOKEN],
+            out_shape=[jax.ShapeDtypeStruct((NY * NZ * ROWS, 512), BF), TOKEN],
             in_specs=[SMEM, VMEM, VMEM],
-            out_specs=[VMEM] * 3,
+            out_specs=[VMEM] * 2,
             scratch_shapes=[pltpu.VMEM((NY * NZ * ROWS, 512), F32)],
             compiler_params=params(),
             cost_estimate=pl.CostEstimate(flops=3_000_000_000, bytes_accessed=5_000_000, transcendentals=0),
@@ -357,13 +353,13 @@
         send = pl.pallas_call(
             spread_kernel,
             out_shape=jax.ShapeDtypeStruct((NY, NZ * ROWS, F), BF),
-            in_specs=[SMEM, ANY] + [VMEM] * (3 + NC * NX),
+            in_specs=[SMEM, ANY] + [VMEM] * (2 + NC * NX),
             out_specs=VMEM,
             scratch_shapes=[pltpu.VMEM((NC * NX * ROWS, F), BF)],
             compiler_params=params(),
             cost_estimate=pl.CostEstimate(flops=5_000_000_000, bytes_accessed=8_000_000, transcendentals=0),
             name="spread",
-        )(coord, token, weight, high, low, *parts)
+        )(coord, token, weight, tile_matrix, *parts)
 
     with jax.named_scope("sums"):
         *others, send = lax.optimization_barrier((*others, send))

time: 152 us -> 150 us (0.987)
    ppermute x22, starting transfers between devices: 36 us -> 29.7 us  [shift(): lax.ppermute(values, axis, [(i, (i + step) % size) for i in range(size)])]
    ppermute x11, starting transfers between devices: 5.51 us -> 10.3 us  [swap(): return lax.ppermute(values, 'c', [(0, 1), (1, 0)])]
  transfers between devices with their start and end apart: 37 -> 37, of which waited for: 12 -> 16; matrix products, arithmetic and copies ran while one was open for 1% -> 2% of each run, Pallas kernels for 28% -> 28%
where the time goes in v7:
time: 150 us; the launch traced here: 149 us
  starting transfers between devices  62.2 us (41%)
  Pallas kernels  43.3 us (29%)
  waiting for transfers between devices  36.3 us (24%)
  local copies, waits for them, and re-layouts  2.74 us (2%)
  between operations  1.62 us (1%)
    ppermute x22, starting transfers between devices, shift(): lax.ppermute(values, axis, [(i, (i + step) % size) for i in range(size)])  29.7 us
    all_to_all x4, starting transfers between devices, exchange(): return lax.all_to_all(values, axes, 0, 0, tiled=True)  22.2 us
    pallas_call x1, Pallas kernels, count(): pl.pallas_call(count_kernel, out_shape=[half, half, TOKEN], in_specs=[SME...  21 us
    all_to_all x4, waiting for transfers between devices, exchange(): return lax.all_to_all(values, axes, 0, 0, tiled=True)  17.7 us
    ppermute x22, waiting for transfers between devices, shift(): lax.ppermute(values, axis, [(i, (i + step) % size) for i in range(size)])  16.2 us
    ppermute x11, starting transfers between devices, swap(): return lax.ppermute(values, 'c', [(0, 1), (1, 0)])  10.3 us
    pallas_call x1, Pallas kernels, per_device(): pl.pallas_call(bucket_kernel, out_shape=[jax.ShapeDtypeStruct((NDEV, 4 *...  8.24 us
    pallas_call x2, Pallas kernels, pair_grad(): pl.pallas_call(functools.partial(grad_kernel, scale), out_shape=jax.Shape...  4.78 us
  transfers between devices with their start and end apart: 37, of which 16 were waited for; matrix products, arithmetic and copies ran while one was open for 2% of the time, Pallas kernels for 28%

profile of v7, /device:TPU:1, one launch (start us, length us, event | category | flops | bytes accessed | tf_op | source)
XLA Modules:
  0.0 148.6 jit_solution(18262407353881603538)
XLA Ops:
  0.6 1.4 multiply_convert_fusion
  2.0 0.8 broadcast_in_dim.2
  2.8 9.0 %all-to-all-start = ((bf16[8,64,512]{2,1,0:T(8,128)(2,1)}), bf16[8,64,512]{2,1,0:T(8,128)(2,1)S(1)}, u32[]{:S(2)}, u32[]{:S(2)}) async-start(bf16[8,64,512]{2,1,0:T(8,128)(2,1)} %broadcast_in_dim.2), calls=%async_computation | async-start | bytes 1048576 | tf_op jit(solution)/shard_map/pair_exchange/all_to_all | solution.py:232
  11.9 8.2 %bucket.1 = (bf16[64,2048]{1,0:T(8,128)(2,1)S(1)}, f32[8,128]{1,0:T(8,128)}) custom-call(s32[2,8192]{1,0:T(2,128)S(1)} %bitcast.29, s32[2,8192]{1,0:T(2,128)S(1)} %bitcast.30), custom_call_target="tpu_custom_call" | custom-call | flops 8999999488 | bytes 400000 | tf_op jit(solution)/shard_map/pair_exchange/bucket/pallas_call | solution.py:287
  20.2 0.9 reshape.22
  21.0 8.8 %all-to-all-done = bf16[8,64,512]{2,1,0:T(8,128)(2,1)S(1)} async-done(((bf16[8,64,512]{2,1,0:T(8,128)(2,1)}), bf16[8,64,512]{2,1,0:T(8,128)(2,1)S(1)}, u32[]{:S(2)}, u32[]{:S(2)}) %all-to-all-start) | async-done | bytes 524320 | tf_op jit(solution)/shard_map/pair_exchange/all_to_all | solution.py:232
  29.8 5.5 %all-to-all-start.1 = ((bf16[64,2,1024]{2,1,0:T(2,128)(2,1)}), bf16[64,2,1024]{2,1,0:T(2,128)(2,1)S(1)}, u32[]{:S(2)}, u32[]{:S(2)}) async-start(bf16[64,2,1024]{2,1,0:T(2,128)(2,1)} %reshape.22), calls=%async_computation.1 | async-start | bytes 524288 | tf_op jit(solution)/shard_map/pair_exchange/all_to_all | solution.py:232
  36.1 0.5 collective-permute-start.7
  36.7 0.9 dynamic-slice_bitcast_fusion
  37.5 2.7 %collective-permute-start = (bf16[512,512]{1,0:T(8,128)(2,1)S(1)}, bf16[512,512]{1,0:T(8,128)(2,1)S(1)}, u32[]{:S(2)}, u32[]{:S(2)}) collective-permute-start(bf16[512,512]{1,0:T(8,128)(2,1)S(1)} %bitcast.23), channel_id=1, source_target_pairs={{0,48},{16,0},{32,16},{48,32},{1,49},{17,1},{33,17},{49,33},{2,50}... | collective-permute-start | bytes 1572872 | tf_op jit(solution)/shard_map/pair_exchange/ppermute | solution.py:228
  40.2 0.4 collective-permute-start.1
  40.6 0.7 collective-permute-start.2
  41.3 1.0 collective-permute-start.3
  42.3 5.1 %all-to-all-done.1 = bf16[64,2,1024]{2,1,0:T(2,128)(2,1)S(1)} async-done(((bf16[64,2,1024]{2,1,0:T(2,128)(2,1)}), bf16[64,2,1024]{2,1,0:T(2,128)(2,1)S(1)}, u32[]{:S(2)}, u32[]{:S(2)}) %all-to-all-start.1) | async-done | bytes 262176 | tf_op jit(solution)/shard_map/pair_exchange/all_to_all | solution.py:232
  47.4 21.0 %count.1 = (f32[2,256,512]{2,1,0:T(8,128)S(1)}, f32[2,256,512]{2,1,0:T(8,128)S(1)}, f32[8,128]{1,0:T(8,128)S(1)}) custom-call(s32[4]{0:T(128)S(1)} %pad_add_fusion.1.coord_ref, bf16[64,2048]{1,0:T(8,128)(2,1)S(1)} %bitcast.28), custom_call_target="tpu_custom_call" | custom-call | flops 24000000000 | bytes 2400000 | tf_op jit(solution)/shard_map/pair_exchange/count/pallas_call | solution.py:245
  68.4 0.6 collective-permute-start.4
  69.1 0.4 collective-permute-start.6
  69.7 0.3 collective-permute-start.11
  70.0 2.9 %pair_grad.2.refs_4_ = f32[64,512]{1,0:T(8,128)S(1)} custom-call(f32[8,128]{1,0:T(8,128)S(1)} %get-tuple-element.35._, bf16[64,512]{1,0:T(8,128)(2,1)S(1)} %get-tuple-element.70.own_ref, f32[2,256,512]{2,1,0:T(8,128)S(1)} %get-tuple-element.40.count_ref, bf16[512,512]{1,0:T(8,128)(2,1)S(1)} %bitcast.27, bf16[512,512]{1,0:T(8,128)(2,1)S(1)} %collective-permute-done.refs_1_, ...), custom_call_target="tpu_custom_call" | custom-call | flops 3000000000 | bytes 3000000 | tf_op jit(solution)/shard_map/hidden_grad/pair_grad/pallas_call | solution.py:262
  73.0 1.9 %pair_grad.3 = f32[64,512]{1,0:T(8,128)S(1)} custom-call(f32[8,128]{1,0:T(8,128)S(1)} %get-tuple-element.35._, bf16[64,512]{1,0:T(8,128)(2,1)S(1)} %get-tuple-element.70.own_ref, f32[2,256,512]{2,1,0:T(8,128)S(1)} %get-tuple-element.36.count_ref, bf16[512,512]{1,0:T(8,128)(2,1)S(1)} %collective-permute-done.3.refs_0_, ...), custom_call_target="tpu_custom_call" | custom-call | flops 3000000000 | bytes 3000000 | tf_op jit(solution)/shard_map/hidden_grad/pair_grad/pallas_call | solution.py:262
  75.0 1.3 collective-permute-start.10
  76.3 1.5 collective-permute-start.8
  77.7 1.5 %collective-permute-start.9 = (bf16[64,640]{1,0:T(8,128)(2,1)S(1)}, bf16[64,640]{1,0:T(8,128)(2,1)S(1)}, u32[]{:S(2)}, u32[]{:S(2)}) collective-permute-start(bf16[64,640]{1,0:T(8,128)(2,1)S(1)} %get-tuple-element.63), channel_id=1, source_target_pairs={{0,128},{64,192},{128,0},{192,64},{1,129},{65,193},{129,1},{193,65... | collective-permute-start | bytes 245768 | tf_op jit(solution)/shard_map/spread/ppermute | solution.py:228
  79.3 1.2 collective-permute-start.12
  80.5 1.8 %tile_sum.1 = (bf16[2048,512]{1,0:T(8,128)(2,1)S(1)}, f32[8,128]{1,0:T(8,128)S(1)}) custom-call(s32[2,65]{1,0:T(2,128)S(1)} %pad_add_fusion.meta_ref, bf16[32,64,128]{2,1,0:T(8,128)(2,1)S(1)} %get-tuple-element.61.own_ref, bf16[32,64,128]{2,1,0:T(8,128)(2,1)S(1)} %collective-permute-done.11.other_ref), custom_call_target="tpu_custom_call" | custom-call | flops 3000000000 | bytes 5000000 | tf_op jit(solution)/shard_map/spread/tile_sum/pallas_call | solution.py:321
  82.3 0.2 collective-permute-done.9.refs_2_
  82.5 2.1 %collective-permute-start.13 = (bf16[64,640]{1,0:T(8,128)(2,1)S(1)}, bf16[64,640]{1,0:T(8,128)(2,1)S(1)}, u32[]{:S(2)}, u32[]{:S(2)}) collective-permute-start(bf16[64,640]{1,0:T(8,128)(2,1)S(1)} %collective-permute-done.8.refs_1_), channel_id=1, source_target_pairs={{0,1},{1,0},{2,3},{3,2},{4,5},{5,4},{6,7},{7,6},{8,9},{9,8},{10,11... | collective-permute-start | bytes 245768 | tf_op jit(solution)/shard_map/spread/ppermute | solution.py:224
  84.7 0.5 collective-permute-start.15
  85.2 0.4 collective-permute-done.13.refs_5_
  85.6 0.4 collective-permute-done.14.refs_6_
  86.1 0.8 weight_terms.1
  86.9 0.8 collective-permute-start.16
  87.8 2.6 %collective-permute-start.17 = (f32[16,512]{1,0:T(8,128)S(1)}, f32[16,512]{1,0:T(8,128)S(1)}, u32[]{:S(2)}, u32[]{:S(2)}) collective-permute-start(f32[16,512]{1,0:T(8,128)S(1)} %get-tuple-element.50), channel_id=1, source_target_pairs={{0,32},{16,48},{32,0},{48,16},{1,33},{17,49},{33,1},{49,17},{2,34}... | collective-permute-start | bytes 98312 | tf_op jit(solution)/shard_map/spread/ppermute | solution.py:228
  90.4 1.1 collective-permute-start.18
  91.5 3.5 %spread.1 = bf16[4,512,512]{2,1,0:T(8,128)(2,1)} custom-call(s32[4]{0:T(128)S(1)} %pad_add_fusion.1.coord_ref, f32[8,128]{1,0:T(8,128)S(1)} %get-tuple-element.52._, bf16[512,512]{1,0:T(8,128)(2,1)S(1)} %copy-done, bf16[2048,512]{1,0:T(8,128)(2,1)S(1)} %get-tuple-element.53.tile_ref, bf16[64,640]{1,0:T(8,128)(2,1)S(1)} %get-tuple-element.62.refs_0_, ...), custom_call_target="tpu_custom_call" | custom-call | flops 5000000000 | bytes 8000000 | tf_op jit(solution)/shard_map/spread/spread/pallas_call | solution.py:353
  95.0 3.6 %all-to-all-start.2 = ((bf16[4,512,512]{2,1,0:T(8,128)(2,1)}), bf16[4,512,512]{2,1,0:T(8,128)(2,1)S(1)}, u32[]{:S(2)}, u32[]{:S(2)}) async-start(bf16[4,512,512]{2,1,0:T(8,128)(2,1)} %spread.1), calls=%async_computation.2 | async-start | bytes 4194304 | tf_op jit(solution)/shard_map/sums/all_to_all | solution.py:232
  98.6 0.5 collective-permute-start.19
  99.1 1.1 collective-permute-start.20
  100.2 3.3 %collective-permute-start.21 = (f32[16,512]{1,0:T(8,128)S(1)}, f32[16,512]{1,0:T(8,128)S(1)}, u32[]{:S(2)}, u32[]{:S(2)}) collective-permute-start(f32[16,512]{1,0:T(8,128)S(1)} %add_add_fusion.refs_0_), channel_id=1, source_target_pairs={{0,10},{2,12},{4,14},{6,0},{8,2},{10,4},{12,6},{14,8},{1,11},{3,13... | collective-permute-start | bytes 98312 | tf_op jit(solution)/shard_map/sums/ppermute | solution.py:228
  103.5 2.0 %collective-permute-start.22 = (f32[16,512]{1,0:T(8,128)S(1)}, f32[16,512]{1,0:T(8,128)S(1)}, u32[]{:S(2)}, u32[]{:S(2)}) collective-permute-start(f32[16,512]{1,0:T(8,128)S(1)} %add_add_fusion.refs_0_), channel_id=1, source_target_pairs={{0,8},{2,10},{4,12},{6,14},{8,0},{10,2},{12,4},{14,6},{1,9},{3,11}... | collective-permute-start | bytes 98312 | tf_op jit(solution)/shard_map/sums/ppermute | solution.py:228
  105.5 1.6 %collective-permute-start.23 = (f32[16,512]{1,0:T(8,128)S(1)}, f32[16,512]{1,0:T(8,128)S(1)}, u32[]{:S(2)}, u32[]{:S(2)}) collective-permute-start(f32[16,512]{1,0:T(8,128)S(1)} %add_add_fusion.refs_0_), channel_id=1, source_target_pairs={{0,6},{2,8},{4,10},{6,12},{8,14},{10,0},{12,2},{14,4},{1,7},{3,9},... | collective-permute-start | bytes 98312 | tf_op jit(solution)/shard_map/sums/ppermute | solution.py:228
  107.1 2.1 %collective-permute-start.24 = (f32[16,512]{1,0:T(8,128)S(1)}, f32[16,512]{1,0:T(8,128)S(1)}, u32[]{:S(2)}, u32[]{:S(2)}) collective-permute-start(f32[16,512]{1,0:T(8,128)S(1)} %add_add_fusion.refs_0_), channel_id=1, source_target_pairs={{0,4},{2,6},{4,8},{6,10},{8,12},{10,14},{12,0},{14,2},{1,5},{3,7},... | collective-permute-start | bytes 98312 | tf_op jit(solution)/shard_map/sums/ppermute | solution.py:228
  109.3 0.9 collective-permute-done.22.refs_4_
  110.2 1.2 collective-permute-done.23.refs_5_
  111.4 0.6 collective-permute-done.24.refs_6_
  112.0 2.5 %collective-permute-done.25.refs_7_ = f32[16,512]{1,0:T(8,128)S(1)} collective-permute-done((f32[16,512]{1,0:T(8,128)S(1)}, f32[16,512]{1,0:T(8,128)S(1)}, u32[]{:S(2)}, u32[]{:S(2)}) %collective-permute-start.25) | collective-permute-done | bytes 32800 | tf_op jit(solution)/shard_map/sums/ppermute | solution.py:228
  114.5 0.6 share_sum.1
  115.1 2.8 %collective-permute-start.26 = (f32[16,512]{1,0:T(8,128)S(1)}, f32[16,512]{1,0:T(8,128)S(1)}, u32[]{:S(2)}, u32[]{:S(2)}) collective-permute-start(f32[16,512]{1,0:T(8,128)S(1)} %share_sum.1), channel_id=1, source_target_pairs={{0,48},{16,0},{32,16},{48,32},{1,49},{17,1},{33,17},{49,33},{2,50}... | collective-permute-start | bytes 98312 | tf_op jit(solution)/shard_map/sums/ppermute | solution.py:228
  117.9 0.6 collective-permute-start.27
  118.5 0.6 collective-permute-start.28
  119.1 3.9 %collective-permute-done.26 = f32[16,512]{1,0:T(8,128)S(1)} collective-permute-done((f32[16,512]{1,0:T(8,128)S(1)}, f32[16,512]{1,0:T(8,128)S(1)}, u32[]{:S(2)}, u32[]{:S(2)}) %collective-permute-start.26) | collective-permute-done | bytes 32800 | tf_op jit(solution)/shard_map/sums/ppermute | solution.py:228
  123.0 1.5 %collective-permute-done.27 = f32[16,512]{1,0:T(8,128)S(1)} collective-permute-done((f32[16,512]{1,0:T(8,128)S(1)}, f32[16,512]{1,0:T(8,128)S(1)}, u32[]{:S(2)}, u32[]{:S(2)}) %collective-permute-start.27) | collective-permute-done | bytes 32800 | tf_op jit(solution)/shard_map/sums/ppermute | solution.py:228
  124.5 0.6 collective-permute-done.28
  125.1 1.1 plane_sum.1
  126.2 1.3 collective-permute-start.29
  127.4 0.9 collective-permute-start.30
  128.3 4.1 %all-to-all-start.3 = ((bf16[8,64,512]{2,1,0:T(8,128)(2,1)}), bf16[8,64,512]{2,1,0:T(8,128)(2,1)S(1)}, u32[]{:S(2)}, u32[]{:S(2)}) async-start(bf16[8,64,512]{2,1,0:T(8,128)(2,1)} %plane_sum.1), calls=%async_computation.3 | async-start | bytes 1048576 | tf_op jit(solution)/shard_map/sums/all_to_all | solution.py:232
  132.4 0.4 collective-permute-start.31
  132.8 4.7 %collective-permute-done.31 = f32[64,512]{1,0:T(8,128)S(1)} collective-permute-done((f32[64,512]{1,0:T(8,128)S(1)}, f32[64,512]{1,0:T(8,128)S(1)}, u32[]{:S(2)}, u32[]{:S(2)}) %collective-permute-start.31) | collective-permute-done | bytes 131104 | tf_op jit(solution)/shard_map/sums/ppermute | solution.py:228
  137.5 3.5 %collective-permute-start.32 = (f32[256,512]{1,0:T(8,128)S(1)}, f32[256,512]{1,0:T(8,128)S(1)}, u32[]{:S(2)}, u32[]{:S(2)}) collective-permute-start(f32[256,512]{1,0:T(8,128)S(1)} %constant_dynamic-update-slice_fusion.near_ref), channel_id=1, source_target_pairs={{0,1},{1,0},{2,3},{3,2},{4,5},{5,4},{6,7},{7,6},{8,9},{9,8},{10,11... | collective-permute-start | bytes 1572872 | tf_op jit(solution)/shard_map/sums/ppermute | solution.py:224
  141.0 1.5 %collective-permute-done.32.far_ref = f32[256,512]{1,0:T(8,128)S(1)} collective-permute-done((f32[256,512]{1,0:T(8,128)S(1)}, f32[256,512]{1,0:T(8,128)S(1)}, u32[]{:S(2)}, u32[]{:S(2)}) %collective-permute-start.32) | collective-permute-done | bytes 524320 | tf_op jit(solution)/shard_map/sums/ppermute | solution.py:224
  142.5 1.6 %place.1 = f32[512,512]{1,0:T(8,128)} custom-call(s32[4]{0:T(128)S(1)} %pad_add_fusion.1.coord_ref, f32[256,512]{1,0:T(8,128)S(1)} %constant_dynamic-update-slice_fusion.near_ref, f32[256,512]{1,0:T(8,128)S(1)} %collective-permute-done.32.far_ref), custom_call_target="tpu_custom_call" | custom-call | flops 1000000 | bytes 2000000 | tf_op jit(solution)/shard_map/sums/place/pallas_call | solution.py:395
  144.1 3.8 %all-to-all-done.3 = bf16[8,64,512]{2,1,0:T(8,128)(2,1)S(1)} async-done(((bf16[8,64,512]{2,1,0:T(8,128)(2,1)}), bf16[8,64,512]{2,1,0:T(8,128)(2,1)S(1)}, u32[]{:S(2)}, u32[]{:S(2)}) %all-to-all-start.3) | async-done | bytes 524320 | tf_op jit(solution)/shard_map/sums/all_to_all | solution.py:232
  147.9 0.7 reduce_sum.12
  (55 shorter events, 0.9 us)
Async XLA Ops:
  0.6 11.2 %copy-start.1 = (s32[8192,2]{0,1:T(2,128)S(1)}, s32[8192,2]{0,1:T(2,128)}, u32[]{:S(2)}) copy-start(s32[8192,2]{0,1:T(2,128)} %param.14) | copy-start | bytes 196612
  0.6 11.2 %copy-start.2 = (s32[8192,2]{0,1:T(2,128)S(1)}, s32[8192,2]{0,1:T(2,128)}, u32[]{:S(2)}) copy-start(s32[8192,2]{0,1:T(2,128)} %param.15) | copy-start | bytes 196612
  2.8 27.0 %all-to-all-start = ((bf16[8,64,512]{2,1,0:T(8,128)(2,1)}), bf16[8,64,512]{2,1,0:T(8,128)(2,1)S(1)}, u32[]{:S(2)}, u32[]{:S(2)}) async-start(bf16[8,64,512]{2,1,0:T(8,128)(2,1)} %broadcast_in_dim.2), calls=%async_computation | async-start | bytes 1048576 | tf_op jit(solution)/shard_map/pair_exchange/all_to_all | solution.py:232
  11.9 24.1 %copy-start.6 = (s32[32]{0:T(128)S(1)}, s32[32]{0:T(128)}, u32[]{:S(2)}) copy-start(s32[32]{0:T(128)} %param.12) | copy-start | bytes 388
  11.9 24.1 %copy-start.7 = (s32[32]{0:T(128)S(1)}, s32[32]{0:T(128)}, u32[]{:S(2)}) copy-start(s32[32]{0:T(128)} %param.11) | copy-start | bytes 388
  11.9 24.8 %copy-start.3 = (bf16[32,128,128]{2,1,0:T(8,128)(2,1)S(1)}, bf16[32,128,128]{2,1,0:T(8,128)(2,1)}, u32[]{:S(2)}) copy-start(bf16[32,128,128]{2,1,0:T(8,128)(2,1)} %param.10) | copy-start | bytes 3145732
  29.8 17.5 %all-to-all-start.1 = ((bf16[64,2,1024]{2,1,0:T(2,128)(2,1)}), bf16[64,2,1024]{2,1,0:T(2,128)(2,1)S(1)}, u32[]{:S(2)}, u32[]{:S(2)}) async-start(bf16[64,2,1024]{2,1,0:T(2,128)(2,1)} %reshape.22), calls=%async_computation.1 | async-start | bytes 524288 | tf_op jit(solution)/shard_map/pair_exchange/all_to_all | solution.py:232
  36.1 33.6 %collective-permute-start.7 = (s32[65]{0:T(128)S(1)}, s32[65]{0:T(128)S(1)}, u32[]{:S(2)}, u32[]{:S(2)}) collective-permute-start(s32[65]{0:T(128)S(1)} %pad_add_fusion.2), channel_id=1, source_target_pairs={{0,1},{1,0},{2,3},{3,2},{4,5},{5,4},{6,7},{7,6},{8,9},{9,8},{10,11... | collective-permute-start | bytes 788 | tf_op jit(solution)/shard_map/tile_matrix/ppermute | solution.py:224
  37.5 30.9 %collective-permute-start = (bf16[512,512]{1,0:T(8,128)(2,1)S(1)}, bf16[512,512]{1,0:T(8,128)(2,1)S(1)}, u32[]{:S(2)}, u32[]{:S(2)}) collective-permute-start(bf16[512,512]{1,0:T(8,128)(2,1)S(1)} %bitcast.23), channel_id=1, source_target_pairs={{0,48},{16,0},{32,16},{48,32},{1,49},{17,1},{33,17},{49,33},{2,50}... | collective-permute-start | bytes 1572872 | tf_op jit(solution)/shard_map/pair_exchange/ppermute | solution.py:228
  40.2 28.2 %collective-permute-start.1 = (bf16[512,512]{1,0:T(8,128)(2,1)S(1)}, bf16[512,512]{1,0:T(8,128)(2,1)S(1)}, u32[]{:S(2)}, u32[]{:S(2)}) collective-permute-start(bf16[512,512]{1,0:T(8,128)(2,1)S(1)} %bitcast.24), channel_id=1, source_target_pairs={{0,32},{16,48},{32,0},{48,16},{1,33},{17,49},{33,1},{49,17},{2,34}... | collective-permute-start | bytes 1572872 | tf_op jit(solution)/shard_map/pair_exchange/ppermute | solution.py:228
  40.6 27.8 %collective-permute-start.2 = (bf16[512,512]{1,0:T(8,128)(2,1)S(1)}, bf16[512,512]{1,0:T(8,128)(2,1)}, u32[]{:S(2)}, u32[]{:S(2)}) collective-permute-start(bf16[512,512]{1,0:T(8,128)(2,1)S(1)} %bitcast.25), channel_id=1, source_target_pairs={{0,16},{16,32},{32,48},{48,0},{1,17},{17,33},{33,49},{49,1},{2,18}... | collective-permute-start | bytes 1572872 | tf_op jit(solution)/shard_map/pair_exchange/ppermute | solution.py:228
  41.3 31.6 %collective-permute-start.3 = (bf16[512,512]{1,0:T(8,128)(2,1)S(1)}, bf16[512,512]{1,0:T(8,128)(2,1)S(1)}, u32[]{:S(2)}, u32[]{:S(2)}) collective-permute-start(bf16[512,512]{1,0:T(8,128)(2,1)S(1)} %bitcast.26), channel_id=1, source_target_pairs={{0,1},{1,0},{2,3},{3,2},{4,5},{5,4},{6,7},{7,6},{8,9},{9,8},{10,11... | collective-permute-start | bytes 1572872 | tf_op jit(solution)/shard_map/tile_matrix/ppermute | solution.py:224
  47.4 22.2 %copy-start.5 = (bf16[64,512]{1,0:T(8,128)(2,1)S(1)}, bf16[64,512]{1,0:T(8,128)(2,1)}, u32[]{:S(2)}) copy-start(bf16[64,512]{1,0:T(8,128)(2,1)} %param.8) | copy-start | bytes 196612
  47.4 22.2 %copy-start.4 = (bf16[32,64,128]{2,1,0:T(8,128)(2,1)S(1)}, bf16[32,64,128]{2,1,0:T(8,128)(2,1)}, u32[]{:S(2)}) copy-start(bf16[32,64,128]{2,1,0:T(8,128)(2,1)} %get-tuple-element.60) | copy-start | bytes 1572868
  68.4 4.5 %collective-permute-start.4 = (bf16[512,512]{1,0:T(8,128)(2,1)S(1)}, bf16[512,512]{1,0:T(8,128)(2,1)S(1)}, u32[]{:S(2)}, u32[]{:S(2)}) collective-permute-start(bf16[512,512]{1,0:T(8,128)(2,1)S(1)} %collective-permute-done.refs_1_), channel_id=1, source_target_pairs={{0,1},{1,0},{2,3},{3,2},{4,5},{5,4},{6,7},{7,6},{8,9},{9,8},{10,11... | collective-permute-start | bytes 1572872 | tf_op jit(solution)/shard_map/tile_matrix/ppermute | solution.py:224
  69.0 3.9 %collective-permute-start.5 = (bf16[512,512]{1,0:T(8,128)(2,1)S(1)}, bf16[512,512]{1,0:T(8,128)(2,1)S(1)}, u32[]{:S(2)}, u32[]{:S(2)}) collective-permute-start(bf16[512,512]{1,0:T(8,128)(2,1)S(1)} %collective-permute-done.1.refs_2_), channel_id=1, source_target_pairs={{0,1},{1,0},{2,3},{3,2},{4,5},{5,4},{6,7},{7,6},{8,9},{9,8},{10,11... | collective-permute-start | bytes 1572872 | tf_op jit(solution)/shard_map/tile_matrix/ppermute | solution.py:224
  69.1 3.8 %collective-permute-start.6 = (bf16[512,512]{1,0:T(8,128)(2,1)}, bf16[512,512]{1,0:T(8,128)(2,1)S(1)}, u32[]{:S(2)}, u32[]{:S(2)}) collective-permute-start(bf16[512,512]{1,0:T(8,128)(2,1)} %collective-permute-done.2.refs_3_), channel_id=1, source_target_pairs={{0,1},{1,0},{2,3},{3,2},{4,5},{5,4},{6,7},{7,6},{8,9},{9,8},{10,11... | collective-permute-start | bytes 1572872 | tf_op jit(solution)/shard_map/tile_matrix/ppermute | solution.py:224
  69.7 10.9 %collective-permute-start.11 = (bf16[32,64,128]{2,1,0:T(8,128)(2,1)S(1)}, bf16[32,64,128]{2,1,0:T(8,128)(2,1)S(1)}, u32[]{:S(2)}, u32[]{:S(2)}) collective-permute-start(bf16[32,64,128]{2,1,0:T(8,128)(2,1)S(1)} %copy-done.4), channel_id=1, source_target_pairs={{0,1},{1,0},{2,3},{3,2},{4,5},{5,4},{6,7},{7,6},{8,9},{9,8},{10,11... | collective-permute-start | bytes 1572872 | tf_op jit(solution)/shard_map/tile_matrix/ppermute | solution.py:224
  75.0 7.3 %collective-permute-start.10 = (bf16[64,640]{1,0:T(8,128)(2,1)S(1)}, bf16[64,640]{1,0:T(8,128)(2,1)S(1)}, u32[]{:S(2)}, u32[]{:S(2)}) collective-permute-start(bf16[64,640]{1,0:T(8,128)(2,1)S(1)} %get-tuple-element.64), channel_id=1, source_target_pairs={{0,64},{64,128},{128,192},{192,0},{1,65},{65,129},{129,193},{193,1... | collective-permute-start | bytes 245768 | tf_op jit(solution)/shard_map/spread/ppermute | solution.py:228
  76.3 6.0 %collective-permute-start.8 = (bf16[64,640]{1,0:T(8,128)(2,1)S(1)}, bf16[64,640]{1,0:T(8,128)(2,1)S(1)}, u32[]{:S(2)}, u32[]{:S(2)}) collective-permute-start(bf16[64,640]{1,0:T(8,128)(2,1)S(1)} %get-tuple-element.65), channel_id=1, source_target_pairs={{0,192},{64,0},{128,64},{192,128},{1,193},{65,1},{129,65},{193,129... | collective-permute-start | bytes 245768 | tf_op jit(solution)/shard_map/spread/ppermute | solution.py:228
  77.7 4.8 %collective-permute-start.9 = (bf16[64,640]{1,0:T(8,128)(2,1)S(1)}, bf16[64,640]{1,0:T(8,128)(2,1)S(1)}, u32[]{:S(2)}, u32[]{:S(2)}) collective-permute-start(bf16[64,640]{1,0:T(8,128)(2,1)S(1)} %get-tuple-element.63), channel_id=1, source_target_pairs={{0,128},{64,192},{128,0},{192,64},{1,129},{65,193},{129,1},{193,65... | collective-permute-start | bytes 245768 | tf_op jit(solution)/shard_map/spread/ppermute | solution.py:228
  79.3 5.9 %collective-permute-start.12 = (bf16[64,640]{1,0:T(8,128)(2,1)S(1)}, bf16[64,640]{1,0:T(8,128)(2,1)S(1)}, u32[]{:S(2)}, u32[]{:S(2)}) collective-permute-start(bf16[64,640]{1,0:T(8,128)(2,1)S(1)} %get-tuple-element.62.refs_0_), channel_id=1, source_target_pairs={{0,1},{1,0},{2,3},{3,2},{4,5},{5,4},{6,7},{7,6},{8,9},{9,8},{10,11... | collective-permute-start | bytes 245768 | tf_op jit(solution)/shard_map/spread/ppermute | solution.py:224
  82.3 9.2 %copy-start = (bf16[512,512]{1,0:T(8,128)(2,1)S(1)}, bf16[512,512]{1,0:T(8,128)(2,1)}, u32[]{:S(2)}) copy-start(bf16[512,512]{1,0:T(8,128)(2,1)} %weight_ref.1) | copy-start | bytes 1572868
  82.5 3.0 %collective-permute-start.13 = (bf16[64,640]{1,0:T(8,128)(2,1)S(1)}, bf16[64,640]{1,0:T(8,128)(2,1)S(1)}, u32[]{:S(2)}, u32[]{:S(2)}) collective-permute-start(bf16[64,640]{1,0:T(8,128)(2,1)S(1)} %collective-permute-done.8.refs_1_), channel_id=1, source_target_pairs={{0,1},{1,0},{2,3},{3,2},{4,5},{5,4},{6,7},{7,6},{8,9},{9,8},{10,11... | collective-permute-start | bytes 245768 | tf_op jit(solution)/shard_map/spread/ppermute | solution.py:224
  84.7 1.3 collective-permute-start.14
  84.7 1.4 collective-permute-start.15
  86.9 8.1 %collective-permute-start.16 = (f32[16,512]{1,0:T(8,128)S(1)}, f32[16,512]{1,0:T(8,128)S(1)}, u32[]{:S(2)}, u32[]{:S(2)}) collective-permute-start(f32[16,512]{1,0:T(8,128)S(1)} %get-tuple-element.49), channel_id=1, source_target_pairs={{0,16},{16,32},{32,48},{48,0},{1,17},{17,33},{33,49},{49,1},{2,18}... | collective-permute-start | bytes 98312 | tf_op jit(solution)/shard_map/spread/ppermute | solution.py:228
  87.8 7.2 %collective-permute-start.17 = (f32[16,512]{1,0:T(8,128)S(1)}, f32[16,512]{1,0:T(8,128)S(1)}, u32[]{:S(2)}, u32[]{:S(2)}) collective-permute-start(f32[16,512]{1,0:T(8,128)S(1)} %get-tuple-element.50), channel_id=1, source_target_pairs={{0,32},{16,48},{32,0},{48,16},{1,33},{17,49},{33,1},{49,17},{2,34}... | collective-permute-start | bytes 98312 | tf_op jit(solution)/shard_map/spread/ppermute | solution.py:228
  90.4 4.6 %collective-permute-start.18 = (f32[16,512]{1,0:T(8,128)S(1)}, f32[16,512]{1,0:T(8,128)S(1)}, u32[]{:S(2)}, u32[]{:S(2)}) collective-permute-start(f32[16,512]{1,0:T(8,128)S(1)} %get-tuple-element.51), channel_id=1, source_target_pairs={{0,48},{16,0},{32,16},{48,32},{1,49},{17,1},{33,17},{49,33},{2,50}... | collective-permute-start | bytes 98312 | tf_op jit(solution)/shard_map/spread/ppermute | solution.py:228
  95.0 30.1 %all-to-all-start.2 = ((bf16[4,512,512]{2,1,0:T(8,128)(2,1)}), bf16[4,512,512]{2,1,0:T(8,128)(2,1)S(1)}, u32[]{:S(2)}, u32[]{:S(2)}) async-start(bf16[4,512,512]{2,1,0:T(8,128)(2,1)} %spread.1), calls=%async_computation.2 | async-start | bytes 4194304 | tf_op jit(solution)/shard_map/sums/all_to_all | solution.py:232
  98.6 8.5 %collective-permute-start.19 = (f32[16,512]{1,0:T(8,128)S(1)}, f32[16,512]{1,0:T(8,128)S(1)}, u32[]{:S(2)}, u32[]{:S(2)}) collective-permute-start(f32[16,512]{1,0:T(8,128)S(1)} %add_add_fusion.refs_0_), channel_id=1, source_target_pairs={{0,14},{2,0},{4,2},{6,4},{8,6},{10,8},{12,10},{14,12},{1,15},{3,1}... | collective-permute-start | bytes 98312 | tf_op jit(solution)/shard_map/sums/ppermute | solution.py:228
  99.1 10.2 %collective-permute-start.20 = (f32[16,512]{1,0:T(8,128)S(1)}, f32[16,512]{1,0:T(8,128)S(1)}, u32[]{:S(2)}, u32[]{:S(2)}) collective-permute-start(f32[16,512]{1,0:T(8,128)S(1)} %add_add_fusion.refs_0_), channel_id=1, source_target_pairs={{0,12},{2,14},{4,0},{6,2},{8,4},{10,6},{12,8},{14,10},{1,13},{3,15... | collective-permute-start | bytes 98312 | tf_op jit(solution)/shard_map/sums/ppermute | solution.py:228
  100.2 9.1 %collective-permute-start.21 = (f32[16,512]{1,0:T(8,128)S(1)}, f32[16,512]{1,0:T(8,128)S(1)}, u32[]{:S(2)}, u32[]{:S(2)}) collective-permute-start(f32[16,512]{1,0:T(8,128)S(1)} %add_add_fusion.refs_0_), channel_id=1, source_target_pairs={{0,10},{2,12},{4,14},{6,0},{8,2},{10,4},{12,6},{14,8},{1,11},{3,13... | collective-permute-start | bytes 98312 | tf_op jit(solution)/shard_map/sums/ppermute | solution.py:228
  103.5 6.7 %collective-permute-start.22 = (f32[16,512]{1,0:T(8,128)S(1)}, f32[16,512]{1,0:T(8,128)S(1)}, u32[]{:S(2)}, u32[]{:S(2)}) collective-permute-start(f32[16,512]{1,0:T(8,128)S(1)} %add_add_fusion.refs_0_), channel_id=1, source_target_pairs={{0,8},{2,10},{4,12},{6,14},{8,0},{10,2},{12,4},{14,6},{1,9},{3,11}... | collective-permute-start | bytes 98312 | tf_op jit(solution)/shard_map/sums/ppermute | solution.py:228
  105.5 5.9 %collective-permute-start.23 = (f32[16,512]{1,0:T(8,128)S(1)}, f32[16,512]{1,0:T(8,128)S(1)}, u32[]{:S(2)}, u32[]{:S(2)}) collective-permute-start(f32[16,512]{1,0:T(8,128)S(1)} %add_add_fusion.refs_0_), channel_id=1, source_target_pairs={{0,6},{2,8},{4,10},{6,12},{8,14},{10,0},{12,2},{14,4},{1,7},{3,9},... | collective-permute-start | bytes 98312 | tf_op jit(solution)/shard_map/sums/ppermute | solution.py:228
  107.1 4.9 %collective-permute-start.24 = (f32[16,512]{1,0:T(8,128)S(1)}, f32[16,512]{1,0:T(8,128)S(1)}, u32[]{:S(2)}, u32[]{:S(2)}) collective-permute-start(f32[16,512]{1,0:T(8,128)S(1)} %add_add_fusion.refs_0_), channel_id=1, source_target_pairs={{0,4},{2,6},{4,8},{6,10},{8,12},{10,14},{12,0},{14,2},{1,5},{3,7},... | collective-permute-start | bytes 98312 | tf_op jit(solution)/shard_map/sums/ppermute | solution.py:228
  109.2 5.3 %collective-permute-start.25 = (f32[16,512]{1,0:T(8,128)S(1)}, f32[16,512]{1,0:T(8,128)S(1)}, u32[]{:S(2)}, u32[]{:S(2)}) collective-permute-start(f32[16,512]{1,0:T(8,128)S(1)} %add_add_fusion.refs_0_), channel_id=1, source_target_pairs={{0,2},{2,4},{4,6},{6,8},{8,10},{10,12},{12,14},{14,0},{1,3},{3,5},... | collective-permute-start | bytes 98312 | tf_op jit(solution)/shard_map/sums/ppermute | solution.py:228
  115.1 7.9 %collective-permute-start.26 = (f32[16,512]{1,0:T(8,128)S(1)}, f32[16,512]{1,0:T(8,128)S(1)}, u32[]{:S(2)}, u32[]{:S(2)}) collective-permute-start(f32[16,512]{1,0:T(8,128)S(1)} %share_sum.1), channel_id=1, source_target_pairs={{0,48},{16,0},{32,16},{48,32},{1,49},{17,1},{33,17},{49,33},{2,50}... | collective-permute-start | bytes 98312 | tf_op jit(solution)/shard_map/sums/ppermute | solution.py:228
  117.9 6.6 %collective-permute-start.27 = (f32[16,512]{1,0:T(8,128)S(1)}, f32[16,512]{1,0:T(8,128)S(1)}, u32[]{:S(2)}, u32[]{:S(2)}) collective-permute-start(f32[16,512]{1,0:T(8,128)S(1)} %share_sum.1), channel_id=1, source_target_pairs={{0,32},{16,48},{32,0},{48,16},{1,33},{17,49},{33,1},{49,17},{2,34}... | collective-permute-start | bytes 98312 | tf_op jit(solution)/shard_map/sums/ppermute | solution.py:228
  118.5 6.6 %collective-permute-start.28 = (f32[16,512]{1,0:T(8,128)S(1)}, f32[16,512]{1,0:T(8,128)S(1)}, u32[]{:S(2)}, u32[]{:S(2)}) collective-permute-start(f32[16,512]{1,0:T(8,128)S(1)} %share_sum.1), channel_id=1, source_target_pairs={{0,16},{16,32},{32,48},{48,0},{1,17},{17,33},{33,49},{49,1},{2,18}... | collective-permute-start | bytes 98312 | tf_op jit(solution)/shard_map/sums/ppermute | solution.py:228
  126.2 6.6 %collective-permute-start.29 = (f32[64,512]{1,0:T(8,128)S(1)}, f32[64,512]{1,0:T(8,128)S(1)}, u32[]{:S(2)}, u32[]{:S(2)}) collective-permute-start(f32[64,512]{1,0:T(8,128)S(1)} %pad_maximum_fusion), channel_id=1, source_target_pairs={{0,192},{64,0},{128,64},{192,128},{1,193},{65,1},{129,65},{193,129... | collective-permute-start | bytes 393224 | tf_op jit(solution)/shard_map/sums/ppermute | solution.py:228
  127.4 5.3 %collective-permute-start.30 = (f32[64,512]{1,0:T(8,128)S(1)}, f32[64,512]{1,0:T(8,128)S(1)}, u32[]{:S(2)}, u32[]{:S(2)}) collective-permute-start(f32[64,512]{1,0:T(8,128)S(1)} %pad_maximum_fusion), channel_id=1, source_target_pairs={{0,128},{64,192},{128,0},{192,64},{1,129},{65,193},{129,1},{193,65... | collective-permute-start | bytes 393224 | tf_op jit(solution)/shard_map/sums/ppermute | solution.py:228
  128.3 19.6 %all-to-all-start.3 = ((bf16[8,64,512]{2,1,0:T(8,128)(2,1)}), bf16[8,64,512]{2,1,0:T(8,128)(2,1)S(1)}, u32[]{:S(2)}, u32[]{:S(2)}) async-start(bf16[8,64,512]{2,1,0:T(8,128)(2,1)} %plane_sum.1), calls=%async_computation.3 | async-start | bytes 1048576 | tf_op jit(solution)/shard_map/sums/all_to_all | solution.py:232
  132.4 5.1 %collective-permute-start.31 = (f32[64,512]{1,0:T(8,128)S(1)}, f32[64,512]{1,0:T(8,128)S(1)}, u32[]{:S(2)}, u32[]{:S(2)}) collective-permute-start(f32[64,512]{1,0:T(8,128)S(1)} %pad_maximum_fusion), channel_id=1, source_target_pairs={{0,64},{64,128},{128,192},{192,0},{1,65},{65,129},{129,193},{193,1... | collective-permute-start | bytes 393224 | tf_op jit(solution)/shard_map/sums/ppermute | solution.py:228
  137.5 5.0 %collective-permute-start.32 = (f32[256,512]{1,0:T(8,128)S(1)}, f32[256,512]{1,0:T(8,128)S(1)}, u32[]{:S(2)}, u32[]{:S(2)}) collective-permute-start(f32[256,512]{1,0:T(8,128)S(1)} %constant_dynamic-update-slice_fusion.near_ref), channel_id=1, source_target_pairs={{0,1},{1,0},{2,3},{3,2},{4,5},{5,4},{6,7},{7,6},{8,9},{9,8},{10,11... | collective-permute-start | bytes 1572872 | tf_op jit(solution)/shard_map/sums/ppermute | solution.py:224
